TPU v7x, 32 devices: a whole 2x2x4 slice. The times are simulated.
32 devices in a mesh: dp: 8 (over y, x, core), ctx: 4 (over z).
Axes of the slice: x: 2, y: 2, z: 4, core: 2. Of those that a mesh axis runs over, the one named last changes fastest.
Arguments:
- tokens: bfloat16 [8192, 2048], P(('dp', 'ctx')), may hold values from -6 to 6
- span_order: int32 [8, 8], P('dp'), may hold values from 0 to 7, each once within a row
- norm_attn: bfloat16 [2048], P(('dp', 'ctx')), may hold values from 0.5 to 1.5
- w_query: bfloat16 [2048, 2048], P(('dp', 'ctx')), may hold values from -0.125 to 0.125
- w_key: bfloat16 [2048, 256], P(('dp', 'ctx')), may hold values from -0.125 to 0.125
- w_value: bfloat16 [2048, 256], P(('dp', 'ctx')), may hold values from -0.125 to 0.125
- w_out: bfloat16 [2048, 2048], P(('dp', 'ctx')), may hold values from -1.5 to 1.5
- norm_mlp: bfloat16 [2048], P(('dp', 'ctx')), may hold values from 0.5 to 1.5
- w_gate: bfloat16 [2048, 5632], P(('dp', 'ctx')), may hold values from -0.125 to 0.125
- w_up: bfloat16 [2048, 5632], P(('dp', 'ctx')), may hold values from -0.125 to 0.125
- w_down: bfloat16 [5632, 2048], P(('dp', 'ctx')), may hold values from -0.15625 to 0.15625
- out_grad: bfloat16 [8192, 2048], P(('dp', 'ctx')), may hold values from -6 to 6
Outputs:
- layer_out: bfloat16 [8192, 2048], P(('dp', 'ctx'))
- input_grad: float32 [8192, 2048], P(('dp', 'ctx'))
- grad_norm_attn: float32 [2048], P(('dp', 'ctx'))
- grad_query: float32 [2048, 2048], P(('dp', 'ctx'))
- grad_key: float32 [2048, 256], P(('dp', 'ctx'))
- grad_value: float32 [2048, 256], P(('dp', 'ctx'))
- grad_out: float32 [2048, 2048], P(('dp', 'ctx'))
- grad_norm_mlp: float32 [2048], P(('dp', 'ctx'))
- grad_gate: float32 [2048, 5632], P(('dp', 'ctx'))
- grad_up: float32 [2048, 5632], P(('dp', 'ctx'))
- grad_down: float32 [5632, 2048], P(('dp', 'ctx'))
Inputs may be any that keep to these rules, and one draw needn't show every extreme that they name: `span_order`: each row is a permutation of the 8 block numbers of one sequence.
All inputs are finite; a program needn't handle non-finite values.
Results may differ from a plain program's by a relative error of at most 0.018.
Values may be sent and summed in bfloat16 or wider, within the bound.
No kernel may reach another device: no remote copies, remote signals or barrier semaphores. Data moves between devices by JAX's collectives and lax.ppermute only.
A program may use at most 448 MiB of HBM per device.

v0:
```python
import jax
import jax.numpy as jnp
from jax import lax
from jax.sharding import PartitionSpec as P

H = 32
KV = 4
HD = 64


epsilon = 1e-05
rope_base = 10000.0
masked_score = -1e30


def rotate(vectors, positions, head_count, direction_sign):
    half_dim = HD // 2
    frequency = jnp.power(rope_base, -jnp.arange(half_dim, dtype=jnp.float32) / half_dim)
    angles = positions[:, None] * frequency[None, :] * direction_sign
    cosine = jnp.cos(angles)[:, None, :]
    sine_part = jnp.sin(angles)[:, None, :]
    shaped = vectors.reshape(vectors.shape[0], head_count, HD)
    first_half = shaped[..., :half_dim]
    second_half = shaped[..., half_dim:]
    turned = jnp.concatenate(
        [
            first_half * cosine - second_half * sine_part,
            second_half * cosine + first_half * sine_part,
        ],
        axis=-1,
    )
    return turned.reshape(vectors.shape[0], head_count * HD)


def normalize_parts(inputs):
    inverse = lax.rsqrt(jnp.mean(inputs * inputs, axis=-1, keepdims=True) + epsilon)
    return (inputs * inverse, inverse)


def norm_backward(grad_normed, normed, inverse, gain):
    scaled = grad_normed * gain
    gain_grad = jnp.sum(grad_normed * normed, axis=0)
    input_part = inverse * (scaled - normed * jnp.mean(scaled * normed, axis=-1, keepdims=True))
    return (input_part, gain_grad)


def contract_rows(left, right):
    return lax.dot_general(
        left, right, (((0,), (0,)), ((), ())), preferred_element_type=jnp.float32
    )


def contract_cols(left, right):
    return lax.dot_general(
        left, right, (((1,), (1,)), ((), ())), preferred_element_type=jnp.float32
    )


def body(
    tokens,
    span_order,
    norm_attn,
    w_query,
    w_key,
    w_value,
    w_out,
    norm_mlp,
    w_gate,
    w_up,
    w_down,
    out_grad,
):
    row_count = tokens.shape[0]
    span_rows = row_count // 2
    group_size = H // KV
    kv_width = KV * HD
    score_scale = HD ** (-0.5)
    ctx_rank = lax.axis_index("ctx")
    ordering = span_order[0]
    offsets = jnp.arange(span_rows, dtype=jnp.int32)
    key_positions = (ordering[:, None] * span_rows + offsets[None, :]).reshape(-1)
    query_positions = lax.dynamic_slice_in_dim(key_positions, ctx_rank * row_count, row_count)
    visible = jnp.tile(query_positions, group_size)[:, None] >= key_positions[None, :]
    query_angles = query_positions.astype(jnp.float32)

    def forward_group(members):
        queries_group, keys_group, values_group = members
        scores = contract_cols(queries_group, keys_group) * score_scale
        scores = jnp.where(visible, scores, masked_score)
        maximum = jnp.max(scores, axis=-1, keepdims=True)
        exponent = jnp.exp(scores - maximum)
        row_total = jnp.sum(exponent, axis=-1, keepdims=True)
        weights_b = (exponent / row_total).astype(jnp.bfloat16)
        mixed_rows = jnp.dot(weights_b, values_group, preferred_element_type=jnp.float32)
        return (mixed_rows, (maximum + jnp.log(row_total))[:, 0])

    def backward_group(members):
        queries_group, keys_group, values_group, grad_group, mixed_rows, logsum_rows = members
        scores = contract_cols(queries_group, keys_group) * score_scale
        scores = jnp.where(visible, scores, masked_score)
        probabilities = jnp.exp(scores - logsum_rows[:, None])
        grad_prob = contract_cols(grad_group, values_group)
        row_delta = jnp.sum(grad_group.astype(jnp.float32) * mixed_rows, axis=-1, keepdims=True)
        grad_score = (probabilities * (grad_prob - row_delta) * score_scale).astype(jnp.bfloat16)
        grad_queries_group = jnp.dot(grad_score, keys_group, preferred_element_type=jnp.float32)
        grad_keys_group = contract_rows(grad_score, queries_group)
        grad_values_group = contract_rows(probabilities.astype(jnp.bfloat16), grad_group)
        return (grad_queries_group, grad_keys_group, grad_values_group)

    gain_attn, full_query, full_key, full_value, full_out = (
        lax.all_gather(norm_attn, ("dp", "ctx"), axis=0, tiled=True),
        lax.all_gather(w_query, ("dp", "ctx"), axis=0, tiled=True),
        lax.all_gather(w_key, ("dp", "ctx"), axis=0, tiled=True),
        lax.all_gather(w_value, ("dp", "ctx"), axis=0, tiled=True),
        lax.all_gather(w_out, ("dp", "ctx"), axis=0, tiled=True),
    )
    inputs = tokens.astype(jnp.float32)
    normed, inverse = normalize_parts(inputs)
    attn_gain = gain_attn.astype(jnp.float32)
    normed_b = (normed * attn_gain).astype(jnp.bfloat16)
    queries = rotate(
        jnp.dot(normed_b, full_query, preferred_element_type=jnp.float32), query_angles, H, 1.0
    ).astype(jnp.bfloat16)
    keys_local = rotate(
        jnp.dot(normed_b, full_key, preferred_element_type=jnp.float32), query_angles, KV, 1.0
    ).astype(jnp.bfloat16)
    values_local = jnp.dot(normed_b, full_value, preferred_element_type=jnp.float32).astype(
        jnp.bfloat16
    )
    keys_seq, values_seq = (
        lax.all_gather(keys_local, "ctx", axis=0, tiled=True),
        lax.all_gather(values_local, "ctx", axis=0, tiled=True),
    )
    seq_rows = keys_seq.shape[0]
    query_groups = (
        queries.reshape(row_count, KV, group_size, HD)
        .transpose(1, 2, 0, 3)
        .reshape(KV, group_size * row_count, HD)
    )
    key_groups = keys_seq.reshape(seq_rows, KV, HD).transpose(1, 0, 2)
    value_groups = values_seq.reshape(seq_rows, KV, HD).transpose(1, 0, 2)
    mixture, logsum = lax.map(forward_group, (query_groups, key_groups, value_groups))
    attended = (
        mixture.reshape(KV, group_size, row_count, HD)
        .transpose(2, 0, 1, 3)
        .reshape(row_count, H * HD)
        .astype(jnp.bfloat16)
    )
    middle = inputs + jnp.dot(attended, full_out, preferred_element_type=jnp.float32)
    gain_mlp, full_gate, full_up, full_down = (
        lax.all_gather(norm_mlp, ("dp", "ctx"), axis=0, tiled=True),
        lax.all_gather(w_gate, ("dp", "ctx"), axis=0, tiled=True),
        lax.all_gather(w_up, ("dp", "ctx"), axis=0, tiled=True),
        lax.all_gather(w_down, ("dp", "ctx"), axis=0, tiled=True),
    )
    normed_mid, inverse_mid = normalize_parts(middle)
    normed_mid_b = (normed_mid * gain_mlp.astype(jnp.float32)).astype(jnp.bfloat16)
    gate_part = jnp.dot(normed_mid_b, full_gate, preferred_element_type=jnp.float32)
    up_part = jnp.dot(normed_mid_b, full_up, preferred_element_type=jnp.float32)
    hidden = (jax.nn.silu(gate_part) * up_part).astype(jnp.bfloat16)
    output = middle + jnp.dot(hidden, full_down, preferred_element_type=jnp.float32)
    layer_out = output.astype(jnp.bfloat16)
    gain_mlp, full_gate, full_up, full_down = (
        lax.all_gather(norm_mlp, ("dp", "ctx"), axis=0, tiled=True),
        lax.all_gather(w_gate, ("dp", "ctx"), axis=0, tiled=True),
        lax.all_gather(w_up, ("dp", "ctx"), axis=0, tiled=True),
        lax.all_gather(w_down, ("dp", "ctx"), axis=0, tiled=True),
    )
    grad_output = out_grad.astype(jnp.float32)
    grad_output_b = grad_output.astype(jnp.bfloat16)
    grad_hidden = contract_cols(grad_output_b, full_down)
    part_down = contract_rows(hidden, grad_output_b)
    sigmoid_gate = jax.nn.sigmoid(gate_part)
    grad_gate_b = (
        grad_hidden * up_part * sigmoid_gate * (1.0 + gate_part * (1.0 - sigmoid_gate))
    ).astype(jnp.bfloat16)
    grad_up_b = (grad_hidden * gate_part * sigmoid_gate).astype(jnp.bfloat16)
    part_gate = contract_rows(normed_mid_b, grad_gate_b)
    part_up = contract_rows(normed_mid_b, grad_up_b)
    grad_normed_mid = contract_cols(grad_gate_b, full_gate) + contract_cols(grad_up_b, full_up)
    input_part_mid, part_gain_mlp = norm_backward(
        grad_normed_mid, normed_mid, inverse_mid, gain_mlp.astype(jnp.float32)
    )
    grad_middle = grad_output + input_part_mid
    grad_norm_mlp, grad_gate, grad_up, grad_down = (
        lax.psum_scatter(part_gain_mlp, ("dp", "ctx"), scatter_dimension=0, tiled=True),
        lax.psum_scatter(part_gate, ("dp", "ctx"), scatter_dimension=0, tiled=True),
        lax.psum_scatter(part_up, ("dp", "ctx"), scatter_dimension=0, tiled=True),
        lax.psum_scatter(part_down, ("dp", "ctx"), scatter_dimension=0, tiled=True),
    )
    gain_attn, full_query, full_key, full_value, full_out = (
        lax.all_gather(norm_attn, ("dp", "ctx"), axis=0, tiled=True),
        lax.all_gather(w_query, ("dp", "ctx"), axis=0, tiled=True),
        lax.all_gather(w_key, ("dp", "ctx"), axis=0, tiled=True),
        lax.all_gather(w_value, ("dp", "ctx"), axis=0, tiled=True),
        lax.all_gather(w_out, ("dp", "ctx"), axis=0, tiled=True),
    )
    attn_gain = gain_attn.astype(jnp.float32)
    grad_branch = grad_middle.astype(jnp.bfloat16)
    part_out = contract_rows(attended, grad_branch)
    grad_attended = contract_cols(grad_branch, full_out).astype(jnp.bfloat16)
    grad_groups = (
        grad_attended.reshape(row_count, KV, group_size, HD)
        .transpose(1, 2, 0, 3)
        .reshape(KV, group_size * row_count, HD)
    )
    grad_query_groups, grad_key_groups, grad_value_groups = lax.map(
        backward_group, (query_groups, key_groups, value_groups, grad_groups, mixture, logsum)
    )
    grad_keys_seq = grad_key_groups.transpose(1, 0, 2).reshape(seq_rows, kv_width)
    grad_values_seq = grad_value_groups.transpose(1, 0, 2).reshape(seq_rows, kv_width)
    grad_keys_local, grad_values_local = (
        lax.psum_scatter(
            grad_keys_seq.astype(jnp.bfloat16), "ctx", scatter_dimension=0, tiled=True
        ).astype(jnp.float32),
        lax.psum_scatter(
            grad_values_seq.astype(jnp.bfloat16), "ctx", scatter_dimension=0, tiled=True
        ).astype(jnp.float32),
    )
    grad_queries = (
        grad_query_groups.reshape(KV, group_size, row_count, HD)
        .transpose(2, 0, 1, 3)
        .reshape(row_count, H * HD)
    )
    grad_query_b = rotate(grad_queries, query_angles, H, -1.0).astype(jnp.bfloat16)
    grad_key_b = rotate(grad_keys_local, query_angles, KV, -1.0).astype(jnp.bfloat16)
    grad_value_b = grad_values_local.astype(jnp.bfloat16)
    part_query = contract_rows(normed_b, grad_query_b)
    part_key = contract_rows(normed_b, grad_key_b)
    part_value = contract_rows(normed_b, grad_value_b)
    grad_normed = (
        contract_cols(grad_query_b, full_query)
        + contract_cols(grad_key_b, full_key)
        + contract_cols(grad_value_b, full_value)
    )
    input_part, part_gain_attn = norm_backward(grad_normed, normed, inverse, attn_gain)
    input_grad = grad_middle + input_part
    grad_norm_attn, grad_query, grad_key, grad_value, grad_out = (
        lax.psum_scatter(part_gain_attn, ("dp", "ctx"), scatter_dimension=0, tiled=True),
        lax.psum_scatter(part_query, ("dp", "ctx"), scatter_dimension=0, tiled=True),
        lax.psum_scatter(part_key, ("dp", "ctx"), scatter_dimension=0, tiled=True),
        lax.psum_scatter(part_value, ("dp", "ctx"), scatter_dimension=0, tiled=True),
        lax.psum_scatter(part_out, ("dp", "ctx"), scatter_dimension=0, tiled=True),
    )
    return (
        layer_out,
        input_grad,
        grad_norm_attn,
        grad_query,
        grad_key,
        grad_value,
        grad_out,
        grad_norm_mlp,
        grad_gate,
        grad_up,
        grad_down,
    )


def solution(mesh):
    placed = (
        P(("dp", "ctx"), None),
        P("dp", None),
        P(("dp", "ctx")),
        P(("dp", "ctx"), None),
        P(("dp", "ctx"), None),
        P(("dp", "ctx"), None),
        P(("dp", "ctx"), None),
        P(("dp", "ctx")),
        P(("dp", "ctx"), None),
        P(("dp", "ctx"), None),
        P(("dp", "ctx"), None),
        P(("dp", "ctx"), None),
    )
    return jax.shard_map(
        body,
        mesh=mesh,
        in_specs=placed,
        out_specs=(
            P(("dp", "ctx"), None),
            P(("dp", "ctx"), None),
            P(("dp", "ctx")),
            P(("dp", "ctx"), None),
            P(("dp", "ctx"), None),
            P(("dp", "ctx"), None),
            P(("dp", "ctx"), None),
            P(("dp", "ctx")),
            P(("dp", "ctx"), None),
            P(("dp", "ctx"), None),
            P(("dp", "ctx"), None),
        ),
        check_vma=False,
    )
```

profile of v0, /device:TPU:0, one launch (start us, length us, event | category | flops | bytes accessed | tf_op | source)
XLA Modules:
  0.0 4856.4 jit_solution(4440620306847812860)
XLA Ops:
  13.7 42.1 all-reduce.5
  58.5 9.0 all-gather.10.cloned.1.call-done
  69.5 16.0 all_gather.45
  86.8 36.5 all-gather.12.cloned.1.call-done
  125.0 17.1 all_gather.47
  143.7 59.8 %all-gather.8.cloned.1.call-done = bf16[2048,2048]{1,0:T(8,128)(2,1)} async-done(((bf16[64,2048]{1,0:T(8,128)(2,1)}), bf16[2048,2048]{1,0:T(8,128)(2,1)}) %all-gather.8.cloned.1.call-update) | async-done | bytes 8388624 | tf_op jit(solution)/shard_map/all_gather | solution.py:112
  203.4 6.8 fusion.80
  211.7 2.5 copy.54
  215.8 36.0 while.28
  218.0 2.4 fusion.147
  220.4 4.2 fusion.148
  227.0 2.4 fusion.147
  229.4 4.2 fusion.148
  236.0 2.4 fusion.147
  238.4 4.2 fusion.148
  245.0 2.4 fusion.147
  247.4 4.2 fusion.148
  255.7 26.6 all-gather.14.cloned.1.call-done
  282.2 6.2 multiply_reduce_fusion.2
  290.0 138.2 %all-gather.16.cloned.1.call-done = bf16[2048,5632]{1,0:T(8,128)(2,1)} async-done(((bf16[64,5632]{1,0:T(8,128)(2,1)}), bf16[2048,5632]{1,0:T(8,128)(2,1)}) %all-gather.16.cloned.1.call-update) | async-done | bytes 23068688 | tf_op jit(solution)/shard_map/all_gather | solution.py:152
  428.2 13.1 fusion.83
  441.3 132.4 %all-gather.18.cloned.1.call-done = bf16[2048,5632]{1,0:T(8,128)(2,1)} async-done(((bf16[64,5632]{1,0:T(8,128)(2,1)}), bf16[2048,5632]{1,0:T(8,128)(2,1)}) %all-gather.18.cloned.1.call-update) | async-done | bytes 23068688 | tf_op jit(solution)/shard_map/all_gather | solution.py:153
  573.7 13.4 fusion.84
  587.1 132.2 %all-gather.20.cloned.1.call-done = bf16[5632,2048]{1,0:T(8,128)(2,1)} async-done(((bf16[176,2048]{1,0:T(8,128)(2,1)}), bf16[5632,2048]{1,0:T(8,128)(2,1)}) %all-gather.20.cloned.1.call-update) | async-done | bytes 23068688 | tf_op jit(solution)/shard_map/all_gather | solution.py:154
  719.4 18.5 multiply_convert_fusion.1
  737.9 12.5 fusion.85
  750.4 14.7 multiply_reduce_fusion
  765.2 2.8 multiply_add_fusion
  769.3 6.7 convolution_convert_fusion
  780.9 93.8 %while.29 = (s32[]{:T(128)}, f32[4,2048,64]{1,2,0:T(8,128)}, bf16[4,1024,64]{1,2,0:T(8,128)(2,1)}, bf16[4,1024,64]{1,2,0:T(8,128)(2,1)}, bf16[4,2048,64]{2,1,0:T...) while((s32[]{:T(128)}, f32[4,2048,64]{1,2,0:T(8,128)}, ...), condition=%wide.region_9.10_spmd.clone, body=%wide.region_7.9_spmd.clone.sunk | while | flops 1369831424 | bytes 86586728 | solution.py:207
  780.9 5.7 fusion.159
  789.6 6.2 multiply_convert_fusion.6
  795.9 3.3 fusion.161
  800.2 3.4 fusion.163
  804.4 5.6 fusion.159
  813.1 6.3 multiply_convert_fusion.6
  819.4 3.3 fusion.161
  823.7 3.4 fusion.163
  827.9 5.6 fusion.159
  836.6 6.2 multiply_convert_fusion.6
  842.8 3.3 fusion.161
  847.2 3.4 fusion.163
  851.3 5.6 fusion.159
  860.0 6.2 multiply_convert_fusion.6
  866.2 3.3 fusion.161
  870.6 3.4 fusion.163
  875.5 19.2 reduce-scatter.10.cloned.1.call-done
  897.8 19.7 reduce-scatter.12.cloned.1.call-done
  917.5 2.8 fusion.71
  923.8 8.3 fusion.75
  933.7 9.4 fusion.66
  943.2 19.6 fusion.87
  962.8 19.7 fusion.88
  982.8 19.6 fusion.89
  1002.4 6.2 fusion.86
  1008.7 12.2 fusion.58
  1024.4 38.8 all-reduce.4
  1064.3 3.5 fusion.63
  1067.8 127.9 %reduce-scatter.18.cloned.1.call-done = f32[64,256]{1,0:T(8,128)} async-done(((f32[2048,256]{1,0:T(8,128)}), f32[64,256]{1,0:T(8,128)}) %reduce-scatter.18.cloned.1.call-update) | async-done | bytes 65552 | tf_op jit(solution)/shard_map/reduce_scatter | solution.py:242
  1195.7 364.8 %reduce-scatter.14.cloned.1.call-done = f32[64,2048]{1,0:T(8,128)} async-done(((f32[2048,2048]{1,0:T(8,128)}), f32[64,2048]{1,0:T(8,128)}) %reduce-scatter.14.cloned.1.call-update) | async-done | bytes 524304 | tf_op jit(solution)/shard_map/reduce_scatter | solution.py:240
  1560.5 365.1 %reduce-scatter.20.cloned.1.call-done = f32[64,2048]{1,0:T(8,128)} async-done(((f32[2048,2048]{1,0:T(8,128)}), f32[64,2048]{1,0:T(8,128)}) %reduce-scatter.20.cloned.1.call-update) | async-done | bytes 524304 | tf_op jit(solution)/shard_map/reduce_scatter | solution.py:243
  1925.5 973.1 %reduce-scatter.22.cloned.1.call-done = f32[64,5632]{1,0:T(8,128)} async-done(((f32[2048,5632]{1,0:T(8,128)}), f32[64,5632]{1,0:T(8,128)}) %reduce-scatter.22.cloned.1.call-update) | async-done | bytes 1441808 | tf_op jit(solution)/shard_map/reduce_scatter | solution.py:187
  2898.6 975.5 %reduce-scatter.24.cloned.1.call-done = f32[64,5632]{1,0:T(8,128)} async-done(((f32[2048,5632]{1,0:T(8,128)}), f32[64,5632]{1,0:T(8,128)}) %reduce-scatter.24.cloned.1.call-update) | async-done | bytes 1441808 | tf_op jit(solution)/shard_map/reduce_scatter | solution.py:188
  3874.1 975.5 %reduce-scatter.26.cloned.1.call-done = f32[176,2048]{1,0:T(8,128)} async-done(((f32[5632,2048]{1,0:T(8,128)}), f32[176,2048]{1,0:T(8,128)}) %reduce-scatter.26.cloned.1.call-update) | async-done | bytes 1441808 | tf_op jit(solution)/shard_map/reduce_scatter | solution.py:189
  (227 shorter events, 72.5 us)
Async XLA Ops:
  7.2 50.1 %copy-start = (bf16[256,2048]{1,0:T(8,128)(2,1)S(1)}, bf16[256,2048]{1,0:T(8,128)(2,1)}, u32[]{:S(2)}) copy-start(bf16[256,2048]{1,0:T(8,128)(2,1)} %param.16) | copy-start | bytes 3145732
  7.2 60.3 %all-gather.10.cloned.1.call-start = ((), (), s32[]{:S(2)}) async-start(), calls=%async_computation.10 | async-start | bytes 1081344 | tf_op jit(solution)/shard_map/all_gather | solution.py:113
  7.9 115.4 %all-gather.12.cloned.1.call-start = ((), (), s32[]{:S(2)}) async-start(), calls=%async_computation.11 | async-start | bytes 1081344 | tf_op jit(solution)/shard_map/all_gather | solution.py:114
  8.7 194.8 %all-gather.8.cloned.1.call-start = ((), (), s32[]{:S(2)}) async-start(), calls=%async_computation.9 | async-start | bytes 8650752 | tf_op jit(solution)/shard_map/all_gather | solution.py:112
  9.4 272.8 %all-gather.14.cloned.1.call-start = ((), (), s32[]{:S(2)}) async-start(), calls=%async_computation.12 | async-start | bytes 8650752 | tf_op jit(solution)/shard_map/all_gather | solution.py:115
  10.0 418.2 %all-gather.16.cloned.1.call-start = ((), (), s32[]{:S(2)}) async-start(), calls=%async_computation.13 | async-start | bytes 23789568 | tf_op jit(solution)/shard_map/all_gather | solution.py:152
  10.6 563.1 %all-gather.18.cloned.1.call-start = ((), (), s32[]{:S(2)}) async-start(), calls=%async_computation.14 | async-start | bytes 23789568 | tf_op jit(solution)/shard_map/all_gather | solution.py:153
  11.1 708.2 %all-gather.20.cloned.1.call-start = ((), (), s32[]{:S(2)}) async-start(), calls=%async_computation.15 | async-start | bytes 23789568 | tf_op jit(solution)/shard_map/all_gather | solution.py:154
  11.9 882.8 %reduce-scatter.10.cloned.1.call-start = ((), (), s32[]{:S(2)}) async-start(), calls=%async_computation.16 | async-start | bytes 655360 | tf_op jit(solution)/shard_map/reduce_scatter | solution.py:213
  55.8 147.6 %copy-start.20 = (f32[2048]{0:T(1024)}, f32[2048]{0:T(1024)S(1)}, u32[]{:S(2)}) copy-start(f32[2048]{0:T(1024)S(1)} %convert_element_type.108) | copy-start | bytes 24580
  57.6 145.9 %copy-start.25 = (f32[256]{0:T(256)}, f32[256]{0:T(256)S(1)}, u32[]{:S(2)}) copy-start(f32[256]{0:T(256)S(1)} %add_rsqrt_fusion.1) | copy-start | bytes 3076
  282.2 7.5 copy-start.24
  288.4 1.3 copy-start.6
  290.0 283.7 %copy-start.8 = (bf16[256,2048]{1,0:T(8,128)(2,1)}, bf16[256,2048]{1,0:T(8,128)(2,1)S(1)}, u32[]{:S(2)}) copy-start(bf16[256,2048]{1,0:T(8,128)(2,1)S(1)} %multiply_convert_fusion.4) | copy-start | bytes 3145732
  750.4 14.7 copy-start.12
  768.0 1.3 copy-start.4
  780.9 114.7 %copy-start.22 = (f32[256,32]{0,1:T(8,128)S(1)}, f32[256,32]{0,1:T(8,128)}, u32[]{:S(2)}) copy-start(f32[256,32]{0,1:T(8,128)} %get-tuple-element.296) | copy-start | bytes 98308
  780.9 114.7 %copy-start.23 = (f32[256,32]{0,1:T(8,128)S(1)}, f32[256,32]{0,1:T(8,128)}, u32[]{:S(2)}) copy-start(f32[256,32]{0,1:T(8,128)} %get-tuple-element.298) | copy-start | bytes 98308
  780.9 114.8 %copy-start.21 = (f32[2048]{0:T(1024)S(1)}, f32[2048]{0:T(1024)}, u32[]{:S(2)}) copy-start(f32[2048]{0:T(1024)} %copy-done.20) | copy-start | bytes 24580
  780.9 114.8 %copy-start.26 = (f32[256]{0:T(256)S(1)}, f32[256]{0:T(256)}, u32[]{:S(2)}) copy-start(f32[256]{0:T(256)} %copy-done.25) | copy-start | bytes 3076
  780.9 5.7 copy-start.2
  788.0 12.1 slice-start
  789.6 10.5 slice-start.1
  795.9 3.3 copy-start.3
  795.9 3.3 copy-start.16
  799.2 1.0 copy-start.18
  800.1 3.5 copy-start.17
  804.4 5.6 copy-start.2
  811.5 12.2 slice-start
  813.0 10.6 slice-start.1
  819.4 3.3 copy-start.3
  819.4 3.3 copy-start.16
  822.7 1.0 copy-start.18
  823.6 3.5 copy-start.17
  827.9 5.6 copy-start.2
  835.0 12.1 slice-start
  836.5 10.5 slice-start.1
  842.8 3.3 copy-start.3
  842.8 3.3 copy-start.16
  846.1 1.0 copy-start.18
  847.0 3.5 copy-start.17
  851.3 5.6 copy-start.2
  858.4 12.1 slice-start
  860.0 10.5 slice-start.1
  866.2 3.3 copy-start.3
  866.2 3.3 copy-start.16
  870.4 3.5 copy-start.17
  874.7 21.0 copy-start.1
  874.7 42.7 reduce-scatter.12.cloned.1.call-start
  875.5 192.3 %reduce-scatter.16.cloned.1.call-start = ((), (), s32[]{:S(2)}) async-start(), calls=%async_computation.19 | async-start | bytes 2162688 | tf_op jit(solution)/shard_map/reduce_scatter | solution.py:241
  897.8 23.1 copy-start.9
  897.8 297.9 %reduce-scatter.18.cloned.1.call-start = ((), (), s32[]{:S(2)}) async-start(), calls=%async_computation.20 | async-start | bytes 2162688 | tf_op jit(solution)/shard_map/reduce_scatter | solution.py:242
  920.3 640.1 %reduce-scatter.14.cloned.1.call-start = ((), (), s32[]{:S(2)}) async-start(), calls=%async_computation.18 | async-start | bytes 17301504 | tf_op jit(solution)/shard_map/reduce_scatter | solution.py:240
  932.1 1.6 copy-start.5
  932.1 993.4 %reduce-scatter.20.cloned.1.call-start = ((), (), s32[]{:S(2)}) async-start(), calls=%async_computation.21 | async-start | bytes 17301504 | tf_op jit(solution)/shard_map/reduce_scatter | solution.py:243
  943.1 1955.5 %reduce-scatter.22.cloned.1.call-start = ((), (), s32[]{:S(2)}) async-start(), calls=%async_computation.22 | async-start | bytes 47579136 | tf_op jit(solution)/shard_map/reduce_scatter | solution.py:187
  962.8 2911.3 %reduce-scatter.24.cloned.1.call-start = ((), (), s32[]{:S(2)}) async-start(), calls=%async_computation.23 | async-start | bytes 47579136 | tf_op jit(solution)/shard_map/reduce_scatter | solution.py:188
  982.5 3867.1 %reduce-scatter.26.cloned.1.call-start = ((), (), s32[]{:S(2)}) async-start(), calls=%async_computation.24 | async-start | bytes 47579136 | tf_op jit(solution)/shard_map/reduce_scatter | solution.py:189
  1002.4 6.3 copy-start.7
  1002.4 6.3 copy-start.10
  1008.6 12.2 copy-start.13
  1020.9 1.2 copy-start.14
  1020.9 1.2 copy-start.15
  1022.1 2.3 copy-start.27
  (6 other events, 5.2 us)
Sparse Core Ops, SparseCore 0:
  11.0 56.4 all-gather.9
  70.5 52.7 all-gather.11
  126.2 77.1 all-gather.7
  206.2 75.9 all-gather.13
  284.9 143.1 all-gather.15
  430.8 142.8 all-gather.17
  576.5 142.7 all-gather.19
  874.9 19.7 reduce-scatter.9
  897.6 19.8 reduce-scatter.11
  920.2 136.4 reduce-scatter.15
  1059.6 136.0 reduce-scatter.17
  1198.4 362.0 reduce-scatter.13
  1563.3 362.1 reduce-scatter.19
  1928.3 970.2 reduce-scatter.21
  2901.3 972.7 reduce-scatter.23
  3876.8 972.7 reduce-scatter.25
where the time goes:
time: 4860 us
  waiting for transfers between devices  4360 us (90%)
  matrix products  302 us (6%)
  blocking collectives  114 us (2%)
    reduce_scatter x1, waiting for transfers between devices, body(): lax.psum_scatter(part_down, ('dp', 'ctx'), scatter_dimension=0, tiled=True)  976 us
    reduce_scatter x1, waiting for transfers between devices, body(): lax.psum_scatter(part_up, ('dp', 'ctx'), scatter_dimension=0, tiled=True)  976 us
    reduce_scatter x1, waiting for transfers between devices, body(): lax.psum_scatter(part_gate, ('dp', 'ctx'), scatter_dimension=0, tiled=True)  973 us
    reduce_scatter x1, waiting for transfers between devices, body(): lax.psum_scatter(part_out, ('dp', 'ctx'), scatter_dimension=0, tiled=True)  365 us
    reduce_scatter x1, waiting for transfers between devices, body(): lax.psum_scatter(part_query, ('dp', 'ctx'), scatter_dimension=0, tiled=True)  365 us
    all_gather x1, waiting for transfers between devices, body(): lax.all_gather(w_gate, ('dp', 'ctx'), axis=0, tiled=True)  138 us
    all_gather x1, waiting for transfers between devices, body(): lax.all_gather(w_up, ('dp', 'ctx'), axis=0, tiled=True)  132 us
    all_gather x1, waiting for transfers between devices, body(): lax.all_gather(w_down, ('dp', 'ctx'), axis=0, tiled=True)  132 us
  transfers between devices with their start and end apart: 16, of which 15 were waited for; matrix products, arithmetic and copies ran while one was open for 4% of the time, Pallas kernels for 0%

commit v1 on v0

v1 whole, which is shorter than its diff:
```python
import jax
import jax.numpy as jnp
from jax import lax
from jax.sharding import Mesh, PartitionSpec as P

H = 32
KV = 4
HD = 64
TP = 4
GROUP = H // KV

epsilon = 1e-05
rope_base = 10000.0
masked_score = -1e30
bf16 = jnp.bfloat16
f32 = jnp.float32


def dot(left, right):
    return jnp.dot(left, right, preferred_element_type=f32)


def contract_rows(left, right):
    return lax.dot_general(left, right, (((0,), (0,)), ((), ())), preferred_element_type=f32)


def contract_cols(left, right):
    return lax.dot_general(left, right, (((1,), (1,)), ((), ())), preferred_element_type=f32)


def rope_tables(positions):
    half_dim = HD // 2
    frequency = jnp.power(rope_base, -jnp.arange(half_dim, dtype=f32) / half_dim)
    angles = positions.astype(f32)[:, None] * frequency[None, :]
    return jnp.cos(angles)[:, None, :], jnp.sin(angles)[:, None, :]


def rotate(vectors, tables, sign):
    cosine, sine = tables
    sine = sine * sign
    rows, width = vectors.shape
    shaped = vectors.reshape(rows, width // HD, HD)
    first, second = shaped[..., : HD // 2], shaped[..., HD // 2 :]
    turned = jnp.concatenate(
        [first * cosine - second * sine, second * cosine + first * sine], axis=-1
    )
    return turned.reshape(rows, width)


def attend(queries, keys, values, visible):
    rows = queries.shape[0]
    stacked = queries.reshape(rows, GROUP, HD).transpose(1, 0, 2).reshape(GROUP * rows, HD)
    scores = contract_cols(stacked, keys) * HD ** (-0.5)
    scores = jnp.where(visible, scores.reshape(GROUP, rows, -1), masked_score)
    maximum = jnp.max(scores, axis=-1, keepdims=True)
    exponent = jnp.exp(scores - maximum)
    total = jnp.sum(exponent, axis=-1, keepdims=True)
    weights = (exponent / total).astype(bf16).reshape(GROUP * rows, -1)
    mixed = dot(weights, values)
    return mixed, maximum + jnp.log(total)


def attend_back(queries, keys, values, visible, grads, mixed, logsum):
    rows = queries.shape[0]

    def stack(v):
        return v.reshape(rows, GROUP, HD).transpose(1, 0, 2).reshape(GROUP * rows, HD)

    queries, grads = stack(queries), stack(grads)
    scores = contract_cols(queries, keys) * HD ** (-0.5)
    scores = jnp.where(visible, scores.reshape(GROUP, rows, -1), masked_score)
    probabilities = jnp.exp(scores - logsum).reshape(GROUP * rows, -1)
    grad_prob = contract_cols(grads, values)
    delta = jnp.sum(grads.astype(f32) * mixed, axis=-1, keepdims=True)
    grad_score = (probabilities * (grad_prob - delta) * HD ** (-0.5)).astype(bf16)
    grad_queries = dot(grad_score, keys)
    grad_keys = contract_rows(grad_score, queries)
    grad_values = contract_rows(probabilities.astype(bf16), grads)
    return unstack(grad_queries, rows), grad_keys, grad_values


def unstack(v, rows):
    return v.reshape(GROUP, rows, HD).transpose(1, 0, 2).reshape(rows, GROUP * HD)


def make_body(reps, ctxs):
    def swap(v, k):
        if k == 0:
            return v
        if k == 1:
            return lax.ppermute(v, "tx", [(0, 1), (1, 0)])
        if k == 2:
            return lax.ppermute(v, "ty", [(0, 1), (1, 0)])
        return lax.ppermute(v, ("ty", "tx"), [(i, i ^ 3) for i in range(TP)])

    def swap_ctx(v, j):
        if j == 0:
            return v
        return lax.ppermute(v, "ctx", [(i, i ^ j) for i in range(ctxs)])

    def gather(v):
        half = v.shape[0] // 2
        a, b = v[:half], v[half:]
        ax, by = swap(a, 1), swap(b, 2)
        ay, bx = swap(a, 2), swap(b, 1)
        axy, bxy = swap(ax, 2), swap(by, 1)
        return jnp.concatenate([a, b, ax, bx, ay, by, axy, bxy], axis=0)

    def scatter_sum(parts):
        half = parts[0].shape[0] // 2
        a = [p[:half] for p in parts]
        b = [p[half:] for p in parts]
        a3, b3 = swap(a[3].astype(bf16), 2), swap(b[3].astype(bf16), 1)
        a2, b1 = swap(a[2].astype(bf16), 2), swap(b[1].astype(bf16), 1)
        a1 = swap((a[1] + a3).astype(bf16), 1)
        b2 = swap((b[2] + b3).astype(bf16), 2)
        return jnp.concatenate([a[0] + a2 + a1, b[0] + b1 + b2], axis=0)

    def spread_columns(blocks, t):
        out = jnp.zeros_like(blocks)
        for k in range(TP):
            mine = lax.dynamic_index_in_dim(blocks, t ^ k, 0, keepdims=True)
            out = lax.dynamic_update_slice_in_dim(out, swap(mine, k), t ^ k, 0)
        return out.reshape(-1, blocks.shape[2])

    def collect_columns(summed, t):
        blocks = summed.reshape(TP, -1, summed.shape[1])
        out = jnp.zeros_like(blocks)
        for k in range(TP):
            mine = lax.dynamic_index_in_dim(blocks, t ^ k, 0, keepdims=True)
            out = lax.dynamic_update_slice_in_dim(out, swap(mine, k), t ^ k, 0)
        return out.transpose(1, 0, 2)

    def whole(v):
        return lax.all_gather(v, ("rep", "ctx"), axis=0, tiled=True)

    def owned(v):
        v = lax.psum_scatter(v.astype(bf16), "rep", scatter_dimension=0, tiled=True)
        return lax.psum_scatter(v, "ctx", scatter_dimension=0, tiled=True)

    def shuffle(v):
        rows, width = v.shape
        return (
            v.reshape(rows, TP, reps * ctxs, -1).transpose(0, 2, 1, 3).reshape(rows, width)
        )

    def unshuffle(v):
        rows, width = v.shape
        return (
            v.reshape(rows, reps * ctxs, TP, -1).transpose(0, 2, 1, 3).reshape(rows, width)
        )

    def body(
        tokens,
        span_order,
        norm_attn,
        w_query,
        w_key,
        w_value,
        w_out,
        norm_mlp,
        w_gate,
        w_up,
        w_down,
        out_grad,
    ):
        count, width = tokens.shape
        own = w_query.shape[0]
        span = count * ctxs // span_order.shape[1]
        q_cols, kv_cols = GROUP * HD, HD
        t = 2 * lax.axis_index("ty") + lax.axis_index("tx")
        c = lax.axis_index("ctx")

        x_all = gather(shuffle(tokens))
        orders = [swap(span_order, k)[0] for k in range(TP)]
        offsets = jnp.arange(span, dtype=jnp.int32)
        per = count // span

        def block_positions(order, member):
            picked = lax.dynamic_slice_in_dim(order, member * per, per)
            return (picked[:, None] * span + offsets[None, :]).reshape(-1)

        query_positions = [block_positions(order, c) for order in orders]
        key_positions = [
            jnp.concatenate([block_positions(order, c ^ j) for j in range(ctxs)])
            for order in orders
        ]
        visible = [
            q[:, None] >= k[None, :] for q, k in zip(query_positions, key_positions)
        ]
        tables = rope_tables(jnp.concatenate(query_positions))

        gain_attn = norm_attn.astype(f32)[:, None]
        gain_mlp = norm_mlp.astype(f32)[:, None]

        def by_member(w, gain):
            w = (w.astype(f32) * gain).astype(bf16)
            return w.reshape(own, TP, -1).transpose(1, 0, 2)

        blocks = jnp.concatenate(
            [by_member(w, gain_attn) for w in (w_query, w_key, w_value)], axis=2
        )
        qkv = whole(spread_columns(blocks, t))
        out = whole(w_out)
        gate = whole(spread_columns(by_member(w_gate, gain_mlp), t))
        up = whole(spread_columns(by_member(w_up, gain_mlp), t))
        down = whole(w_down)

        g_all = gather(out_grad)

        x32 = x_all.astype(f32)
        inverse_all = lax.rsqrt(jnp.mean(x32 * x32, axis=-1, keepdims=True) + epsilon)
        projected = dot(x_all, qkv) * inverse_all
        queries = rotate(projected[:, :q_cols], tables, 1.0).astype(bf16)
        keys = rotate(projected[:, q_cols : q_cols + kv_cols], tables, 1.0).astype(bf16)
        values = projected[:, q_cols + kv_cols :].astype(bf16)
        pair = jnp.concatenate([keys, values], axis=1).reshape(TP, count, 2 * kv_cols)
        pairs = jnp.concatenate([swap_ctx(pair, j) for j in range(ctxs)], axis=1)
        keys_seq, values_seq = pairs[..., :kv_cols], pairs[..., kv_cols:]
        queries = queries.reshape(TP, count, q_cols)

        kept, parts = [None] * TP, [None] * TP
        for k in (3, 2, 1, 0):
            mixed, logsum = attend(queries[k], keys_seq[k], values_seq[k], visible[k])
            attended = unstack(mixed, count).astype(bf16)
            parts[k] = dot(attended, out)
            kept[k] = (mixed, logsum, attended)
        inputs = tokens.astype(f32)
        middle = inputs + scatter_sum(parts)
        inverse_mid = lax.rsqrt(jnp.mean(middle * middle, axis=-1, keepdims=True) + epsilon)
        normed_mid = middle * inverse_mid
        n2_all = gather(shuffle(normed_mid.astype(bf16)))

        gate_part = dot(n2_all, gate)
        up_part = dot(n2_all, up)
        sigmoid = jax.nn.sigmoid(gate_part)
        hidden = (gate_part * sigmoid * up_part).astype(bf16)
        grad_hidden = contract_cols(g_all, down)
        grad_gate_b = (
            grad_hidden * up_part * sigmoid * (1.0 + gate_part * (1.0 - sigmoid))
        ).astype(bf16)
        grad_up_b = (grad_hidden * gate_part * sigmoid).astype(bf16)
        back_mid = contract_cols(grad_gate_b, gate) + contract_cols(grad_up_b, up)
        e2 = unshuffle(scatter_sum([back_mid[k * count : (k + 1) * count] for k in range(TP)]))
        sum_gate = collect_columns(owned(contract_rows(n2_all, grad_gate_b)), t)
        sum_up = collect_columns(owned(contract_rows(n2_all, grad_up_b)), t)
        grad_down = owned(contract_rows(hidden, g_all)).astype(f32)
        forward = dot(hidden, down)
        layer_out = (
            middle + scatter_sum([forward[k * count : (k + 1) * count] for k in range(TP)])
        ).astype(bf16)

        grad_middle = out_grad.astype(f32) + inverse_mid * (
            e2 - normed_mid * jnp.mean(e2 * normed_mid, axis=-1, keepdims=True)
        )
        db_all = gather(grad_middle.astype(bf16))
        attended_all = jnp.concatenate([kept[k][2] for k in range(TP)], axis=0)
        grad_attended = contract_cols(db_all, out).astype(bf16).reshape(TP, count, q_cols)
        sum_out = owned(contract_rows(attended_all, db_all)).astype(f32)
        grad_queries, grad_pairs = [], []
        for k in range(TP):
            mixed, logsum, _ = kept[k]
            dq, dk, dv = attend_back(
                queries[k], keys_seq[k], values_seq[k], visible[k], grad_attended[k], mixed, logsum
            )
            grad_queries.append(dq)
            grad_pairs.append(jnp.concatenate([dk, dv], axis=1).reshape(ctxs, count, 2 * kv_cols))
        grad_pairs = jnp.stack(grad_pairs, axis=1)
        local = grad_pairs[0]
        for j in range(1, ctxs):
            local = local + swap_ctx(grad_pairs[j].astype(bf16), j).astype(f32)
        local = local.reshape(TP * count, 2 * kv_cols)
        grad_proj = jnp.concatenate(
            [
                rotate(jnp.concatenate(grad_queries, axis=0), tables, -1.0),
                rotate(local[:, :kv_cols], tables, -1.0),
                local[:, kv_cols:],
            ],
            axis=1,
        )
        back = contract_cols(grad_proj.astype(bf16), qkv)
        e1 = unshuffle(scatter_sum([back[k * count : (k + 1) * count] for k in range(TP)]))
        sum_qkv = collect_columns(
            owned(contract_rows(x_all, (grad_proj * inverse_all).astype(bf16))), t
        ).astype(f32)
        inverse = lax.rsqrt(jnp.mean(inputs * inputs, axis=-1, keepdims=True) + epsilon)
        normed = inputs * inverse
        input_grad = grad_middle + inverse * (
            e1 - normed * jnp.mean(e1 * normed, axis=-1, keepdims=True)
        )

        def rows_of(v):
            return v.reshape(own, -1).astype(f32)

        raw_query = rows_of(sum_qkv[..., :q_cols])
        raw_key = rows_of(sum_qkv[..., q_cols : q_cols + kv_cols])
        raw_value = rows_of(sum_qkv[..., q_cols + kv_cols :])
        raw_gate, raw_up = rows_of(sum_gate), rows_of(sum_up)
        grad_norm_attn = (
            jnp.sum(raw_query * w_query.astype(f32), axis=1)
            + jnp.sum(raw_key * w_key.astype(f32), axis=1)
            + jnp.sum(raw_value * w_value.astype(f32), axis=1)
        )
        grad_norm_mlp = jnp.sum(raw_gate * w_gate.astype(f32), axis=1) + jnp.sum(
            raw_up * w_up.astype(f32), axis=1
        )
        return (
            layer_out,
            input_grad,
            grad_norm_attn,
            raw_query * gain_attn,
            raw_key * gain_attn,
            raw_value * gain_attn,
            sum_out,
            grad_norm_mlp,
            raw_gate * gain_mlp,
            raw_up * gain_mlp,
            grad_down,
        )

    return body


def solution(mesh):
    sequences, ctxs = mesh.shape["dp"], mesh.shape["ctx"]
    reps = sequences // TP
    grid = Mesh(mesh.devices.reshape(2, 2, reps, ctxs), ("ty", "tx", "rep", "ctx"))
    rows = ("ty", "tx", "rep", "ctx")
    matrix, vector = P(rows, None), P(rows)
    return jax.shard_map(
        make_body(reps, ctxs),
        mesh=grid,
        in_specs=(
            matrix,
            P(("ty", "tx", "rep"), None),
            vector,
            matrix,
            matrix,
            matrix,
            matrix,
            vector,
            matrix,
            matrix,
            matrix,
            matrix,
        ),
        out_specs=(
            matrix,
            matrix,
            vector,
            matrix,
            matrix,
            matrix,
            matrix,
            vector,
            matrix,
            matrix,
            matrix,
        ),
        check_vma=False,
    )
```

time: 4860 us -> 853 us (0.18)
  waiting for transfers between devices: 4360 us -> 338 us
  blocking collectives: 114 us -> 0 us
  matrix products: 302 us -> 189 us
  starting transfers between devices: 1.27 us -> 103 us
  local copies, waits for them, and re-layouts: 33.3 us -> 102 us
  other arithmetic: 30.2 us -> 94.4 us
    reduce_scatter x9 -> x10, waiting for transfers between devices: 3820 us -> 130 us  [the longest x5 113 us: owned(): return lax.psum_scatter(v, 'ctx', scatter_dimension=0, tiled=True)]
    all_gather x7 -> x5, waiting for transfers between devices: 535 us -> 0.01 us  [whole(): return lax.all_gather(v, ('rep', 'ctx'), axis=0, tiled=True)]
    ppermute x0 -> x75, waiting for transfers between devices: none -> 205 us  [the longest x31 80.5 us: swap(): return lax.ppermute(v, 'ty', [(0, 1), (1, 0)])]
    ppermute x0 -> x75, starting transfers between devices: none -> 102 us  [the longest x31 38.9 us: swap(): return lax.ppermute(v, 'tx', [(0, 1), (1, 0)])]
    unnamed x2 -> x0, blocking collectives: 80.9 us -> none
    dot_general x19 -> x13, matrix products: 118 us -> 56.9 us  [contract_cols(): lax.dot_general(left, right, (((1,), (1,)), ((), ())), preferred_element_...]
    dot_general x15 -> x13, matrix products: 98.5 us -> 61.8 us  [contract_rows(): lax.dot_general(left, right, (((0,), (0,)), ((), ())), preferred_element_...]
  transfers between devices with their start and end apart: 16 -> 90, of which waited for: 15 -> 50; matrix products, arithmetic and copies ran while one was open for 4% -> 29% of each run, Pallas kernels for 0% -> 0%
where the time goes in v1:
time: 853 us; the launch traced here: 843 us
  waiting for transfers between devices  338 us (40%)
  matrix products  189 us (22%)
  starting transfers between devices  103 us (12%)
  local copies, waits for them, and re-layouts  102 us (12%)
  other arithmetic  94.4 us (11%)
  between operations  16.5 us (2%)
    reduce_scatter x5, waiting for transfers between devices, owned(): return lax.psum_scatter(v, 'ctx', scatter_dimension=0, tiled=True)  113 us
    ppermute x31, waiting for transfers between devices, swap(): return lax.ppermute(v, 'ty', [(0, 1), (1, 0)])  80.5 us
    ppermute x31, waiting for transfers between devices, swap(): return lax.ppermute(v, 'tx', [(0, 1), (1, 0)])  78.7 us
    dot_general x16, matrix products, dot(): return jnp.dot(left, right, preferred_element_type=f32)  69.8 us
    dot_general x13, matrix products, contract_rows(): lax.dot_general(left, right, (((0,), (0,)), ((), ())), preferred_element_...  61.8 us
    dot_general x13, matrix products, contract_cols(): lax.dot_general(left, right, (((1,), (1,)), ((), ())), preferred_element_...  56.9 us
    ppermute x31, starting transfers between devices, swap(): return lax.ppermute(v, 'tx', [(0, 1), (1, 0)])  38.9 us
    ppermute x31, starting transfers between devices, swap(): return lax.ppermute(v, 'ty', [(0, 1), (1, 0)])  37.9 us
  transfers between devices with their start and end apart: 90, of which 50 were waited for; matrix products, arithmetic and copies ran while one was open for 29% of the time, Pallas kernels for 0%

profile of v1, /device:TPU:0, one launch (start us, length us, event | category | flops | bytes accessed | tf_op | source)
XLA Modules:
  0.0 843.0 jit_solution(13235616334891907700)
XLA Ops:
  15.9 3.4 collective-permute-done.6
  19.3 4.1 collective-permute-done.7
  32.6 3.4 collective-permute-done.30
  59.6 5.8 collective-permute-done.11
  79.6 4.9 collective-permute-done.28
  86.0 6.8 collective-permute-done.29
  110.5 8.7 %collective-permute-done.40 = bf16[128,2048]{1,0:T(8,128)(2,1)S(1)} collective-permute-done((bf16[128,2048]{1,0:T(8,128)(2,1)}, bf16[128,2048]{1,0:T(8,128)(2,1)S(1)}, u32[]{:S(2)}, u32[]{:S(2)}) %collective-permute-start.40) | collective-permute-done | bytes 524320 | tf_op jit(solution)/shard_map/ppermute | solution.py:91
  126.0 3.3 collective-permute-done.4
  135.7 6.0 convolution_multiply_fusion
  149.2 7.5 collective-permute-done.12
  156.7 10.6 %collective-permute-done.13 = bf16[4,256,128]{1,2,0:T(8,128)(2,1)S(1)} collective-permute-done((bf16[4,256,128]{1,2,0:T(8,128)(2,1)S(1)}, bf16[4,256,128]{1,2,0:T(8,128)(2,1)S(1)}, u32[]{:S(2)}, u32[]{:S(2)}) %collective-permute-start.13) | collective-permute-done | bytes 262176 | tf_op jit(solution)/shard_map/ppermute | solution.py:99
  172.2 5.1 fusion.6
  185.2 5.3 fusion.7
  206.4 5.2 fusion.5
  220.2 5.1 fusion.4
  231.4 3.3 collective-permute-done.20
  249.7 7.1 collective-permute-done.21
  259.7 6.3 collective-permute-done.22
  268.7 3.2 collective-permute-done.25
  273.7 11.8 %fusion.172 = f32[1024,1408]{1,0:T(8,128)} fusion(bf16[1024,2048]{1,0:T(8,128)(2,1)} %constant_dynamic-update-slice_fusion.20, bf16[1408,2048]{1,0:T(8,128)(2,1)} %all-gather.14.cloned.1.call-done), kind=kOutput, calls=%fused_computation.441 | convolution fusion | flops 5905580032 | bytes 15728640 | tf_op jit(solution)/shard_map/dot_general | solution.py:28
  285.4 12.2 %fusion.171 = f32[1024,1408]{1,0:T(8,128)} fusion(bf16[1024,2048]{0,1:T(8,128)(2,1)} %constant_dynamic-update-slice_fusion.12, bf16[2048,1408]{1,0:T(8,128)(2,1)} %all-gather.12.cloned.1.call-done), kind=kOutput, calls=%fused_computation.440 | convolution fusion | flops 5905580032 | bytes 15728640 | tf_op jit(solution)/shard_map/dot_general | solution.py:20
  297.6 16.6 %multiply_convert_fusion.5 = (bf16[1024,1408]{1,0:T(8,128)(2,1)S(1)}, bf16[1024,1408]{1,0:T(8,128)(2,1)}, bf16[1024,1408]{1,0:T(8,128)(2,1)S(1)}) fusion(f32[1024,1408]{1,0:T(8,128)} %fusion.172, f32[1024,1408]{1,0:T(8,128)} %fusion.171, bf16[1024,2048]{0,1:T(8,128)(2,1)} %constant_dynamic-update-slice_fusion.12, ...), kind=kOutput, calls=%fused_computation.33 | convolution fusion | flops 5928648704 | bytes 30146560 | tf_op jit(solution)/shard_map/dot_general | solution.py:20
  314.2 9.0 %fusion.173 = f32[1024,2048]{1,0:T(8,128)} fusion(bf16[1024,1408]{1,0:T(8,128)(2,1)S(1)} %get-tuple-element.19, bf16[2048,1408]{1,0:T(8,128)(2,1)S(1)} %copy-done.84), kind=kOutput, calls=%fused_computation.442 | convolution fusion | flops 5905580032 | bytes 17039360 | tf_op jit(solution)/shard_map/dot_general | solution.py:28
  323.2 10.2 %fusion.165 = (bf16[1024,2048]{1,0:T(8,128)(2,1)S(1)}, f32[1024,2048]{1,0:T(8,128)S(1)}) fusion(f32[1024,2048]{1,0:T(8,128)} %fusion.173, bf16[1024,1408]{1,0:T(8,128)(2,1)S(1)} %get-tuple-element.17, bf16[2048,1408]{1,0:T(8,128)(2,1)} %all-gather.10.cloned.1.call-done), kind=kOutput, calls=%fused_computation.434 | convolution fusion | flops 5909774336 | bytes 29622272 | tf_op jit(solution)/shard_map/dot_general | solution.py:28
  337.3 7.8 collective-permute-done.46
  347.8 4.0 collective-permute-done.45
  351.8 7.8 collective-permute-done.47
  361.8 3.4 collective-permute-done.48
  365.2 4.0 collective-permute-done.50
  373.8 3.1 copy.122
  387.2 9.5 %collective-permute-done.51 = bf16[128,2048]{1,0:T(8,128)(2,1)S(1)} collective-permute-done((bf16[128,2048]{1,0:T(8,128)(2,1)S(1)}, bf16[128,2048]{1,0:T(8,128)(2,1)S(1)}, u32[]{:S(2)}, u32[]{:S(2)}) %collective-permute-start.51) | collective-permute-done | bytes 524320 | tf_op jit(solution)/shard_map/ppermute | solution.py:91
  404.1 5.5 collective-permute-done.55
  415.2 3.3 multiply_convert_fusion.3
  421.9 3.5 multiply_convert_fusion.2
  429.3 3.3 multiply_convert_fusion.1
  436.6 3.7 multiply_convert_fusion
  458.6 3.2 fusion.179
  475.7 3.4 fusion.149
  479.4 10.6 %collective-permute-start.57 = (bf16[4,256,128]{1,0,2:T(4,128)(2,1)S(1)}, bf16[4,256,128]{1,0,2:T(4,128)(2,1)S(1)}, u32[]{:S(2)}, u32[]{:S(2)}) collective-permute-start(bf16[4,256,128]{1,0,2:T(4,128)(2,1)S(1)} %get-tuple-element.58), channel_id=1, source_target_pairs={{0,1},{1,0},{2,3},{3,2},{4,5},{5,4},{6,7},{7,6},{8,9},{9,8},{10,11... | collective-permute-start | bytes 786440 | tf_op jit(solution)/shard_map/ppermute | solution.py:99
  494.4 8.5 %collective-permute-done.58 = bf16[4,256,128]{1,0,2:T(4,128)(2,1)S(1)} collective-permute-done((bf16[4,256,128]{1,0,2:T(4,128)(2,1)S(1)}, bf16[4,256,128]{1,0,2:T(4,128)(2,1)S(1)}, u32[]{:S(2)}, u32[]{:S(2)}) %collective-permute-start.58) | collective-permute-done | bytes 262176 | tf_op jit(solution)/shard_map/ppermute | solution.py:99
  504.0 7.2 convolution_convert_fusion.3
  511.3 6.2 convolution_convert_fusion.4
  517.6 11.1 %convolution_convert_fusion.2 = bf16[2048,1408]{1,0:T(8,128)(2,1)} fusion(bf16[1024,2048]{0,1:T(8,128)(2,1)} %constant_dynamic-update-slice_fusion.12, bf16[1024,1408]{1,0:T(8,128)(2,1)} %copy-done.86), kind=kOutput, calls=%fused_computation.23 | convolution fusion | flops 5908463616 | bytes 12845056 | tf_op jit(solution)/shard_map/dot_general | solution.py:24
  528.8 11.0 %convolution_convert_fusion.1 = bf16[2048,1408]{1,0:T(8,128)(2,1)} fusion(bf16[1024,2048]{0,1:T(8,128)(2,1)} %constant_dynamic-update-slice_fusion.12, bf16[1024,1408]{1,0:T(8,128)(2,1)} %copy-done.87), kind=kOutput, calls=%fused_computation.22 | convolution fusion | flops 5908463616 | bytes 12845056 | tf_op jit(solution)/shard_map/dot_general | solution.py:24
  539.9 10.7 %convolution_convert_fusion = bf16[1408,2048]{1,0:T(8,128)(2,1)} fusion(bf16[1024,1408]{1,0:T(8,128)(2,1)} %get-tuple-element.18, bf16[1024,2048]{1,0:T(8,128)(2,1)} %constant_dynamic-update-slice_fusion.20), kind=kOutput, calls=%fused_computation.21 | convolution fusion | flops 5908463616 | bytes 12845056 | tf_op jit(solution)/shard_map/dot_general | solution.py:24
  552.7 16.9 %reduce-scatter.23.cloned.1.call-done = bf16[1024,1408]{1,0:T(8,128)(2,1)} async-done(((bf16[2048,1408]{1,0:T(8,128)(2,1)}), bf16[1024,1408]{1,0:T(8,128)(2,1)}) %reduce-scatter.23.cloned.1.call-update) | async-done | bytes 2883600 | tf_op jit(solution)/shard_map/reduce_scatter | solution.py:138
  569.8 11.7 %fusion.167 = (bf16[1024,2048]{1,0:T(8,128)(2,1)S(1)}, f32[1024,2048]{1,0:T(8,128)}) fusion(bf16[1024,1408]{1,0:T(8,128)(2,1)} %get-tuple-element.18, bf16[1408,2048]{1,0:T(8,128)(2,1)} %all-gather.14.cloned.1.call-done), kind=kOutput, calls=%fused_computation.436 | convolution fusion | flops 5907677184 | bytes 21233664 | tf_op jit(solution)/shard_map/dot_general | solution.py:20
  584.5 3.5 fusion.166
  592.8 4.6 collective-permute-done.34
  601.6 7.0 collective-permute-done.61
  611.4 8.6 %collective-permute-done.33 = bf16[128,2048]{1,0:T(8,128)(2,1)} collective-permute-done((bf16[128,2048]{1,0:T(8,128)(2,1)}, bf16[128,2048]{1,0:T(8,128)(2,1)}, u32[]{:S(2)}, u32[]{:S(2)}) %collective-permute-start.33) | collective-permute-done | bytes 524320 | tf_op jit(solution)/shard_map/ppermute | solution.py:93
  622.1 3.3 fusion.39
  627.2 4.1 collective-permute-done.60
  633.1 7.1 collective-permute-done.64
  640.2 11.2 %collective-permute-done.62 = bf16[128,2048]{1,0:T(8,128)(2,1)S(1)} collective-permute-done((bf16[128,2048]{1,0:T(8,128)(2,1)}, bf16[128,2048]{1,0:T(8,128)(2,1)S(1)}, u32[]{:S(2)}, u32[]{:S(2)}) %collective-permute-start.62) | collective-permute-done | bytes 524320 | tf_op jit(solution)/shard_map/ppermute | solution.py:91
  657.4 3.6 collective-permute-done.63
  661.0 3.6 collective-permute-done.65
  670.5 3.1 copy.134
  673.7 3.2 copy.136
  683.0 6.0 fusion.17
  701.0 6.2 reduce-scatter.21.cloned.1.call-done
  712.1 53.4 %reduce-scatter.25.cloned.1.call-done = bf16[256,1408]{1,0:T(8,128)(2,1)} async-done(((bf16[1024,1408]{1,0:T(8,128)(2,1)}), bf16[256,1408]{1,0:T(8,128)(2,1)}) %reduce-scatter.25.cloned.1.call-update) | async-done | bytes 720912 | tf_op jit(solution)/shard_map/reduce_scatter | solution.py:139
  770.4 53.2 %reduce-scatter.29.cloned.1.call-done = bf16[176,2048]{1,0:T(8,128)(2,1)} async-done(((bf16[704,2048]{1,0:T(8,128)(2,1)}), bf16[176,2048]{1,0:T(8,128)(2,1)}) %reduce-scatter.29.cloned.1.call-update) | async-done | bytes 720912 | tf_op jit(solution)/shard_map/reduce_scatter | solution.py:139
  829.7 3.3 collective-permute-done.74
  (604 shorter events, 316.6 us)
Async XLA Ops:
  7.2 128.5 %all-gather.6.cloned.1.call-start = ((), (), s32[]{:S(2)}) async-start(), calls=%async_computation.10 | async-start | bytes 2949120 | tf_op jit(solution)/shard_map/all_gather | solution.py:135
  24.3 169.2 %all-gather.8.cloned.1.call-start = ((), (), s32[]{:S(2)}) async-start(), calls=%async_computation.11 | async-start | bytes 2359296 | tf_op jit(solution)/shard_map/all_gather | solution.py:135
  25.0 248.6 %all-gather.14.cloned.1.call-start = ((), (), s32[]{:S(2)}) async-start(), calls=%async_computation.14 | async-start | bytes 6488064 | tf_op jit(solution)/shard_map/all_gather | solution.py:135
  25.8 259.6 %all-gather.12.cloned.1.call-start = ((), (), s32[]{:S(2)}) async-start(), calls=%async_computation.13 | async-start | bytes 6488064 | tf_op jit(solution)/shard_map/all_gather | solution.py:135
  40.1 257.5 %all-gather.10.cloned.1.call-start = ((), (), s32[]{:S(2)}) async-start(), calls=%async_computation.12 | async-start | bytes 6488064 | tf_op jit(solution)/shard_map/all_gather | solution.py:135
  41.8 53.7 %collective-permute-start = (bf16[128,2048]{0,1:T(8,128)(2,1)}, bf16[128,2048]{0,1:T(8,128)(2,1)}, u32[]{:S(2)}, u32[]{:S(2)}) collective-permute-start(bf16[128,2048]{0,1:T(8,128)(2,1)} %bitcast.11), channel_id=1, source_target_pairs={{0,8},{8,0},{1,9},{9,1},{2,10},{10,2},{3,11},{11,3},{4,12},{12,4},... | collective-permute-start | bytes 1572872 | tf_op jit(solution)/shard_map/ppermute | solution.py:91
  42.8 58.8 %collective-permute-start.2 = (bf16[128,2048]{0,1:T(8,128)(2,1)}, bf16[128,2048]{0,1:T(8,128)(2,1)}, u32[]{:S(2)}, u32[]{:S(2)}) collective-permute-start(bf16[128,2048]{0,1:T(8,128)(2,1)} %bitcast.11), channel_id=1, source_target_pairs={{0,16},{16,0},{1,17},{17,1},{2,18},{18,2},{3,19},{19,3},{4,20},{20... | collective-permute-start | bytes 1572872 | tf_op jit(solution)/shard_map/ppermute | solution.py:93
  44.8 53.2 %collective-permute-start.1 = (bf16[128,2048]{0,1:T(8,128)(2,1)}, bf16[128,2048]{0,1:T(8,128)(2,1)}, u32[]{:S(2)}, u32[]{:S(2)}) collective-permute-start(bf16[128,2048]{0,1:T(8,128)(2,1)} %bitcast.13), channel_id=1, source_target_pairs={{0,8},{8,0},{1,9},{9,1},{2,10},{10,2},{3,11},{11,3},{4,12},{12,4},... | collective-permute-start | bytes 1572872 | tf_op jit(solution)/shard_map/ppermute | solution.py:91
  45.7 58.2 %collective-permute-start.3 = (bf16[128,2048]{0,1:T(8,128)(2,1)}, bf16[128,2048]{0,1:T(8,128)(2,1)}, u32[]{:S(2)}, u32[]{:S(2)}) collective-permute-start(bf16[128,2048]{0,1:T(8,128)(2,1)} %bitcast.13), channel_id=1, source_target_pairs={{0,16},{16,0},{1,17},{17,1},{2,18},{18,2},{3,19},{19,3},{4,20},{20... | collective-permute-start | bytes 1572872 | tf_op jit(solution)/shard_map/ppermute | solution.py:93
  46.7 18.7 %collective-permute-start.11 = (s32[1,8]{1,0:T(1,128)S(1)}, s32[1,8]{1,0:T(1,128)S(1)}, u32[]{:S(2)}, u32[]{:S(2)}) collective-permute-start(s32[1,8]{1,0:T(1,128)S(1)} %copy-done.77), channel_id=1, source_target_pairs={{0,24},{8,16},{16,8},{24,0},{1,25},{9,17},{17,9},{25,1},{2,26},{10... | collective-permute-start | bytes 104 | tf_op jit(solution)/shard_map/ppermute | solution.py:94
  92.9 15.1 %collective-permute-start.39 = (bf16[128,2048]{1,0:T(8,128)(2,1)}, bf16[128,2048]{1,0:T(8,128)(2,1)S(1)}, u32[]{:S(2)}, u32[]{:S(2)}) collective-permute-start(bf16[128,2048]{1,0:T(8,128)(2,1)} %get-tuple-element.68), channel_id=1, source_target_pairs={{0,8},{8,0},{1,9},{9,1},{2,10},{10,2},{3,11},{11,3},{4,12},{12,4},... | collective-permute-start | bytes 1572872 | tf_op jit(solution)/shard_map/ppermute | solution.py:91
  95.5 455.2 %reduce-scatter.11.cloned.1.call-start = ((), (), s32[]{:S(2)}) async-start(), calls=%async_computation.15 | async-start | bytes 3932160 | tf_op jit(solution)/shard_map/reduce_scatter | solution.py:138
  95.5 27.7 %collective-permute-start.41 = (bf16[128,2048]{1,0:T(8,128)(2,1)}, bf16[128,2048]{1,0:T(8,128)(2,1)S(1)}, u32[]{:S(2)}, u32[]{:S(2)}) collective-permute-start(bf16[128,2048]{1,0:T(8,128)(2,1)} %get-tuple-element.68), channel_id=1, source_target_pairs={{0,16},{16,0},{1,17},{17,1},{2,18},{18,2},{3,19},{19,3},{4,20},{20... | collective-permute-start | bytes 1572872 | tf_op jit(solution)/shard_map/ppermute | solution.py:93
  98.0 21.2 %collective-permute-start.40 = (bf16[128,2048]{1,0:T(8,128)(2,1)}, bf16[128,2048]{1,0:T(8,128)(2,1)S(1)}, u32[]{:S(2)}, u32[]{:S(2)}) collective-permute-start(bf16[128,2048]{1,0:T(8,128)(2,1)} %get-tuple-element.67), channel_id=1, source_target_pairs={{0,8},{8,0},{1,9},{9,1},{2,10},{10,2},{3,11},{11,3},{4,12},{12,4},... | collective-permute-start | bytes 1572872 | tf_op jit(solution)/shard_map/ppermute | solution.py:91
  101.6 20.4 %collective-permute-start.42 = (bf16[128,2048]{1,0:T(8,128)(2,1)}, bf16[128,2048]{1,0:T(8,128)(2,1)}, u32[]{:S(2)}, u32[]{:S(2)}) collective-permute-start(bf16[128,2048]{1,0:T(8,128)(2,1)} %get-tuple-element.67), channel_id=1, source_target_pairs={{0,16},{16,0},{1,17},{17,1},{2,18},{18,2},{3,19},{19,3},{4,20},{20... | collective-permute-start | bytes 1572872 | tf_op jit(solution)/shard_map/ppermute | solution.py:93
  103.9 25.4 %collective-permute-start.4 = (bf16[128,2048]{0,1:T(8,128)(2,1)}, bf16[128,2048]{0,1:T(8,128)(2,1)S(1)}, u32[]{:S(2)}, u32[]{:S(2)}) collective-permute-start(bf16[128,2048]{0,1:T(8,128)(2,1)} %collective-permute-done), channel_id=1, source_target_pairs={{0,16},{16,0},{1,17},{17,1},{2,18},{18,2},{3,19},{19,3},{4,20},{20... | collective-permute-start | bytes 1572872 | tf_op jit(solution)/shard_map/ppermute | solution.py:93
  108.0 22.2 %collective-permute-start.5 = (bf16[128,2048]{0,1:T(8,128)(2,1)}, bf16[128,2048]{0,1:T(8,128)(2,1)S(1)}, u32[]{:S(2)}, u32[]{:S(2)}) collective-permute-start(bf16[128,2048]{0,1:T(8,128)(2,1)} %collective-permute-done.3), channel_id=1, source_target_pairs={{0,8},{8,0},{1,9},{9,1},{2,10},{10,2},{3,11},{11,3},{4,12},{12,4},... | collective-permute-start | bytes 1572872 | tf_op jit(solution)/shard_map/ppermute | solution.py:91
  119.2 15.7 %collective-permute-start.43 = (bf16[128,2048]{1,0:T(8,128)(2,1)S(1)}, bf16[128,2048]{1,0:T(8,128)(2,1)S(1)}, u32[]{:S(2)}, u32[]{:S(2)}) collective-permute-start(bf16[128,2048]{1,0:T(8,128)(2,1)S(1)} %collective-permute-done.39), channel_id=1, source_target_pairs={{0,16},{16,0},{1,17},{17,1},{2,18},{18,2},{3,19},{19,3},{4,20},{20... | collective-permute-start | bytes 1572872 | tf_op jit(solution)/shard_map/ppermute | solution.py:93
  122.0 122.0 %collective-permute-start.44 = (bf16[128,2048]{1,0:T(8,128)(2,1)}, bf16[128,2048]{1,0:T(8,128)(2,1)}, u32[]{:S(2)}, u32[]{:S(2)}) collective-permute-start(bf16[128,2048]{1,0:T(8,128)(2,1)} %collective-permute-done.42), channel_id=1, source_target_pairs={{0,8},{8,0},{1,9},{9,1},{2,10},{10,2},{3,11},{11,3},{4,12},{12,4},... | collective-permute-start | bytes 1572872 | tf_op jit(solution)/shard_map/ppermute | solution.py:91
  142.5 14.2 %collective-permute-start.12 = (bf16[4,256,128]{1,2,0:T(8,128)(2,1)S(1)}, bf16[4,256,128]{1,2,0:T(8,128)(2,1)S(1)}, u32[]{:S(2)}, u32[]{:S(2)}) collective-permute-start(bf16[4,256,128]{1,2,0:T(8,128)(2,1)S(1)} %bitcast.506), channel_id=1, source_target_pairs={{0,1},{1,0},{2,3},{3,2},{4,5},{5,4},{6,7},{7,6},{8,9},{9,8},{10,11... | collective-permute-start | bytes 786440 | tf_op jit(solution)/shard_map/ppermute | solution.py:99
  143.9 23.4 %collective-permute-start.13 = (bf16[4,256,128]{1,2,0:T(8,128)(2,1)S(1)}, bf16[4,256,128]{1,2,0:T(8,128)(2,1)S(1)}, u32[]{:S(2)}, u32[]{:S(2)}) collective-permute-start(bf16[4,256,128]{1,2,0:T(8,128)(2,1)S(1)} %bitcast.507), channel_id=1, source_target_pairs={{0,2},{1,3},{2,0},{3,1},{4,6},{5,7},{6,4},{7,5},{8,10},{9,11},{10,... | collective-permute-start | bytes 786440 | tf_op jit(solution)/shard_map/ppermute | solution.py:99
  146.8 20.5 %collective-permute-start.14 = (bf16[4,256,128]{1,2,0:T(8,128)(2,1)S(1)}, bf16[4,256,128]{1,2,0:T(8,128)(2,1)S(1)}, u32[]{:S(2)}, u32[]{:S(2)}) collective-permute-start(bf16[4,256,128]{1,2,0:T(8,128)(2,1)S(1)} %bitcast.508), channel_id=1, source_target_pairs={{0,3},{1,2},{2,1},{3,0},{4,7},{5,6},{6,5},{7,4},{8,11},{9,10},{10,... | collective-permute-start | bytes 786440 | tf_op jit(solution)/shard_map/ppermute | solution.py:99
  196.2 29.1 %collective-permute-start.19 = (bf16[128,2048]{1,0:T(8,128)(2,1)S(1)}, bf16[128,2048]{1,0:T(8,128)(2,1)S(1)}, u32[]{:S(2)}, u32[]{:S(2)}) collective-permute-start(bf16[128,2048]{1,0:T(8,128)(2,1)S(1)} %get-tuple-element.72), channel_id=1, source_target_pairs={{0,8},{8,0},{1,9},{9,1},{2,10},{10,2},{3,11},{11,3},{4,12},{12,4},... | collective-permute-start | bytes 1572872 | tf_op jit(solution)/shard_map/ppermute | solution.py:91
  199.3 32.1 %collective-permute-start.15 = (bf16[128,2048]{1,0:T(8,128)(2,1)S(1)}, bf16[128,2048]{1,0:T(8,128)(2,1)S(1)}, u32[]{:S(2)}, u32[]{:S(2)}) collective-permute-start(bf16[128,2048]{1,0:T(8,128)(2,1)S(1)} %slice.637), channel_id=1, source_target_pairs={{0,16},{16,0},{1,17},{17,1},{2,18},{18,2},{3,19},{19,3},{4,20},{20... | collective-permute-start | bytes 1572872 | tf_op jit(solution)/shard_map/ppermute | solution.py:93
  200.9 25.9 %collective-permute-start.16 = (bf16[128,2048]{1,0:T(8,128)(2,1)S(1)}, bf16[128,2048]{1,0:T(8,128)(2,1)S(1)}, u32[]{:S(2)}, u32[]{:S(2)}) collective-permute-start(bf16[128,2048]{1,0:T(8,128)(2,1)S(1)} %get-tuple-element.71), channel_id=1, source_target_pairs={{0,16},{16,0},{1,17},{17,1},{2,18},{18,2},{3,19},{19,3},{4,20},{20... | collective-permute-start | bytes 1572872 | tf_op jit(solution)/shard_map/ppermute | solution.py:93
  214.6 16.9 %collective-permute-start.18 = (bf16[128,2048]{1,0:T(8,128)(2,1)S(1)}, bf16[128,2048]{1,0:T(8,128)(2,1)S(1)}, u32[]{:S(2)}, u32[]{:S(2)}) collective-permute-start(bf16[128,2048]{1,0:T(8,128)(2,1)S(1)} %slice.636), channel_id=1, source_target_pairs={{0,8},{8,0},{1,9},{9,1},{2,10},{10,2},{3,11},{11,3},{4,12},{12,4},... | collective-permute-start | bytes 1572872 | tf_op jit(solution)/shard_map/ppermute | solution.py:91
  241.9 14.9 %collective-permute-start.21 = (bf16[128,2048]{0,1:T(8,128)(2,1)S(1)}, bf16[128,2048]{0,1:T(8,128)(2,1)S(1)}, u32[]{:S(2)}, u32[]{:S(2)}) collective-permute-start(bf16[128,2048]{0,1:T(8,128)(2,1)S(1)} %bitcast.477), channel_id=1, source_target_pairs={{0,8},{8,0},{1,9},{9,1},{2,10},{10,2},{3,11},{11,3},{4,12},{12,4},... | collective-permute-start | bytes 1572872 | tf_op jit(solution)/shard_map/ppermute | solution.py:91
  243.5 14.9 %collective-permute-start.24 = (bf16[128,2048]{0,1:T(8,128)(2,1)S(1)}, bf16[128,2048]{0,1:T(8,128)(2,1)S(1)}, u32[]{:S(2)}, u32[]{:S(2)}) collective-permute-start(bf16[128,2048]{0,1:T(8,128)(2,1)S(1)} %bitcast.480), channel_id=1, source_target_pairs={{0,16},{16,0},{1,17},{17,1},{2,18},{18,2},{3,19},{19,3},{4,20},{20... | collective-permute-start | bytes 1572872 | tf_op jit(solution)/shard_map/ppermute | solution.py:93
  245.9 20.1 %collective-permute-start.22 = (bf16[128,2048]{0,1:T(8,128)(2,1)S(1)}, bf16[128,2048]{0,1:T(8,128)(2,1)S(1)}, u32[]{:S(2)}, u32[]{:S(2)}) collective-permute-start(bf16[128,2048]{0,1:T(8,128)(2,1)S(1)} %bitcast.481), channel_id=1, source_target_pairs={{0,8},{8,0},{1,9},{9,1},{2,10},{10,2},{3,11},{11,3},{4,12},{12,4},... | collective-permute-start | bytes 1572872 | tf_op jit(solution)/shard_map/ppermute | solution.py:91
  247.5 19.4 %collective-permute-start.23 = (bf16[128,2048]{0,1:T(8,128)(2,1)S(1)}, bf16[128,2048]{0,1:T(8,128)(2,1)S(1)}, u32[]{:S(2)}, u32[]{:S(2)}) collective-permute-start(bf16[128,2048]{0,1:T(8,128)(2,1)S(1)} %bitcast.479), channel_id=1, source_target_pairs={{0,16},{16,0},{1,17},{17,1},{2,18},{18,2},{3,19},{19,3},{4,20},{20... | collective-permute-start | bytes 1572872 | tf_op jit(solution)/shard_map/ppermute | solution.py:93
  256.8 15.1 %collective-permute-start.25 = (bf16[128,2048]{0,1:T(8,128)(2,1)S(1)}, bf16[128,2048]{0,1:T(8,128)(2,1)S(1)}, u32[]{:S(2)}, u32[]{:S(2)}) collective-permute-start(bf16[128,2048]{0,1:T(8,128)(2,1)S(1)} %collective-permute-done.21), channel_id=1, source_target_pairs={{0,16},{16,0},{1,17},{17,1},{2,18},{18,2},{3,19},{19,3},{4,20},{20... | collective-permute-start | bytes 1572872 | tf_op jit(solution)/shard_map/ppermute | solution.py:93
  258.3 14.4 %collective-permute-start.26 = (bf16[128,2048]{0,1:T(8,128)(2,1)S(1)}, bf16[128,2048]{0,1:T(8,128)(2,1)S(1)}, u32[]{:S(2)}, u32[]{:S(2)}) collective-permute-start(bf16[128,2048]{0,1:T(8,128)(2,1)S(1)} %collective-permute-done.24), channel_id=1, source_target_pairs={{0,8},{8,0},{1,9},{9,1},{2,10},{10,2},{3,11},{11,3},{4,12},{12,4},... | collective-permute-start | bytes 1572872 | tf_op jit(solution)/shard_map/ppermute | solution.py:91
  335.2 16.6 %collective-permute-start.45 = (bf16[128,2048]{1,0:T(8,128)(2,1)S(1)}, bf16[128,2048]{1,0:T(8,128)(2,1)S(1)}, u32[]{:S(2)}, u32[]{:S(2)}) collective-permute-start(bf16[128,2048]{1,0:T(8,128)(2,1)S(1)} %get-tuple-element.38), channel_id=1, source_target_pairs={{0,16},{16,0},{1,17},{17,1},{2,18},{18,2},{3,19},{19,3},{4,20},{20... | collective-permute-start | bytes 1572872 | tf_op jit(solution)/shard_map/ppermute | solution.py:93
  335.8 16.0 %collective-permute-start.49 = (bf16[128,2048]{1,0:T(8,128)(2,1)S(1)}, bf16[128,2048]{1,0:T(8,128)(2,1)S(1)}, u32[]{:S(2)}, u32[]{:S(2)}) collective-permute-start(bf16[128,2048]{1,0:T(8,128)(2,1)S(1)} %get-tuple-element.39), channel_id=1, source_target_pairs={{0,8},{8,0},{1,9},{9,1},{2,10},{10,2},{3,11},{11,3},{4,12},{12,4},... | collective-permute-start | bytes 1572872 | tf_op jit(solution)/shard_map/ppermute | solution.py:91
  345.2 14.4 %collective-permute-start.47 = (bf16[128,2048]{1,0:T(8,128)(2,1)S(1)}, bf16[128,2048]{1,0:T(8,128)(2,1)S(1)}, u32[]{:S(2)}, u32[]{:S(2)}) collective-permute-start(bf16[128,2048]{1,0:T(8,128)(2,1)S(1)} %fusion.34), channel_id=1, source_target_pairs={{0,8},{8,0},{1,9},{9,1},{2,10},{10,2},{3,11},{11,3},{4,12},{12,4},... | collective-permute-start | bytes 1572872 | tf_op jit(solution)/shard_map/ppermute | solution.py:91
  347.7 17.5 %collective-permute-start.48 = (bf16[128,2048]{1,0:T(8,128)(2,1)S(1)}, bf16[128,2048]{1,0:T(8,128)(2,1)S(1)}, u32[]{:S(2)}, u32[]{:S(2)}) collective-permute-start(bf16[128,2048]{1,0:T(8,128)(2,1)S(1)} %get-tuple-element.40), channel_id=1, source_target_pairs={{0,8},{8,0},{1,9},{9,1},{2,10},{10,2},{3,11},{11,3},{4,12},{12,4},... | collective-permute-start | bytes 1572872 | tf_op jit(solution)/shard_map/ppermute | solution.py:91
  386.6 15.7 %collective-permute-start.52 = (bf16[128,2048]{1,0:T(8,128)(2,1)S(1)}, bf16[128,2048]{1,0:T(8,128)(2,1)S(1)}, u32[]{:S(2)}, u32[]{:S(2)}) collective-permute-start(bf16[128,2048]{1,0:T(8,128)(2,1)S(1)} %get-tuple-element.65), channel_id=1, source_target_pairs={{0,8},{8,0},{1,9},{9,1},{2,10},{10,2},{3,11},{11,3},{4,12},{12,4},... | collective-permute-start | bytes 1572872 | tf_op jit(solution)/shard_map/ppermute | solution.py:91
  386.9 17.1 %collective-permute-start.53 = (bf16[128,2048]{1,0:T(8,128)(2,1)S(1)}, bf16[128,2048]{1,0:T(8,128)(2,1)S(1)}, u32[]{:S(2)}, u32[]{:S(2)}) collective-permute-start(bf16[128,2048]{1,0:T(8,128)(2,1)S(1)} %get-tuple-element.66), channel_id=1, source_target_pairs={{0,16},{16,0},{1,17},{17,1},{2,18},{18,2},{3,19},{19,3},{4,20},{20... | collective-permute-start | bytes 1572872 | tf_op jit(solution)/shard_map/ppermute | solution.py:93
  479.4 15.0 %collective-permute-start.57 = (bf16[4,256,128]{1,0,2:T(4,128)(2,1)S(1)}, bf16[4,256,128]{1,0,2:T(4,128)(2,1)S(1)}, u32[]{:S(2)}, u32[]{:S(2)}) collective-permute-start(bf16[4,256,128]{1,0,2:T(4,128)(2,1)S(1)} %get-tuple-element.58), channel_id=1, source_target_pairs={{0,1},{1,0},{2,3},{3,2},{4,5},{5,4},{6,7},{7,6},{8,9},{9,8},{10,11... | collective-permute-start | bytes 786440 | tf_op jit(solution)/shard_map/ppermute | solution.py:99
  511.2 40.2 %reduce-scatter.15.cloned.1.call-start = ((), (), s32[]{:S(2)}) async-start(), calls=%async_computation.17 | async-start | bytes 3145728 | tf_op jit(solution)/shard_map/reduce_scatter | solution.py:138
  517.5 34.6 %reduce-scatter.19.cloned.1.call-start = ((), (), s32[]{:S(2)}) async-start(), calls=%async_computation.19 | async-start | bytes 8650752 | tf_op jit(solution)/shard_map/reduce_scatter | solution.py:138
  528.7 40.9 %reduce-scatter.23.cloned.1.call-start = ((), (), s32[]{:S(2)}) async-start(), calls=%async_computation.21 | async-start | bytes 8650752 | tf_op jit(solution)/shard_map/reduce_scatter | solution.py:138
  539.8 71.6 %reduce-scatter.27.cloned.1.call-start = ((), (), s32[]{:S(2)}) async-start(), calls=%async_computation.23 | async-start | bytes 8650752 | tf_op jit(solution)/shard_map/reduce_scatter | solution.py:138
  550.6 128.9 %reduce-scatter.13.cloned.1.call-start = ((), (), s32[]{:S(2)}) async-start(), calls=%async_computation.16 | async-start | bytes 1638400 | tf_op jit(solution)/shard_map/reduce_scatter | solution.py:139
  551.4 137.7 %reduce-scatter.17.cloned.1.call-start = ((), (), s32[]{:S(2)}) async-start(), calls=%async_computation.18 | async-start | bytes 1310720 | tf_op jit(solution)/shard_map/reduce_scatter | solution.py:139
  551.9 155.3 %reduce-scatter.21.cloned.1.call-start = ((), (), s32[]{:S(2)}) async-start(), calls=%async_computation.20 | async-start | bytes 3604480 | tf_op jit(solution)/shard_map/reduce_scatter | solution.py:139
  552.7 212.8 %reduce-scatter.25.cloned.1.call-start = ((), (), s32[]{:S(2)}) async-start(), calls=%async_computation.22 | async-start | bytes 3604480 | tf_op jit(solution)/shard_map/reduce_scatter | solution.py:139
  569.7 254.0 %reduce-scatter.29.cloned.1.call-start = ((), (), s32[]{:S(2)}) async-start(), calls=%async_computation.24 | async-start | bytes 3604480 | tf_op jit(solution)/shard_map/reduce_scatter | solution.py:139
  582.7 14.8 %collective-permute-start.34 = (bf16[128,2048]{1,0:T(8,128)(2,1)S(1)}, bf16[128,2048]{1,0:T(8,128)(2,1)S(1)}, u32[]{:S(2)}, u32[]{:S(2)}) collective-permute-start(bf16[128,2048]{1,0:T(8,128)(2,1)S(1)} %get-tuple-element.45), channel_id=1, source_target_pairs={{0,16},{16,0},{1,17},{17,1},{2,18},{18,2},{3,19},{19,3},{4,20},{20... | collective-permute-start | bytes 1572872 | tf_op jit(solution)/shard_map/ppermute | solution.py:93
  589.4 19.3 %collective-permute-start.61 = (bf16[128,2048]{1,0:T(8,128)(2,1)S(1)}, bf16[128,2048]{1,0:T(8,128)(2,1)S(1)}, u32[]{:S(2)}, u32[]{:S(2)}) collective-permute-start(bf16[128,2048]{1,0:T(8,128)(2,1)S(1)} %get-tuple-element.37), channel_id=1, source_target_pairs={{0,16},{16,0},{1,17},{17,1},{2,18},{18,2},{3,19},{19,3},{4,20},{20... | collective-permute-start | bytes 1572872 | tf_op jit(solution)/shard_map/ppermute | solution.py:93
  590.8 29.2 %collective-permute-start.33 = (bf16[128,2048]{1,0:T(8,128)(2,1)}, bf16[128,2048]{1,0:T(8,128)(2,1)}, u32[]{:S(2)}, u32[]{:S(2)}) collective-permute-start(bf16[128,2048]{1,0:T(8,128)(2,1)} %get-tuple-element.42), channel_id=1, source_target_pairs={{0,16},{16,0},{1,17},{17,1},{2,18},{18,2},{3,19},{19,3},{4,20},{20... | collective-permute-start | bytes 1572872 | tf_op jit(solution)/shard_map/ppermute | solution.py:93
  591.4 30.5 %collective-permute-start.37 = (bf16[128,2048]{1,0:T(8,128)(2,1)}, bf16[128,2048]{1,0:T(8,128)(2,1)}, u32[]{:S(2)}, u32[]{:S(2)}) collective-permute-start(bf16[128,2048]{1,0:T(8,128)(2,1)} %get-tuple-element.43), channel_id=1, source_target_pairs={{0,8},{8,0},{1,9},{9,1},{2,10},{10,2},{3,11},{11,3},{4,12},{12,4},... | collective-permute-start | bytes 1572872 | tf_op jit(solution)/shard_map/ppermute | solution.py:91
  599.6 22.5 %collective-permute-start.35 = (bf16[128,2048]{1,0:T(8,128)(2,1)}, bf16[128,2048]{1,0:T(8,128)(2,1)}, u32[]{:S(2)}, u32[]{:S(2)}) collective-permute-start(bf16[128,2048]{1,0:T(8,128)(2,1)} %fusion.38), channel_id=1, source_target_pairs={{0,8},{8,0},{1,9},{9,1},{2,10},{10,2},{3,11},{11,3},{4,12},{12,4},... | collective-permute-start | bytes 1572872 | tf_op jit(solution)/shard_map/ppermute | solution.py:91
  601.4 53.5 %collective-permute-start.36 = (bf16[128,2048]{1,0:T(8,128)(2,1)}, bf16[128,2048]{1,0:T(8,128)(2,1)}, u32[]{:S(2)}, u32[]{:S(2)}) collective-permute-start(bf16[128,2048]{1,0:T(8,128)(2,1)} %get-tuple-element.44), channel_id=1, source_target_pairs={{0,8},{8,0},{1,9},{9,1},{2,10},{10,2},{3,11},{11,3},{4,12},{12,4},... | collective-permute-start | bytes 1572872 | tf_op jit(solution)/shard_map/ppermute | solution.py:91
  608.7 22.6 %collective-permute-start.60 = (bf16[128,2048]{1,0:T(8,128)(2,1)}, bf16[128,2048]{1,0:T(8,128)(2,1)}, u32[]{:S(2)}, u32[]{:S(2)}) collective-permute-start(bf16[128,2048]{1,0:T(8,128)(2,1)} %get-tuple-element.34), channel_id=1, source_target_pairs={{0,16},{16,0},{1,17},{17,1},{2,18},{18,2},{3,19},{19,3},{4,20},{20... | collective-permute-start | bytes 1572872 | tf_op jit(solution)/shard_map/ppermute | solution.py:93
  620.0 20.1 %collective-permute-start.64 = (bf16[128,2048]{1,0:T(8,128)(2,1)}, bf16[128,2048]{1,0:T(8,128)(2,1)S(1)}, u32[]{:S(2)}, u32[]{:S(2)}) collective-permute-start(bf16[128,2048]{1,0:T(8,128)(2,1)} %get-tuple-element.35), channel_id=1, source_target_pairs={{0,8},{8,0},{1,9},{9,1},{2,10},{10,2},{3,11},{11,3},{4,12},{12,4},... | collective-permute-start | bytes 1572872 | tf_op jit(solution)/shard_map/ppermute | solution.py:91
  621.8 29.6 %collective-permute-start.62 = (bf16[128,2048]{1,0:T(8,128)(2,1)}, bf16[128,2048]{1,0:T(8,128)(2,1)S(1)}, u32[]{:S(2)}, u32[]{:S(2)}) collective-permute-start(bf16[128,2048]{1,0:T(8,128)(2,1)} %fusion.30), channel_id=1, source_target_pairs={{0,8},{8,0},{1,9},{9,1},{2,10},{10,2},{3,11},{11,3},{4,12},{12,4},... | collective-permute-start | bytes 1572872 | tf_op jit(solution)/shard_map/ppermute | solution.py:91
  625.4 29.5 %collective-permute-start.38 = (bf16[128,2048]{1,0:T(8,128)(2,1)S(1)}, bf16[128,2048]{1,0:T(8,128)(2,1)S(1)}, u32[]{:S(2)}, u32[]{:S(2)}) collective-permute-start(bf16[128,2048]{1,0:T(8,128)(2,1)S(1)} %get-tuple-element.33), channel_id=1, source_target_pairs={{0,16},{16,0},{1,17},{17,1},{2,18},{18,2},{3,19},{19,3},{4,20},{20... | collective-permute-start | bytes 1572872 | tf_op jit(solution)/shard_map/ppermute | solution.py:93
  631.3 29.7 %collective-permute-start.63 = (bf16[128,2048]{1,0:T(8,128)(2,1)S(1)}, bf16[128,2048]{1,0:T(8,128)(2,1)S(1)}, u32[]{:S(2)}, u32[]{:S(2)}) collective-permute-start(bf16[128,2048]{1,0:T(8,128)(2,1)S(1)} %copy-done.64), channel_id=1, source_target_pairs={{0,8},{8,0},{1,9},{9,1},{2,10},{10,2},{3,11},{11,3},{4,12},{12,4},... | collective-permute-start | bytes 1572872 | tf_op jit(solution)/shard_map/ppermute | solution.py:91
  708.5 117.5 %collective-permute-start.69 = (bf16[1,64,1408]{2,1,0:T(8,128)(2,1)S(1)}, bf16[1,64,1408]{2,1,0:T(8,128)(2,1)S(1)}, u32[]{:S(2)}, u32[]{:S(2)}) collective-permute-start(bf16[1,64,1408]{2,1,0:T(8,128)(2,1)S(1)} %get-tuple-element.85), channel_id=1, source_target_pairs={{0,8},{8,0},{1,9},{9,1},{2,10},{10,2},{3,11},{11,3},{4,12},{12,4},... | collective-permute-start | bytes 540680 | tf_op jit(solution)/shard_map/ppermute | solution.py:91
  710.1 118.4 %collective-permute-start.70 = (bf16[1,64,1408]{2,1,0:T(8,128)(2,1)S(1)}, bf16[1,64,1408]{2,1,0:T(8,128)(2,1)S(1)}, u32[]{:S(2)}, u32[]{:S(2)}) collective-permute-start(bf16[1,64,1408]{2,1,0:T(8,128)(2,1)S(1)} %get-tuple-element.84), channel_id=1, source_target_pairs={{0,16},{16,0},{1,17},{17,1},{2,18},{18,2},{3,19},{19,3},{4,20},{20... | collective-permute-start | bytes 540680 | tf_op jit(solution)/shard_map/ppermute | solution.py:93
  711.5 116.9 %collective-permute-start.71 = (bf16[1,64,1408]{2,1,0:T(8,128)(2,1)S(1)}, bf16[1,64,1408]{2,1,0:T(8,128)(2,1)S(1)}, u32[]{:S(2)}, u32[]{:S(2)}) collective-permute-start(bf16[1,64,1408]{2,1,0:T(8,128)(2,1)S(1)} %get-tuple-element.83), channel_id=1, source_target_pairs={{0,24},{8,16},{16,8},{24,0},{1,25},{9,17},{17,9},{25,1},{2,26},{10... | collective-permute-start | bytes 540680 | tf_op jit(solution)/shard_map/ppermute | solution.py:94
  767.5 61.3 %collective-permute-start.72 = (bf16[1,64,1408]{2,1,0:T(8,128)(2,1)}, bf16[1,64,1408]{2,1,0:T(8,128)(2,1)S(1)}, u32[]{:S(2)}, u32[]{:S(2)}) collective-permute-start(bf16[1,64,1408]{2,1,0:T(8,128)(2,1)} %get-tuple-element.81), channel_id=1, source_target_pairs={{0,8},{8,0},{1,9},{9,1},{2,10},{10,2},{3,11},{11,3},{4,12},{12,4},... | collective-permute-start | bytes 540680 | tf_op jit(solution)/shard_map/ppermute | solution.py:91
  768.9 60.7 %collective-permute-start.73 = (bf16[1,64,1408]{2,1,0:T(8,128)(2,1)}, bf16[1,64,1408]{2,1,0:T(8,128)(2,1)S(1)}, u32[]{:S(2)}, u32[]{:S(2)}) collective-permute-start(bf16[1,64,1408]{2,1,0:T(8,128)(2,1)} %get-tuple-element.80), channel_id=1, source_target_pairs={{0,16},{16,0},{1,17},{17,1},{2,18},{18,2},{3,19},{19,3},{4,20},{20... | collective-permute-start | bytes 540680 | tf_op jit(solution)/shard_map/ppermute | solution.py:93
  (122 other events, 1458.4 us)
Sparse Core Ops, SparseCore 0:
  24.4 34.1 all-gather.5
  60.2 28.0 all-gather.7
  90.0 65.0 all-gather.13
  157.1 63.7 all-gather.11
  222.9 59.1 all-gather.9
  511.4 10.2 reduce-scatter.10
  524.0 10.8 reduce-scatter.14
  537.2 14.9 reduce-scatter.18
  554.6 15.0 reduce-scatter.22
  571.8 15.0 reduce-scatter.26
  589.3 32.4 reduce-scatter.12
  624.0 25.9 reduce-scatter.16
  652.3 54.8 reduce-scatter.20
  709.4 56.0 reduce-scatter.24
  767.6 56.0 reduce-scatter.28

commit v2 on v1

v2 whole, which is shorter than its diff:
```python
import jax
import jax.numpy as jnp
from jax import lax
from jax.experimental import pallas as pl
from jax.experimental.pallas import tpu as pltpu
from jax.sharding import Mesh, PartitionSpec as P

H = 32
KV = 4
HD = 64
TP = 4
GROUP = H // KV
LANES = 128
ROWS = 64

epsilon = 1e-05
rope_base = 10000.0
masked_score = -1e30
bf16 = jnp.bfloat16
f32 = jnp.float32


def after(value, *others):
    return lax.optimization_barrier((value,) + others)[0]


def phase(*values):
    return lax.optimization_barrier(values)


def nn(left, right):
    return lax.dot_general(left, right, (((1,), (0,)), ((), ())), preferred_element_type=f32)


def nt(left, right):
    return lax.dot_general(left, right, (((1,), (1,)), ((), ())), preferred_element_type=f32)


def tn(left, right):
    return lax.dot_general(left, right, (((0,), (0,)), ((), ())), preferred_element_type=f32)


def turn(vectors, cosine, sine):
    half = HD // 2
    out = []
    for at in range(0, vectors.shape[0], HD):
        first, second = vectors[at : at + half], vectors[at + half : at + HD]
        out += [first * cosine - second * sine, second * cosine + first * sine]
    return jnp.concatenate(out, axis=0)


def project_kernel(x_ref, w_ref, cos_ref, sin_ref, qt_ref, kv_ref, inv_ref):
    x = x_ref[...].astype(f32)
    inverse = lax.rsqrt(jnp.mean(x * x, axis=1, keepdims=True) + epsilon)
    inv_ref[...] = inverse
    flat = (nn(x_ref[...], w_ref[...]) * inverse).T
    cosine, sine = cos_ref[...], sin_ref[...]
    q = GROUP * HD
    qt_ref[...] = (turn(flat[:q], cosine, sine) * HD**-0.5).astype(bf16)
    kv = jnp.concatenate([turn(flat[q : q + HD], cosine, sine), flat[q + HD :]], axis=0)
    kv_ref[...] = kv.T.astype(bf16)


def project(x, w, cosine, sine, rows):
    total, width = x.shape
    n = w.shape[1]
    steps, q = total // rows, GROUP * HD
    return pl.pallas_call(
        project_kernel,
        grid=(steps,),
        in_specs=[
            pl.BlockSpec((rows, width), lambda i: (i, 0)),
            pl.BlockSpec((width, n), lambda i: (0, 0)),
            pl.BlockSpec((HD // 2, rows), lambda i: (0, i)),
            pl.BlockSpec((HD // 2, rows), lambda i: (0, i)),
        ],
        out_specs=[
            pl.BlockSpec((None, q, rows), lambda i: (i, 0, 0)),
            pl.BlockSpec((rows, 2 * HD), lambda i: (i, 0)),
            pl.BlockSpec((rows, 1), lambda i: (i, 0)),
        ],
        out_shape=[
            jax.ShapeDtypeStruct((steps, q, rows), bf16),
            jax.ShapeDtypeStruct((total, 2 * HD), bf16),
            jax.ShapeDtypeStruct((total, 1), f32),
        ],
        compiler_params=pltpu.CompilerParams(vmem_limit_bytes=40 << 20),
        cost_estimate=pl.CostEstimate(
            flops=2 * total * width * n,
            bytes_accessed=2 * (total * width + width * n + total * n),
            transcendentals=0,
        ),
        name="project",
    )(x, w, cosine, sine)


def attend_kernel(qp_ref, kp_ref, qt_ref, kv_ref, wo_ref, ot_ref, lse_ref, part_ref, bias_ref):
    bias_ref[...] = jnp.where(qp_ref[...] >= kp_ref[...], 0.0, masked_score)
    kv = kv_ref[...]
    vt = kv.astype(f32).T[HD:].astype(bf16)
    zero = jnp.zeros((HD, qt_ref.shape[1]), bf16)
    for h in range(GROUP):
        at = slice(h * HD, (h + 1) * HD)
        scores = nn(kv, jnp.concatenate([qt_ref[at, :], zero], axis=0)) + bias_ref[...]
        top = jnp.max(scores, axis=0, keepdims=True)
        exponent = jnp.exp(scores - top)
        total = jnp.sum(exponent, axis=0, keepdims=True)
        ot_ref[at, :] = (nn(vt, exponent.astype(bf16)) / total).astype(bf16)
        lse_ref[h : h + 1, :] = top + jnp.log(total)
    part_ref[...] = tn(ot_ref[...], wo_ref[...]).astype(part_ref.dtype)


def attend(qp, kp, qt, kv, wo, kind):
    n, rows = qt.shape
    keys, width = kv.shape[0], wo.shape[1]
    return pl.pallas_call(
        attend_kernel,
        out_shape=[
            jax.ShapeDtypeStruct((n, rows), bf16),
            jax.ShapeDtypeStruct((GROUP, rows), f32),
            jax.ShapeDtypeStruct((rows, width), kind),
        ],
        scratch_shapes=[pltpu.VMEM((keys, rows), f32)],
        compiler_params=pltpu.CompilerParams(vmem_limit_bytes=40 << 20),
        cost_estimate=pl.CostEstimate(
            flops=2 * rows * n * (keys * 2 * 4 + width),
            bytes_accessed=2 * (n * rows * 2 + keys * 2 * HD + n * width + rows * width),
            transcendentals=GROUP * rows * keys,
        ),
        name="attend",
    )(qp, kp, qt, kv, wo)


def attend_back_kernel(
    qp_ref,
    kp_ref,
    qt_ref,
    kv_ref,
    wo_ref,
    ot_ref,
    lse_ref,
    db_ref,
    inv_ref,
    cos_ref,
    sin_ref,
    dq_ref,
    dqs_ref,
    dkv_ref,
    bias_ref,
    dat_ref,
    dqt_ref,
):
    bias_ref[...] = jnp.where(qp_ref[...] >= kp_ref[...], 0.0, masked_score)
    kv = kv_ref[...]
    kt = kv.astype(f32).T[:HD].astype(bf16)
    zero = jnp.zeros((HD, qt_ref.shape[1]), bf16)
    dat_ref[...] = nt(wo_ref[...], db_ref[...]).astype(bf16)
    for h in range(GROUP):
        at = slice(h * HD, (h + 1) * HD)
        q_low = jnp.concatenate([qt_ref[at, :], zero], axis=0)
        da_high = jnp.concatenate([zero, dat_ref[at, :]], axis=0)
        weights = jnp.exp(nn(kv, q_low) + bias_ref[...] - lse_ref[h : h + 1, :])
        delta = jnp.sum(
            dat_ref[at, :].astype(f32) * ot_ref[at, :].astype(f32), axis=0, keepdims=True
        )
        ds = (weights * (nn(kv, da_high) - delta)).astype(bf16)
        dkv = nt(ds, q_low) + nt(weights.astype(bf16), da_high)
        if h == 0:
            dkv_ref[...] = dkv
        else:
            dkv_ref[...] += dkv
        dqt_ref[at, :] = nn(kt, ds)
    dq = (turn(dqt_ref[...], cos_ref[...], -sin_ref[...]) * HD**-0.5).T
    dq_ref[...] = dq.astype(bf16)
    dqs_ref[...] = (dq * inv_ref[...]).astype(bf16)


def attend_back(qp, kp, qt, kv, wo, ot, lse, db, inv, cosine, sine):
    n, rows = qt.shape
    keys, width = kv.shape[0], wo.shape[1]
    return pl.pallas_call(
        attend_back_kernel,
        out_shape=[
            jax.ShapeDtypeStruct((rows, n), bf16),
            jax.ShapeDtypeStruct((rows, n), bf16),
            jax.ShapeDtypeStruct((keys, 2 * HD), f32),
        ],
        scratch_shapes=[
            pltpu.VMEM((keys, rows), f32),
            pltpu.VMEM((n, rows), bf16),
            pltpu.VMEM((n, rows), f32),
        ],
        compiler_params=pltpu.CompilerParams(vmem_limit_bytes=40 << 20),
        cost_estimate=pl.CostEstimate(
            flops=2 * rows * n * (keys * 5 * 4 + width),
            bytes_accessed=2 * (n * rows * 4 + keys * 6 * HD + n * width + rows * width),
            transcendentals=GROUP * rows * keys,
        ),
        name="attend_back",
    )(qp, kp, qt, kv, wo, ot, lse, db, inv, cosine, sine)


def reorder_lanes(v, ordered):
    shape, size = ordered
    out = []
    for index in shape:
        out.append(v[:, index * size : (index + 1) * size])
    return jnp.concatenate(out, axis=1)


def block_orders(width, holders):
    held = [m * holders + h for h in range(holders) for m in range(TP)]
    natural = [held.index(i) for i in range(len(held))]
    size = width // len(held)
    return (held, size), (natural, size)


def small_call(kernel, name, inputs, outputs):
    size = sum(v.size * v.dtype.itemsize for v in (*inputs, *outputs))
    return pl.pallas_call(
        kernel,
        out_shape=outputs,
        compiler_params=pltpu.CompilerParams(vmem_limit_bytes=40 << 20),
        cost_estimate=pl.CostEstimate(flops=size, bytes_accessed=size, transcendentals=0),
        name=name,
    )(*inputs)


def hold_tokens(tokens, held):
    def kernel(x_ref, out_ref):
        out_ref[...] = reorder_lanes(x_ref[...].astype(f32), held).astype(bf16)

    return small_call(
        kernel, "hold_tokens", [tokens], [jax.ShapeDtypeStruct(tokens.shape, bf16)]
    )[0]


def summed(own_ref, a2_ref, a1_ref, b1_ref, b2_ref, at, half):
    first, second = (a2_ref, a1_ref) if at < half else (b1_ref, b2_ref)
    rows = slice(at, at + ROWS)
    come = slice(at % half, at % half + ROWS)
    return own_ref[rows, :] + first[come, :].astype(f32) + second[come, :].astype(f32)


def finish_middle(tokens, pieces, held):
    rows, width = tokens.shape

    def kernel(x_ref, *refs):
        sums, (mid_ref, inv_ref, n2_ref) = refs[:5], refs[5:]
        for at in range(0, rows, ROWS):
            here = slice(at, at + ROWS)
            middle = x_ref[here, :].astype(f32) + summed(*sums, at, rows // 2)
            inverse = lax.rsqrt(jnp.mean(middle * middle, axis=1, keepdims=True) + epsilon)
            mid_ref[here, :] = middle
            inv_ref[here, :] = inverse
            n2_ref[here, :] = reorder_lanes(middle * inverse, held).astype(bf16)

    return small_call(
        kernel,
        "finish_middle",
        [tokens, *pieces],
        [
            jax.ShapeDtypeStruct((rows, width), f32),
            jax.ShapeDtypeStruct((rows, 1), f32),
            jax.ShapeDtypeStruct((rows, width), bf16),
        ],
    )


def finish_norm_back(grad, normed_from, inverse, pieces, natural, last):
    rows, width = grad.shape

    def kernel(g_ref, x_ref, inv_ref, *refs):
        sums, outs = refs[:5], refs[5:]
        for at in range(0, rows, ROWS):
            here = slice(at, at + ROWS)
            scaled = reorder_lanes(summed(*sums, at, rows // 2), natural)
            inverse = inv_ref[here, :]
            normed = x_ref[here, :].astype(f32) * inverse
            mean = jnp.mean(scaled * normed, axis=1, keepdims=True)
            total = g_ref[here, :].astype(f32) + inverse * (scaled - normed * mean)
            outs[0][here, :] = total
            if not last:
                outs[1][here, :] = total.astype(bf16)

    shapes = [jax.ShapeDtypeStruct((rows, width), f32)]
    if not last:
        shapes.append(jax.ShapeDtypeStruct((rows, width), bf16))
    return small_call(
        kernel, "finish_norm_back", [grad, normed_from, inverse, *pieces], shapes
    )


def interleaved(i):
    return slice(2 * i * LANES, (2 * i + 1) * LANES), slice((2 * i + 1) * LANES, (2 * i + 2) * LANES)


def activate_kernel(n_ref, w_ref, m_ref, slope_ref):
    both = nn(n_ref[...], w_ref[...])
    for i in range(m_ref.shape[1] // LANES):
        gate_at, up_at = interleaved(i)
        gate, up = both[:, gate_at], both[:, up_at]
        sigmoid = jax.nn.sigmoid(gate)
        silu = gate * sigmoid
        m_ref[:, i * LANES : (i + 1) * LANES] = (silu * up).astype(bf16)
        slope_ref[:, gate_at] = (up * (sigmoid + silu * (1.0 - sigmoid))).astype(bf16)
        slope_ref[:, up_at] = silu.astype(bf16)


def activate(n2, gate_up, tile=256):
    total, width = n2.shape
    ff = gate_up.shape[1] // 2
    return pl.pallas_call(
        activate_kernel,
        grid=(pl.cdiv(ff, tile),),
        in_specs=[
            pl.BlockSpec((total, width), lambda j: (0, 0)),
            pl.BlockSpec((width, 2 * tile), lambda j: (0, j)),
        ],
        out_specs=[
            pl.BlockSpec((total, tile), lambda j: (0, j)),
            pl.BlockSpec((total, 2 * tile), lambda j: (0, j)),
        ],
        out_shape=[
            jax.ShapeDtypeStruct((total, ff), bf16),
            jax.ShapeDtypeStruct((total, 2 * ff), bf16),
        ],
        compiler_params=pltpu.CompilerParams(vmem_limit_bytes=48 << 20),
        cost_estimate=pl.CostEstimate(
            flops=4 * total * width * ff,
            bytes_accessed=2 * (total * width + 2 * width * ff + 3 * total * ff),
            transcendentals=total * ff,
        ),
        name="activate",
    )(n2, gate_up)


def activate_back_kernel(g_ref, down_ref, slope_ref, d_ref):
    dm = nt(g_ref[...], down_ref[...])
    for i in range(dm.shape[1] // LANES):
        part = dm[:, i * LANES : (i + 1) * LANES]
        for at in interleaved(i):
            d_ref[:, at] = (part * slope_ref[:, at].astype(f32)).astype(bf16)


def activate_back(g, down, slopes, tile=256):
    total, width = g.shape
    ff = down.shape[0]
    return pl.pallas_call(
        activate_back_kernel,
        grid=(pl.cdiv(ff, tile),),
        in_specs=[
            pl.BlockSpec((total, width), lambda j: (0, 0)),
            pl.BlockSpec((tile, width), lambda j: (j, 0)),
            pl.BlockSpec((total, 2 * tile), lambda j: (0, j)),
        ],
        out_specs=pl.BlockSpec((total, 2 * tile), lambda j: (0, j)),
        out_shape=jax.ShapeDtypeStruct((total, 2 * ff), bf16),
        compiler_params=pltpu.CompilerParams(vmem_limit_bytes=48 << 20),
        cost_estimate=pl.CostEstimate(
            flops=2 * total * width * ff,
            bytes_accessed=2 * (total * width + width * ff + 4 * total * ff),
            transcendentals=0,
        ),
        name="activate_back",
    )(g, down, slopes)


def split_gate_up(w_gate, w_up, gain):
    own, total = w_gate.shape
    ff = total // TP

    def kernel(gate_ref, up_ref, gain_ref, out_ref):
        for g in range(TP):
            for j in range(ff // LANES):
                here = slice(g * ff + j * LANES, g * ff + (j + 1) * LANES)
                for ref, at in zip((gate_ref, up_ref), interleaved(j)):
                    out_ref[g, :, at] = (ref[:, here].astype(f32) * gain_ref[...]).astype(bf16)

    return small_call(
        kernel,
        "split_gate_up",
        [w_gate, w_up, gain],
        [jax.ShapeDtypeStruct((TP, own, 2 * ff), bf16)],
    )[0]


def merge_gate_up(raw, w_gate, w_up, gain):
    own, total = w_gate.shape
    ff = total // TP

    def kernel(in_ref, gate_ref, up_ref, gain_ref, dgate_ref, dup_ref, dgain_ref):
        dgain = jnp.zeros((own, LANES), f32)
        for g in range(TP):
            for j in range(ff // LANES):
                here = slice(g * ff + j * LANES, g * ff + (j + 1) * LANES)
                for ref, out_ref, at in zip(
                    (gate_ref, up_ref), (dgate_ref, dup_ref), interleaved(j)
                ):
                    part = in_ref[g, :, at].astype(f32)
                    dgain += part * ref[:, here].astype(f32)
                    out_ref[:, here] = part * gain_ref[...]
        dgain_ref[...] = jnp.sum(dgain, axis=1, keepdims=True)

    return small_call(
        kernel,
        "merge_gate_up",
        [raw, w_gate, w_up, gain],
        [
            jax.ShapeDtypeStruct((own, total), f32),
            jax.ShapeDtypeStruct((own, total), f32),
            jax.ShapeDtypeStruct((own, 1), f32),
        ],
    )


def make_body(reps, ctxs):
    pair = [(0, 1), (1, 0)]

    def swap(v, k):
        if k == 0:
            return v
        if k == 1:
            return lax.ppermute(v, "tx", pair)
        if k == 2:
            return lax.ppermute(v, "ty", pair)
        return lax.ppermute(v, ("ty", "tx"), [(i, i ^ 3) for i in range(TP)])

    def swap_ctx(v, j):
        return lax.ppermute(v, "ctx", [(i, i ^ j) for i in range(ctxs)]) if j else v

    def halves(v):
        half = v.shape[0] // 2
        return v[:half], v[half:]

    def joined(a, b):
        return jnp.concatenate([p for k in range(TP) for p in (a[k], b[k])], axis=0)

    def gather(v):
        a, b = halves(v)
        ax, by = swap(a, 1), swap(b, 2)
        ay, bx = swap(a, 2), swap(b, 1)
        return joined((a, ax, ay, swap(ax, 2)), (b, bx, by, swap(by, 1)))

    def scatter_far(part):
        a, b = halves(part.astype(bf16))
        return swap(a, 2), swap(b, 1)

    def scatter_near(part_x, part_y, far):
        a1, b1 = halves(part_x)
        a2, b2 = halves(part_y)
        a1 = (a1.astype(f32) + far[0].astype(f32)).astype(bf16)
        b2 = (b2.astype(f32) + far[1].astype(f32)).astype(bf16)
        return [swap(a2.astype(bf16), 2), swap(a1, 1), swap(b1.astype(bf16), 1), swap(b2, 2)]

    def scatter_sum(parts):
        a2, a1, b1, b2 = scatter_near(parts[1], parts[2], scatter_far(parts[3]))
        come = [a2.astype(f32) + a1.astype(f32), b1.astype(f32) + b2.astype(f32)]
        return parts[0].astype(f32) + jnp.concatenate(come, axis=0)

    def exchange(blocks, t):
        out = jnp.zeros_like(blocks)
        for k in range(TP):
            mine = lax.dynamic_index_in_dim(blocks, t ^ k, 0, keepdims=True)
            out = lax.dynamic_update_slice_in_dim(out, swap(mine, k), t ^ k, 0)
        return out

    def spread(blocks, t):
        return exchange(blocks, t).reshape(-1, blocks.shape[2])

    def collect(summed, t):
        return exchange(summed.reshape(TP, -1, summed.shape[1]), t)

    def whole(v):
        return lax.all_gather(v, ("rep", "ctx"), axis=0, tiled=True)

    def over_reps(left, right):
        if reps != 2:
            part = tn(left, right).astype(bf16)
            return lax.psum_scatter(part, "rep", scatter_dimension=0, tiled=True)
        r = lax.axis_index("rep")
        half = left.shape[1] // 2
        other = lax.dynamic_slice_in_dim(left, (1 - r) * half, half, 1)
        sent = lax.ppermute(tn(other, right).astype(bf16), "rep", pair)
        mine = lax.dynamic_slice_in_dim(left, r * half, half, 1)
        return (tn(mine, right) + sent.astype(f32)).astype(bf16)

    def owned(part):
        return lax.psum_scatter(part, "ctx", scatter_dimension=0, tiled=True)

    def body(
        tokens,
        span_order,
        norm_attn,
        w_query,
        w_key,
        w_value,
        w_out,
        norm_mlp,
        w_gate,
        w_up,
        w_down,
        out_grad,
    ):
        count, width = tokens.shape
        own = w_query.shape[0]
        held, natural = block_orders(width, reps * ctxs)
        span = count * ctxs // span_order.shape[1]
        q_cols, kv_cols = GROUP * HD, HD
        t = 2 * lax.axis_index("ty") + lax.axis_index("tx")
        c = lax.axis_index("ctx")

        def part_of(v, k):
            return v[k * count : (k + 1) * count]

        orders = [swap(span_order, k)[0] for k in range(TP)]
        offsets = jnp.arange(span, dtype=jnp.int32)
        per = count // span

        def block_positions(order, member):
            picked = lax.dynamic_slice_in_dim(order, member * per, per)
            return (picked[:, None] * span + offsets[None, :]).reshape(-1)

        query_positions = [block_positions(order, c) for order in orders]
        key_positions = [
            jnp.concatenate([block_positions(order, c ^ j) for j in range(ctxs)])
            for order in orders
        ]
        half_dim = HD // 2
        frequency = jnp.power(rope_base, -jnp.arange(half_dim, dtype=f32) / half_dim)
        angles = frequency[:, None] * jnp.concatenate(query_positions).astype(f32)[None, :]
        cosine, sine = jnp.cos(angles), jnp.sin(angles)

        gain_attn = norm_attn.astype(f32)[:, None]
        gain_mlp = norm_mlp.astype(f32)[:, None]

        def by_group(w):
            w = (w.astype(f32) * gain_attn).astype(bf16)
            return w.reshape(own, TP, -1).transpose(1, 0, 2)

        out = whole(w_out)
        blocks = jnp.concatenate([by_group(w) for w in (w_query, w_key, w_value)], axis=2)
        a, b = halves(hold_tokens(tokens, held))
        qkv_mine, ax, by = phase(spread(blocks, t), swap(a, 1), swap(b, 2))
        qkv = whole(qkv_mine)
        gate_up_blocks = split_gate_up(after(w_gate, qkv_mine), w_up, gain_mlp)
        ay, bx, axy, bxy, gate_up_blocks = phase(
            swap(a, 2), swap(b, 1), swap(ax, 2), swap(by, 1), gate_up_blocks
        )
        x_all = joined((a, ax, ay, axy), (b, bx, by, bxy))
        gate_up_mine = spread(gate_up_blocks, t)
        gate_up = whole(gate_up_mine)
        down = whole(after(w_down, gate_up_mine))

        qt, kv, inverse_all = project(x_all, qkv, cosine, sine, count)
        kv = kv.reshape(TP, count, 2 * kv_cols)
        kv, g_all = phase(
            jnp.stack([swap_ctx(kv, j) for j in range(ctxs)], axis=1),
            gather(after(out_grad, kv)),
        )
        kv_seq = kv.reshape(TP, ctxs * count, 2 * kv_cols)
        mixed, logsum, parts = [None] * TP, [None] * TP, [None] * TP

        def attend_to(k, queries):
            mixed[k], logsum[k], parts[k] = attend(
                query_positions[k][None, :],
                key_positions[k][:, None],
                queries,
                kv_seq[k],
                out,
                bf16 if k else f32,
            )

        attend_to(3, qt[3])
        far = scatter_far(parts[3])
        qt = after(qt, parts[3])
        attend_to(2, qt[2])
        attend_to(1, qt[1])
        far, parts[1], parts[2], qt = phase(far, parts[1], parts[2], qt)
        near = scatter_near(parts[1], parts[2], far)
        attend_to(0, qt[0])
        middle, inverse_mid, n2 = finish_middle(tokens, [parts[0], *near], held)
        n2_all = gather(n2)

        act, slopes = activate(n2_all, gate_up)
        part_down = over_reps(act, g_all)
        slopes, part_down = phase(slopes, part_down)
        sum_down = owned(part_down)
        grad_act = activate_back(g_all, down, slopes)
        back_far = nt(part_of(grad_act, 3), gate_up)
        far = scatter_far(back_far)
        back_near = nt(after(grad_act, back_far)[: 3 * count], gate_up)
        far, back_near = phase(far, back_near)
        near = scatter_near(part_of(back_near, 1), part_of(back_near, 2), far)
        part_gate_up = over_reps(n2_all, after(grad_act, back_near))
        near, part_gate_up = phase(near, part_gate_up)
        sum_gate_up = owned(part_gate_up)
        grad_middle, db = finish_norm_back(
            out_grad, middle, inverse_mid, [part_of(back_near, 0), *near], natural, False
        )

        dq, dqs, dkv = [None] * TP, [None] * TP, [None] * TP

        def attend_back_to(k, grads):
            dq[k], dqs[k], dkv[k] = attend_back(
                query_positions[k][None, :],
                key_positions[k][:, None],
                qt[k],
                kv_seq[k],
                out,
                mixed[k],
                logsum[k],
                grads,
                part_of(inverse_all, k),
                cosine[:, k * count : (k + 1) * count],
                sine[:, k * count : (k + 1) * count],
            )

        a, b = halves(db)
        ax, by = swap(a, 1), swap(b, 2)
        attend_back_to(0, db)
        a, b, ax, by, dq[0] = phase(a, b, ax, by, dq[0])
        ay, bx = swap(a, 2), swap(b, 1)
        forward = nn(after(act, ax), down)
        ay, bx, forward = phase(ay, bx, forward)
        axy, bxy = swap(ax, 2), swap(by, 1)
        attend_back_to(1, jnp.concatenate([ax, bx], axis=0))
        attend_back_to(2, jnp.concatenate([ay, by], axis=0))
        axy, bxy, dq[1], dq[2] = phase(axy, bxy, dq[1], dq[2])
        attend_back_to(3, jnp.concatenate([axy, bxy], axis=0))
        db_all = joined((a, ax, ay, axy), (b, bx, by, bxy))
        layer_out = (
            middle + scatter_sum([part_of(after(forward, axy), k) for k in range(TP)])
        ).astype(bf16)
        dkv = jnp.stack(dkv).reshape(TP, ctxs, count, 2 * kv_cols)
        local = dkv[:, 0]
        for j in range(1, ctxs):
            local = local + swap_ctx(dkv[:, j].astype(bf16), j).astype(f32)
        part_out = over_reps(jnp.concatenate(mixed, axis=1).T, db_all)
        local, part_out = phase(local, part_out)
        sum_out = owned(part_out)
        local = local.reshape(TP * count, 2 * kv_cols)
        first, second = local[:, :half_dim], local[:, half_dim:kv_cols]
        dkv = jnp.concatenate(
            [
                first * cosine.T + second * sine.T,
                second * cosine.T - first * sine.T,
                local[:, kv_cols:],
            ],
            axis=1,
        )
        grad_proj = jnp.concatenate([jnp.concatenate(dq, axis=0), dkv.astype(bf16)], axis=1)
        scaled_proj = jnp.concatenate(
            [jnp.concatenate(dqs, axis=0), (dkv * inverse_all).astype(bf16)], axis=1
        )
        back_far = nt(part_of(grad_proj, 3), qkv)
        far = scatter_far(back_far)
        back_near = nt(after(grad_proj, back_far)[: 3 * count], qkv)
        far, back_near = phase(far, back_near)
        near = scatter_near(part_of(back_near, 1), part_of(back_near, 2), far)
        part_qkv = over_reps(x_all, after(scaled_proj, back_near))
        near, part_qkv = phase(near, part_qkv)
        sum_qkv = owned(part_qkv)
        (input_grad,) = finish_norm_back(
            grad_middle,
            tokens,
            part_of(inverse_all, 0),
            [part_of(back_near, 0), *near],
            natural,
            True,
        )

        sum_gate_up = collect(after(sum_gate_up, input_grad), t)
        grad_gate, grad_up, grad_norm_mlp = merge_gate_up(sum_gate_up, w_gate, w_up, gain_mlp)
        sum_down, sum_out, sum_qkv = after((sum_down, sum_out, sum_qkv), grad_norm_mlp)
        sum_qkv = collect(sum_qkv, t)

        def rows_of(v):
            return v.transpose(1, 0, 2).reshape(own, -1).astype(f32)

        raw_query = rows_of(sum_qkv[..., :q_cols])
        raw_key = rows_of(sum_qkv[..., q_cols : q_cols + kv_cols])
        raw_value = rows_of(sum_qkv[..., q_cols + kv_cols :])
        grad_norm_attn = (
            jnp.sum(raw_query * w_query.astype(f32), axis=1)
            + jnp.sum(raw_key * w_key.astype(f32), axis=1)
            + jnp.sum(raw_value * w_value.astype(f32), axis=1)
        )
        return (
            layer_out,
            input_grad,
            grad_norm_attn,
            raw_query * gain_attn,
            raw_key * gain_attn,
            raw_value * gain_attn,
            sum_out.astype(f32),
            grad_norm_mlp[:, 0],
            grad_gate,
            grad_up,
            sum_down.astype(f32),
        )

    return body


def solution(mesh):
    sequences, ctxs = mesh.shape["dp"], mesh.shape["ctx"]
    reps = sequences // TP
    names = ("ty", "tx", "rep", "ctx")
    grid = Mesh(mesh.devices.reshape(2, 2, reps, ctxs), names)
    matrix, vector = P(names, None), P(names)
    order = P(("ty", "tx", "rep"), None)
    weights = [vector, matrix, matrix, matrix, matrix, vector, matrix, matrix, matrix]
    return jax.shard_map(
        make_body(reps, ctxs),
        mesh=grid,
        in_specs=(matrix, order, *weights, matrix),
        out_specs=(matrix, matrix, *weights),
        check_vma=False,
    )
```

time: 853 us -> 660 us (0.77)
  waiting for transfers between devices: 338 us -> 231 us
  Pallas kernels: 0 us -> 103 us
  matrix products: 189 us -> 89.3 us
  other arithmetic: 94.4 us -> 41.5 us
  starting transfers between devices: 103 us -> 83.1 us
  local copies, waits for them, and re-layouts: 102 us -> 92.6 us
    reduce_scatter x10 -> x4, waiting for transfers between devices: 130 us -> 18.2 us  [owned(): return lax.psum_scatter(part, 'ctx', scatter_dimension=0, tiled=True)]
    pallas_call x0 -> x17, Pallas kernels: none -> 103 us  [the longest x4 27.1 us: attend_back(): pl.pallas_call(attend_back_kernel, out_shape=[jax.ShapeDtypeStruct((rows,...]
    dot_general x42 -> x13, matrix products: 189 us -> 89.3 us  [the longest x8 53.6 us: tn(): lax.dot_general(left, right, (((0,), (0,)), ((), ())), preferred_element_...]
    ppermute x68, waiting for transfers between devices: 187 us -> 212 us  [the longest x29 74.9 us: swap(): return lax.ppermute(v, 'tx', pair)]
    unnamed x233 -> x274, local copies, waits for them, and re-layouts: 36.3 us -> 57.5 us
    another operation x16 -> x4, local copies, waits for them, and re-layouts: 20.5 us -> 0.25 us  [the longest x8 17.2 us: body(): grad_pairs = jnp.stack(grad_pairs, axis=1)]
    reduce_sum x12 -> x0, other arithmetic: 19.4 us -> none  [the longest x4 11.3 us: attend(): total = jnp.sum(exponent, axis=-1, keepdims=True)]
    ppermute x68, starting transfers between devices: 94.3 us -> 75.7 us  [the longest x29 34.8 us: swap(): return lax.ppermute(v, 'tx', pair)]
  transfers between devices with their start and end apart: 90 -> 81, of which waited for: 50 -> 33; matrix products, arithmetic and copies ran while one was open for 29% -> 26% of each run, Pallas kernels for 0% -> 14%
where the time goes in v2:
time: 660 us; the launch traced here: 657 us
  waiting for transfers between devices  231 us (35%)
  Pallas kernels  103 us (16%)
  local copies, waits for them, and re-layouts  92.6 us (14%)
  matrix products  89.3 us (14%)
  starting transfers between devices  83.1 us (13%)
  other arithmetic  41.5 us (6%)
  between operations  16.2 us (2%)
    ppermute x29, waiting for transfers between devices, swap(): return lax.ppermute(v, 'tx', pair)  74.9 us
    ppermute x29, waiting for transfers between devices, swap(): return lax.ppermute(v, 'ty', pair)  68.4 us
    ppermute x6, waiting for transfers between devices, swap_ctx(): return lax.ppermute(v, 'ctx', [(i, i ^ j) for i in range(ctxs)]) if j else v  63.5 us
    unnamed x274, local copies, waits for them, and re-layouts  57.5 us
    dot_general x8, matrix products, tn(): lax.dot_general(left, right, (((0,), (0,)), ((), ())), preferred_element_...  53.6 us
    ppermute x29, starting transfers between devices, swap(): return lax.ppermute(v, 'tx', pair)  34.8 us
    ppermute x29, starting transfers between devices, swap(): return lax.ppermute(v, 'ty', pair)  31.9 us
    pallas_call x4, Pallas kernels, attend_back(): pl.pallas_call(attend_back_kernel, out_shape=[jax.ShapeDtypeStruct((rows,...  27.1 us
  transfers between devices with their start and end apart: 81, of which 33 were waited for; matrix products, arithmetic and copies ran while one was open for 26% of the time, Pallas kernels for 14%

profile of v2, /device:TPU:0, one launch (start us, length us, event | category | flops | bytes accessed | tf_op | source)
XLA Modules:
  0.0 657.0 jit_solution(14786886607931560642)
XLA Ops:
  10.0 2.9 collective-permute-start.4
  17.4 2.9 collective-permute-start.3
  20.3 7.4 %collective-permute-done.1 = bf16[1,64,640]{2,1,0:T(8,128)(2,1)S(1)} collective-permute-done((bf16[1,64,640]{2,1,0:T(8,128)(2,1)S(1)}, bf16[1,64,640]{2,1,0:T(8,128)(2,1)S(1)}, u32[]{:S(2)}, u32[]{:S(2)}) %collective-permute-start.1) | collective-permute-done | bytes 81952 | tf_op jit(solution)/shard_map/ppermute | solution.py:424
  27.7 2.4 collective-permute-done.2
  36.7 10.2 %collective-permute-done.6 = bf16[128,2048]{1,0:T(8,128)(2,1)} collective-permute-done((bf16[128,2048]{1,0:T(8,128)(2,1)}, bf16[128,2048]{1,0:T(8,128)(2,1)}, u32[]{:S(2)}, u32[]{:S(2)}) %collective-permute-start.6) | collective-permute-done | bytes 524320 | tf_op jit(solution)/shard_map/ppermute | solution.py:426
  48.4 7.1 %collective-permute-done.8 = bf16[128,2048]{1,0:T(8,128)(2,1)} collective-permute-done((bf16[128,2048]{1,0:T(8,128)(2,1)}, bf16[128,2048]{1,0:T(8,128)(2,1)}, u32[]{:S(2)}, u32[]{:S(2)}) %collective-permute-start.8) | collective-permute-done | bytes 524320 | tf_op jit(solution)/shard_map/ppermute | solution.py:426
  59.9 7.7 %collective-permute-done.27 = bf16[1,64,2816]{2,1,0:T(8,128)(2,1)S(1)} collective-permute-done((bf16[1,64,2816]{2,1,0:T(8,128)(2,1)S(1)}, bf16[1,64,2816]{2,1,0:T(8,128)(2,1)S(1)}, u32[]{:S(2)}, u32[]{:S(2)}) %collective-permute-start.27) | collective-permute-done | bytes 360480 | tf_op jit(solution)/shard_map/ppermute | solution.py:424
  67.6 5.2 collective-permute-done.28
  98.1 4.8 project.1
  102.9 3.6 collective-permute-start.14
  110.7 8.0 %collective-permute-done.14 = bf16[4,256,128]{2,1,0:T(8,128)(2,1)S(1)} collective-permute-done((bf16[4,256,128]{2,1,0:T(8,128)(2,1)S(1)}, bf16[4,256,128]{2,1,0:T(8,128)(2,1)S(1)}, u32[]{:S(2)}, u32[]{:S(2)}) %collective-permute-start.14) | collective-permute-done | bytes 262176 | tf_op jit(solution)/shard_map/ppermute | solution.py:430
  120.3 29.7 %collective-permute-done.13 = bf16[4,256,128]{2,1,0:T(8,128)(2,1)S(1)} collective-permute-done((bf16[4,256,128]{2,1,0:T(8,128)(2,1)S(1)}, bf16[4,256,128]{2,1,0:T(8,128)(2,1)S(1)}, u32[]{:S(2)}, u32[]{:S(2)}) %collective-permute-start.13) | collective-permute-done | bytes 262176 | tf_op jit(solution)/shard_map/ppermute | solution.py:430
  156.2 8.6 %collective-permute-done.17 = bf16[128,2048]{1,0:T(8,128)(2,1)S(1)} collective-permute-done((bf16[128,2048]{1,0:T(8,128)(2,1)S(1)}, bf16[128,2048]{1,0:T(8,128)(2,1)S(1)}, u32[]{:S(2)}, u32[]{:S(2)}) %collective-permute-start.17) | collective-permute-done | bytes 524320 | tf_op jit(solution)/shard_map/ppermute | solution.py:426
  166.6 5.6 collective-permute-done.19
  179.4 6.1 attend.4
  188.2 6.1 attend.5
  194.9 6.3 attend.6
  214.5 6.0 attend.7
  222.7 3.5 collective-permute-done.25.refs_3_
  238.1 2.4 constant_dynamic-update-slice_fusion.20
  240.4 8.3 %collective-permute-done.30 = bf16[128,2048]{1,0:T(8,128)(2,1)} collective-permute-done((bf16[128,2048]{1,0:T(8,128)(2,1)}, bf16[128,2048]{1,0:T(8,128)(2,1)}, u32[]{:S(2)}, u32[]{:S(2)}) %collective-permute-start.30) | collective-permute-done | bytes 524320 | tf_op jit(solution)/shard_map/ppermute | solution.py:424
  253.1 5.7 collective-permute-done.31
  266.8 19.5 %activate.1 = (bf16[1024,1408]{1,0:T(8,128)(2,1)S(1)}, bf16[1024,2816]{1,0:T(8,128)(2,1)}) custom-call(bf16[1024,2048]{1,0:T(8,128)(2,1)} %constant_dynamic-update-slice_fusion.14.n_ref, bf16[2048,2816]{1,0:T(8,128)(2,1)} %all-gather.11.cloned.1.call-done.w_ref), custom_call_target="tpu_custom_call" | custom-call | flops 11811160064 | bytes 24379392 | tf_op jit(solution)/shard_map/activate/pallas_call | solution.py:313
  286.2 8.3 %convolution_convert_fusion.1 = bf16[704,2048]{1,0:T(8,128)(2,1)} fusion(bf16[1024,2048]{1,0:T(8,128)(2,1)} %constant_dynamic-update-slice_fusion.7.g_ref, bf16[1024,1408]{1,0:T(8,128)(2,1)S(1)} %get-tuple-element.157, s32[]{:T(128)S(6)} %select_n.99), kind=kOutput, calls=%fused_computation.5 | convolution fusion | flops 2954231808 | bytes 8650756 | tf_op jit(solution)/shard_map/dot_general | solution.py:40
  294.5 5.6 collective-permute-done.36
  300.2 8.6 %add_convert_fusion.1 = bf16[704,2048]{1,0:T(8,128)(2,1)} fusion(bf16[704,2048]{1,0:T(8,128)(2,1)} %collective-permute-done.36, bf16[1024,2048]{1,0:T(8,128)(2,1)} %constant_dynamic-update-slice_fusion.7.g_ref, bf16[1024,1408]{1,0:T(8,128)(2,1)} %copy-done.14, s32[]{:T(128)S(6)} %select_n.98), kind=kOutput, calls=%fused_computation.1 | convolution fusion | flops 2957115392 | bytes 11534340 | tf_op jit(solution)/shard_map/dot_general | solution.py:40
  308.8 13.3 %activate_back.1 = bf16[1024,2816]{1,0:T(8,128)(2,1)} custom-call(bf16[1024,2048]{1,0:T(8,128)(2,1)} %constant_dynamic-update-slice_fusion.7.g_ref, bf16[1408,2048]{1,0:T(8,128)(2,1)} %all-gather.9.cloned.1.call-done.down_ref, bf16[1024,2816]{1,0:T(8,128)(2,1)} %get-tuple-element.139.slope_ref), custom_call_target="tpu_custom_call" | custom-call | flops 5905580032 | bytes 21495808 | tf_op jit(solution)/shard_map/activate_back/pallas_call | solution.py:349
  322.1 8.0 %fusion.18 = bf16[256,2048]{1,0:T(8,128)(2,1)S(1)} fusion(bf16[2048,2816]{1,0:T(8,128)(2,1)} %all-gather.11.cloned.1.call-done.w_ref, bf16[1024,2816]{1,0:T(8,128)(2,1)} %activate_back.1), kind=kOutput, calls=%fused_computation.23 | convolution fusion | flops 2952790016 | bytes 14024704 | tf_op jit(solution)/shard_map/dot_general | solution.py:36
  332.7 12.7 %fusion = f32[768,2048]{1,0:T(8,128)} fusion(bf16[2048,2816]{1,0:T(8,128)(2,1)S(1)} %bitcast.211, bf16[1024,2816]{1,0:T(8,128)(2,1)} %activate_back.1), kind=kOutput, calls=%fused_computation.3 | convolution fusion | flops 8858370048 | bytes 22151168 | tf_op jit(solution)/shard_map/dot_general | solution.py:36
  345.4 11.3 %convolution_convert_fusion = bf16[1024,2816]{1,0:T(8,128)(2,1)} fusion(bf16[1024,2816]{1,0:T(8,128)(2,1)} %activate_back.1, bf16[1024,2048]{1,0:T(8,128)(2,1)} %constant_dynamic-update-slice_fusion.14.n_ref, s32[]{:T(128)S(6)} %select_n.101), kind=kOutput, calls=%fused_computation.2 | convolution fusion | flops 5908463616 | bytes 13631492 | tf_op jit(solution)/shard_map/dot_general | solution.py:40
  356.7 3.3 convert.25
  362.3 2.9 add_convert_fusion.7
  368.0 12.1 %add_convert_fusion = bf16[1024,2816]{1,0:T(8,128)(2,1)} fusion(bf16[1024,2816]{1,0:T(8,128)(2,1)} %collective-permute-done.43, bf16[1024,2816]{1,0:T(8,128)(2,1)} %activate_back.1, bf16[1024,2048]{1,0:T(8,128)(2,1)} %constant_dynamic-update-slice_fusion.14.n_ref, s32[]{:T(128)S(6)} %select_n.100), kind=kOutput, calls=%fused_computation | convolution fusion | flops 5914230784 | bytes 19398660 | tf_op jit(solution)/shard_map/dot_general | solution.py:40
  380.2 10.5 %collective-permute-done.41.refs_3_ = bf16[128,2048]{1,0:T(8,128)(2,1)} collective-permute-done((bf16[128,2048]{1,0:T(8,128)(2,1)}, bf16[128,2048]{1,0:T(8,128)(2,1)}, u32[]{:S(2)}, u32[]{:S(2)}) %collective-permute-start.41) | collective-permute-done | bytes 524320 | tf_op jit(solution)/shard_map/ppermute | solution.py:424
  403.8 3.3 finish_norm_back.2
  410.5 6.8 %attend_back.4 = (bf16[256,512]{1,0:T(8,128)(2,1)S(1)}, bf16[256,512]{1,0:T(8,128)(2,1)S(1)}, f32[1024,128]{1,0:T(8,128)S(1)}) custom-call(s32[1,256]{1,0:T(1,128)S(1)} %bitcast.191, s32[1024,1]{1,0:T(8,128)S(1)} %copy-done.27, bf16[512,256]{1,0:T(8,128)(2,1)S(1)} %copy-done.64, bf16[1024,128]{1,0:T(8,128)(2,1)S(1)} %bitcast.181, ...), custom_call_target="tpu_custom_call" | custom-call | flops 5905580032 | bytes 4980736 | tf_op jit(solution)/shard_map/attend_back/pallas_call | solution.py:181
  417.3 4.5 collective-permute-done.44
  426.2 9.2 %fusion.106 = f32[1024,2048]{1,0:T(8,128)S(1)} fusion(bf16[1024,1408]{1,0:T(8,128)(2,1)S(1)} %copy-done.15, bf16[1408,2048]{1,0:T(8,128)(2,1)} %all-gather.9.cloned.1.call-done.down_ref), kind=kOutput, calls=%fused_computation.261 | convolution fusion | flops 5905580032 | bytes 17039360 | tf_op jit(solution)/shard_map/dot_general | solution.py:32
  435.6 9.8 %collective-permute-done.46 = bf16[128,2048]{1,0:T(8,128)(2,1)S(1)} collective-permute-done((bf16[128,2048]{1,0:T(8,128)(2,1)S(1)}, bf16[128,2048]{1,0:T(8,128)(2,1)S(1)}, u32[]{:S(2)}, u32[]{:S(2)}) %collective-permute-start.46) | collective-permute-done | bytes 524320 | tf_op jit(solution)/shard_map/ppermute | solution.py:426
  445.8 6.8 %attend_back.5 = (bf16[256,512]{1,0:T(8,128)(2,1)S(1)}, bf16[256,512]{1,0:T(8,128)(2,1)S(1)}, f32[1024,128]{1,0:T(8,128)S(1)}) custom-call(s32[1,256]{1,0:T(1,128)S(1)} %bitcast.189, s32[1024,1]{1,0:T(8,128)S(1)} %copy-done.23, bf16[512,256]{1,0:T(8,128)(2,1)S(1)} %copy-done.62, bf16[1024,128]{1,0:T(8,128)(2,1)S(1)} %bitcast.179, ...), custom_call_target="tpu_custom_call" | custom-call | flops 5905580032 | bytes 4980736 | tf_op jit(solution)/shard_map/attend_back/pallas_call | solution.py:181
  453.3 6.8 %attend_back.6 = (bf16[256,512]{1,0:T(8,128)(2,1)S(1)}, bf16[256,512]{1,0:T(8,128)(2,1)S(1)}, f32[1024,128]{1,0:T(8,128)S(1)}) custom-call(s32[1,256]{1,0:T(1,128)S(1)} %bitcast.193, s32[1024,1]{1,0:T(8,128)S(1)} %copy-done.25, bf16[512,256]{1,0:T(8,128)(2,1)S(1)} %copy-done.61, bf16[1024,128]{1,0:T(8,128)(2,1)S(1)} %bitcast.177, ...), custom_call_target="tpu_custom_call" | custom-call | flops 5905580032 | bytes 4980736 | tf_op jit(solution)/shard_map/attend_back/pallas_call | solution.py:181
  464.5 4.9 convolution_convert_fusion.2
  469.5 6.8 %attend_back.7 = (bf16[256,512]{1,0:T(8,128)(2,1)S(1)}, bf16[256,512]{1,0:T(8,128)(2,1)S(1)}, f32[1024,128]{1,0:T(8,128)S(1)}) custom-call(s32[1,256]{1,0:T(1,128)S(1)} %bitcast.187, s32[1024,1]{1,0:T(8,128)S(1)} %copy-done.21, bf16[512,256]{1,0:T(8,128)(2,1)S(1)} %copy-done.58, bf16[1024,128]{1,0:T(8,128)(2,1)S(1)} %bitcast.175, ...), custom_call_target="tpu_custom_call" | custom-call | flops 5905580032 | bytes 4980736 | tf_op jit(solution)/shard_map/attend_back/pallas_call | solution.py:181
  477.4 4.3 collective-permute-start.56
  484.6 9.3 %collective-permute-done.58 = bf16[4,256,128]{2,1,0:T(8,128)(2,1)S(1)} collective-permute-done((bf16[4,256,128]{2,1,0:T(8,128)(2,1)S(1)}, bf16[4,256,128]{2,1,0:T(8,128)(2,1)S(1)}, u32[]{:S(2)}, u32[]{:S(2)}) %collective-permute-start.58) | collective-permute-done | bytes 262176 | tf_op jit(solution)/shard_map/ppermute | solution.py:430
  495.4 16.5 %collective-permute-done.57 = bf16[4,256,128]{2,1,0:T(8,128)(2,1)S(1)} collective-permute-done((bf16[4,256,128]{2,1,0:T(8,128)(2,1)S(1)}, bf16[4,256,128]{2,1,0:T(8,128)(2,1)S(1)}, u32[]{:S(2)}, u32[]{:S(2)}) %collective-permute-start.57) | collective-permute-done | bytes 262176 | tf_op jit(solution)/shard_map/ppermute | solution.py:430
  512.7 3.7 fusion.2
  517.8 4.0 fusion.28
  527.6 4.8 fusion.20
  532.4 6.1 collective-permute-done.60
  543.5 2.5 add_convert_fusion.3
  549.2 3.1 add_convert_fusion.6
  552.3 5.1 collective-permute-done.62.refs_1_
  559.6 2.9 add_convert_fusion.2
  562.5 9.9 %collective-permute-done.64.refs_3_ = bf16[128,2048]{1,0:T(8,128)(2,1)} collective-permute-done((bf16[128,2048]{1,0:T(8,128)(2,1)}, bf16[128,2048]{1,0:T(8,128)(2,1)}, u32[]{:S(2)}, u32[]{:S(2)}) %collective-permute-start.64) | collective-permute-done | bytes 524320 | tf_op jit(solution)/shard_map/ppermute | solution.py:424
  574.8 8.8 %collective-permute-done.53 = bf16[128,2048]{1,0:T(8,128)(2,1)} collective-permute-done((bf16[128,2048]{1,0:T(8,128)(2,1)}, bf16[128,2048]{1,0:T(8,128)(2,1)}, u32[]{:S(2)}, u32[]{:S(2)}) %collective-permute-start.53) | collective-permute-done | bytes 524320 | tf_op jit(solution)/shard_map/ppermute | solution.py:424
  587.8 4.1 finish_norm_back.3
  596.0 2.4 convert_add_fusion.1
  599.5 5.5 collective-permute-done.67
  605.0 6.4 collective-permute-done.68
  611.5 2.7 merge_gate_up.1
  614.3 18.2 %reduce-scatter.9.cloned.1.call-done = bf16[256,640]{1,0:T(8,128)(2,1)} async-done(((bf16[1024,640]{1,0:T(8,128)(2,1)}), bf16[256,640]{1,0:T(8,128)(2,1)}) %reduce-scatter.9.cloned.1.call-update) | async-done | bytes 327696 | tf_op jit(solution)/shard_map/reduce_scatter | solution.py:489
  635.8 3.3 fusion.4
  643.5 2.4 convert_element_type.273
  (533 shorter events, 189.7 us)
Async XLA Ops:
  7.2 87.0 %all-gather.5.cloned.1.call-start = ((), (), s32[]{:S(2)}) async-start(), calls=%async_computation.4 | async-start | bytes 2949120 | tf_op jit(solution)/shard_map/all_gather | solution.py:475
  10.0 20.1 %collective-permute-start.4 = (bf16[128,2048]{1,0:T(8,128)(2,1)}, bf16[128,2048]{1,0:T(8,128)(2,1)}, u32[]{:S(2)}, u32[]{:S(2)}) collective-permute-start(bf16[128,2048]{1,0:T(8,128)(2,1)} %get-tuple-element.255), channel_id=1, source_target_pairs={{0,8},{8,0},{1,9},{9,1},{2,10},{10,2},{3,11},{11,3},{4,12},{12,4},... | collective-permute-start | bytes 1572872 | tf_op jit(solution)/shard_map/ppermute | solution.py:424
  12.9 17.2 %collective-permute-start.5 = (bf16[128,2048]{1,0:T(8,128)(2,1)}, bf16[128,2048]{1,0:T(8,128)(2,1)S(1)}, u32[]{:S(2)}, u32[]{:S(2)}) collective-permute-start(bf16[128,2048]{1,0:T(8,128)(2,1)} %get-tuple-element.254), channel_id=1, source_target_pairs={{0,16},{16,0},{1,17},{17,1},{2,18},{18,2},{3,19},{19,3},{4,20},{20... | collective-permute-start | bytes 1572872 | tf_op jit(solution)/shard_map/ppermute | solution.py:426
  30.8 144.0 %all-gather.7.cloned.1.call-start = ((), (), s32[]{:S(2)}) async-start(), calls=%async_computation.5 | async-start | bytes 2359296 | tf_op jit(solution)/shard_map/all_gather | solution.py:475
  31.6 235.2 %all-gather.11.cloned.1.call-start = ((), (), s32[]{:S(2)}) async-start(), calls=%async_computation.7 | async-start | bytes 12976128 | tf_op jit(solution)/shard_map/all_gather | solution.py:475
  31.6 15.2 %collective-permute-start.6 = (bf16[128,2048]{1,0:T(8,128)(2,1)}, bf16[128,2048]{1,0:T(8,128)(2,1)}, u32[]{:S(2)}, u32[]{:S(2)}) collective-permute-start(bf16[128,2048]{1,0:T(8,128)(2,1)} %get-tuple-element.255), channel_id=1, source_target_pairs={{0,16},{16,0},{1,17},{17,1},{2,18},{18,2},{3,19},{19,3},{4,20},{20... | collective-permute-start | bytes 1572872 | tf_op jit(solution)/shard_map/ppermute | solution.py:426
  33.2 15.2 %collective-permute-start.7 = (bf16[128,2048]{1,0:T(8,128)(2,1)}, bf16[128,2048]{1,0:T(8,128)(2,1)}, u32[]{:S(2)}, u32[]{:S(2)}) collective-permute-start(bf16[128,2048]{1,0:T(8,128)(2,1)} %get-tuple-element.254), channel_id=1, source_target_pairs={{0,8},{8,0},{1,9},{9,1},{2,10},{10,2},{3,11},{11,3},{4,12},{12,4},... | collective-permute-start | bytes 1572872 | tf_op jit(solution)/shard_map/ppermute | solution.py:424
  33.8 21.7 %collective-permute-start.8 = (bf16[128,2048]{1,0:T(8,128)(2,1)}, bf16[128,2048]{1,0:T(8,128)(2,1)}, u32[]{:S(2)}, u32[]{:S(2)}) collective-permute-start(bf16[128,2048]{1,0:T(8,128)(2,1)} %collective-permute-done.4), channel_id=1, source_target_pairs={{0,16},{16,0},{1,17},{17,1},{2,18},{18,2},{3,19},{19,3},{4,20},{20... | collective-permute-start | bytes 1572872 | tf_op jit(solution)/shard_map/ppermute | solution.py:426
  34.9 21.1 %collective-permute-start.9 = (bf16[128,2048]{1,0:T(8,128)(2,1)S(1)}, bf16[128,2048]{1,0:T(8,128)(2,1)}, u32[]{:S(2)}, u32[]{:S(2)}) collective-permute-start(bf16[128,2048]{1,0:T(8,128)(2,1)S(1)} %collective-permute-done.5), channel_id=1, source_target_pairs={{0,8},{8,0},{1,9},{9,1},{2,10},{10,2},{3,11},{11,3},{4,12},{12,4},... | collective-permute-start | bytes 1572872 | tf_op jit(solution)/shard_map/ppermute | solution.py:424
  57.5 15.3 %collective-permute-start.28 = (bf16[1,64,2816]{2,1,0:T(8,128)(2,1)S(1)}, bf16[1,64,2816]{2,1,0:T(8,128)(2,1)S(1)}, u32[]{:S(2)}, u32[]{:S(2)}) collective-permute-start(bf16[1,64,2816]{2,1,0:T(8,128)(2,1)S(1)} %get-tuple-element.226), channel_id=1, source_target_pairs={{0,16},{16,0},{1,17},{17,1},{2,18},{18,2},{3,19},{19,3},{4,20},{20... | collective-permute-start | bytes 1081352 | tf_op jit(solution)/shard_map/ppermute | solution.py:426
  59.0 13.8 %collective-permute-start.29 = (bf16[1,64,2816]{2,1,0:T(8,128)(2,1)S(1)}, bf16[1,64,2816]{2,1,0:T(8,128)(2,1)S(1)}, u32[]{:S(2)}, u32[]{:S(2)}) collective-permute-start(bf16[1,64,2816]{2,1,0:T(8,128)(2,1)S(1)} %get-tuple-element.225), channel_id=1, source_target_pairs={{0,24},{8,16},{16,8},{24,0},{1,25},{9,17},{17,9},{25,1},{2,26},{10... | collective-permute-start | bytes 1081352 | tf_op jit(solution)/shard_map/ppermute | solution.py:427
  74.0 234.8 %all-gather.9.cloned.1.call-start = ((), (), s32[]{:S(2)}) async-start(), calls=%async_computation.6 | async-start | bytes 6488064 | tf_op jit(solution)/shard_map/all_gather | solution.py:475
  94.1 497.8 %reduce-scatter.11.cloned.1.call-start = ((), (), s32[]{:S(2)}) async-start(), calls=%async_computation.11 | async-start | bytes 7208960 | tf_op jit(solution)/shard_map/reduce_scatter | solution.py:489
  102.9 15.8 %collective-permute-start.14 = (bf16[4,256,128]{2,1,0:T(8,128)(2,1)S(1)}, bf16[4,256,128]{2,1,0:T(8,128)(2,1)S(1)}, u32[]{:S(2)}, u32[]{:S(2)}) collective-permute-start(bf16[4,256,128]{2,1,0:T(8,128)(2,1)S(1)} %bitcast.182), channel_id=1, source_target_pairs={{0,3},{1,2},{2,1},{3,0},{4,7},{5,6},{6,5},{7,4},{8,11},{9,10},{10,... | collective-permute-start | bytes 786440 | tf_op jit(solution)/shard_map/ppermute | solution.py:430
  106.5 43.5 %collective-permute-start.13 = (bf16[4,256,128]{2,1,0:T(8,128)(2,1)S(1)}, bf16[4,256,128]{2,1,0:T(8,128)(2,1)S(1)}, u32[]{:S(2)}, u32[]{:S(2)}) collective-permute-start(bf16[4,256,128]{2,1,0:T(8,128)(2,1)S(1)} %bitcast.183), channel_id=1, source_target_pairs={{0,2},{1,3},{2,0},{3,1},{4,6},{5,7},{6,4},{7,5},{8,10},{9,11},{10,... | collective-permute-start | bytes 786440 | tf_op jit(solution)/shard_map/ppermute | solution.py:430
  106.5 43.5 %collective-permute-start.12 = (bf16[4,256,128]{2,1,0:T(8,128)(2,1)S(1)}, bf16[4,256,128]{2,1,0:T(8,128)(2,1)S(1)}, u32[]{:S(2)}, u32[]{:S(2)}) collective-permute-start(bf16[4,256,128]{2,1,0:T(8,128)(2,1)S(1)} %bitcast.184), channel_id=1, source_target_pairs={{0,1},{1,0},{2,3},{3,2},{4,5},{5,4},{6,7},{7,6},{8,9},{9,8},{10,11... | collective-permute-start | bytes 786440 | tf_op jit(solution)/shard_map/ppermute | solution.py:430
  107.4 42.7 %collective-permute-start.15 = (bf16[128,2048]{1,0:T(8,128)(2,1)S(1)}, bf16[128,2048]{1,0:T(8,128)(2,1)S(1)}, u32[]{:S(2)}, u32[]{:S(2)}) collective-permute-start(bf16[128,2048]{1,0:T(8,128)(2,1)S(1)} %get-tuple-element.253), channel_id=1, source_target_pairs={{0,8},{8,0},{1,9},{9,1},{2,10},{10,2},{3,11},{11,3},{4,12},{12,4},... | collective-permute-start | bytes 1572872 | tf_op jit(solution)/shard_map/ppermute | solution.py:424
  108.6 43.6 %collective-permute-start.18 = (bf16[128,2048]{1,0:T(8,128)(2,1)S(1)}, bf16[128,2048]{1,0:T(8,128)(2,1)S(1)}, u32[]{:S(2)}, u32[]{:S(2)}) collective-permute-start(bf16[128,2048]{1,0:T(8,128)(2,1)S(1)} %get-tuple-element.252), channel_id=1, source_target_pairs={{0,16},{16,0},{1,17},{17,1},{2,18},{18,2},{3,19},{19,3},{4,20},{20... | collective-permute-start | bytes 1572872 | tf_op jit(solution)/shard_map/ppermute | solution.py:426
  118.7 36.7 %collective-permute-start.16 = (bf16[128,2048]{1,0:T(8,128)(2,1)S(1)}, bf16[128,2048]{1,0:T(8,128)(2,1)S(1)}, u32[]{:S(2)}, u32[]{:S(2)}) collective-permute-start(bf16[128,2048]{1,0:T(8,128)(2,1)S(1)} %get-tuple-element.252), channel_id=1, source_target_pairs={{0,8},{8,0},{1,9},{9,1},{2,10},{10,2},{3,11},{11,3},{4,12},{12,4},... | collective-permute-start | bytes 1572872 | tf_op jit(solution)/shard_map/ppermute | solution.py:424
  150.0 14.9 %collective-permute-start.17 = (bf16[128,2048]{1,0:T(8,128)(2,1)S(1)}, bf16[128,2048]{1,0:T(8,128)(2,1)S(1)}, u32[]{:S(2)}, u32[]{:S(2)}) collective-permute-start(bf16[128,2048]{1,0:T(8,128)(2,1)S(1)} %get-tuple-element.253), channel_id=1, source_target_pairs={{0,16},{16,0},{1,17},{17,1},{2,18},{18,2},{3,19},{19,3},{4,20},{20... | collective-permute-start | bytes 1572872 | tf_op jit(solution)/shard_map/ppermute | solution.py:426
  150.2 22.0 %collective-permute-start.19 = (bf16[128,2048]{1,0:T(8,128)(2,1)S(1)}, bf16[128,2048]{1,0:T(8,128)(2,1)S(1)}, u32[]{:S(2)}, u32[]{:S(2)}) collective-permute-start(bf16[128,2048]{1,0:T(8,128)(2,1)S(1)} %collective-permute-done.15), channel_id=1, source_target_pairs={{0,16},{16,0},{1,17},{17,1},{2,18},{18,2},{3,19},{19,3},{4,20},{20... | collective-permute-start | bytes 1572872 | tf_op jit(solution)/shard_map/ppermute | solution.py:426
  152.3 20.7 %collective-permute-start.20 = (bf16[128,2048]{1,0:T(8,128)(2,1)S(1)}, bf16[128,2048]{1,0:T(8,128)(2,1)S(1)}, u32[]{:S(2)}, u32[]{:S(2)}) collective-permute-start(bf16[128,2048]{1,0:T(8,128)(2,1)S(1)} %collective-permute-done.18), channel_id=1, source_target_pairs={{0,8},{8,0},{1,9},{9,1},{2,10},{10,2},{3,11},{11,3},{4,12},{12,4},... | collective-permute-start | bytes 1572872 | tf_op jit(solution)/shard_map/ppermute | solution.py:424
  185.6 15.6 %collective-permute-start.21 = (bf16[128,2048]{1,0:T(8,128)(2,1)S(1)}, bf16[128,2048]{1,0:T(8,128)(2,1)S(1)}, u32[]{:S(2)}, u32[]{:S(2)}) collective-permute-start(bf16[128,2048]{1,0:T(8,128)(2,1)S(1)} %get-tuple-element.251), channel_id=1, source_target_pairs={{0,16},{16,0},{1,17},{17,1},{2,18},{18,2},{3,19},{19,3},{4,20},{20... | collective-permute-start | bytes 1572872 | tf_op jit(solution)/shard_map/ppermute | solution.py:426
  185.9 15.3 %collective-permute-start.22 = (bf16[128,2048]{1,0:T(8,128)(2,1)S(1)}, bf16[128,2048]{1,0:T(8,128)(2,1)S(1)}, u32[]{:S(2)}, u32[]{:S(2)}) collective-permute-start(bf16[128,2048]{1,0:T(8,128)(2,1)S(1)} %get-tuple-element.250), channel_id=1, source_target_pairs={{0,8},{8,0},{1,9},{9,1},{2,10},{10,2},{3,11},{11,3},{4,12},{12,4},... | collective-permute-start | bytes 1572872 | tf_op jit(solution)/shard_map/ppermute | solution.py:424
  202.1 19.8 %collective-permute-start.23 = (bf16[128,2048]{1,0:T(8,128)(2,1)}, bf16[128,2048]{1,0:T(8,128)(2,1)}, u32[]{:S(2)}, u32[]{:S(2)}) collective-permute-start(bf16[128,2048]{1,0:T(8,128)(2,1)} %slice.274), channel_id=1, source_target_pairs={{0,16},{16,0},{1,17},{17,1},{2,18},{18,2},{3,19},{19,3},{4,20},{20... | collective-permute-start | bytes 1572872 | tf_op jit(solution)/shard_map/ppermute | solution.py:426
  205.6 16.3 %collective-permute-start.24 = (bf16[128,2048]{1,0:T(8,128)(2,1)}, bf16[128,2048]{1,0:T(8,128)(2,1)S(1)}, u32[]{:S(2)}, u32[]{:S(2)}) collective-permute-start(bf16[128,2048]{1,0:T(8,128)(2,1)} %add_convert_fusion.10), channel_id=1, source_target_pairs={{0,8},{8,0},{1,9},{9,1},{2,10},{10,2},{3,11},{11,3},{4,12},{12,4},... | collective-permute-start | bytes 1572872 | tf_op jit(solution)/shard_map/ppermute | solution.py:424
  205.6 20.6 %collective-permute-start.25 = (bf16[128,2048]{1,0:T(8,128)(2,1)}, bf16[128,2048]{1,0:T(8,128)(2,1)S(1)}, u32[]{:S(2)}, u32[]{:S(2)}) collective-permute-start(bf16[128,2048]{1,0:T(8,128)(2,1)} %slice.276), channel_id=1, source_target_pairs={{0,8},{8,0},{1,9},{9,1},{2,10},{10,2},{3,11},{11,3},{4,12},{12,4},... | collective-permute-start | bytes 1572872 | tf_op jit(solution)/shard_map/ppermute | solution.py:424
  208.6 18.4 %collective-permute-start.26 = (bf16[128,2048]{1,0:T(8,128)(2,1)}, bf16[128,2048]{1,0:T(8,128)(2,1)}, u32[]{:S(2)}, u32[]{:S(2)}) collective-permute-start(bf16[128,2048]{1,0:T(8,128)(2,1)} %add_convert_fusion.9), channel_id=1, source_target_pairs={{0,16},{16,0},{1,17},{17,1},{2,18},{18,2},{3,19},{19,3},{4,20},{20... | collective-permute-start | bytes 1572872 | tf_op jit(solution)/shard_map/ppermute | solution.py:426
  233.6 15.2 %collective-permute-start.30 = (bf16[128,2048]{1,0:T(8,128)(2,1)}, bf16[128,2048]{1,0:T(8,128)(2,1)}, u32[]{:S(2)}, u32[]{:S(2)}) collective-permute-start(bf16[128,2048]{1,0:T(8,128)(2,1)} %get-tuple-element.243), channel_id=1, source_target_pairs={{0,8},{8,0},{1,9},{9,1},{2,10},{10,2},{3,11},{11,3},{4,12},{12,4},... | collective-permute-start | bytes 1572872 | tf_op jit(solution)/shard_map/ppermute | solution.py:424
  234.2 15.3 %collective-permute-start.33 = (bf16[128,2048]{1,0:T(8,128)(2,1)}, bf16[128,2048]{1,0:T(8,128)(2,1)}, u32[]{:S(2)}, u32[]{:S(2)}) collective-permute-start(bf16[128,2048]{1,0:T(8,128)(2,1)} %get-tuple-element.242), channel_id=1, source_target_pairs={{0,16},{16,0},{1,17},{17,1},{2,18},{18,2},{3,19},{19,3},{4,20},{20... | collective-permute-start | bytes 1572872 | tf_op jit(solution)/shard_map/ppermute | solution.py:426
  235.4 23.5 %collective-permute-start.31 = (bf16[128,2048]{1,0:T(8,128)(2,1)}, bf16[128,2048]{1,0:T(8,128)(2,1)}, u32[]{:S(2)}, u32[]{:S(2)}) collective-permute-start(bf16[128,2048]{1,0:T(8,128)(2,1)} %get-tuple-element.242), channel_id=1, source_target_pairs={{0,8},{8,0},{1,9},{9,1},{2,10},{10,2},{3,11},{11,3},{4,12},{12,4},... | collective-permute-start | bytes 1572872 | tf_op jit(solution)/shard_map/ppermute | solution.py:424
  236.8 24.0 %collective-permute-start.32 = (bf16[128,2048]{1,0:T(8,128)(2,1)}, bf16[128,2048]{1,0:T(8,128)(2,1)S(1)}, u32[]{:S(2)}, u32[]{:S(2)}) collective-permute-start(bf16[128,2048]{1,0:T(8,128)(2,1)} %get-tuple-element.243), channel_id=1, source_target_pairs={{0,16},{16,0},{1,17},{17,1},{2,18},{18,2},{3,19},{19,3},{4,20},{20... | collective-permute-start | bytes 1572872 | tf_op jit(solution)/shard_map/ppermute | solution.py:426
  248.8 16.3 %collective-permute-start.34 = (bf16[128,2048]{1,0:T(8,128)(2,1)}, bf16[128,2048]{1,0:T(8,128)(2,1)S(1)}, u32[]{:S(2)}, u32[]{:S(2)}) collective-permute-start(bf16[128,2048]{1,0:T(8,128)(2,1)} %collective-permute-done.30), channel_id=1, source_target_pairs={{0,16},{16,0},{1,17},{17,1},{2,18},{18,2},{3,19},{19,3},{4,20},{20... | collective-permute-start | bytes 1572872 | tf_op jit(solution)/shard_map/ppermute | solution.py:426
  249.5 16.5 %collective-permute-start.35 = (bf16[128,2048]{1,0:T(8,128)(2,1)}, bf16[128,2048]{1,0:T(8,128)(2,1)S(1)}, u32[]{:S(2)}, u32[]{:S(2)}) collective-permute-start(bf16[128,2048]{1,0:T(8,128)(2,1)} %collective-permute-done.33), channel_id=1, source_target_pairs={{0,8},{8,0},{1,9},{9,1},{2,10},{10,2},{3,11},{11,3},{4,12},{12,4},... | collective-permute-start | bytes 1572872 | tf_op jit(solution)/shard_map/ppermute | solution.py:424
  330.2 15.1 %collective-permute-start.37 = (bf16[128,2048]{1,0:T(8,128)(2,1)S(1)}, bf16[128,2048]{1,0:T(8,128)(2,1)S(1)}, u32[]{:S(2)}, u32[]{:S(2)}) collective-permute-start(bf16[128,2048]{1,0:T(8,128)(2,1)S(1)} %get-tuple-element.241), channel_id=1, source_target_pairs={{0,16},{16,0},{1,17},{17,1},{2,18},{18,2},{3,19},{19,3},{4,20},{20... | collective-permute-start | bytes 1572872 | tf_op jit(solution)/shard_map/ppermute | solution.py:426
  361.1 19.0 %collective-permute-start.39 = (bf16[128,2048]{1,0:T(8,128)(2,1)}, bf16[128,2048]{1,0:T(8,128)(2,1)}, u32[]{:S(2)}, u32[]{:S(2)}) collective-permute-start(bf16[128,2048]{1,0:T(8,128)(2,1)} %get-tuple-element.220), channel_id=1, source_target_pairs={{0,16},{16,0},{1,17},{17,1},{2,18},{18,2},{3,19},{19,3},{4,20},{20... | collective-permute-start | bytes 1572872 | tf_op jit(solution)/shard_map/ppermute | solution.py:426
  365.2 15.1 %collective-permute-start.40 = (bf16[128,2048]{1,0:T(8,128)(2,1)}, bf16[128,2048]{1,0:T(8,128)(2,1)}, u32[]{:S(2)}, u32[]{:S(2)}) collective-permute-start(bf16[128,2048]{1,0:T(8,128)(2,1)} %get-tuple-element.212), channel_id=1, source_target_pairs={{0,8},{8,0},{1,9},{9,1},{2,10},{10,2},{3,11},{11,3},{4,12},{12,4},... | collective-permute-start | bytes 1572872 | tf_op jit(solution)/shard_map/ppermute | solution.py:424
  365.9 24.9 %collective-permute-start.41 = (bf16[128,2048]{1,0:T(8,128)(2,1)}, bf16[128,2048]{1,0:T(8,128)(2,1)}, u32[]{:S(2)}, u32[]{:S(2)}) collective-permute-start(bf16[128,2048]{1,0:T(8,128)(2,1)} %get-tuple-element.219), channel_id=1, source_target_pairs={{0,8},{8,0},{1,9},{9,1},{2,10},{10,2},{3,11},{11,3},{4,12},{12,4},... | collective-permute-start | bytes 1572872 | tf_op jit(solution)/shard_map/ppermute | solution.py:424
  367.2 23.6 %collective-permute-start.42 = (bf16[128,2048]{1,0:T(8,128)(2,1)}, bf16[128,2048]{1,0:T(8,128)(2,1)}, u32[]{:S(2)}, u32[]{:S(2)}) collective-permute-start(bf16[128,2048]{1,0:T(8,128)(2,1)} %get-tuple-element.211), channel_id=1, source_target_pairs={{0,16},{16,0},{1,17},{17,1},{2,18},{18,2},{3,19},{19,3},{4,20},{20... | collective-permute-start | bytes 1572872 | tf_op jit(solution)/shard_map/ppermute | solution.py:426
  390.8 223.5 %reduce-scatter.5.cloned.1.call-start = ((), (), s32[]{:S(2)}) async-start(), calls=%async_computation.8 | async-start | bytes 3604480 | tf_op jit(solution)/shard_map/reduce_scatter | solution.py:489
  401.8 212.5 %reduce-scatter.7.cloned.1.call-start = ((), (), s32[]{:S(2)}) async-start(), calls=%async_computation.9 | async-start | bytes 1310720 | tf_op jit(solution)/shard_map/reduce_scatter | solution.py:489
  422.1 38.0 %collective-permute-start.48 = (bf16[128,2048]{1,0:T(8,128)(2,1)S(1)}, bf16[128,2048]{1,0:T(8,128)(2,1)S(1)}, u32[]{:S(2)}, u32[]{:S(2)}) collective-permute-start(bf16[128,2048]{1,0:T(8,128)(2,1)S(1)} %collective-permute-done.44), channel_id=1, source_target_pairs={{0,16},{16,0},{1,17},{17,1},{2,18},{18,2},{3,19},{19,3},{4,20},{20... | collective-permute-start | bytes 1572872 | tf_op jit(solution)/shard_map/ppermute | solution.py:426
  423.4 22.0 %collective-permute-start.46 = (bf16[128,2048]{1,0:T(8,128)(2,1)S(1)}, bf16[128,2048]{1,0:T(8,128)(2,1)S(1)}, u32[]{:S(2)}, u32[]{:S(2)}) collective-permute-start(bf16[128,2048]{1,0:T(8,128)(2,1)S(1)} %get-tuple-element.154), channel_id=1, source_target_pairs={{0,16},{16,0},{1,17},{17,1},{2,18},{18,2},{3,19},{19,3},{4,20},{20... | collective-permute-start | bytes 1572872 | tf_op jit(solution)/shard_map/ppermute | solution.py:426
  424.1 21.3 %collective-permute-start.47 = (bf16[128,2048]{1,0:T(8,128)(2,1)S(1)}, bf16[128,2048]{1,0:T(8,128)(2,1)S(1)}, u32[]{:S(2)}, u32[]{:S(2)}) collective-permute-start(bf16[128,2048]{1,0:T(8,128)(2,1)S(1)} %get-tuple-element.155), channel_id=1, source_target_pairs={{0,8},{8,0},{1,9},{9,1},{2,10},{10,2},{3,11},{11,3},{4,12},{12,4},... | collective-permute-start | bytes 1572872 | tf_op jit(solution)/shard_map/ppermute | solution.py:424
  425.6 34.5 %collective-permute-start.49 = (bf16[128,2048]{1,0:T(8,128)(2,1)S(1)}, bf16[128,2048]{1,0:T(8,128)(2,1)S(1)}, u32[]{:S(2)}, u32[]{:S(2)}) collective-permute-start(bf16[128,2048]{1,0:T(8,128)(2,1)S(1)} %collective-permute-done.45), channel_id=1, source_target_pairs={{0,8},{8,0},{1,9},{9,1},{2,10},{10,2},{3,11},{11,3},{4,12},{12,4},... | collective-permute-start | bytes 1572872 | tf_op jit(solution)/shard_map/ppermute | solution.py:424
  469.3 43.4 %collective-permute-start.59 = (bf16[256,2048]{1,0:T(8,128)(2,1)}, bf16[256,2048]{1,0:T(8,128)(2,1)}, u32[]{:S(2)}, u32[]{:S(2)}) collective-permute-start(bf16[256,2048]{1,0:T(8,128)(2,1)} %convolution_convert_fusion.2), channel_id=1, source_target_pairs={{0,4},{4,0},{1,5},{5,1},{2,6},{6,2},{3,7},{7,3},{8,12},{12,8},{9,1... | collective-permute-start | bytes 3145736 | tf_op jit(solution)/shard_map/ppermute | solution.py:484
  477.3 16.7 %collective-permute-start.58 = (bf16[4,256,128]{2,1,0:T(8,128)(2,1)S(1)}, bf16[4,256,128]{2,1,0:T(8,128)(2,1)S(1)}, u32[]{:S(2)}, u32[]{:S(2)}) collective-permute-start(bf16[4,256,128]{2,1,0:T(8,128)(2,1)S(1)} %get-tuple-element.232), channel_id=1, source_target_pairs={{0,3},{1,2},{2,1},{3,0},{4,7},{5,6},{6,5},{7,4},{8,11},{9,10},{10,... | collective-permute-start | bytes 786440 | tf_op jit(solution)/shard_map/ppermute | solution.py:430
  477.4 34.5 %collective-permute-start.57 = (bf16[4,256,128]{2,1,0:T(8,128)(2,1)S(1)}, bf16[4,256,128]{2,1,0:T(8,128)(2,1)S(1)}, u32[]{:S(2)}, u32[]{:S(2)}) collective-permute-start(bf16[4,256,128]{2,1,0:T(8,128)(2,1)S(1)} %get-tuple-element.233), channel_id=1, source_target_pairs={{0,2},{1,3},{2,0},{3,1},{4,6},{5,7},{6,4},{7,5},{8,10},{9,11},{10,... | collective-permute-start | bytes 786440 | tf_op jit(solution)/shard_map/ppermute | solution.py:430
  477.4 34.4 %collective-permute-start.56 = (bf16[4,256,128]{2,1,0:T(8,128)(2,1)S(1)}, bf16[4,256,128]{2,1,0:T(8,128)(2,1)S(1)}, u32[]{:S(2)}, u32[]{:S(2)}) collective-permute-start(bf16[4,256,128]{2,1,0:T(8,128)(2,1)S(1)} %get-tuple-element.231), channel_id=1, source_target_pairs={{0,1},{1,0},{2,3},{3,2},{4,5},{5,4},{6,7},{7,6},{8,9},{9,8},{10,11... | collective-permute-start | bytes 786440 | tf_op jit(solution)/shard_map/ppermute | solution.py:430
  483.1 64.3 %collective-permute-start.51 = (bf16[128,2048]{1,0:T(8,128)(2,1)}, bf16[128,2048]{1,0:T(8,128)(2,1)}, u32[]{:S(2)}, u32[]{:S(2)}) collective-permute-start(bf16[128,2048]{1,0:T(8,128)(2,1)} %get-tuple-element.216), channel_id=1, source_target_pairs={{0,16},{16,0},{1,17},{17,1},{2,18},{18,2},{3,19},{19,3},{4,20},{20... | collective-permute-start | bytes 1572872 | tf_op jit(solution)/shard_map/ppermute | solution.py:426
  493.9 54.2 %collective-permute-start.54 = (bf16[128,2048]{1,0:T(8,128)(2,1)}, bf16[128,2048]{1,0:T(8,128)(2,1)}, u32[]{:S(2)}, u32[]{:S(2)}) collective-permute-start(bf16[128,2048]{1,0:T(8,128)(2,1)} %get-tuple-element.214), channel_id=1, source_target_pairs={{0,8},{8,0},{1,9},{9,1},{2,10},{10,2},{3,11},{11,3},{4,12},{12,4},... | collective-permute-start | bytes 1572872 | tf_op jit(solution)/shard_map/ppermute | solution.py:424
  524.2 14.3 %collective-permute-start.60 = (bf16[128,2048]{1,0:T(8,128)(2,1)}, bf16[128,2048]{1,0:T(8,128)(2,1)}, u32[]{:S(2)}, u32[]{:S(2)}) collective-permute-start(bf16[128,2048]{1,0:T(8,128)(2,1)} %get-tuple-element.230), channel_id=1, source_target_pairs={{0,16},{16,0},{1,17},{17,1},{2,18},{18,2},{3,19},{19,3},{4,20},{20... | collective-permute-start | bytes 1572872 | tf_op jit(solution)/shard_map/ppermute | solution.py:426
  525.4 13.9 %collective-permute-start.61 = (bf16[128,2048]{1,0:T(8,128)(2,1)}, bf16[128,2048]{1,0:T(8,128)(2,1)}, u32[]{:S(2)}, u32[]{:S(2)}) collective-permute-start(bf16[128,2048]{1,0:T(8,128)(2,1)} %get-tuple-element.229), channel_id=1, source_target_pairs={{0,8},{8,0},{1,9},{9,1},{2,10},{10,2},{3,11},{11,3},{4,12},{12,4},... | collective-permute-start | bytes 1572872 | tf_op jit(solution)/shard_map/ppermute | solution.py:424
  527.2 105.4 %reduce-scatter.9.cloned.1.call-start = ((), (), s32[]{:S(2)}) async-start(), calls=%async_computation.10 | async-start | bytes 1638400 | tf_op jit(solution)/shard_map/reduce_scatter | solution.py:489
  541.7 16.9 %collective-permute-start.66 = (bf16[1024,640]{1,0:T(8,128)(2,1)S(1)}, bf16[1024,640]{1,0:T(8,128)(2,1)S(1)}, u32[]{:S(2)}, u32[]{:S(2)}) collective-permute-start(bf16[1024,640]{1,0:T(8,128)(2,1)S(1)} %fusion.11), channel_id=1, source_target_pairs={{0,4},{4,0},{1,5},{5,1},{2,6},{6,2},{3,7},{7,3},{8,12},{12,8},{9,1... | collective-permute-start | bytes 3932168 | tf_op jit(solution)/shard_map/ppermute | solution.py:484
  542.6 14.7 %collective-permute-start.62 = (bf16[128,2048]{1,0:T(8,128)(2,1)S(1)}, bf16[128,2048]{1,0:T(8,128)(2,1)S(1)}, u32[]{:S(2)}, u32[]{:S(2)}) collective-permute-start(bf16[128,2048]{1,0:T(8,128)(2,1)S(1)} %get-tuple-element.218), channel_id=1, source_target_pairs={{0,16},{16,0},{1,17},{17,1},{2,18},{18,2},{3,19},{19,3},{4,20},{20... | collective-permute-start | bytes 1572872 | tf_op jit(solution)/shard_map/ppermute | solution.py:426
  546.1 16.4 %collective-permute-start.63 = (bf16[128,2048]{1,0:T(8,128)(2,1)}, bf16[128,2048]{1,0:T(8,128)(2,1)S(1)}, u32[]{:S(2)}, u32[]{:S(2)}) collective-permute-start(bf16[128,2048]{1,0:T(8,128)(2,1)} %get-tuple-element.210), channel_id=1, source_target_pairs={{0,8},{8,0},{1,9},{9,1},{2,10},{10,2},{3,11},{11,3},{4,12},{12,4},... | collective-permute-start | bytes 1572872 | tf_op jit(solution)/shard_map/ppermute | solution.py:424
  547.4 25.0 %collective-permute-start.64 = (bf16[128,2048]{1,0:T(8,128)(2,1)}, bf16[128,2048]{1,0:T(8,128)(2,1)}, u32[]{:S(2)}, u32[]{:S(2)}) collective-permute-start(bf16[128,2048]{1,0:T(8,128)(2,1)} %get-tuple-element.217), channel_id=1, source_target_pairs={{0,8},{8,0},{1,9},{9,1},{2,10},{10,2},{3,11},{11,3},{4,12},{12,4},... | collective-permute-start | bytes 1572872 | tf_op jit(solution)/shard_map/ppermute | solution.py:424
  548.1 24.3 %collective-permute-start.65 = (bf16[128,2048]{1,0:T(8,128)(2,1)}, bf16[128,2048]{1,0:T(8,128)(2,1)}, u32[]{:S(2)}, u32[]{:S(2)}) collective-permute-start(bf16[128,2048]{1,0:T(8,128)(2,1)} %get-tuple-element.209), channel_id=1, source_target_pairs={{0,16},{16,0},{1,17},{17,1},{2,18},{18,2},{3,19},{19,3},{4,20},{20... | collective-permute-start | bytes 1572872 | tf_op jit(solution)/shard_map/ppermute | solution.py:426
  557.4 26.3 %collective-permute-start.53 = (bf16[128,2048]{1,0:T(8,128)(2,1)}, bf16[128,2048]{1,0:T(8,128)(2,1)}, u32[]{:S(2)}, u32[]{:S(2)}) collective-permute-start(bf16[128,2048]{1,0:T(8,128)(2,1)} %get-tuple-element.215), channel_id=1, source_target_pairs={{0,8},{8,0},{1,9},{9,1},{2,10},{10,2},{3,11},{11,3},{4,12},{12,4},... | collective-permute-start | bytes 1572872 | tf_op jit(solution)/shard_map/ppermute | solution.py:424
  558.6 25.0 %collective-permute-start.55 = (bf16[128,2048]{1,0:T(8,128)(2,1)}, bf16[128,2048]{1,0:T(8,128)(2,1)}, u32[]{:S(2)}, u32[]{:S(2)}) collective-permute-start(bf16[128,2048]{1,0:T(8,128)(2,1)} %get-tuple-element.208), channel_id=1, source_target_pairs={{0,16},{16,0},{1,17},{17,1},{2,18},{18,2},{3,19},{19,3},{4,20},{20... | collective-permute-start | bytes 1572872 | tf_op jit(solution)/shard_map/ppermute | solution.py:426
  572.4 23.6 %collective-permute-start.50 = (bf16[128,2048]{1,0:T(8,128)(2,1)}, bf16[128,2048]{1,0:T(8,128)(2,1)}, u32[]{:S(2)}, u32[]{:S(2)}) collective-permute-start(bf16[128,2048]{1,0:T(8,128)(2,1)} %get-tuple-element.213), channel_id=1, source_target_pairs={{0,16},{16,0},{1,17},{17,1},{2,18},{18,2},{3,19},{19,3},{4,20},{20... | collective-permute-start | bytes 1572872 | tf_op jit(solution)/shard_map/ppermute | solution.py:426
  573.6 22.4 %collective-permute-start.52 = (bf16[128,2048]{1,0:T(8,128)(2,1)}, bf16[128,2048]{1,0:T(8,128)(2,1)}, u32[]{:S(2)}, u32[]{:S(2)}) collective-permute-start(bf16[128,2048]{1,0:T(8,128)(2,1)} %get-tuple-element.207), channel_id=1, source_target_pairs={{0,8},{8,0},{1,9},{9,1},{2,10},{10,2},{3,11},{11,3},{4,12},{12,4},... | collective-permute-start | bytes 1572872 | tf_op jit(solution)/shard_map/ppermute | solution.py:424
  594.9 16.5 %collective-permute-start.68 = (bf16[1,64,2816]{2,1,0:T(8,128)(2,1)S(1)}, bf16[1,64,2816]{2,1,0:T(8,128)(2,1)S(1)}, u32[]{:S(2)}, u32[]{:S(2)}) collective-permute-start(bf16[1,64,2816]{2,1,0:T(8,128)(2,1)S(1)} %get-tuple-element.222), channel_id=1, source_target_pairs={{0,16},{16,0},{1,17},{17,1},{2,18},{18,2},{3,19},{19,3},{4,20},{20... | collective-permute-start | bytes 1081352 | tf_op jit(solution)/shard_map/ppermute | solution.py:426
  (140 other events, 1218.5 us)
Sparse Core Ops, SparseCore 0:
  31.0 34.1 all-gather.4
  66.8 28.0 all-gather.6
  97.1 121.7 all-gather.10
  220.3 59.8 all-gather.8
  390.9 107.7 reduce-scatter.10
  500.9 69.4 reduce-scatter.4
  572.6 26.9 reduce-scatter.6
  602.6 29.8 reduce-scatter.8

commit v3 on v2

v3 whole, which is shorter than its diff:
```python
import jax
import jax.numpy as jnp
from jax import lax
from jax.experimental import pallas as pl
from jax.experimental.pallas import tpu as pltpu
from jax.sharding import Mesh, PartitionSpec as P

H = 32
KV = 4
HD = 64
TP = 4
GROUP = H // KV
LANES = 128
ROWS = 64
ROOM = 60 << 20
ATTEND_ROOM = 60 << 20
DOWN_STEPS = 2

epsilon = 1e-05
rope_base = 10000.0
masked_score = -1e30
bf16 = jnp.bfloat16
f32 = jnp.float32


def after(value, *others):
    return lax.optimization_barrier((value,) + others)[0]


def phase(*values):
    return lax.optimization_barrier(values)


def nn(left, right):
    return lax.dot_general(left, right, (((1,), (0,)), ((), ())), preferred_element_type=f32)


def nt(left, right):
    return lax.dot_general(left, right, (((1,), (1,)), ((), ())), preferred_element_type=f32)


def tn(left, right):
    return lax.dot_general(left, right, (((0,), (0,)), ((), ())), preferred_element_type=f32)


def like(shape, kind):
    return jax.ShapeDtypeStruct(shape, kind)


def size_of(values):
    return sum(v.size * v.dtype.itemsize for v in values)


def small_call(
    kernel, name, inputs, outputs, flops=0, scratch=(), scalars=0, transcendentals=0, room=ROOM
):
    specs, arrays = [pl.BlockSpec(memory_space=pltpu.SMEM)] * scalars, list(inputs[:scalars])
    for v in inputs[scalars:]:
        if isinstance(v, tuple):
            specs.append(row_block(*v))
            arrays.append(v[0])
        else:
            specs.append(whole_block(v.shape))
            arrays.append(v)
    size = size_of((*arrays, *outputs))
    return pl.pallas_call(
        kernel,
        grid=(1,),
        in_specs=specs,
        out_specs=[whole_block(v.shape) for v in outputs],
        out_shape=outputs,
        scratch_shapes=list(scratch),
        compiler_params=pltpu.CompilerParams(vmem_limit_bytes=room),
        cost_estimate=pl.CostEstimate(
            flops=max(flops, size), bytes_accessed=size, transcendentals=transcendentals
        ),
        name=name,
    )(*arrays)


def row_block(array, index):
    shape = array.shape[1:]
    return pl.BlockSpec((None,) + shape, lambda i: (index,) + (0,) * len(shape))


def whole_block(shape):
    return pl.BlockSpec(shape, lambda i: (0,) * len(shape))


def turn(vectors, cosine, sine):
    half = HD // 2
    out = []
    for at in range(0, vectors.shape[0], HD):
        first, second = vectors[at : at + half], vectors[at + half : at + HD]
        out += [first * cosine - second * sine, second * cosine + first * sine]
    return jnp.concatenate(out, axis=0)


def project(pieces, w, cosine, sine):
    half, width = pieces[0].shape
    rows, n, q = 2 * half, w.shape[1], GROUP * HD

    def kernel(*refs):
        x_refs, (w_ref, cos_ref, sin_ref, kv_ref), outs = refs[:8], refs[8:12], refs[12:]
        for k in range(TP):
            xb = jnp.concatenate([x_refs[2 * k][...], x_refs[2 * k + 1][...]], axis=0)
            x = xb.astype(f32)
            inverse = lax.rsqrt(jnp.mean(x * x, axis=1, keepdims=True) + epsilon)
            outs[TP + k][...] = inverse
            flat = (nn(xb, w_ref[...]) * inverse).T
            cosine, sine = cos_ref[k], sin_ref[k]
            outs[k][...] = (turn(flat[:q], cosine, sine) * HD**-0.5).astype(bf16)
            kv = jnp.concatenate([turn(flat[q : q + HD], cosine, sine), flat[q + HD :]], axis=0)
            kv_ref[k] = kv.T.astype(bf16)

    kv, *outs = small_call(
        kernel,
        "project",
        [*pieces, w, cosine, sine],
        [like((TP, rows, 2 * HD), bf16)]
        + [like((q, rows), bf16)] * TP
        + [like((rows, 1), f32)] * TP,
        flops=2 * TP * rows * width * n,
    )
    return outs[:TP], kv, outs[TP:]


def set_bias(order_ref, k, bias_ref):
    keys, rows = bias_ref.shape
    span = keys // order_ref.shape[1]
    lane = lax.broadcasted_iota(jnp.int32, (span, rows), 1)
    query = jnp.where(lane < span, order_ref[k, 0], order_ref[k, 1] - 1) * span + lane
    row = lax.broadcasted_iota(jnp.int32, (span, rows), 0)
    for b in range(keys // span):
        key = order_ref[k, b] * span + row
        bias_ref[b * span : (b + 1) * span, :] = jnp.where(query >= key, 0.0, masked_score)


def attend(members, orders, queries, kv_pieces, wo, kind):
    n, rows = queries[0].shape
    holders, width = len(kv_pieces), wo.shape[1]
    keys, count = holders * rows, len(members)

    def kernel(order_ref, wo_ref, *refs):
        for i, k in enumerate(members):
            qt_ref, *kv_refs = refs[i * (1 + holders) : (i + 1) * (1 + holders)]
            outs = refs[count * (1 + holders) :]
            ot_ref, lse_ref, part_ref = outs[3 * i : 3 * i + 3]
            bias_ref = outs[-1]
            set_bias(order_ref, k, bias_ref)
            kv = jnp.concatenate([ref[...] for ref in kv_refs], axis=0)
            vt = kv.astype(f32).T[HD:].astype(bf16)
            zero = jnp.zeros((HD, rows), bf16)
            for h in range(GROUP):
                at = slice(h * HD, (h + 1) * HD)
                scores = nn(kv, jnp.concatenate([qt_ref[at, :], zero], axis=0)) + bias_ref[...]
                top = jnp.max(scores, axis=0, keepdims=True)
                exponent = jnp.exp(scores - top)
                total = jnp.sum(exponent, axis=0, keepdims=True)
                ot_ref[at, :] = (nn(vt, exponent.astype(bf16)) / total).astype(bf16)
                lse_ref[h : h + 1, :] = top + jnp.log(total)
            part_ref[...] = tn(ot_ref[...], wo_ref[...]).astype(part_ref.dtype)

    inputs, outputs = [orders, wo], []
    for i, k in enumerate(members):
        inputs += [queries[i], *[(piece, k) for piece in kv_pieces]]
        outputs += [like((n, rows), bf16), like((GROUP, rows), f32), like((rows, width), kind)]
    results = small_call(
        kernel,
        "attend",
        inputs,
        outputs,
        flops=2 * rows * n * (keys * 2 * 4 + width) * count,
        scratch=[pltpu.VMEM((keys, rows), f32)],
        scalars=1,
        transcendentals=GROUP * rows * keys * count,
        room=ATTEND_ROOM,
    )
    return [results[3 * i : 3 * i + 3] for i in range(count)]


def attend_back(members, orders, wo, kv_pieces, details):
    n, rows = details[0][0].shape
    holders, width = len(kv_pieces), wo.shape[1]
    keys, half, count = holders * rows, rows // 2, len(members)
    step = 8 + holders

    def kernel(order_ref, wo_ref, *refs):
        outs, (bias_ref, dat_ref, dqt_ref, dkv_ref) = refs[count * step : -4], refs[-4:]
        for i, k in enumerate(members):
            own = refs[i * step : (i + 1) * step]
            kv_refs, (qt_ref, ot_ref, lse_ref, a_ref, b_ref) = own[:holders], own[holders:-3]
            inv_ref, cos_ref, sin_ref = own[-3:]
            dq_ref, dqs_ref, own_ref, far_ref = outs[4 * i : 4 * i + 4]
            set_bias(order_ref, k, bias_ref)
            kv = jnp.concatenate([ref[...] for ref in kv_refs], axis=0)
            kt = kv.astype(f32).T[:HD].astype(bf16)
            zero = jnp.zeros((HD, rows), bf16)
            dat_ref[:, :half] = nt(wo_ref[...], a_ref[...]).astype(bf16)
            dat_ref[:, half:] = nt(wo_ref[...], b_ref[...]).astype(bf16)
            for h in range(GROUP):
                at = slice(h * HD, (h + 1) * HD)
                q_low = jnp.concatenate([qt_ref[at, :], zero], axis=0)
                da_high = jnp.concatenate([zero, dat_ref[at, :]], axis=0)
                weights = jnp.exp(nn(kv, q_low) + bias_ref[...] - lse_ref[h : h + 1, :])
                delta = jnp.sum(
                    dat_ref[at, :].astype(f32) * ot_ref[at, :].astype(f32), axis=0, keepdims=True
                )
                ds = (weights * (nn(kv, da_high) - delta)).astype(bf16)
                dkv = nt(ds, q_low) + nt(weights.astype(bf16), da_high)
                if h == 0:
                    dkv_ref[...] = dkv
                else:
                    dkv_ref[...] += dkv
                dqt_ref[at, :] = nn(kt, ds)
            dq = (turn(dqt_ref[...], cos_ref[...], -sin_ref[...]) * HD**-0.5).T
            dq_ref[...] = dq.astype(bf16)
            dqs_ref[...] = (dq * inv_ref[...]).astype(bf16)
            own_ref[...] = dkv_ref[:rows, :]
            far_ref[...] = dkv_ref[rows:, :].astype(bf16)

    inputs, outputs = [orders, wo], []
    for k, detail in zip(members, details):
        inputs += [*[(piece, k) for piece in kv_pieces], *detail]
        outputs += [
            like((rows, n), bf16),
            like((rows, n), bf16),
            like((rows, 2 * HD), f32),
            like((keys - rows, 2 * HD), bf16),
        ]
    results = small_call(
        kernel,
        "attend_back",
        inputs,
        outputs,
        flops=2 * rows * n * (keys * 5 * 4 + width) * count,
        scratch=[
            pltpu.VMEM((keys, rows), f32),
            pltpu.VMEM((n, rows), bf16),
            pltpu.VMEM((n, rows), f32),
            pltpu.VMEM((keys, 2 * HD), f32),
        ],
        scalars=1,
        transcendentals=GROUP * rows * keys * count,
        room=ATTEND_ROOM,
    )
    return [results[4 * i : 4 * i + 4] for i in range(count)]


def out_gradient(mixed, grads):
    n, rows = mixed[0].shape
    width = grads[0].shape[1]

    def kernel(*refs):
        total = 0.0
        for k in range(TP):
            db = jnp.concatenate([refs[TP + 2 * k][...], refs[TP + 2 * k + 1][...]], axis=0)
            total = total + nn(refs[k][...], db)
        refs[-1][...] = total.astype(bf16)

    return small_call(
        kernel,
        "out_gradient",
        [*mixed, *grads],
        [like((n, width), bf16)],
        flops=2 * TP * rows * n * width,
    )[0]


def finish_keys(own, near, last, dq, dqs, inverse, cosine, sine):
    rows, n = dq[0].shape

    def kernel(*refs):
        own_refs, refs = refs[:TP], refs[TP:]
        near_refs, refs = refs[: len(near)], refs[len(near) :]
        last_refs, refs = refs[: len(last)], refs[len(last) :]
        dq_refs, dqs_refs, refs = refs[:TP], refs[TP : 2 * TP], refs[2 * TP :]
        inv_refs, (cos_ref, sin_ref, plain_ref, scaled_ref) = refs[:TP], refs[TP:]
        for k in range(TP):
            total = own_refs[k][...]
            for ref in near_refs if k < TP - 1 else last_refs:
                total = total + ref[k % (TP - 1)].astype(f32)
            total = total.T
            keys = turn(total[:HD], cos_ref[k], -sin_ref[k])
            total = jnp.concatenate([keys, total[HD:]], axis=0).T
            at = slice(k * rows, (k + 1) * rows)
            plain_ref[at, :n] = dq_refs[k][...]
            plain_ref[at, n:] = total.astype(bf16)
            scaled_ref[at, :n] = dqs_refs[k][...]
            scaled_ref[at, n:] = (total * inv_refs[k][...]).astype(bf16)

    shape = like((TP * rows, n + 2 * HD), bf16)
    return small_call(
        kernel,
        "finish_keys",
        [*own, *near, *last, *dq, *dqs, *inverse, cosine, sine],
        [shape, shape],
    )


def join_rows(pieces):
    rows, width = pieces[0].shape

    def kernel(*refs):
        for i, ref in enumerate(refs[:-1]):
            refs[-1][i * rows : (i + 1) * rows, :] = ref[...]

    return small_call(
        kernel, "join_rows", pieces, [like((len(pieces) * rows, width), pieces[0].dtype)]
    )[0]


def reorder_lanes(v, ordered):
    order, size = ordered
    return jnp.concatenate([v[:, i * size : (i + 1) * size] for i in order], axis=1)


def block_orders(width, holders):
    held = [m * holders + h for h in range(holders) for m in range(TP)]
    natural = [held.index(i) for i in range(len(held))]
    size = width // len(held)
    return (held, size), (natural, size)


def hold_tokens(tokens, held):
    half = tokens.shape[0] // 2

    def kernel(x_ref, a_ref, b_ref):
        a_ref[...] = reorder_lanes(x_ref[:half, :].astype(f32), held).astype(bf16)
        b_ref[...] = reorder_lanes(x_ref[half:, :].astype(f32), held).astype(bf16)

    shape = like((half, tokens.shape[1]), bf16)
    return small_call(kernel, "hold_tokens", [tokens], [shape, shape])


def summed(refs, at, half):
    own_ref, a2_ref, a1_ref, b1_ref, b2_ref = refs
    first, second = (a2_ref, a1_ref) if at < half else (b1_ref, b2_ref)
    come = slice(at % half, at % half + ROWS)
    total = own_ref[at : at + ROWS, :].astype(f32)
    return total + first[come, :].astype(f32) + second[come, :].astype(f32)


def finish_middle(tokens, pieces, held):
    rows, width = tokens.shape
    half = rows // 2

    def kernel(x_ref, *refs):
        sums, (mid_ref, inv_ref, a_ref, b_ref) = refs[:5], refs[5:]
        for at in range(0, rows, ROWS):
            here = slice(at, at + ROWS)
            middle = x_ref[here, :].astype(f32) + summed(sums, at, half)
            inverse = lax.rsqrt(jnp.mean(middle * middle, axis=1, keepdims=True) + epsilon)
            mid_ref[here, :] = middle
            inv_ref[here, :] = inverse
            out = a_ref if at < half else b_ref
            come = slice(at % half, at % half + ROWS)
            out[come, :] = reorder_lanes(middle * inverse, held).astype(bf16)

    return small_call(
        kernel,
        "finish_middle",
        [tokens, *pieces],
        [
            like((rows, width), f32),
            like((rows, 1), f32),
            like((half, width), bf16),
            like((half, width), bf16),
        ],
    )


def finish_norm_back(grad, normed_from, inverse, pieces, natural, last):
    rows, width = grad.shape
    half = rows // 2

    def kernel(g_ref, x_ref, inv_ref, *refs):
        sums, outs = refs[:5], refs[5:]
        for at in range(0, rows, ROWS):
            here = slice(at, at + ROWS)
            scaled = reorder_lanes(summed(sums, at, half), natural)
            inverse = inv_ref[here, :]
            normed = x_ref[here, :].astype(f32) * inverse
            mean = jnp.mean(scaled * normed, axis=1, keepdims=True)
            total = g_ref[here, :].astype(f32) + inverse * (scaled - normed * mean)
            outs[0][here, :] = total
            if not last:
                out = outs[1] if at < half else outs[2]
                out[at % half : at % half + ROWS, :] = total.astype(bf16)

    shapes = [like((rows, width), f32)]
    if not last:
        shapes += [like((half, width), bf16)] * 2
    return small_call(
        kernel, "finish_norm_back", [grad, normed_from, inverse, *pieces], shapes
    )


def finish_layer(middle, pieces):
    rows, width = middle.shape

    def kernel(mid_ref, *refs):
        for at in range(0, rows, ROWS):
            here = slice(at, at + ROWS)
            total = mid_ref[here, :] + summed(refs[:5], at, rows // 2)
            refs[5][here, :] = total.astype(bf16)

    return small_call(
        kernel, "finish_layer", [middle, *pieces], [like((rows, width), bf16)]
    )[0]


def interleaved(i):
    return slice(2 * i * LANES, (2 * i + 1) * LANES), slice((2 * i + 1) * LANES, (2 * i + 2) * LANES)


def activate(pieces, gate_up, tile=256):
    half, width = pieces[0].shape
    total, ff = half * len(pieces), gate_up.shape[1] // 2

    def kernel(*refs):
        n_refs, (w_ref, m_ref, slope_ref, n2_ref) = refs[: len(pieces)], refs[len(pieces) :]

        @pl.when(pl.program_id(0) == 0)
        def _():
            for i, ref in enumerate(n_refs):
                n2_ref[i * half : (i + 1) * half, :] = ref[...]

        both = nn(n2_ref[...], w_ref[...])
        for i in range(tile // LANES):
            gate_at, up_at = interleaved(i)
            gate, up = both[:, gate_at], both[:, up_at]
            sigmoid = jax.nn.sigmoid(gate)
            silu = gate * sigmoid
            m_ref[:, i * LANES : (i + 1) * LANES] = (silu * up).astype(bf16)
            slope_ref[:, gate_at] = (up * (sigmoid + silu * (1.0 - sigmoid))).astype(bf16)
            slope_ref[:, up_at] = silu.astype(bf16)

    return pl.pallas_call(
        kernel,
        grid=(pl.cdiv(ff, tile),),
        in_specs=[whole_block(v.shape) for v in pieces]
        + [pl.BlockSpec((width, 2 * tile), lambda j: (0, j))],
        out_specs=[
            pl.BlockSpec((total, tile), lambda j: (0, j)),
            pl.BlockSpec((total, 2 * tile), lambda j: (0, j)),
        ],
        out_shape=[like((total, ff), bf16), like((total, 2 * ff), bf16)],
        scratch_shapes=[pltpu.VMEM((total, width), bf16)],
        compiler_params=pltpu.CompilerParams(vmem_limit_bytes=ROOM),
        cost_estimate=pl.CostEstimate(
            flops=4 * total * width * ff,
            bytes_accessed=2 * (total * width + 2 * width * ff + 3 * total * ff),
            transcendentals=total * ff,
        ),
        name="activate",
    )(*pieces, gate_up)


def activate_back(g, down, slopes, tile=256):
    total, width = g.shape
    ff = down.shape[0]

    def kernel(g_ref, down_ref, slope_ref, d_ref):
        dm = nt(g_ref[...], down_ref[...])
        for i in range(tile // LANES):
            part = dm[:, i * LANES : (i + 1) * LANES]
            for at in interleaved(i):
                d_ref[:, at] = (part * slope_ref[:, at].astype(f32)).astype(bf16)

    return pl.pallas_call(
        kernel,
        grid=(pl.cdiv(ff, tile),),
        in_specs=[
            pl.BlockSpec((total, width), lambda j: (0, 0)),
            pl.BlockSpec((tile, width), lambda j: (j, 0)),
            pl.BlockSpec((total, 2 * tile), lambda j: (0, j)),
        ],
        out_specs=pl.BlockSpec((total, 2 * tile), lambda j: (0, j)),
        out_shape=like((total, 2 * ff), bf16),
        compiler_params=pltpu.CompilerParams(vmem_limit_bytes=ROOM),
        cost_estimate=pl.CostEstimate(
            flops=2 * total * width * ff,
            bytes_accessed=2 * (total * width + width * ff + 4 * total * ff),
            transcendentals=0,
        ),
        name="activate_back",
    )(g, down, slopes)


def weight_grad(left, right, index, come=None):
    total, width = left.shape
    n = right.shape[1]
    rows, columns = width // 4, n // 2 if n % (2 * LANES) == 0 else n

    def kernel(index_ref, left_ref, right_ref, *refs):
        part = tn(left_ref[...], right_ref[...])
        if come is not None:
            part = part + refs[0][...].astype(f32)
        refs[-1][...] = part.astype(bf16)

    out = pl.BlockSpec((rows, columns), lambda i, j, index: (i, j))
    more = [] if come is None else [come]
    return pl.pallas_call(
        kernel,
        grid_spec=pltpu.PrefetchScalarGridSpec(
            num_scalar_prefetch=1,
            grid=(2, n // columns),
            in_specs=[
                pl.BlockSpec((total, rows), lambda i, j, index: (0, 2 * index[0] + i)),
                pl.BlockSpec((total, columns), lambda i, j, index: (0, j)),
            ]
            + [out] * len(more),
            out_specs=out,
        ),
        out_shape=like((width // 2, n), bf16),
        compiler_params=pltpu.CompilerParams(vmem_limit_bytes=ROOM),
        cost_estimate=pl.CostEstimate(
            flops=total * width * n,
            bytes_accessed=total * width + 2 * total * n + 2 * width * n,
            transcendentals=0,
        ),
        name="weight_grad",
    )(index[None], left, right, *more)


def split_qkv(w_query, w_key, w_value, gain):
    own, n = w_query.shape[0], GROUP * HD

    def kernel(q_ref, k_ref, v_ref, gain_ref, out_ref):
        for g in range(TP):
            parts = [ref[:, g * HD : (g + 1) * HD].astype(f32) for ref in (k_ref, v_ref)]
            query = q_ref[:, g * n : (g + 1) * n].astype(f32)
            out_ref[g, :, :n] = (query * gain_ref[...]).astype(bf16)
            out_ref[g, :, n:] = (jnp.concatenate(parts, axis=1) * gain_ref[...]).astype(bf16)

    return small_call(
        kernel,
        "split_qkv",
        [w_query, w_key, w_value, gain],
        [like((TP, own, n + 2 * HD), bf16)],
    )[0]


def merge_qkv(raw, w_query, w_key, w_value, gain):
    own, n = w_query.shape[0], GROUP * HD

    def kernel(in_ref, q_ref, k_ref, v_ref, gain_ref, dq_ref, dk_ref, dv_ref, dgain_ref):
        keys, values = [], []
        dgain = jnp.zeros((own, 1), f32)
        for g in range(TP):
            here = slice(g * n, (g + 1) * n)
            part = in_ref[g, :, :n].astype(f32)
            dgain += jnp.sum(part * q_ref[:, here].astype(f32), axis=1, keepdims=True)
            dq_ref[:, here] = part * gain_ref[...]
            part = in_ref[g, :, n:].astype(f32)
            keys.append(part[:, :HD])
            values.append(part[:, HD:])
        for parts, ref, out_ref in ((keys, k_ref, dk_ref), (values, v_ref, dv_ref)):
            part = jnp.concatenate(parts, axis=1)
            dgain += jnp.sum(part * ref[...].astype(f32), axis=1, keepdims=True)
            out_ref[...] = part * gain_ref[...]
        dgain_ref[...] = dgain

    return small_call(
        kernel,
        "merge_qkv",
        [raw, w_query, w_key, w_value, gain],
        [like(w.shape, f32) for w in (w_query, w_key, w_value)] + [like((own, 1), f32)],
    )


def split_gate_up(w_gate, w_up, gain):
    own, total = w_gate.shape
    ff = total // TP

    def kernel(gate_ref, up_ref, gain_ref, out_ref):
        for g in range(TP):
            for j in range(ff // LANES):
                here = slice(g * ff + j * LANES, g * ff + (j + 1) * LANES)
                for ref, at in zip((gate_ref, up_ref), interleaved(j)):
                    out_ref[g, :, at] = (ref[:, here].astype(f32) * gain_ref[...]).astype(bf16)

    return small_call(
        kernel,
        "split_gate_up",
        [w_gate, w_up, gain],
        [jax.ShapeDtypeStruct((TP, own, 2 * ff), bf16)],
    )[0]


def merge_gate_up(raw, w_gate, w_up, gain):
    own, total = w_gate.shape
    ff = total // TP

    def kernel(in_ref, gate_ref, up_ref, gain_ref, dgate_ref, dup_ref, dgain_ref):
        dgain = jnp.zeros((own, LANES), f32)
        for g in range(TP):
            for j in range(ff // LANES):
                here = slice(g * ff + j * LANES, g * ff + (j + 1) * LANES)
                for ref, out_ref, at in zip(
                    (gate_ref, up_ref), (dgate_ref, dup_ref), interleaved(j)
                ):
                    part = in_ref[g, :, at].astype(f32)
                    dgain += part * ref[:, here].astype(f32)
                    out_ref[:, here] = part * gain_ref[...]
        dgain_ref[...] = jnp.sum(dgain, axis=1, keepdims=True)

    return small_call(
        kernel,
        "merge_gate_up",
        [raw, w_gate, w_up, gain],
        [
            jax.ShapeDtypeStruct((own, total), f32),
            jax.ShapeDtypeStruct((own, total), f32),
            jax.ShapeDtypeStruct((own, 1), f32),
        ],
    )


def make_body(reps, ctxs):
    pair = [(0, 1), (1, 0)]

    def swap(v, k):
        if k == 0:
            return v
        if k == 1:
            return lax.ppermute(v, "tx", pair)
        if k == 2:
            return lax.ppermute(v, "ty", pair)
        return lax.ppermute(v, ("ty", "tx"), [(i, i ^ 3) for i in range(TP)])

    def swap_ctx(v, j):
        return lax.ppermute(v, "ctx", [(i, i ^ j) for i in range(ctxs)]) if j else v

    def halves(v):
        half = v.shape[0] // 2
        return v[:half], v[half:]

    def in_order(a, b):
        return [p for k in range(TP) for p in (a[k], b[k])]

    def gather(a, b):
        ax, by = swap(a, 1), swap(b, 2)
        ay, bx = swap(a, 2), swap(b, 1)
        return in_order((a, ax, ay, swap(ax, 2)), (b, bx, by, swap(by, 1)))

    def scatter_far(parts):
        a, b = halves(parts[3])
        return swap(a, 2), swap(b, 1)

    def scatter_near(parts, far):
        a1, b1 = halves(parts[1])
        a2, b2 = halves(parts[2])
        a1 = (a1.astype(f32) + far[0].astype(f32)).astype(bf16)
        b2 = (b2.astype(f32) + far[1].astype(f32)).astype(bf16)
        return [swap(a2, 2), swap(a1, 1), swap(b1, 1), swap(b2, 2)]

    def by_member(v):
        return v.reshape(TP, -1, v.shape[1])

    def exchange(blocks, t, *first):
        out = jnp.zeros_like(blocks)
        for k in range(TP):
            come = swap(lax.dynamic_index_in_dim(blocks, t ^ k, 0, keepdims=True), k)
            come = after(come, *first) if first else come
            out = lax.dynamic_update_slice_in_dim(out, come, t ^ k, 0)
        return out

    def spread(blocks, t, *first):
        return exchange(blocks, t, *first).reshape(-1, blocks.shape[2])

    def collect(summed_rows, t, *first):
        return exchange(summed_rows.reshape(TP, -1, summed_rows.shape[1]), t, *first)

    def whole(v):
        return lax.all_gather(v, ("rep", "ctx"), axis=0, tiled=True)

    def split_reps(full):
        if reps != 2:
            return lax.psum_scatter(full, "rep", scatter_dimension=0, tiled=True)
        r = lax.axis_index("rep")
        half = full.shape[0] // 2
        sent = lax.dynamic_slice_in_dim(full, (1 - r) * half, half, 0)
        mine = lax.dynamic_slice_in_dim(full, r * half, half, 0)
        sent = lax.ppermute(sent, "rep", pair)
        return (mine.astype(f32) + sent.astype(f32)).astype(bf16)

    def over_reps_first(left, right):
        if reps != 2:
            return tn(left, right).astype(bf16)
        index = 1 - lax.axis_index("rep")
        half = left.shape[1] // 2
        if half % (2 * LANES) == 0:
            return weight_grad(left, right, index)
        return tn(lax.dynamic_slice_in_dim(left, index * half, half, 1), right).astype(bf16)

    def over_reps_last(left, right, first):
        if reps != 2:
            return lax.psum_scatter(first, "rep", scatter_dimension=0, tiled=True)
        index = lax.axis_index("rep")
        half = left.shape[1] // 2
        come = lax.ppermute(first, "rep", pair)
        if half % (2 * LANES) == 0:
            return weight_grad(left, right, index, come)
        mine = lax.dynamic_slice_in_dim(left, index * half, half, 1)
        return (tn(mine, right) + come.astype(f32)).astype(bf16)

    def over_reps(left, right):
        return over_reps_last(left, right, over_reps_first(left, right))

    def owned(part):
        return lax.psum_scatter(part, "ctx", scatter_dimension=0, tiled=True)

    def half_of(v, j, other):
        index = lax.axis_index("ctx") // j % 2
        v = v.reshape(2, -1, v.shape[1])
        return lax.dynamic_index_in_dim(v, 1 - index if other else index, 0, False)

    def body(
        tokens,
        span_order,
        norm_attn,
        w_query,
        w_key,
        w_value,
        w_out,
        norm_mlp,
        w_gate,
        w_up,
        w_down,
        out_grad,
    ):
        count, width = tokens.shape
        held, natural = block_orders(width, reps * ctxs)
        span = count * ctxs // span_order.shape[1]
        per = count // span
        t = 2 * lax.axis_index("ty") + lax.axis_index("tx")
        c = lax.axis_index("ctx")
        gain_attn = norm_attn.astype(f32)[:, None]
        gain_mlp = norm_mlp.astype(f32)[:, None]

        out = whole(w_out)
        qkv_blocks = split_qkv(w_query, w_key, w_value, gain_attn)
        a, b = hold_tokens(after(tokens, qkv_blocks), held)
        qkv_mine, a, b = phase(spread(after(qkv_blocks, a), t), a, b)
        ax, by = swap(a, 1), swap(b, 2)
        ay, bx, axy, bxy = swap(a, 2), swap(b, 1), swap(ax, 2), swap(by, 1)
        qkv = whole(after(qkv_mine, out, ax, by))
        gate_up_blocks = split_gate_up(after(w_gate, qkv_mine), w_up, gain_mlp)
        orders = [swap(after(span_order, qkv_mine), k) for k in range(TP)]
        ay, bx, axy, bxy, gate_up_blocks = phase(ay, bx, axy, bxy, gate_up_blocks)
        x_pieces = in_order((a, ax, ay, axy), (b, bx, by, bxy))

        orders = jnp.concatenate(orders, axis=0).reshape(TP, ctxs, per)
        orders = jnp.concatenate(
            [lax.dynamic_slice_in_dim(orders, c ^ j, 1, 1) for j in range(ctxs)], axis=1
        ).reshape(TP, ctxs * per)
        positions = orders[:, :per, None] * span + jnp.arange(span, dtype=jnp.int32)
        half_dim = HD // 2
        frequency = jnp.power(rope_base, -jnp.arange(half_dim, dtype=f32) / half_dim)
        angles = frequency[:, None] * positions.reshape(TP, 1, count).astype(f32)
        cosine, sine = jnp.cos(angles), jnp.sin(angles)

        qt, kv, inverse = project(x_pieces, qkv, cosine, sine)
        gate_up_mine = spread(after(gate_up_blocks, axy, bxy), t, kv)
        kv_far = [swap_ctx(kv, j) for j in range(1, ctxs)]
        ga, gb = halves(after(out_grad, kv))
        kv, kv_far, gate_up_mine, gax, gby, x_all = phase(
            kv, kv_far, gate_up_mine, swap(ga, 1), swap(gb, 2), join_rows(after(x_pieces, kv))
        )
        kv_pieces = [kv, *kv_far]
        gate_up = whole(gate_up_mine)
        down = whole(after(w_down, gate_up_mine))
        mixed, logsum, parts = [None] * TP, [None] * TP, [None] * TP

        def attend_to(members, queries):
            results = attend(
                members,
                orders,
                [queries[k] for k in members],
                kv_pieces,
                out,
                f32 if 0 in members else bf16,
            )
            for k, (mixed[k], logsum[k], parts[k]) in zip(members, results):
                pass

        attend_to((3,), qt)
        queries, gay, gbx = phase(qt, swap(ga, 2), swap(gb, 1), parts[3])[:3]
        far = scatter_far(parts)
        attend_to((2, 1), queries)
        far, parts[1], parts[2], queries, gaxy, gbxy = phase(
            far, parts[1], parts[2], queries, swap(gax, 2), swap(gby, 1)
        )
        near = scatter_near(parts, far)
        attend_to((0,), queries)
        g_all = join_rows(in_order((ga, gax, gay, gaxy), (gb, gbx, gby, gbxy)))
        near, parts[0], g_all = phase(near, parts[0], g_all)
        middle, inverse_mid, a, b = finish_middle(tokens, [parts[0], *near], held)
        n2_pieces = gather(a, b)

        act, slopes = activate(n2_pieces, gate_up)
        n2_all = join_rows(after(n2_pieces, act))
        part_down = over_reps(act, g_all)
        slopes, part_down, n2_all = phase(slopes, part_down, n2_all)
        down_sent = jnp.split(half_of(part_down, ctxs // 2, True), DOWN_STEPS, axis=1)
        down_come = []

        def send_down(*first):
            piece = after(down_sent[len(down_come)], *first)
            down_come.append(swap_ctx(piece, ctxs // 2))
            return down_come[-1]

        grad_act = activate_back(g_all, down, slopes)
        sent = over_reps_first(n2_all, grad_act)
        sent, down_come[-1] = phase(sent, send_down(down))
        part_gate_up = over_reps_last(n2_all, after(grad_act, sent), sent)
        sum_gate_up = owned(part_gate_up)
        parts = by_member(nt(after(grad_act, part_gate_up), gate_up).astype(bf16))
        parts, down_come[-1] = phase(parts, send_down(sent))
        far = scatter_far(parts)
        near = scatter_near(parts, far)
        forward = nn(after(act, far), down).astype(bf16)
        near, forward = phase(near, forward)
        grad_middle, a, b = finish_norm_back(
            out_grad, middle, inverse_mid, [(parts, 0), *near], natural, False
        )
        part_down = half_of(part_down, ctxs // 2, False).astype(f32)
        part_down = part_down + jnp.concatenate(down_come, axis=1).astype(f32)

        back_of = [None] * TP

        def attend_back_to(members, *grads):
            results = attend_back(
                members,
                orders,
                out,
                kv_pieces,
                [
                    (qt[k], mixed[k], logsum[k], *g, inverse[k], (cosine, k), (sine, k))
                    for k, g in zip(members, grads)
                ],
            )
            for k, back_of[k] in zip(members, results):
                pass

        attend_back_to((0,), (a, b))
        ax, by, ay, bx, back_of[0] = phase(
            swap(a, 1), swap(b, 2), swap(a, 2), swap(b, 1), back_of[0]
        )
        forward = by_member(forward)
        attend_back_to((1, 2), (ax, bx), (ay, by))
        axy, bxy, far, back_of[1], back_of[2] = phase(
            swap(ax, 2), swap(by, 1), scatter_far(forward), back_of[1], back_of[2]
        )
        keys_near = [
            swap_ctx(jnp.stack([back_of[k][3][(j - 1) * count : j * count] for k in range(3)]), j)
            for j in range(1, ctxs)
        ]
        attend_back_to((3,), (axy, bxy))
        keys_near, back_of[3] = phase(keys_near, back_of[3])
        keys_last = [
            swap_ctx(back_of[3][3][None, (j - 1) * count : j * count], j) for j in range(1, ctxs)
        ]
        db_pieces = in_order((a, ax, ay, axy), (b, bx, by, bxy))
        part_out = out_gradient(mixed, after(db_pieces, back_of[3]))
        forward_near = scatter_near(after(forward, keys_near), far)
        keys_last, part_out = phase(keys_last, split_reps(part_out))
        sum_out = owned(part_out)
        grad_proj, scaled_proj = finish_keys(
            [v[2] for v in back_of],
            keys_near,
            keys_last,
            [v[0] for v in back_of],
            [v[1] for v in back_of],
            inverse,
            cosine,
            sine,
        )
        parts = by_member(nt(grad_proj, qkv).astype(bf16))
        down_come = swap_ctx(
            half_of(after(part_down, keys_last).astype(bf16), ctxs // 4, True), ctxs // 4
        )
        parts, sum_gate_up, down_come = phase(parts, sum_gate_up, down_come)
        far = scatter_far(parts)
        sent = over_reps_first(x_all, after(scaled_proj, parts))
        far, sent, forward_near = phase(far, sent, forward_near)
        near = scatter_near(parts, far)
        part_qkv = over_reps_last(x_all, after(scaled_proj, sent), sent)
        sum_qkv = owned(part_qkv)
        layer_out = finish_layer(middle, [(forward, 0), *forward_near])
        near, layer_out = phase(near, layer_out, part_qkv)[:2]
        sum_down = half_of(part_down, ctxs // 4, False) + down_come.astype(f32)
        (input_grad,) = finish_norm_back(
            grad_middle, tokens, inverse[0], [(parts, 0), *near], natural, True
        )
        raw_gate_up = collect(after(sum_gate_up, input_grad), t)

        grad_gate, grad_up, grad_norm_mlp = merge_gate_up(
            raw_gate_up, w_gate, w_up, gain_mlp
        )
        sum_out, sum_qkv = after((sum_out, sum_qkv), input_grad)
        grad_query, grad_key, grad_value, grad_norm_attn = merge_qkv(
            collect(sum_qkv, t), w_query, w_key, w_value, gain_attn
        )
        return (
            layer_out,
            input_grad,
            grad_norm_attn[:, 0],
            grad_query,
            grad_key,
            grad_value,
            sum_out.astype(f32),
            grad_norm_mlp[:, 0],
            grad_gate,
            grad_up,
            sum_down,
        )

    return body


def solution(mesh):
    sequences, ctxs = mesh.shape["dp"], mesh.shape["ctx"]
    reps = sequences // TP
    names = ("ty", "tx", "rep", "ctx")
    grid = Mesh(mesh.devices.reshape(2, 2, reps, ctxs), names)
    matrix, vector = P(names, None), P(names)
    order = P(("ty", "tx", "rep"), None)
    weights = [vector, matrix, matrix, matrix, matrix, vector, matrix, matrix, matrix]
    return jax.shard_map(
        make_body(reps, ctxs),
        mesh=grid,
        in_specs=(matrix, order, *weights, matrix),
        out_specs=(matrix, matrix, *weights),
        check_vma=False,
    )
```

time: 660 us -> 629 us (0.953)
  Pallas kernels: 103 us -> 203 us
  local copies, waits for them, and re-layouts: 92.6 us -> 39.5 us
  matrix products: 89.3 us -> 48.9 us
  waiting for transfers between devices: 231 us -> 202 us
  other arithmetic: 41.5 us -> 27.6 us
    pallas_call x17 -> x27, Pallas kernels: 103 us -> 203 us  [the longest x21 136 us: small_call(): pl.pallas_call(kernel, grid=(1,), in_specs=specs, out_specs=[whole_block(...]
    unnamed x274 -> x123, local copies, waits for them, and re-layouts: 57.5 us -> 10.6 us
    dot_general x8 -> x2, matrix products: 53.6 us -> 13.4 us  [tn(): lax.dot_general(left, right, (((0,), (0,)), ((), ())), preferred_element_...]
    ppermute x6 -> x12, waiting for transfers between devices: 63.5 us -> 30.5 us  [swap_ctx(): return lax.ppermute(v, 'ctx', [(i, i ^ j) for i in range(ctxs)]) if j else v]
    all_gather x4, waiting for transfers between devices: 0.02 us -> 29.3 us  [whole(): return lax.all_gather(v, ('rep', 'ctx'), axis=0, tiled=True)]
    reduce_scatter x4 -> x3, waiting for transfers between devices: 18.2 us -> 0.04 us  [owned(): return lax.psum_scatter(part, 'ctx', scatter_dimension=0, tiled=True)]
    ppermute x29, waiting for transfers between devices: 74.9 us -> 65.1 us  [swap(): return lax.ppermute(v, 'tx', pair)]
    slice x7 -> x0, local copies, waits for them, and re-layouts: 9.4 us -> none  [the longest x3 5.7 us: part_of(): return v[k * count:(k + 1) * count]]
  transfers between devices with their start and end apart: 81 -> 86, of which waited for: 33 -> 40; matrix products, arithmetic and copies ran while one was open for 26% -> 17% of each run, Pallas kernels for 14% -> 32%
where the time goes in v3:
time: 629 us; the launch traced here: 621 us
  Pallas kernels  203 us (32%)
  waiting for transfers between devices  202 us (32%)
  starting transfers between devices  84.6 us (13%)
  matrix products  48.9 us (8%)
  local copies, waits for them, and re-layouts  39.5 us (6%)
  other arithmetic  27.6 us (4%)
  between operations  15.3 us (2%)
    pallas_call x21, Pallas kernels, small_call(): pl.pallas_call(kernel, grid=(1,), in_specs=specs, out_specs=[whole_block(...  136 us
    ppermute x29, waiting for transfers between devices, swap(): return lax.ppermute(v, 'tx', pair)  65.1 us
    ppermute x29, waiting for transfers between devices, swap(): return lax.ppermute(v, 'ty', pair)  59.7 us
    pallas_call x4, Pallas kernels, weight_grad(): pl.pallas_call(kernel, grid_spec=pltpu.PrefetchScalarGridSpec(num_scalar_...  34.2 us
    ppermute x29, starting transfers between devices, swap(): return lax.ppermute(v, 'tx', pair)  33.3 us
    ppermute x12, waiting for transfers between devices, swap_ctx(): return lax.ppermute(v, 'ctx', [(i, i ^ j) for i in range(ctxs)]) if j else v  30.5 us
    all_gather x4, waiting for transfers between devices, whole(): return lax.all_gather(v, ('rep', 'ctx'), axis=0, tiled=True)  29.3 us
    ppermute x29, starting transfers between devices, swap(): return lax.ppermute(v, 'ty', pair)  27.2 us
  transfers between devices with their start and end apart: 86, of which 40 were waited for; matrix products, arithmetic and copies ran while one was open for 17% of the time, Pallas kernels for 32%

profile of v3, /device:TPU:0, one launch (start us, length us, event | category | flops | bytes accessed | tf_op | source)
XLA Modules:
  0.0 621.1 jit_solution(638455202726817889)
XLA Ops:
  14.7 3.0 collective-permute-start
  20.5 2.6 collective-permute-done.1
  25.9 11.1 %collective-permute-done.10.refs_5_ = bf16[128,2048]{1,0:T(8,128)(2,1)S(1)} collective-permute-done((bf16[128,2048]{1,0:T(8,128)(2,1)}, bf16[128,2048]{1,0:T(8,128)(2,1)S(1)}, u32[]{:S(2)}, u32[]{:S(2)}) %collective-permute-start.10) | collective-permute-done | bytes 524320 | tf_op jit(solution)/shard_map/ppermute | solution.py:630
  37.2 4.3 all-gather.5.cloned.1.call-done.wo_ref
  48.9 3.3 split_gate_up.1
  52.2 5.8 collective-permute-done.3
  61.3 9.9 %collective-permute-done.11.refs_7_ = bf16[128,2048]{1,0:T(8,128)(2,1)S(1)} collective-permute-done((bf16[128,2048]{1,0:T(8,128)(2,1)S(1)}, bf16[128,2048]{1,0:T(8,128)(2,1)S(1)}, u32[]{:S(2)}, u32[]{:S(2)}) %collective-permute-start.11) | collective-permute-done | bytes 524320 | tf_op jit(solution)/shard_map/ppermute | solution.py:628
  79.5 7.5 %project.1 = (bf16[4,256,128]{2,1,0:T(8,128)(2,1)}, bf16[512,256]{1,0:T(8,128)(2,1)}, bf16[512,256]{1,0:T(8,128)(2,1)}, bf16[512,256]{1,0:T(8,128)(2,1)}, bf16[5...) custom-call(bf16[128,2048]{1,0:T(8,128)(2,1)} %get-tuple-element.231.refs_, ...), custom_call_target="tpu_custom_call" | custom-call | flops 2684354560 | bytes 8392704 | tf_op jit(solution)/shard_map/project/pallas_call | solution.py:66
  96.2 4.4 join_rows.3.left_ref
  101.7 7.1 %collective-permute-done.13.refs_3_.refs_8_.refs_2_.refs_14_ = bf16[4,256,128]{2,1,0:T(8,128)(2,1)} collective-permute-done((bf16[4,256,128]{2,1,0:T(8,128)(2,1)}, bf16[4,256,128]{2,1,0:T(8,128)(2,1)}, u32[]{:S(2)}, u32[]{:S(2)}) %collective-permute-start.13) | collective-permute-done | bytes 262176 | tf_op jit(solution)/shard_map/ppermute | solution.py:634
  113.7 8.8 %attend.3 = (bf16[512,256]{1,0:T(8,128)(2,1)}, f32[8,256]{1,0:T(8,128)}, bf16[256,2048]{1,0:T(8,128)(2,1)}) custom-call(s32[4,8]{1,0:T(4,128)} %copy.45.order_ref, bf16[512,2048]{1,0:T(8,128)(2,1)} %all-gather.5.cloned.1.call-done.wo_ref, bf16[512,256]{1,0:T(8,128)(2,1)} %get-tuple-element.222.refs_0_.refs_4_, ...), custom_call_target="tpu_custom_call" | custom-call | flops 2684354560 | bytes 4726912 | tf_op jit(solution)/shard_map/attend/pallas_call | solution.py:66
  129.0 15.4 %attend.4 = (bf16[512,256]{1,0:T(8,128)(2,1)}, f32[8,256]{1,0:T(8,128)}, bf16[256,2048]{1,0:T(8,128)(2,1)}, bf16[512,256]{1,0:T(8,128)(2,1)}, f32[8,256]{1,0:T(8,128)}, /*index=5*/bf16[256,2048]{1,0:T(8,128)(2,1)}) custom-call(s32[4,8]{1,0:T(4,128)} %copy.45.order_ref, bf16[512,2048]{1,0:T(8,128)(2,1)} %all-gather.5.cloned.1.call-done.wo_ref, ...), custom_call_target="tpu_custom_call" | custom-call | flops 5368709120 | bytes 7356544 | tf_op jit(solution)/shard_map/attend/pallas_call | solution.py:66
  144.5 2.9 collective-permute-done.24.refs_6_
  157.2 4.5 join_rows.4.g_ref
  161.7 9.1 %attend.5 = (bf16[512,256]{1,0:T(8,128)(2,1)}, f32[8,256]{1,0:T(8,128)}, f32[256,2048]{1,0:T(8,128)}) custom-call(s32[4,8]{1,0:T(4,128)} %copy.45.order_ref, bf16[512,2048]{1,0:T(8,128)(2,1)} %all-gather.5.cloned.1.call-done.wo_ref, bf16[512,256]{1,0:T(8,128)(2,1)} %get-tuple-element.258.refs_0_.refs_4_, ...), custom_call_target="tpu_custom_call" | custom-call | flops 2684354560 | bytes 5775488 | tf_op jit(solution)/shard_map/attend/pallas_call | solution.py:66
  172.1 3.3 collective-permute-done.28.refs_3_
  176.2 5.0 finish_middle.1
  185.3 11.0 %collective-permute-done.30.refs_2_ = bf16[128,2048]{1,0:T(8,128)(2,1)S(1)} collective-permute-done((bf16[128,2048]{1,0:T(8,128)(2,1)}, bf16[128,2048]{1,0:T(8,128)(2,1)S(1)}, u32[]{:S(2)}, u32[]{:S(2)}) %collective-permute-start.30) | collective-permute-done | bytes 524320 | tf_op jit(solution)/shard_map/ppermute | solution.py:628
  198.3 8.8 %collective-permute-done.31.refs_3_ = bf16[128,2048]{1,0:T(8,128)(2,1)S(1)} collective-permute-done((bf16[128,2048]{1,0:T(8,128)(2,1)}, bf16[128,2048]{1,0:T(8,128)(2,1)S(1)}, u32[]{:S(2)}, u32[]{:S(2)}) %collective-permute-start.31) | collective-permute-done | bytes 524320 | tf_op jit(solution)/shard_map/ppermute | solution.py:628
  207.2 5.6 collective-permute-done.34.refs_6_
  212.8 6.6 %all-gather.11.cloned.1.call-done.refs_8_ = bf16[2048,2816]{1,0:T(8,128)(2,1)} async-done(((bf16[256,2816]{1,0:T(8,128)(2,1)}), bf16[2048,2816]{1,0:T(8,128)(2,1)}) %all-gather.11.cloned.1.call-update) | async-done | bytes 11534352 | tf_op jit(solution)/shard_map/all_gather | solution.py:677
  219.4 19.7 %activate.1 = (bf16[1024,1408]{1,0:T(8,128)(2,1)}, bf16[1024,2816]{1,0:T(8,128)(2,1)}) custom-call(bf16[128,2048]{1,0:T(8,128)(2,1)} %get-tuple-element.278.refs_0_, bf16[128,2048]{1,0:T(8,128)(2,1)} %get-tuple-element.279.refs_1_, bf16[128,2048]{1,0:T(8,128)(2,1)} %copy-done.25, bf16[128,2048]{1,0:T(8,128)(2,1)} %copy-done.27, ...), custom_call_target="tpu_custom_call" | custom-call | flops 11811160064 | bytes 24379392 | tf_op jit(solution)/shard_map/activate/pallas_call | solution.py:439
  239.1 6.2 convolution_convert_fusion.3
  245.7 4.3 join_rows.5.left_ref
  250.8 7.2 %add_convert_fusion = bf16[704,2048]{1,0:T(8,128)(2,1)S(1)} fusion(bf16[704,2048]{1,0:T(8,128)(2,1)} %collective-permute-done.36, bf16[1024,2048]{1,0:T(8,128)(2,1)} %join_rows.4.g_ref, bf16[1024,1408]{1,0:T(8,128)(2,1)} %get-tuple-element.295, s32[]{:T(128)S(6)} %select_n.111), kind=kOutput, calls=%fused_computation | convolution fusion | flops 2957115392 | bytes 11534340 | tf_op jit(solution)/shard_map/dot_general | solution.py:43
  261.2 18.4 %all-gather.9.cloned.1.call-done.down_ref = bf16[1408,2048]{1,0:T(8,128)(2,1)} async-done(((bf16[176,2048]{1,0:T(8,128)(2,1)}), bf16[1408,2048]{1,0:T(8,128)(2,1)}) %all-gather.9.cloned.1.call-update) | async-done | bytes 5767184 | tf_op jit(solution)/shard_map/all_gather | solution.py:677
  280.7 12.8 %activate_back.1.right_ref = bf16[1024,2816]{1,0:T(8,128)(2,1)} custom-call(bf16[1024,2048]{1,0:T(8,128)(2,1)} %join_rows.4.g_ref, bf16[1408,2048]{1,0:T(8,128)(2,1)} %all-gather.9.cloned.1.call-done.down_ref, bf16[1024,2816]{1,0:T(8,128)(2,1)} %get-tuple-element.286.slope_ref), custom_call_target="tpu_custom_call" | custom-call | flops 5905580032 | bytes 21495808 | tf_op jit(solution)/shard_map/activate_back/pallas_call | solution.py:471
  293.5 11.5 %weight_grad.4 = bf16[1024,2816]{1,0:T(8,128)(2,1)} custom-call(s32[1]{0:T(128)} %bitcast.8.index_ref, bf16[1024,2048]{1,0:T(8,128)(2,1)} %join_rows.5.left_ref, bf16[1024,2816]{1,0:T(8,128)(2,1)} %activate_back.1.right_ref), custom_call_target="tpu_custom_call" | custom-call | flops 5905580032 | bytes 19398656 | tf_op jit(solution)/shard_map/weight_grad/pallas_call | solution.py:504
  305.0 8.5 %collective-permute-done.37 = bf16[352,1024]{1,0:T(8,128)(2,1)} collective-permute-done((bf16[352,1024]{1,0:T(8,128)(2,1)}, bf16[352,1024]{1,0:T(8,128)(2,1)}, u32[]{:S(2)}, u32[]{:S(2)}) %collective-permute-start.37) | collective-permute-done | bytes 720928 | tf_op jit(solution)/shard_map/ppermute | solution.py:634
  313.5 9.7 %collective-permute-done.38.refs_0_ = bf16[1024,2816]{1,0:T(8,128)(2,1)} collective-permute-done((bf16[1024,2816]{1,0:T(8,128)(2,1)}, bf16[1024,2816]{1,0:T(8,128)(2,1)}, u32[]{:S(2)}, u32[]{:S(2)}) %collective-permute-start.38) | collective-permute-done | bytes 5767200 | tf_op jit(solution)/shard_map/ppermute | solution.py:703
  323.2 13.1 %weight_grad.5 = bf16[1024,2816]{1,0:T(8,128)(2,1)} custom-call(s32[1]{0:T(128)} %bitcast.7.index_ref, bf16[1024,2048]{1,0:T(8,128)(2,1)} %join_rows.5.left_ref, bf16[1024,2816]{1,0:T(8,128)(2,1)} %activate_back.1.right_ref, bf16[1024,2816]{1,0:T(8,128)(2,1)} %collective-permute-done.38.refs_0_), custom_call_target="tpu_custom_call" | custom-call | flops 5905580032 | bytes 19398656 | tf_op jit(solution)/shard_map/weight_grad/pallas_call | solution.py:504
  336.4 16.7 %convolution_convert_fusion = bf16[1024,2048]{1,0:T(8,128)(2,1)S(1)} fusion(bf16[1024,2816]{1,0:T(8,128)(2,1)} %activate_back.1.right_ref, bf16[2048,2816]{1,0:T(8,128)(2,1)} %all-gather.11.cloned.1.call-done.refs_8_), kind=kOutput, calls=%fused_computation.1 | convolution fusion | flops 11813257216 | bytes 21495808 | tf_op jit(solution)/shard_map/dot_general | solution.py:39
  353.0 5.2 collective-permute-done.39
  363.7 11.0 %collective-permute-done.41 = bf16[128,2048]{1,0:T(8,128)(2,1)} collective-permute-done((bf16[128,2048]{1,0:T(8,128)(2,1)}, bf16[128,2048]{1,0:T(8,128)(2,1)}, u32[]{:S(2)}, u32[]{:S(2)}) %collective-permute-start.41) | collective-permute-done | bytes 524320 | tf_op jit(solution)/shard_map/ppermute | solution.py:630
  380.8 11.2 %convolution_convert_fusion.2 = bf16[1024,2048]{1,0:T(8,128)(2,1)} fusion(bf16[1024,1408]{1,0:T(8,128)(2,1)S(1)} %copy-done.14, bf16[1408,2048]{1,0:T(8,128)(2,1)} %all-gather.9.cloned.1.call-done.down_ref), kind=kOutput, calls=%fused_computation.3 | convolution fusion | flops 5907677184 | bytes 12845056 | tf_op jit(solution)/shard_map/dot_general | solution.py:35
  392.1 5.8 collective-permute-done.42.refs_2_
  397.9 6.1 finish_norm_back.2
  410.5 9.6 %attend_back.3 = (bf16[256,512]{1,0:T(8,128)(2,1)}, bf16[256,512]{1,0:T(8,128)(2,1)}, f32[256,128]{1,0:T(8,128)}, bf16[768,128]{1,0:T(8,128)(2,1)}) custom-call(s32[4,8]{1,0:T(4,128)} %copy.45.order_ref, bf16[512,2048]{1,0:T(8,128)(2,1)} %all-gather.5.cloned.1.call-done.wo_ref, bf16[4,256,128]{2,1,0:T(8,128)(2,1)} %get-tuple-element.239.refs_1_.refs_6_.refs_0_.refs_12_, ...), custom_call_target="tpu_custom_call" | custom-call | flops 5905580032 | bytes 5842048 | tf_op jit(solution)/shard_map/attend_back/pallas_call | solution.py:66
  422.7 9.2 %collective-permute-done.47.refs_20_.refs_9_ = bf16[128,2048]{1,0:T(8,128)(2,1)} collective-permute-done((bf16[128,2048]{1,0:T(8,128)(2,1)}, bf16[128,2048]{1,0:T(8,128)(2,1)}, u32[]{:S(2)}, u32[]{:S(2)}) %collective-permute-start.47) | collective-permute-done | bytes 524320 | tf_op jit(solution)/shard_map/ppermute | solution.py:630
  432.6 17.0 %attend_back.4 = (bf16[256,512]{1,0:T(8,128)(2,1)}, bf16[256,512]{1,0:T(8,128)(2,1)}, f32[256,128]{1,0:T(8,128)}, bf16[768,128]{1,0:T(8,128)(2,1)}, bf16[256,512...) custom-call(s32[4,8]{1,0:T(4,128)} %copy.45.order_ref, ...), custom_call_target="tpu_custom_call" | custom-call | flops 11811160064 | bytes 9586816 | tf_op jit(solution)/shard_map/attend_back/pallas_call | solution.py:66
  454.8 4.4 collective-permute-start.54
  459.2 9.9 %attend_back.5 = (bf16[256,512]{1,0:T(8,128)(2,1)}, bf16[256,512]{1,0:T(8,128)(2,1)}, f32[256,128]{1,0:T(8,128)}, bf16[768,128]{1,0:T(8,128)(2,1)}) custom-call(s32[4,8]{1,0:T(4,128)} %copy.45.order_ref, bf16[512,2048]{1,0:T(8,128)(2,1)} %all-gather.5.cloned.1.call-done.wo_ref, bf16[4,256,128]{2,1,0:T(8,128)(2,1)} %get-tuple-element.239.refs_1_.refs_6_.refs_0_.refs_12_, ...), custom_call_target="tpu_custom_call" | custom-call | flops 5905580032 | bytes 5842048 | tf_op jit(solution)/shard_map/attend_back/pallas_call | solution.py:66
  469.1 6.1 out_gradient.1
  477.6 3.0 bitcast_add_fusion
  485.0 2.6 fusion.5
  487.7 2.7 add_convert_fusion.1
  498.1 4.3 finish_keys.1
  502.5 7.7 %convolution_convert_fusion.1 = bf16[1024,2048]{1,0:T(8,128)(2,1)} fusion(bf16[1024,640]{1,0:T(8,128)(2,1)} %get-tuple-element.367, bf16[2048,640]{1,0:T(8,128)(2,1)} %all-gather.7.cloned.1.call-done.refs_8_), kind=kOutput, calls=%fused_computation.2 | convolution fusion | flops 2686451712 | bytes 8126464 | tf_op jit(solution)/shard_map/dot_general | solution.py:39
  510.2 9.7 %collective-permute-done.61 = bf16[176,2048]{1,0:T(8,128)(2,1)S(1)} collective-permute-done((bf16[176,2048]{1,0:T(8,128)(2,1)S(1)}, bf16[176,2048]{1,0:T(8,128)(2,1)S(1)}, u32[]{:S(2)}, u32[]{:S(2)}) %collective-permute-start.61) | collective-permute-done | bytes 720928 | tf_op jit(solution)/shard_map/ppermute | solution.py:634
  519.9 2.9 slice_bitcast_fusion
  523.9 4.8 weight_grad.6
  528.7 3.4 collective-permute-done.63
  533.0 3.2 collective-permute-done.72.refs_0_
  537.3 4.8 weight_grad.7
  543.3 2.7 fusion.4
  548.9 3.9 finish_layer.1
  552.8 4.3 collective-permute-done.62.refs_1_
  558.4 10.1 %collective-permute-done.69.refs_2_ = bf16[128,2048]{1,0:T(8,128)(2,1)S(1)} collective-permute-done((bf16[128,2048]{1,0:T(8,128)(2,1)}, bf16[128,2048]{1,0:T(8,128)(2,1)S(1)}, u32[]{:S(2)}, u32[]{:S(2)}) %collective-permute-start.69) | collective-permute-done | bytes 524320 | tf_op jit(solution)/shard_map/ppermute | solution.py:628
  569.4 5.9 finish_norm_back.3
  578.0 2.5 fusion.3
  582.8 5.4 collective-permute-done.76
  588.2 4.1 collective-permute-done.77
  593.6 3.4 collective-permute-start.73
  598.2 4.5 merge_gate_up.1
  (335 shorter events, 146.2 us)
Async XLA Ops:
  7.2 34.3 %all-gather.5.cloned.1.call-start = ((), (), s32[]{:S(2)}) async-start(), calls=%async_computation.3 | async-start | bytes 2359296 | tf_op jit(solution)/shard_map/all_gather | solution.py:677
  7.9 71.6 %all-gather.7.cloned.1.call-start = ((), (), s32[]{:S(2)}) async-start(), calls=%async_computation.4 | async-start | bytes 2949120 | tf_op jit(solution)/shard_map/all_gather | solution.py:677
  41.5 177.9 %all-gather.11.cloned.1.call-start = ((), (), s32[]{:S(2)}) async-start(), calls=%async_computation.6 | async-start | bytes 12976128 | tf_op jit(solution)/shard_map/all_gather | solution.py:677
  42.3 19.0 %collective-permute-start.7 = (bf16[128,2048]{1,0:T(8,128)(2,1)}, bf16[128,2048]{1,0:T(8,128)(2,1)S(1)}, u32[]{:S(2)}, u32[]{:S(2)}) collective-permute-start(bf16[128,2048]{1,0:T(8,128)(2,1)} %get-tuple-element.231.refs_0_), channel_id=1, source_target_pairs={{0,16},{16,0},{1,17},{17,1},{2,18},{18,2},{3,19},{19,3},{4,20},{20... | collective-permute-start | bytes 1572872 | tf_op jit(solution)/shard_map/ppermute | solution.py:630
  43.8 17.4 %collective-permute-start.8 = (bf16[128,2048]{1,0:T(8,128)(2,1)}, bf16[128,2048]{1,0:T(8,128)(2,1)S(1)}, u32[]{:S(2)}, u32[]{:S(2)}) collective-permute-start(bf16[128,2048]{1,0:T(8,128)(2,1)} %get-tuple-element.232.refs_1_), channel_id=1, source_target_pairs={{0,8},{8,0},{1,9},{9,1},{2,10},{10,2},{3,11},{11,3},{4,12},{12,4},... | collective-permute-start | bytes 1572872 | tf_op jit(solution)/shard_map/ppermute | solution.py:628
  58.1 13.1 %collective-permute-start.11 = (bf16[128,2048]{1,0:T(8,128)(2,1)S(1)}, bf16[128,2048]{1,0:T(8,128)(2,1)S(1)}, u32[]{:S(2)}, u32[]{:S(2)}) collective-permute-start(bf16[128,2048]{1,0:T(8,128)(2,1)S(1)} %collective-permute-done.10.refs_5_), channel_id=1, source_target_pairs={{0,8},{8,0},{1,9},{9,1},{2,10},{10,2},{3,11},{11,3},{4,12},{12,4},... | collective-permute-start | bytes 1572872 | tf_op jit(solution)/shard_map/ppermute | solution.py:628
  74.8 14.8 %collective-permute-start.17 = (bf16[1,64,2816]{2,1,0:T(8,128)(2,1)}, bf16[1,64,2816]{2,1,0:T(8,128)(2,1)S(1)}, u32[]{:S(2)}, u32[]{:S(2)}) collective-permute-start(bf16[1,64,2816]{2,1,0:T(8,128)(2,1)} %get-tuple-element.431), channel_id=1, source_target_pairs={{0,24},{8,16},{16,8},{24,0},{1,25},{9,17},{17,9},{25,1},{2,26},{10... | collective-permute-start | bytes 1081352 | tf_op jit(solution)/shard_map/ppermute | solution.py:631
  76.7 15.2 %collective-permute-start.16 = (bf16[1,64,2816]{2,1,0:T(8,128)(2,1)}, bf16[1,64,2816]{2,1,0:T(8,128)(2,1)S(1)}, u32[]{:S(2)}, u32[]{:S(2)}) collective-permute-start(bf16[1,64,2816]{2,1,0:T(8,128)(2,1)} %get-tuple-element.432), channel_id=1, source_target_pairs={{0,16},{16,0},{1,17},{17,1},{2,18},{18,2},{3,19},{19,3},{4,20},{20... | collective-permute-start | bytes 1081352 | tf_op jit(solution)/shard_map/ppermute | solution.py:630
  77.3 14.8 %collective-permute-start.15 = (bf16[1,64,2816]{2,1,0:T(8,128)(2,1)S(1)}, bf16[1,64,2816]{2,1,0:T(8,128)(2,1)}, u32[]{:S(2)}, u32[]{:S(2)}) collective-permute-start(bf16[1,64,2816]{2,1,0:T(8,128)(2,1)S(1)} %get-tuple-element.433), channel_id=1, source_target_pairs={{0,8},{8,0},{1,9},{9,1},{2,10},{10,2},{3,11},{11,3},{4,12},{12,4},... | collective-permute-start | bytes 1081352 | tf_op jit(solution)/shard_map/ppermute | solution.py:628
  87.1 14.6 %collective-permute-start.12 = (bf16[4,256,128]{2,1,0:T(8,128)(2,1)}, bf16[4,256,128]{2,1,0:T(8,128)(2,1)}, u32[]{:S(2)}, u32[]{:S(2)}) collective-permute-start(bf16[4,256,128]{2,1,0:T(8,128)(2,1)} %get-tuple-element.239.refs_1_.refs_6_.refs_0_.refs_12_), channel_id=1, source_target_pairs={{0,1},{1,0},{2,3},{3,2},{4,5},{5,4},{6,7},{7,6},{8,9},{9,8},{10,11... | collective-permute-start | bytes 786440 | tf_op jit(solution)/shard_map/ppermute | solution.py:634
  88.6 20.2 %collective-permute-start.13 = (bf16[4,256,128]{2,1,0:T(8,128)(2,1)}, bf16[4,256,128]{2,1,0:T(8,128)(2,1)}, u32[]{:S(2)}, u32[]{:S(2)}) collective-permute-start(bf16[4,256,128]{2,1,0:T(8,128)(2,1)} %get-tuple-element.239.refs_1_.refs_6_.refs_0_.refs_12_), channel_id=1, source_target_pairs={{0,2},{1,3},{2,0},{3,1},{4,6},{5,7},{6,4},{7,5},{8,10},{9,11},{10,... | collective-permute-start | bytes 786440 | tf_op jit(solution)/shard_map/ppermute | solution.py:634
  89.6 19.2 %collective-permute-start.14 = (bf16[4,256,128]{2,1,0:T(8,128)(2,1)}, bf16[4,256,128]{2,1,0:T(8,128)(2,1)}, u32[]{:S(2)}, u32[]{:S(2)}) collective-permute-start(bf16[4,256,128]{2,1,0:T(8,128)(2,1)} %get-tuple-element.239.refs_1_.refs_6_.refs_0_.refs_12_), channel_id=1, source_target_pairs={{0,3},{1,2},{2,1},{3,0},{4,7},{5,6},{6,5},{7,4},{8,11},{9,10},{10,... | collective-permute-start | bytes 786440 | tf_op jit(solution)/shard_map/ppermute | solution.py:634
  92.7 16.1 %collective-permute-start.18 = (bf16[128,2048]{1,0:T(8,128)(2,1)S(1)}, bf16[128,2048]{1,0:T(8,128)(2,1)S(1)}, u32[]{:S(2)}, u32[]{:S(2)}) collective-permute-start(bf16[128,2048]{1,0:T(8,128)(2,1)S(1)} %get-tuple-element.438.refs_0_), channel_id=1, source_target_pairs={{0,8},{8,0},{1,9},{9,1},{2,10},{10,2},{3,11},{11,3},{4,12},{12,4},... | collective-permute-start | bytes 1572872 | tf_op jit(solution)/shard_map/ppermute | solution.py:628
  94.0 14.7 %collective-permute-start.19 = (bf16[128,2048]{1,0:T(8,128)(2,1)S(1)}, bf16[128,2048]{1,0:T(8,128)(2,1)S(1)}, u32[]{:S(2)}, u32[]{:S(2)}) collective-permute-start(bf16[128,2048]{1,0:T(8,128)(2,1)S(1)} %get-tuple-element.437.refs_1_), channel_id=1, source_target_pairs={{0,16},{16,0},{1,17},{17,1},{2,18},{18,2},{3,19},{19,3},{4,20},{20... | collective-permute-start | bytes 1572872 | tf_op jit(solution)/shard_map/ppermute | solution.py:630
  109.7 169.9 %all-gather.9.cloned.1.call-start = ((), (), s32[]{:S(2)}) async-start(), calls=%async_computation.5 | async-start | bytes 6488064 | tf_op jit(solution)/shard_map/all_gather | solution.py:677
  110.3 409.6 %reduce-scatter.4.cloned.1.call-start = ((), (), s32[]{:S(2)}) async-start(), calls=%async_computation.7 | async-start | bytes 7208960 | tf_op jit(solution)/shard_map/reduce_scatter | solution.py:713
  111.2 16.5 %collective-permute-start.22 = (bf16[128,2048]{1,0:T(8,128)(2,1)S(1)}, bf16[128,2048]{1,0:T(8,128)(2,1)S(1)}, u32[]{:S(2)}, u32[]{:S(2)}) collective-permute-start(bf16[128,2048]{1,0:T(8,128)(2,1)S(1)} %get-tuple-element.438.refs_0_), channel_id=1, source_target_pairs={{0,16},{16,0},{1,17},{17,1},{2,18},{18,2},{3,19},{19,3},{4,20},{20... | collective-permute-start | bytes 1572872 | tf_op jit(solution)/shard_map/ppermute | solution.py:630
  112.4 16.6 %collective-permute-start.23 = (bf16[128,2048]{1,0:T(8,128)(2,1)S(1)}, bf16[128,2048]{1,0:T(8,128)(2,1)S(1)}, u32[]{:S(2)}, u32[]{:S(2)}) collective-permute-start(bf16[128,2048]{1,0:T(8,128)(2,1)S(1)} %get-tuple-element.437.refs_1_), channel_id=1, source_target_pairs={{0,8},{8,0},{1,9},{9,1},{2,10},{10,2},{3,11},{11,3},{4,12},{12,4},... | collective-permute-start | bytes 1572872 | tf_op jit(solution)/shard_map/ppermute | solution.py:628
  124.9 19.6 %collective-permute-start.20 = (bf16[128,2048]{1,0:T(8,128)(2,1)}, bf16[128,2048]{1,0:T(8,128)(2,1)}, u32[]{:S(2)}, u32[]{:S(2)}) collective-permute-start(bf16[128,2048]{1,0:T(8,128)(2,1)} %get-tuple-element.436), channel_id=1, source_target_pairs={{0,16},{16,0},{1,17},{17,1},{2,18},{18,2},{3,19},{19,3},{4,20},{20... | collective-permute-start | bytes 1572872 | tf_op jit(solution)/shard_map/ppermute | solution.py:630
  125.8 18.7 %collective-permute-start.21 = (bf16[128,2048]{1,0:T(8,128)(2,1)}, bf16[128,2048]{1,0:T(8,128)(2,1)}, u32[]{:S(2)}, u32[]{:S(2)}) collective-permute-start(bf16[128,2048]{1,0:T(8,128)(2,1)} %get-tuple-element.435), channel_id=1, source_target_pairs={{0,8},{8,0},{1,9},{9,1},{2,10},{10,2},{3,11},{11,3},{4,12},{12,4},... | collective-permute-start | bytes 1572872 | tf_op jit(solution)/shard_map/ppermute | solution.py:628
  126.7 20.7 %collective-permute-start.24 = (bf16[128,2048]{1,0:T(8,128)(2,1)S(1)}, bf16[128,2048]{1,0:T(8,128)(2,1)}, u32[]{:S(2)}, u32[]{:S(2)}) collective-permute-start(bf16[128,2048]{1,0:T(8,128)(2,1)S(1)} %collective-permute-done.18.refs_2_), channel_id=1, source_target_pairs={{0,16},{16,0},{1,17},{17,1},{2,18},{18,2},{3,19},{19,3},{4,20},{20... | collective-permute-start | bytes 1572872 | tf_op jit(solution)/shard_map/ppermute | solution.py:630
  127.7 20.0 %collective-permute-start.25 = (bf16[128,2048]{1,0:T(8,128)(2,1)S(1)}, bf16[128,2048]{1,0:T(8,128)(2,1)S(1)}, u32[]{:S(2)}, u32[]{:S(2)}) collective-permute-start(bf16[128,2048]{1,0:T(8,128)(2,1)S(1)} %copy-done.24), channel_id=1, source_target_pairs={{0,8},{8,0},{1,9},{9,1},{2,10},{10,2},{3,11},{11,3},{4,12},{12,4},... | collective-permute-start | bytes 1572872 | tf_op jit(solution)/shard_map/ppermute | solution.py:628
  151.0 19.8 %collective-permute-start.29 = (bf16[128,2048]{1,0:T(8,128)(2,1)S(1)}, bf16[128,2048]{1,0:T(8,128)(2,1)S(1)}, u32[]{:S(2)}, u32[]{:S(2)}) collective-permute-start(bf16[128,2048]{1,0:T(8,128)(2,1)S(1)} %add_convert_fusion.2), channel_id=1, source_target_pairs={{0,16},{16,0},{1,17},{17,1},{2,18},{18,2},{3,19},{19,3},{4,20},{20... | collective-permute-start | bytes 1572872 | tf_op jit(solution)/shard_map/ppermute | solution.py:630
  154.5 16.3 %collective-permute-start.27 = (bf16[128,2048]{1,0:T(8,128)(2,1)S(1)}, bf16[128,2048]{1,0:T(8,128)(2,1)S(1)}, u32[]{:S(2)}, u32[]{:S(2)}) collective-permute-start(bf16[128,2048]{1,0:T(8,128)(2,1)S(1)} %add_convert_fusion.3), channel_id=1, source_target_pairs={{0,8},{8,0},{1,9},{9,1},{2,10},{10,2},{3,11},{11,3},{4,12},{12,4},... | collective-permute-start | bytes 1572872 | tf_op jit(solution)/shard_map/ppermute | solution.py:628
  155.2 16.9 %collective-permute-start.26 = (bf16[128,2048]{1,0:T(8,128)(2,1)}, bf16[128,2048]{1,0:T(8,128)(2,1)S(1)}, u32[]{:S(2)}, u32[]{:S(2)}) collective-permute-start(bf16[128,2048]{1,0:T(8,128)(2,1)} %slice.187), channel_id=1, source_target_pairs={{0,16},{16,0},{1,17},{17,1},{2,18},{18,2},{3,19},{19,3},{4,20},{20... | collective-permute-start | bytes 1572872 | tf_op jit(solution)/shard_map/ppermute | solution.py:630
  156.5 18.9 %collective-permute-start.28 = (bf16[128,2048]{1,0:T(8,128)(2,1)}, bf16[128,2048]{1,0:T(8,128)(2,1)S(1)}, u32[]{:S(2)}, u32[]{:S(2)}) collective-permute-start(bf16[128,2048]{1,0:T(8,128)(2,1)} %slice.189), channel_id=1, source_target_pairs={{0,8},{8,0},{1,9},{9,1},{2,10},{10,2},{3,11},{11,3},{4,12},{12,4},... | collective-permute-start | bytes 1572872 | tf_op jit(solution)/shard_map/ppermute | solution.py:628
  181.2 15.1 %collective-permute-start.30 = (bf16[128,2048]{1,0:T(8,128)(2,1)}, bf16[128,2048]{1,0:T(8,128)(2,1)S(1)}, u32[]{:S(2)}, u32[]{:S(2)}) collective-permute-start(bf16[128,2048]{1,0:T(8,128)(2,1)} %get-tuple-element.278.refs_0_), channel_id=1, source_target_pairs={{0,8},{8,0},{1,9},{9,1},{2,10},{10,2},{3,11},{11,3},{4,12},{12,4},... | collective-permute-start | bytes 1572872 | tf_op jit(solution)/shard_map/ppermute | solution.py:628
  181.7 15.1 %collective-permute-start.33 = (bf16[128,2048]{1,0:T(8,128)(2,1)}, bf16[128,2048]{1,0:T(8,128)(2,1)S(1)}, u32[]{:S(2)}, u32[]{:S(2)}) collective-permute-start(bf16[128,2048]{1,0:T(8,128)(2,1)} %get-tuple-element.279.refs_1_), channel_id=1, source_target_pairs={{0,16},{16,0},{1,17},{17,1},{2,18},{18,2},{3,19},{19,3},{4,20},{20... | collective-permute-start | bytes 1572872 | tf_op jit(solution)/shard_map/ppermute | solution.py:630
  183.2 24.0 %collective-permute-start.31 = (bf16[128,2048]{1,0:T(8,128)(2,1)}, bf16[128,2048]{1,0:T(8,128)(2,1)S(1)}, u32[]{:S(2)}, u32[]{:S(2)}) collective-permute-start(bf16[128,2048]{1,0:T(8,128)(2,1)} %get-tuple-element.279.refs_1_), channel_id=1, source_target_pairs={{0,8},{8,0},{1,9},{9,1},{2,10},{10,2},{3,11},{11,3},{4,12},{12,4},... | collective-permute-start | bytes 1572872 | tf_op jit(solution)/shard_map/ppermute | solution.py:628
  183.8 23.4 %collective-permute-start.32 = (bf16[128,2048]{1,0:T(8,128)(2,1)}, bf16[128,2048]{1,0:T(8,128)(2,1)S(1)}, u32[]{:S(2)}, u32[]{:S(2)}) collective-permute-start(bf16[128,2048]{1,0:T(8,128)(2,1)} %get-tuple-element.278.refs_0_), channel_id=1, source_target_pairs={{0,16},{16,0},{1,17},{17,1},{2,18},{18,2},{3,19},{19,3},{4,20},{20... | collective-permute-start | bytes 1572872 | tf_op jit(solution)/shard_map/ppermute | solution.py:630
  196.3 16.5 %collective-permute-start.34 = (bf16[128,2048]{1,0:T(8,128)(2,1)S(1)}, bf16[128,2048]{1,0:T(8,128)(2,1)S(1)}, u32[]{:S(2)}, u32[]{:S(2)}) collective-permute-start(bf16[128,2048]{1,0:T(8,128)(2,1)S(1)} %collective-permute-done.30.refs_2_), channel_id=1, source_target_pairs={{0,16},{16,0},{1,17},{17,1},{2,18},{18,2},{3,19},{19,3},{4,20},{20... | collective-permute-start | bytes 1572872 | tf_op jit(solution)/shard_map/ppermute | solution.py:630
  196.9 15.9 %collective-permute-start.35 = (bf16[128,2048]{1,0:T(8,128)(2,1)S(1)}, bf16[128,2048]{1,0:T(8,128)(2,1)S(1)}, u32[]{:S(2)}, u32[]{:S(2)}) collective-permute-start(bf16[128,2048]{1,0:T(8,128)(2,1)S(1)} %collective-permute-done.33.refs_5_), channel_id=1, source_target_pairs={{0,8},{8,0},{1,9},{9,1},{2,10},{10,2},{3,11},{11,3},{4,12},{12,4},... | collective-permute-start | bytes 1572872 | tf_op jit(solution)/shard_map/ppermute | solution.py:628
  279.6 33.9 %collective-permute-start.37 = (bf16[352,1024]{1,0:T(8,128)(2,1)}, bf16[352,1024]{1,0:T(8,128)(2,1)}, u32[]{:S(2)}, u32[]{:S(2)}) collective-permute-start(bf16[352,1024]{1,0:T(8,128)(2,1)} %get-tuple-element.289), channel_id=1, source_target_pairs={{0,2},{1,3},{2,0},{3,1},{4,6},{5,7},{6,4},{7,5},{8,10},{9,11},{10,... | collective-permute-start | bytes 2162696 | tf_op jit(solution)/shard_map/ppermute | solution.py:634
  313.5 44.7 %collective-permute-start.39 = (bf16[352,1024]{1,0:T(8,128)(2,1)}, bf16[352,1024]{1,0:T(8,128)(2,1)}, u32[]{:S(2)}, u32[]{:S(2)}) collective-permute-start(bf16[352,1024]{1,0:T(8,128)(2,1)} %get-tuple-element.293), channel_id=1, source_target_pairs={{0,2},{1,3},{2,0},{3,1},{4,6},{5,7},{6,4},{7,5},{8,10},{9,11},{10,... | collective-permute-start | bytes 2162696 | tf_op jit(solution)/shard_map/ppermute | solution.py:634
  336.3 256.1 %reduce-scatter.6.cloned.1.call-start = ((), (), s32[]{:S(2)}) async-start(), calls=%async_computation.8 | async-start | bytes 1310720 | tf_op jit(solution)/shard_map/reduce_scatter | solution.py:713
  359.6 15.1 %collective-permute-start.41 = (bf16[128,2048]{1,0:T(8,128)(2,1)}, bf16[128,2048]{1,0:T(8,128)(2,1)}, u32[]{:S(2)}, u32[]{:S(2)}) collective-permute-start(bf16[128,2048]{1,0:T(8,128)(2,1)} %get-tuple-element.421), channel_id=1, source_target_pairs={{0,16},{16,0},{1,17},{17,1},{2,18},{18,2},{3,19},{19,3},{4,20},{20... | collective-permute-start | bytes 1572872 | tf_op jit(solution)/shard_map/ppermute | solution.py:630
  361.6 15.1 %collective-permute-start.44 = (bf16[128,2048]{1,0:T(8,128)(2,1)}, bf16[128,2048]{1,0:T(8,128)(2,1)}, u32[]{:S(2)}, u32[]{:S(2)}) collective-permute-start(bf16[128,2048]{1,0:T(8,128)(2,1)} %get-tuple-element.419), channel_id=1, source_target_pairs={{0,8},{8,0},{1,9},{9,1},{2,10},{10,2},{3,11},{11,3},{4,12},{12,4},... | collective-permute-start | bytes 1572872 | tf_op jit(solution)/shard_map/ppermute | solution.py:628
  363.0 29.0 %collective-permute-start.40 = (bf16[128,2048]{1,0:T(8,128)(2,1)}, bf16[128,2048]{1,0:T(8,128)(2,1)S(1)}, u32[]{:S(2)}, u32[]{:S(2)}) collective-permute-start(bf16[128,2048]{1,0:T(8,128)(2,1)} %get-tuple-element.422), channel_id=1, source_target_pairs={{0,16},{16,0},{1,17},{17,1},{2,18},{18,2},{3,19},{19,3},{4,20},{20... | collective-permute-start | bytes 1572872 | tf_op jit(solution)/shard_map/ppermute | solution.py:630
  363.6 28.5 %collective-permute-start.43 = (bf16[128,2048]{1,0:T(8,128)(2,1)}, bf16[128,2048]{1,0:T(8,128)(2,1)S(1)}, u32[]{:S(2)}, u32[]{:S(2)}) collective-permute-start(bf16[128,2048]{1,0:T(8,128)(2,1)} %get-tuple-element.420), channel_id=1, source_target_pairs={{0,8},{8,0},{1,9},{9,1},{2,10},{10,2},{3,11},{11,3},{4,12},{12,4},... | collective-permute-start | bytes 1572872 | tf_op jit(solution)/shard_map/ppermute | solution.py:628
  378.6 19.2 %collective-permute-start.42 = (bf16[128,2048]{1,0:T(8,128)(2,1)S(1)}, bf16[128,2048]{1,0:T(8,128)(2,1)}, u32[]{:S(2)}, u32[]{:S(2)}) collective-permute-start(bf16[128,2048]{1,0:T(8,128)(2,1)S(1)} %get-tuple-element.418), channel_id=1, source_target_pairs={{0,8},{8,0},{1,9},{9,1},{2,10},{10,2},{3,11},{11,3},{4,12},{12,4},... | collective-permute-start | bytes 1572872 | tf_op jit(solution)/shard_map/ppermute | solution.py:628
  380.2 17.7 %collective-permute-start.45 = (bf16[128,2048]{1,0:T(8,128)(2,1)S(1)}, bf16[128,2048]{1,0:T(8,128)(2,1)}, u32[]{:S(2)}, u32[]{:S(2)}) collective-permute-start(bf16[128,2048]{1,0:T(8,128)(2,1)S(1)} %get-tuple-element.417), channel_id=1, source_target_pairs={{0,16},{16,0},{1,17},{17,1},{2,18},{18,2},{3,19},{19,3},{4,20},{20... | collective-permute-start | bytes 1572872 | tf_op jit(solution)/shard_map/ppermute | solution.py:630
  404.0 16.2 %collective-permute-start.46 = (bf16[128,2048]{1,0:T(8,128)(2,1)}, bf16[128,2048]{1,0:T(8,128)(2,1)S(1)}, u32[]{:S(2)}, u32[]{:S(2)}) collective-permute-start(bf16[128,2048]{1,0:T(8,128)(2,1)} %get-tuple-element.350.refs_7_.refs_4_), channel_id=1, source_target_pairs={{0,8},{8,0},{1,9},{9,1},{2,10},{10,2},{3,11},{11,3},{4,12},{12,4},... | collective-permute-start | bytes 1572872 | tf_op jit(solution)/shard_map/ppermute | solution.py:628
  405.5 26.4 %collective-permute-start.48 = (bf16[128,2048]{1,0:T(8,128)(2,1)}, bf16[128,2048]{1,0:T(8,128)(2,1)}, u32[]{:S(2)}, u32[]{:S(2)}) collective-permute-start(bf16[128,2048]{1,0:T(8,128)(2,1)} %get-tuple-element.350.refs_7_.refs_4_), channel_id=1, source_target_pairs={{0,16},{16,0},{1,17},{17,1},{2,18},{18,2},{3,19},{19,3},{4,20},{20... | collective-permute-start | bytes 1572872 | tf_op jit(solution)/shard_map/ppermute | solution.py:630
  405.9 26.0 %collective-permute-start.47 = (bf16[128,2048]{1,0:T(8,128)(2,1)}, bf16[128,2048]{1,0:T(8,128)(2,1)}, u32[]{:S(2)}, u32[]{:S(2)}) collective-permute-start(bf16[128,2048]{1,0:T(8,128)(2,1)} %get-tuple-element.351.refs_8_.refs_5_), channel_id=1, source_target_pairs={{0,16},{16,0},{1,17},{17,1},{2,18},{18,2},{3,19},{19,3},{4,20},{20... | collective-permute-start | bytes 1572872 | tf_op jit(solution)/shard_map/ppermute | solution.py:630
  407.5 24.4 %collective-permute-start.49 = (bf16[128,2048]{1,0:T(8,128)(2,1)}, bf16[128,2048]{1,0:T(8,128)(2,1)}, u32[]{:S(2)}, u32[]{:S(2)}) collective-permute-start(bf16[128,2048]{1,0:T(8,128)(2,1)} %get-tuple-element.351.refs_8_.refs_5_), channel_id=1, source_target_pairs={{0,8},{8,0},{1,9},{9,1},{2,10},{10,2},{3,11},{11,3},{4,12},{12,4},... | collective-permute-start | bytes 1572872 | tf_op jit(solution)/shard_map/ppermute | solution.py:628
  410.3 40.2 %collective-permute-start.52 = (bf16[128,2048]{1,0:T(8,128)(2,1)}, bf16[128,2048]{1,0:T(8,128)(2,1)S(1)}, u32[]{:S(2)}, u32[]{:S(2)}) collective-permute-start(bf16[128,2048]{1,0:T(8,128)(2,1)} %get-tuple-element.416), channel_id=1, source_target_pairs={{0,16},{16,0},{1,17},{17,1},{2,18},{18,2},{3,19},{19,3},{4,20},{20... | collective-permute-start | bytes 1572872 | tf_op jit(solution)/shard_map/ppermute | solution.py:630
  421.0 29.6 %collective-permute-start.53 = (bf16[128,2048]{1,0:T(8,128)(2,1)}, bf16[128,2048]{1,0:T(8,128)(2,1)S(1)}, u32[]{:S(2)}, u32[]{:S(2)}) collective-permute-start(bf16[128,2048]{1,0:T(8,128)(2,1)} %get-tuple-element.415), channel_id=1, source_target_pairs={{0,8},{8,0},{1,9},{9,1},{2,10},{10,2},{3,11},{11,3},{4,12},{12,4},... | collective-permute-start | bytes 1572872 | tf_op jit(solution)/shard_map/ppermute | solution.py:628
  431.9 19.8 %collective-permute-start.50 = (bf16[128,2048]{1,0:T(8,128)(2,1)}, bf16[128,2048]{1,0:T(8,128)(2,1)}, u32[]{:S(2)}, u32[]{:S(2)}) collective-permute-start(bf16[128,2048]{1,0:T(8,128)(2,1)} %copy-done.59), channel_id=1, source_target_pairs={{0,16},{16,0},{1,17},{17,1},{2,18},{18,2},{3,19},{19,3},{4,20},{20... | collective-permute-start | bytes 1572872 | tf_op jit(solution)/shard_map/ppermute | solution.py:630
  432.3 19.4 %collective-permute-start.51 = (bf16[128,2048]{1,0:T(8,128)(2,1)}, bf16[128,2048]{1,0:T(8,128)(2,1)}, u32[]{:S(2)}, u32[]{:S(2)}) collective-permute-start(bf16[128,2048]{1,0:T(8,128)(2,1)} %collective-permute-done.47.refs_20_.refs_9_), channel_id=1, source_target_pairs={{0,8},{8,0},{1,9},{9,1},{2,10},{10,2},{3,11},{11,3},{4,12},{12,4},... | collective-permute-start | bytes 1572872 | tf_op jit(solution)/shard_map/ppermute | solution.py:628
  453.4 15.7 %collective-permute-start.56 = (bf16[3,256,128]{2,1,0:T(8,128)(2,1)}, bf16[3,256,128]{2,1,0:T(8,128)(2,1)}, u32[]{:S(2)}, u32[]{:S(2)}) collective-permute-start(bf16[3,256,128]{2,1,0:T(8,128)(2,1)} %pad_maximum_fusion.2), channel_id=1, source_target_pairs={{0,3},{1,2},{2,1},{3,0},{4,7},{5,6},{6,5},{7,4},{8,11},{9,10},{10,... | collective-permute-start | bytes 589832 | tf_op jit(solution)/shard_map/ppermute | solution.py:634
  454.1 15.0 %collective-permute-start.55 = (bf16[3,256,128]{2,1,0:T(8,128)(2,1)}, bf16[3,256,128]{2,1,0:T(8,128)(2,1)}, u32[]{:S(2)}, u32[]{:S(2)}) collective-permute-start(bf16[3,256,128]{2,1,0:T(8,128)(2,1)} %pad_maximum_fusion.1), channel_id=1, source_target_pairs={{0,2},{1,3},{2,0},{3,1},{4,6},{5,7},{6,4},{7,5},{8,10},{9,11},{10,... | collective-permute-start | bytes 589832 | tf_op jit(solution)/shard_map/ppermute | solution.py:634
  454.8 14.3 %collective-permute-start.54 = (bf16[3,256,128]{2,1,0:T(8,128)(2,1)}, bf16[3,256,128]{2,1,0:T(8,128)(2,1)}, u32[]{:S(2)}, u32[]{:S(2)}) collective-permute-start(bf16[3,256,128]{2,1,0:T(8,128)(2,1)} %pad_maximum_fusion), channel_id=1, source_target_pairs={{0,1},{1,0},{2,3},{3,2},{4,5},{5,4},{6,7},{7,6},{8,9},{9,8},{10,11... | collective-permute-start | bytes 589832 | tf_op jit(solution)/shard_map/ppermute | solution.py:634
  491.1 28.8 %collective-permute-start.61 = (bf16[176,2048]{1,0:T(8,128)(2,1)S(1)}, bf16[176,2048]{1,0:T(8,128)(2,1)S(1)}, u32[]{:S(2)}, u32[]{:S(2)}) collective-permute-start(bf16[176,2048]{1,0:T(8,128)(2,1)S(1)} %dynamic-slice_bitcast_fusion.1), channel_id=1, source_target_pairs={{0,1},{1,0},{2,3},{3,2},{4,5},{5,4},{6,7},{7,6},{8,9},{9,8},{10,11... | collective-permute-start | bytes 2162696 | tf_op jit(solution)/shard_map/ppermute | solution.py:634
  494.0 28.8 %collective-permute-start.66 = (bf16[128,2048]{1,0:T(8,128)(2,1)}, bf16[128,2048]{1,0:T(8,128)(2,1)S(1)}, u32[]{:S(2)}, u32[]{:S(2)}) collective-permute-start(bf16[128,2048]{1,0:T(8,128)(2,1)} %get-tuple-element.412), channel_id=1, source_target_pairs={{0,8},{8,0},{1,9},{9,1},{2,10},{10,2},{3,11},{11,3},{4,12},{12,4},... | collective-permute-start | bytes 1572872 | tf_op jit(solution)/shard_map/ppermute | solution.py:628
  494.8 33.9 %collective-permute-start.68 = (bf16[128,2048]{1,0:T(8,128)(2,1)}, bf16[128,2048]{1,0:T(8,128)(2,1)S(1)}, u32[]{:S(2)}, u32[]{:S(2)}) collective-permute-start(bf16[128,2048]{1,0:T(8,128)(2,1)} %get-tuple-element.411), channel_id=1, source_target_pairs={{0,16},{16,0},{1,17},{17,1},{2,18},{18,2},{3,19},{19,3},{4,20},{20... | collective-permute-start | bytes 1572872 | tf_op jit(solution)/shard_map/ppermute | solution.py:630
  496.4 32.3 %collective-permute-start.65 = (bf16[128,2048]{1,0:T(8,128)(2,1)}, bf16[128,2048]{1,0:T(8,128)(2,1)S(1)}, u32[]{:S(2)}, u32[]{:S(2)}) collective-permute-start(bf16[128,2048]{1,0:T(8,128)(2,1)} %get-tuple-element.414), channel_id=1, source_target_pairs={{0,16},{16,0},{1,17},{17,1},{2,18},{18,2},{3,19},{19,3},{4,20},{20... | collective-permute-start | bytes 1572872 | tf_op jit(solution)/shard_map/ppermute | solution.py:630
  496.8 31.9 %collective-permute-start.67 = (bf16[128,2048]{1,0:T(8,128)(2,1)}, bf16[128,2048]{1,0:T(8,128)(2,1)}, u32[]{:S(2)}, u32[]{:S(2)}) collective-permute-start(bf16[128,2048]{1,0:T(8,128)(2,1)} %get-tuple-element.413), channel_id=1, source_target_pairs={{0,8},{8,0},{1,9},{9,1},{2,10},{10,2},{3,11},{11,3},{4,12},{12,4},... | collective-permute-start | bytes 1572872 | tf_op jit(solution)/shard_map/ppermute | solution.py:628
  498.1 94.4 %reduce-scatter.8.cloned.1.call-start = ((), (), s32[]{:S(2)}) async-start(), calls=%async_computation.9 | async-start | bytes 1638400 | tf_op jit(solution)/shard_map/reduce_scatter | solution.py:713
  542.1 15.0 %collective-permute-start.62 = (bf16[128,2048]{1,0:T(8,128)(2,1)}, bf16[128,2048]{1,0:T(8,128)(2,1)S(1)}, u32[]{:S(2)}, u32[]{:S(2)}) collective-permute-start(bf16[128,2048]{1,0:T(8,128)(2,1)} %get-tuple-element.410), channel_id=1, source_target_pairs={{0,16},{16,0},{1,17},{17,1},{2,18},{18,2},{3,19},{19,3},{4,20},{20... | collective-permute-start | bytes 1572872 | tf_op jit(solution)/shard_map/ppermute | solution.py:630
  543.3 15.0 %collective-permute-start.70 = (bf16[128,2048]{1,0:T(8,128)(2,1)}, bf16[128,2048]{1,0:T(8,128)(2,1)S(1)}, u32[]{:S(2)}, u32[]{:S(2)}) collective-permute-start(bf16[128,2048]{1,0:T(8,128)(2,1)} %get-tuple-element.407), channel_id=1, source_target_pairs={{0,8},{8,0},{1,9},{9,1},{2,10},{10,2},{3,11},{11,3},{4,12},{12,4},... | collective-permute-start | bytes 1572872 | tf_op jit(solution)/shard_map/ppermute | solution.py:628
  546.1 22.4 %collective-permute-start.69 = (bf16[128,2048]{1,0:T(8,128)(2,1)}, bf16[128,2048]{1,0:T(8,128)(2,1)S(1)}, u32[]{:S(2)}, u32[]{:S(2)}) collective-permute-start(bf16[128,2048]{1,0:T(8,128)(2,1)} %get-tuple-element.406), channel_id=1, source_target_pairs={{0,8},{8,0},{1,9},{9,1},{2,10},{10,2},{3,11},{11,3},{4,12},{12,4},... | collective-permute-start | bytes 1572872 | tf_op jit(solution)/shard_map/ppermute | solution.py:628
  548.1 20.4 %collective-permute-start.71 = (bf16[128,2048]{1,0:T(8,128)(2,1)}, bf16[128,2048]{1,0:T(8,128)(2,1)S(1)}, u32[]{:S(2)}, u32[]{:S(2)}) collective-permute-start(bf16[128,2048]{1,0:T(8,128)(2,1)} %get-tuple-element.405), channel_id=1, source_target_pairs={{0,16},{16,0},{1,17},{17,1},{2,18},{18,2},{3,19},{19,3},{4,20},{20... | collective-permute-start | bytes 1572872 | tf_op jit(solution)/shard_map/ppermute | solution.py:630
  577.1 15.2 %collective-permute-start.77 = (bf16[1,64,2816]{2,1,0:T(8,128)(2,1)S(1)}, bf16[1,64,2816]{2,1,0:T(8,128)(2,1)S(1)}, u32[]{:S(2)}, u32[]{:S(2)}) collective-permute-start(bf16[1,64,2816]{2,1,0:T(8,128)(2,1)S(1)} %get-tuple-element.426), channel_id=1, source_target_pairs={{0,16},{16,0},{1,17},{17,1},{2,18},{18,2},{3,19},{19,3},{4,20},{20... | collective-permute-start | bytes 1081352 | tf_op jit(solution)/shard_map/ppermute | solution.py:630
  580.5 16.6 %collective-permute-start.78 = (bf16[1,64,2816]{2,1,0:T(8,128)(2,1)S(1)}, bf16[1,64,2816]{2,1,0:T(8,128)(2,1)S(1)}, u32[]{:S(2)}, u32[]{:S(2)}) collective-permute-start(bf16[1,64,2816]{2,1,0:T(8,128)(2,1)S(1)} %get-tuple-element.425), channel_id=1, source_target_pairs={{0,24},{8,16},{16,8},{24,0},{1,25},{9,17},{17,9},{25,1},{2,26},{10... | collective-permute-start | bytes 1081352 | tf_op jit(solution)/shard_map/ppermute | solution.py:631
  (83 other events, 820.6 us)
Sparse Core Ops, SparseCore 0:
  9.6 31.7 all-gather.4
  43.1 33.3 all-gather.6
  109.8 109.5 all-gather.10
  220.8 58.7 all-gather.8
  336.4 105.5 reduce-scatter.3
  498.2 28.4 reduce-scatter.5
  542.2 28.1 reduce-scatter.7

commit v4 on v3

--- a/solution.py
+++ b/solution.py
@@ -14,7 +14,7 @@
 ROWS = 64
 ROOM = 60 << 20
 ATTEND_ROOM = 60 << 20
-DOWN_STEPS = 2
+DOWN_STEPS = 4
 
 epsilon = 1e-05
 rope_base = 10000.0
@@ -815,20 +815,18 @@
         grad_act = activate_back(g_all, down, slopes)
         sent = over_reps_first(n2_all, grad_act)
         sent, down_come[-1] = phase(sent, send_down(down))
-        part_gate_up = over_reps_last(n2_all, after(grad_act, sent), sent)
+        parts = by_member(nt(after(grad_act, sent), gate_up).astype(bf16))
+        parts, down_come[-1] = phase(parts, send_down(grad_act))
+        part_gate_up = over_reps_last(n2_all, after(grad_act, parts), sent)
+        part_gate_up, down_come[-1] = phase(part_gate_up, send_down(sent))
         sum_gate_up = owned(part_gate_up)
-        parts = by_member(nt(after(grad_act, part_gate_up), gate_up).astype(bf16))
-        parts, down_come[-1] = phase(parts, send_down(sent))
-        far = scatter_far(parts)
+        far = scatter_far(after(parts, part_gate_up))
         near = scatter_near(parts, far)
         forward = nn(after(act, far), down).astype(bf16)
         near, forward = phase(near, forward)
         grad_middle, a, b = finish_norm_back(
             out_grad, middle, inverse_mid, [(parts, 0), *near], natural, False
         )
-        part_down = half_of(part_down, ctxs // 2, False).astype(f32)
-        part_down = part_down + jnp.concatenate(down_come, axis=1).astype(f32)
-
         back_of = [None] * TP
 
         def attend_back_to(members, *grads):
@@ -866,8 +864,9 @@
         db_pieces = in_order((a, ax, ay, axy), (b, bx, by, bxy))
         part_out = out_gradient(mixed, after(db_pieces, back_of[3]))
         forward_near = scatter_near(after(forward, keys_near), far)
-        keys_last, part_out = phase(keys_last, split_reps(part_out))
-        sum_out = owned(part_out)
+        keys_last, part_out, forward_near[0], forward_near[2] = phase(
+            keys_last, part_out, forward_near[0], forward_near[2]
+        )
         grad_proj, scaled_proj = finish_keys(
             [v[2] for v in back_of],
             keys_near,
@@ -879,31 +878,37 @@
             sine,
         )
         parts = by_member(nt(grad_proj, qkv).astype(bf16))
-        down_come = swap_ctx(
-            half_of(after(part_down, keys_last).astype(bf16), ctxs // 4, True), ctxs // 4
-        )
-        parts, sum_gate_up, down_come = phase(parts, sum_gate_up, down_come)
-        far = scatter_far(parts)
-        sent = over_reps_first(x_all, after(scaled_proj, parts))
-        far, sent, forward_near = phase(far, sent, forward_near)
-        near = scatter_near(parts, far)
+        parts, down_come[-1], forward_near, sum_gate_up = phase(
+            parts, send_down(keys_near), forward_near, sum_gate_up
+        )
+        across = phase(*halves(parts[3]))
+        far_back = swap(across[0], 2), swap(across[1], 1)
+        sent = over_reps_first(x_all, after(scaled_proj, across))
         part_qkv = over_reps_last(x_all, after(scaled_proj, sent), sent)
+        far_back, part_qkv = phase(far_back, part_qkv)
         sum_qkv = owned(part_qkv)
-        layer_out = finish_layer(middle, [(forward, 0), *forward_near])
-        near, layer_out = phase(near, layer_out, part_qkv)[:2]
-        sum_down = half_of(part_down, ctxs // 4, False) + down_come.astype(f32)
+        near = scatter_near(parts, far_back)
+        layer_out = finish_layer(after(middle, far_back), [(forward, 0), *forward_near])
+        sum_out = owned(split_reps(after(part_out, far_back)))
+        near, layer_out = phase(near, layer_out)
         (input_grad,) = finish_norm_back(
             grad_middle, tokens, inverse[0], [(parts, 0), *near], natural, True
         )
-        raw_gate_up = collect(after(sum_gate_up, input_grad), t)
-
+        raw_gate_up = collect(after(sum_gate_up, near), t)
         grad_gate, grad_up, grad_norm_mlp = merge_gate_up(
-            raw_gate_up, w_gate, w_up, gain_mlp
-        )
-        sum_out, sum_qkv = after((sum_out, sum_qkv), input_grad)
+            after(raw_gate_up, input_grad), w_gate, w_up, gain_mlp
+        )
+        sum_qkv = after(sum_qkv, near)
         grad_query, grad_key, grad_value, grad_norm_attn = merge_qkv(
             collect(sum_qkv, t), w_query, w_key, w_value, gain_attn
         )
+        part_down = half_of(after(part_down, input_grad), ctxs // 2, False).astype(f32)
+        part_down = part_down + jnp.concatenate(down_come, axis=1).astype(f32)
+        down_come = swap_ctx(
+            half_of(part_down.astype(bf16), ctxs // 4, True), ctxs // 4
+        )
+        down_come = after(down_come, grad_query)
+        sum_down = half_of(part_down, ctxs // 4, False) + down_come.astype(f32)
         return (
             layer_out,
             input_grad,
@@ -911,7 +916,7 @@
             grad_query,
             grad_key,
             grad_value,
-            sum_out.astype(f32),
+            after(sum_out, grad_query).astype(f32),
             grad_norm_mlp[:, 0],
             grad_gate,
             grad_up,

time: 629 us -> 618 us (0.983)
  waiting for transfers between devices: 202 us -> 182 us
  local copies, waits for them, and re-layouts: 39.5 us -> 47.7 us
    ppermute x3, waiting for transfers between devices: 13.7 us -> 0.75 us  [over_reps_last(): come = lax.ppermute(first, 'rep', pair)]
    ppermute x12 -> x14, starting transfers between devices: 15 us -> 17.3 us  [swap_ctx(): return lax.ppermute(v, 'ctx', [(i, i ^ j) for i in range(ctxs)]) if j else v]
    ppermute x12 -> x14, waiting for transfers between devices: 30.5 us -> 28.5 us  [swap_ctx(): return lax.ppermute(v, 'ctx', [(i, i ^ j) for i in range(ctxs)]) if j else v]
    slice x8 -> x9, local copies, waits for them, and re-layouts: 14.1 us -> 15.6 us  [halves(): return (v[:half], v[half:])]
  transfers between devices with their start and end apart: 86 -> 88, of which waited for: 40 -> 38; matrix products, arithmetic and copies ran while one was open for 17% -> 18% of each run, Pallas kernels for 32% -> 32%
where the time goes in v4:
time: 618 us; the launch traced here: 610 us
  Pallas kernels  203 us (33%)
  waiting for transfers between devices  182 us (29%)
  starting transfers between devices  86.8 us (14%)
  matrix products  50.3 us (8%)
  local copies, waits for them, and re-layouts  47.7 us (8%)
  other arithmetic  25.1 us (4%)
  between operations  15.3 us (2%)
    pallas_call x21, Pallas kernels, small_call(): pl.pallas_call(kernel, grid=(1,), in_specs=specs, out_specs=[whole_block(...  136 us
    ppermute x29, waiting for transfers between devices, swap(): return lax.ppermute(v, 'tx', pair)  61.3 us
    ppermute x29, waiting for transfers between devices, swap(): return lax.ppermute(v, 'ty', pair)  56.2 us
    pallas_call x4, Pallas kernels, weight_grad(): pl.pallas_call(kernel, grid_spec=pltpu.PrefetchScalarGridSpec(num_scalar_...  33.6 us
    ppermute x29, starting transfers between devices, swap(): return lax.ppermute(v, 'tx', pair)  31.4 us
    all_gather x4, waiting for transfers between devices, whole(): return lax.all_gather(v, ('rep', 'ctx'), axis=0, tiled=True)  31.3 us
    ppermute x14, waiting for transfers between devices, swap_ctx(): return lax.ppermute(v, 'ctx', [(i, i ^ j) for i in range(ctxs)]) if j else v  28.5 us
    ppermute x29, starting transfers between devices, swap(): return lax.ppermute(v, 'ty', pair)  28.2 us
  transfers between devices with their start and end apart: 88, of which 38 were waited for; matrix products, arithmetic and copies ran while one was open for 18% of the time, Pallas kernels for 32%

profile of v4, /device:TPU:0, one launch (start us, length us, event | category | flops | bytes accessed | tf_op | source)
XLA Modules:
  0.0 610.1 jit_solution(12823071314744450504)
XLA Ops:
  11.2 2.5 hold_tokens.1
  14.8 3.0 collective-permute-start
  20.5 2.6 collective-permute-done.1
  25.9 11.1 %collective-permute-done.10.refs_5_ = bf16[128,2048]{1,0:T(8,128)(2,1)S(1)} collective-permute-done((bf16[128,2048]{1,0:T(8,128)(2,1)}, bf16[128,2048]{1,0:T(8,128)(2,1)S(1)}, u32[]{:S(2)}, u32[]{:S(2)}) %collective-permute-start.10) | collective-permute-done | bytes 524320 | tf_op jit(solution)/shard_map/ppermute | solution.py:630
  37.2 4.3 all-gather.5.cloned.1.call-done.wo_ref
  46.5 2.4 collective-permute-start.5
  48.9 3.3 split_gate_up.1
  52.2 5.8 collective-permute-done.3
  61.3 9.9 %collective-permute-done.11.refs_7_ = bf16[128,2048]{1,0:T(8,128)(2,1)S(1)} collective-permute-done((bf16[128,2048]{1,0:T(8,128)(2,1)S(1)}, bf16[128,2048]{1,0:T(8,128)(2,1)S(1)}, u32[]{:S(2)}, u32[]{:S(2)}) %collective-permute-start.11) | collective-permute-done | bytes 524320 | tf_op jit(solution)/shard_map/ppermute | solution.py:628
  79.6 7.5 %project.1 = (bf16[4,256,128]{2,1,0:T(8,128)(2,1)}, bf16[512,256]{1,0:T(8,128)(2,1)}, bf16[512,256]{1,0:T(8,128)(2,1)}, bf16[512,256]{1,0:T(8,128)(2,1)}, bf16[5...) custom-call(bf16[128,2048]{1,0:T(8,128)(2,1)} %get-tuple-element.244.refs_, ...), custom_call_target="tpu_custom_call" | custom-call | flops 2684354560 | bytes 8392704 | tf_op jit(solution)/shard_map/project/pallas_call | solution.py:66
  96.2 4.4 join_rows.3.left_ref
  101.6 7.1 %collective-permute-done.13.refs_3_.refs_8_.refs_2_.refs_14_ = bf16[4,256,128]{2,1,0:T(8,128)(2,1)} collective-permute-done((bf16[4,256,128]{2,1,0:T(8,128)(2,1)}, bf16[4,256,128]{2,1,0:T(8,128)(2,1)}, u32[]{:S(2)}, u32[]{:S(2)}) %collective-permute-start.13) | collective-permute-done | bytes 262176 | tf_op jit(solution)/shard_map/ppermute | solution.py:634
  113.7 8.8 %attend.3 = (bf16[512,256]{1,0:T(8,128)(2,1)}, f32[8,256]{1,0:T(8,128)}, bf16[256,2048]{1,0:T(8,128)(2,1)}) custom-call(s32[4,8]{1,0:T(4,128)} %copy.45.order_ref, bf16[512,2048]{1,0:T(8,128)(2,1)} %all-gather.5.cloned.1.call-done.wo_ref, bf16[512,256]{1,0:T(8,128)(2,1)} %get-tuple-element.235.refs_0_.refs_4_, ...), custom_call_target="tpu_custom_call" | custom-call | flops 2684354560 | bytes 4726912 | tf_op jit(solution)/shard_map/attend/pallas_call | solution.py:66
  129.0 15.5 %attend.4 = (bf16[512,256]{1,0:T(8,128)(2,1)}, f32[8,256]{1,0:T(8,128)}, bf16[256,2048]{1,0:T(8,128)(2,1)}, bf16[512,256]{1,0:T(8,128)(2,1)}, f32[8,256]{1,0:T(8,128)}, /*index=5*/bf16[256,2048]{1,0:T(8,128)(2,1)}) custom-call(s32[4,8]{1,0:T(4,128)} %copy.45.order_ref, bf16[512,2048]{1,0:T(8,128)(2,1)} %all-gather.5.cloned.1.call-done.wo_ref, ...), custom_call_target="tpu_custom_call" | custom-call | flops 5368709120 | bytes 7356544 | tf_op jit(solution)/shard_map/attend/pallas_call | solution.py:66
  144.4 2.9 collective-permute-done.24.refs_6_
  157.2 4.5 join_rows.4.g_ref
  161.7 9.1 %attend.5 = (bf16[512,256]{1,0:T(8,128)(2,1)}, f32[8,256]{1,0:T(8,128)}, f32[256,2048]{1,0:T(8,128)}) custom-call(s32[4,8]{1,0:T(4,128)} %copy.45.order_ref, bf16[512,2048]{1,0:T(8,128)(2,1)} %all-gather.5.cloned.1.call-done.wo_ref, bf16[512,256]{1,0:T(8,128)(2,1)} %get-tuple-element.271.refs_0_.refs_4_, ...), custom_call_target="tpu_custom_call" | custom-call | flops 2684354560 | bytes 5775488 | tf_op jit(solution)/shard_map/attend/pallas_call | solution.py:66
  172.1 3.3 collective-permute-done.28.refs_3_
  176.1 5.0 finish_middle.1
  185.2 11.0 %collective-permute-done.30.refs_2_ = bf16[128,2048]{1,0:T(8,128)(2,1)S(1)} collective-permute-done((bf16[128,2048]{1,0:T(8,128)(2,1)}, bf16[128,2048]{1,0:T(8,128)(2,1)S(1)}, u32[]{:S(2)}, u32[]{:S(2)}) %collective-permute-start.30) | collective-permute-done | bytes 524320 | tf_op jit(solution)/shard_map/ppermute | solution.py:628
  198.2 8.8 %collective-permute-done.31.refs_3_ = bf16[128,2048]{1,0:T(8,128)(2,1)S(1)} collective-permute-done((bf16[128,2048]{1,0:T(8,128)(2,1)}, bf16[128,2048]{1,0:T(8,128)(2,1)S(1)}, u32[]{:S(2)}, u32[]{:S(2)}) %collective-permute-start.31) | collective-permute-done | bytes 524320 | tf_op jit(solution)/shard_map/ppermute | solution.py:628
  207.1 5.6 collective-permute-done.34.refs_6_
  212.7 6.7 %all-gather.11.cloned.1.call-done.refs_8_ = bf16[2048,2816]{1,0:T(8,128)(2,1)} async-done(((bf16[256,2816]{1,0:T(8,128)(2,1)}), bf16[2048,2816]{1,0:T(8,128)(2,1)}) %all-gather.11.cloned.1.call-update) | async-done | bytes 11534352 | tf_op jit(solution)/shard_map/all_gather | solution.py:677
  219.4 19.8 %activate.1 = (bf16[1024,1408]{1,0:T(8,128)(2,1)}, bf16[1024,2816]{1,0:T(8,128)(2,1)}) custom-call(bf16[128,2048]{1,0:T(8,128)(2,1)} %get-tuple-element.291.refs_0_, bf16[128,2048]{1,0:T(8,128)(2,1)} %get-tuple-element.292.refs_1_, bf16[128,2048]{1,0:T(8,128)(2,1)} %copy-done.18, bf16[128,2048]{1,0:T(8,128)(2,1)} %copy-done.20, ...), custom_call_target="tpu_custom_call" | custom-call | flops 11811160064 | bytes 24379392 | tf_op jit(solution)/shard_map/activate/pallas_call | solution.py:439
  239.2 6.2 %convolution_convert_fusion.3 = bf16[704,2048]{1,0:T(8,128)(2,1)S(1)} fusion(bf16[1024,2048]{1,0:T(8,128)(2,1)} %join_rows.4.g_ref, bf16[1024,1408]{1,0:T(8,128)(2,1)} %get-tuple-element.311, s32[]{:T(128)S(6)} %select_n.112), kind=kOutput, calls=%fused_computation.4 | convolution fusion | flops 2954231808 | bytes 8650756 | tf_op jit(solution)/shard_map/dot_general | solution.py:43
  245.8 4.4 join_rows.5.left_ref
  250.9 7.2 %add_convert_fusion = bf16[704,2048]{1,0:T(8,128)(2,1)S(1)} fusion(bf16[704,2048]{1,0:T(8,128)(2,1)} %collective-permute-done.36, bf16[1024,2048]{1,0:T(8,128)(2,1)} %join_rows.4.g_ref, bf16[1024,1408]{1,0:T(8,128)(2,1)} %get-tuple-element.311, s32[]{:T(128)S(6)} %select_n.111), kind=kOutput, calls=%fused_computation | convolution fusion | flops 2957115392 | bytes 11534340 | tf_op jit(solution)/shard_map/dot_general | solution.py:43
  259.2 20.3 %all-gather.9.cloned.1.call-done.down_ref = bf16[1408,2048]{1,0:T(8,128)(2,1)} async-done(((bf16[176,2048]{1,0:T(8,128)(2,1)}), bf16[1408,2048]{1,0:T(8,128)(2,1)}) %all-gather.9.cloned.1.call-update) | async-done | bytes 5767184 | tf_op jit(solution)/shard_map/all_gather | solution.py:677
  280.7 12.8 %activate_back.1.right_ref = bf16[1024,2816]{1,0:T(8,128)(2,1)} custom-call(bf16[1024,2048]{1,0:T(8,128)(2,1)} %join_rows.4.g_ref, bf16[1408,2048]{1,0:T(8,128)(2,1)} %all-gather.9.cloned.1.call-done.down_ref, bf16[1024,2816]{1,0:T(8,128)(2,1)} %get-tuple-element.299.slope_ref), custom_call_target="tpu_custom_call" | custom-call | flops 5905580032 | bytes 21495808 | tf_op jit(solution)/shard_map/activate_back/pallas_call | solution.py:471
  293.5 11.5 %weight_grad.4 = bf16[1024,2816]{1,0:T(8,128)(2,1)} custom-call(s32[1]{0:T(128)} %bitcast.7.index_ref, bf16[1024,2048]{1,0:T(8,128)(2,1)} %join_rows.5.left_ref, bf16[1024,2816]{1,0:T(8,128)(2,1)} %activate_back.1.right_ref), custom_call_target="tpu_custom_call" | custom-call | flops 5905580032 | bytes 19398656 | tf_op jit(solution)/shard_map/weight_grad/pallas_call | solution.py:504
  308.0 18.2 %convolution_convert_fusion = bf16[1024,2048]{1,0:T(8,128)(2,1)} fusion(bf16[1024,2816]{1,0:T(8,128)(2,1)} %activate_back.1.right_ref, bf16[2048,2816]{1,0:T(8,128)(2,1)} %all-gather.11.cloned.1.call-done.refs_8_), kind=kOutput, calls=%fused_computation.1 | convolution fusion | flops 11813257216 | bytes 21495808 | tf_op jit(solution)/shard_map/dot_general | solution.py:39
  326.2 5.9 collective-permute-done.38
  332.9 12.8 %weight_grad.5 = bf16[1024,2816]{1,0:T(8,128)(2,1)} custom-call(s32[1]{0:T(128)} %bitcast.13.index_ref, bf16[1024,2048]{1,0:T(8,128)(2,1)} %join_rows.5.left_ref, bf16[1024,2816]{1,0:T(8,128)(2,1)} %activate_back.1.right_ref, bf16[1024,2816]{1,0:T(8,128)(2,1)} %collective-permute-done.40.refs_0_), custom_call_target="tpu_custom_call" | custom-call | flops 5905580032 | bytes 19398656 | tf_op jit(solution)/shard_map/weight_grad/pallas_call | solution.py:504
  353.2 9.4 %collective-permute-done.42 = bf16[128,2048]{1,0:T(8,128)(2,1)S(1)} collective-permute-done((bf16[128,2048]{1,0:T(8,128)(2,1)S(1)}, bf16[128,2048]{1,0:T(8,128)(2,1)S(1)}, u32[]{:S(2)}, u32[]{:S(2)}) %collective-permute-start.42) | collective-permute-done | bytes 524320 | tf_op jit(solution)/shard_map/ppermute | solution.py:630
  368.0 11.2 %convolution_convert_fusion.2 = bf16[1024,2048]{1,0:T(8,128)(2,1)} fusion(bf16[1024,1408]{1,0:T(8,128)(2,1)S(1)} %copy-done.8, bf16[1408,2048]{1,0:T(8,128)(2,1)} %all-gather.9.cloned.1.call-done.down_ref), kind=kOutput, calls=%fused_computation.3 | convolution fusion | flops 5907677184 | bytes 12845056 | tf_op jit(solution)/shard_map/dot_general | solution.py:35
  379.3 6.3 %collective-permute-done.43.refs_2_ = bf16[128,2048]{1,0:T(8,128)(2,1)} collective-permute-done((bf16[128,2048]{1,0:T(8,128)(2,1)S(1)}, bf16[128,2048]{1,0:T(8,128)(2,1)}, u32[]{:S(2)}, u32[]{:S(2)}) %collective-permute-start.43) | collective-permute-done | bytes 524320 | tf_op jit(solution)/shard_map/ppermute | solution.py:628
  385.7 6.0 finish_norm_back.2
  398.3 9.7 %attend_back.3 = (bf16[256,512]{1,0:T(8,128)(2,1)}, bf16[256,512]{1,0:T(8,128)(2,1)}, f32[256,128]{1,0:T(8,128)}, bf16[768,128]{1,0:T(8,128)(2,1)}) custom-call(s32[4,8]{1,0:T(4,128)} %copy.45.order_ref, bf16[512,2048]{1,0:T(8,128)(2,1)} %all-gather.5.cloned.1.call-done.wo_ref, bf16[4,256,128]{2,1,0:T(8,128)(2,1)} %get-tuple-element.252.refs_1_.refs_6_.refs_0_.refs_12_, ...), custom_call_target="tpu_custom_call" | custom-call | flops 5905580032 | bytes 5842048 | tf_op jit(solution)/shard_map/attend_back/pallas_call | solution.py:66
  410.5 9.0 %collective-permute-done.48.refs_20_.refs_9_ = bf16[128,2048]{1,0:T(8,128)(2,1)} collective-permute-done((bf16[128,2048]{1,0:T(8,128)(2,1)}, bf16[128,2048]{1,0:T(8,128)(2,1)}, u32[]{:S(2)}, u32[]{:S(2)}) %collective-permute-start.48) | collective-permute-done | bytes 524320 | tf_op jit(solution)/shard_map/ppermute | solution.py:630
  420.5 17.0 %attend_back.4 = (bf16[256,512]{1,0:T(8,128)(2,1)}, bf16[256,512]{1,0:T(8,128)(2,1)}, f32[256,128]{1,0:T(8,128)}, bf16[768,128]{1,0:T(8,128)(2,1)}, bf16[256,512...) custom-call(s32[4,8]{1,0:T(4,128)} %copy.45.order_ref, ...), custom_call_target="tpu_custom_call" | custom-call | flops 11811160064 | bytes 9586816 | tf_op jit(solution)/shard_map/attend_back/pallas_call | solution.py:66
  442.7 4.4 collective-permute-start.55
  447.1 9.9 %attend_back.5 = (bf16[256,512]{1,0:T(8,128)(2,1)}, bf16[256,512]{1,0:T(8,128)(2,1)}, f32[256,128]{1,0:T(8,128)}, bf16[768,128]{1,0:T(8,128)(2,1)}) custom-call(s32[4,8]{1,0:T(4,128)} %copy.45.order_ref, bf16[512,2048]{1,0:T(8,128)(2,1)} %all-gather.5.cloned.1.call-done.wo_ref, bf16[4,256,128]{2,1,0:T(8,128)(2,1)} %get-tuple-element.252.refs_1_.refs_6_.refs_0_.refs_12_, ...), custom_call_target="tpu_custom_call" | custom-call | flops 5905580032 | bytes 5842048 | tf_op jit(solution)/shard_map/attend_back/pallas_call | solution.py:66
  457.0 6.5 %collective-permute-done.56.refs_5_ = bf16[3,256,128]{2,1,0:T(8,128)(2,1)} collective-permute-done((bf16[3,256,128]{2,1,0:T(8,128)(2,1)}, bf16[3,256,128]{2,1,0:T(8,128)(2,1)}, u32[]{:S(2)}, u32[]{:S(2)}) %collective-permute-start.56) | collective-permute-done | bytes 196640 | tf_op jit(solution)/shard_map/ppermute | solution.py:634
  472.3 2.4 collective-permute-start.60
  474.7 2.9 fusion.4
  477.6 6.1 %out_gradient.1 = bf16[512,2048]{1,0:T(8,128)(2,1)} custom-call(bf16[512,256]{1,0:T(8,128)(2,1)} %get-tuple-element.318.refs_5_.refs_0_, bf16[512,256]{1,0:T(8,128)(2,1)} %get-tuple-element.329.refs_5_.refs_1_, bf16[512,256]{1,0:T(8,128)(2,1)} %get-tuple-element.333.refs_17_.refs_2_, bf16[512,256]{1,0:T(8,128)(2,1)} %get-tuple-element.350.refs_5_.refs_3_, ...), custom_call_target="tpu_custom_call" | custom-call | flops 2147483648 | bytes 7340032 | tf_op jit(solution)/shard_map/out_gradient/pallas_call | solution.py:66
  485.0 4.6 finish_keys.1
  489.7 7.5 %convolution_convert_fusion.1 = bf16[1024,2048]{1,0:T(8,128)(2,1)} fusion(bf16[1024,640]{1,0:T(8,128)(2,1)} %get-tuple-element.384, bf16[2048,640]{1,0:T(8,128)(2,1)} %all-gather.7.cloned.1.call-done.refs_8_), kind=kOutput, calls=%fused_computation.2 | convolution fusion | flops 2686451712 | bytes 8126464 | tf_op jit(solution)/shard_map/dot_general | solution.py:39
  497.2 3.8 collective-permute-done.63
  501.0 2.9 slice_bitcast_fusion
  503.9 4.5 weight_grad.6
  512.5 4.8 weight_grad.7
  517.3 6.2 %collective-permute-done.67 = bf16[128,2048]{1,0:T(8,128)(2,1)} collective-permute-done((bf16[128,2048]{1,0:T(8,128)(2,1)}, bf16[128,2048]{1,0:T(8,128)(2,1)}, u32[]{:S(2)}, u32[]{:S(2)}) %collective-permute-start.67) | collective-permute-done | bytes 524320 | tf_op jit(solution)/shard_map/ppermute | solution.py:630
  525.0 2.9 fusion.2
  532.2 3.9 finish_layer.1
  536.1 10.3 %collective-permute-done.70.refs_2_ = bf16[128,2048]{1,0:T(8,128)(2,1)} collective-permute-done((bf16[128,2048]{1,0:T(8,128)(2,1)}, bf16[128,2048]{1,0:T(8,128)(2,1)}, u32[]{:S(2)}, u32[]{:S(2)}) %collective-permute-start.70) | collective-permute-done | bytes 524320 | tf_op jit(solution)/shard_map/ppermute | solution.py:628
  546.4 5.7 finish_norm_back.3
  553.4 2.4 constant_dynamic-slice_fusion.1
  559.7 2.6 add_convert_fusion.1
  567.6 5.1 collective-permute-done.78
  577.4 4.5 merge_gate_up.1
  583.8 3.0 collective-permute-start.75
  592.2 5.1 collective-permute-done.80
  598.7 2.4 bitcast_add_fusion
  (321 shorter events, 147.8 us)
Async XLA Ops:
  7.2 34.3 %all-gather.5.cloned.1.call-start = ((), (), s32[]{:S(2)}) async-start(), calls=%async_computation.3 | async-start | bytes 2359296 | tf_op jit(solution)/shard_map/all_gather | solution.py:677
  7.9 71.6 %all-gather.7.cloned.1.call-start = ((), (), s32[]{:S(2)}) async-start(), calls=%async_computation.4 | async-start | bytes 2949120 | tf_op jit(solution)/shard_map/all_gather | solution.py:677
  41.5 177.9 %all-gather.11.cloned.1.call-start = ((), (), s32[]{:S(2)}) async-start(), calls=%async_computation.6 | async-start | bytes 12976128 | tf_op jit(solution)/shard_map/all_gather | solution.py:677
  42.3 19.0 %collective-permute-start.7 = (bf16[128,2048]{1,0:T(8,128)(2,1)}, bf16[128,2048]{1,0:T(8,128)(2,1)S(1)}, u32[]{:S(2)}, u32[]{:S(2)}) collective-permute-start(bf16[128,2048]{1,0:T(8,128)(2,1)} %get-tuple-element.244.refs_0_), channel_id=1, source_target_pairs={{0,16},{16,0},{1,17},{17,1},{2,18},{18,2},{3,19},{19,3},{4,20},{20... | collective-permute-start | bytes 1572872 | tf_op jit(solution)/shard_map/ppermute | solution.py:630
  43.8 17.4 %collective-permute-start.8 = (bf16[128,2048]{1,0:T(8,128)(2,1)}, bf16[128,2048]{1,0:T(8,128)(2,1)S(1)}, u32[]{:S(2)}, u32[]{:S(2)}) collective-permute-start(bf16[128,2048]{1,0:T(8,128)(2,1)} %get-tuple-element.245.refs_1_), channel_id=1, source_target_pairs={{0,8},{8,0},{1,9},{9,1},{2,10},{10,2},{3,11},{11,3},{4,12},{12,4},... | collective-permute-start | bytes 1572872 | tf_op jit(solution)/shard_map/ppermute | solution.py:628
  76.7 15.2 %collective-permute-start.16 = (bf16[1,64,2816]{2,1,0:T(8,128)(2,1)}, bf16[1,64,2816]{2,1,0:T(8,128)(2,1)S(1)}, u32[]{:S(2)}, u32[]{:S(2)}) collective-permute-start(bf16[1,64,2816]{2,1,0:T(8,128)(2,1)} %get-tuple-element.458), channel_id=1, source_target_pairs={{0,16},{16,0},{1,17},{17,1},{2,18},{18,2},{3,19},{19,3},{4,20},{20... | collective-permute-start | bytes 1081352 | tf_op jit(solution)/shard_map/ppermute | solution.py:630
  77.3 14.8 %collective-permute-start.15 = (bf16[1,64,2816]{2,1,0:T(8,128)(2,1)S(1)}, bf16[1,64,2816]{2,1,0:T(8,128)(2,1)}, u32[]{:S(2)}, u32[]{:S(2)}) collective-permute-start(bf16[1,64,2816]{2,1,0:T(8,128)(2,1)S(1)} %get-tuple-element.459), channel_id=1, source_target_pairs={{0,8},{8,0},{1,9},{9,1},{2,10},{10,2},{3,11},{11,3},{4,12},{12,4},... | collective-permute-start | bytes 1081352 | tf_op jit(solution)/shard_map/ppermute | solution.py:628
  88.6 20.2 %collective-permute-start.13 = (bf16[4,256,128]{2,1,0:T(8,128)(2,1)}, bf16[4,256,128]{2,1,0:T(8,128)(2,1)}, u32[]{:S(2)}, u32[]{:S(2)}) collective-permute-start(bf16[4,256,128]{2,1,0:T(8,128)(2,1)} %get-tuple-element.252.refs_1_.refs_6_.refs_0_.refs_12_), channel_id=1, source_target_pairs={{0,2},{1,3},{2,0},{3,1},{4,6},{5,7},{6,4},{7,5},{8,10},{9,11},{10,... | collective-permute-start | bytes 786440 | tf_op jit(solution)/shard_map/ppermute | solution.py:634
  89.6 19.2 %collective-permute-start.14 = (bf16[4,256,128]{2,1,0:T(8,128)(2,1)}, bf16[4,256,128]{2,1,0:T(8,128)(2,1)}, u32[]{:S(2)}, u32[]{:S(2)}) collective-permute-start(bf16[4,256,128]{2,1,0:T(8,128)(2,1)} %get-tuple-element.252.refs_1_.refs_6_.refs_0_.refs_12_), channel_id=1, source_target_pairs={{0,3},{1,2},{2,1},{3,0},{4,7},{5,6},{6,5},{7,4},{8,11},{9,10},{10,... | collective-permute-start | bytes 786440 | tf_op jit(solution)/shard_map/ppermute | solution.py:634
  92.7 16.1 %collective-permute-start.18 = (bf16[128,2048]{1,0:T(8,128)(2,1)S(1)}, bf16[128,2048]{1,0:T(8,128)(2,1)S(1)}, u32[]{:S(2)}, u32[]{:S(2)}) collective-permute-start(bf16[128,2048]{1,0:T(8,128)(2,1)S(1)} %get-tuple-element.464.refs_0_), channel_id=1, source_target_pairs={{0,8},{8,0},{1,9},{9,1},{2,10},{10,2},{3,11},{11,3},{4,12},{12,4},... | collective-permute-start | bytes 1572872 | tf_op jit(solution)/shard_map/ppermute | solution.py:628
  109.6 169.9 %all-gather.9.cloned.1.call-start = ((), (), s32[]{:S(2)}) async-start(), calls=%async_computation.5 | async-start | bytes 6488064 | tf_op jit(solution)/shard_map/all_gather | solution.py:677
  110.2 390.8 %reduce-scatter.4.cloned.1.call-start = ((), (), s32[]{:S(2)}) async-start(), calls=%async_computation.7 | async-start | bytes 7208960 | tf_op jit(solution)/shard_map/reduce_scatter | solution.py:713
  111.1 16.5 %collective-permute-start.22 = (bf16[128,2048]{1,0:T(8,128)(2,1)S(1)}, bf16[128,2048]{1,0:T(8,128)(2,1)S(1)}, u32[]{:S(2)}, u32[]{:S(2)}) collective-permute-start(bf16[128,2048]{1,0:T(8,128)(2,1)S(1)} %get-tuple-element.464.refs_0_), channel_id=1, source_target_pairs={{0,16},{16,0},{1,17},{17,1},{2,18},{18,2},{3,19},{19,3},{4,20},{20... | collective-permute-start | bytes 1572872 | tf_op jit(solution)/shard_map/ppermute | solution.py:630
  112.3 16.6 %collective-permute-start.23 = (bf16[128,2048]{1,0:T(8,128)(2,1)S(1)}, bf16[128,2048]{1,0:T(8,128)(2,1)S(1)}, u32[]{:S(2)}, u32[]{:S(2)}) collective-permute-start(bf16[128,2048]{1,0:T(8,128)(2,1)S(1)} %get-tuple-element.463.refs_1_), channel_id=1, source_target_pairs={{0,8},{8,0},{1,9},{9,1},{2,10},{10,2},{3,11},{11,3},{4,12},{12,4},... | collective-permute-start | bytes 1572872 | tf_op jit(solution)/shard_map/ppermute | solution.py:628
  124.8 19.6 %collective-permute-start.20 = (bf16[128,2048]{1,0:T(8,128)(2,1)}, bf16[128,2048]{1,0:T(8,128)(2,1)}, u32[]{:S(2)}, u32[]{:S(2)}) collective-permute-start(bf16[128,2048]{1,0:T(8,128)(2,1)} %get-tuple-element.462), channel_id=1, source_target_pairs={{0,16},{16,0},{1,17},{17,1},{2,18},{18,2},{3,19},{19,3},{4,20},{20... | collective-permute-start | bytes 1572872 | tf_op jit(solution)/shard_map/ppermute | solution.py:630
  125.7 18.7 %collective-permute-start.21 = (bf16[128,2048]{1,0:T(8,128)(2,1)}, bf16[128,2048]{1,0:T(8,128)(2,1)}, u32[]{:S(2)}, u32[]{:S(2)}) collective-permute-start(bf16[128,2048]{1,0:T(8,128)(2,1)} %get-tuple-element.461), channel_id=1, source_target_pairs={{0,8},{8,0},{1,9},{9,1},{2,10},{10,2},{3,11},{11,3},{4,12},{12,4},... | collective-permute-start | bytes 1572872 | tf_op jit(solution)/shard_map/ppermute | solution.py:628
  126.6 20.7 %collective-permute-start.24 = (bf16[128,2048]{1,0:T(8,128)(2,1)S(1)}, bf16[128,2048]{1,0:T(8,128)(2,1)}, u32[]{:S(2)}, u32[]{:S(2)}) collective-permute-start(bf16[128,2048]{1,0:T(8,128)(2,1)S(1)} %collective-permute-done.18.refs_2_), channel_id=1, source_target_pairs={{0,16},{16,0},{1,17},{17,1},{2,18},{18,2},{3,19},{19,3},{4,20},{20... | collective-permute-start | bytes 1572872 | tf_op jit(solution)/shard_map/ppermute | solution.py:630
  127.6 20.0 %collective-permute-start.25 = (bf16[128,2048]{1,0:T(8,128)(2,1)S(1)}, bf16[128,2048]{1,0:T(8,128)(2,1)S(1)}, u32[]{:S(2)}, u32[]{:S(2)}) collective-permute-start(bf16[128,2048]{1,0:T(8,128)(2,1)S(1)} %copy-done.17), channel_id=1, source_target_pairs={{0,8},{8,0},{1,9},{9,1},{2,10},{10,2},{3,11},{11,3},{4,12},{12,4},... | collective-permute-start | bytes 1572872 | tf_op jit(solution)/shard_map/ppermute | solution.py:628
  151.0 19.8 %collective-permute-start.29 = (bf16[128,2048]{1,0:T(8,128)(2,1)S(1)}, bf16[128,2048]{1,0:T(8,128)(2,1)S(1)}, u32[]{:S(2)}, u32[]{:S(2)}) collective-permute-start(bf16[128,2048]{1,0:T(8,128)(2,1)S(1)} %add_convert_fusion.2), channel_id=1, source_target_pairs={{0,16},{16,0},{1,17},{17,1},{2,18},{18,2},{3,19},{19,3},{4,20},{20... | collective-permute-start | bytes 1572872 | tf_op jit(solution)/shard_map/ppermute | solution.py:630
  154.5 16.4 %collective-permute-start.27 = (bf16[128,2048]{1,0:T(8,128)(2,1)S(1)}, bf16[128,2048]{1,0:T(8,128)(2,1)S(1)}, u32[]{:S(2)}, u32[]{:S(2)}) collective-permute-start(bf16[128,2048]{1,0:T(8,128)(2,1)S(1)} %add_convert_fusion.3), channel_id=1, source_target_pairs={{0,8},{8,0},{1,9},{9,1},{2,10},{10,2},{3,11},{11,3},{4,12},{12,4},... | collective-permute-start | bytes 1572872 | tf_op jit(solution)/shard_map/ppermute | solution.py:628
  155.2 16.9 %collective-permute-start.26 = (bf16[128,2048]{1,0:T(8,128)(2,1)}, bf16[128,2048]{1,0:T(8,128)(2,1)S(1)}, u32[]{:S(2)}, u32[]{:S(2)}) collective-permute-start(bf16[128,2048]{1,0:T(8,128)(2,1)} %slice.187), channel_id=1, source_target_pairs={{0,16},{16,0},{1,17},{17,1},{2,18},{18,2},{3,19},{19,3},{4,20},{20... | collective-permute-start | bytes 1572872 | tf_op jit(solution)/shard_map/ppermute | solution.py:630
  156.4 18.9 %collective-permute-start.28 = (bf16[128,2048]{1,0:T(8,128)(2,1)}, bf16[128,2048]{1,0:T(8,128)(2,1)S(1)}, u32[]{:S(2)}, u32[]{:S(2)}) collective-permute-start(bf16[128,2048]{1,0:T(8,128)(2,1)} %slice.189), channel_id=1, source_target_pairs={{0,8},{8,0},{1,9},{9,1},{2,10},{10,2},{3,11},{11,3},{4,12},{12,4},... | collective-permute-start | bytes 1572872 | tf_op jit(solution)/shard_map/ppermute | solution.py:628
  181.1 15.1 %collective-permute-start.30 = (bf16[128,2048]{1,0:T(8,128)(2,1)}, bf16[128,2048]{1,0:T(8,128)(2,1)S(1)}, u32[]{:S(2)}, u32[]{:S(2)}) collective-permute-start(bf16[128,2048]{1,0:T(8,128)(2,1)} %get-tuple-element.291.refs_0_), channel_id=1, source_target_pairs={{0,8},{8,0},{1,9},{9,1},{2,10},{10,2},{3,11},{11,3},{4,12},{12,4},... | collective-permute-start | bytes 1572872 | tf_op jit(solution)/shard_map/ppermute | solution.py:628
  181.6 15.1 %collective-permute-start.33 = (bf16[128,2048]{1,0:T(8,128)(2,1)}, bf16[128,2048]{1,0:T(8,128)(2,1)S(1)}, u32[]{:S(2)}, u32[]{:S(2)}) collective-permute-start(bf16[128,2048]{1,0:T(8,128)(2,1)} %get-tuple-element.292.refs_1_), channel_id=1, source_target_pairs={{0,16},{16,0},{1,17},{17,1},{2,18},{18,2},{3,19},{19,3},{4,20},{20... | collective-permute-start | bytes 1572872 | tf_op jit(solution)/shard_map/ppermute | solution.py:630
  183.1 23.9 %collective-permute-start.31 = (bf16[128,2048]{1,0:T(8,128)(2,1)}, bf16[128,2048]{1,0:T(8,128)(2,1)S(1)}, u32[]{:S(2)}, u32[]{:S(2)}) collective-permute-start(bf16[128,2048]{1,0:T(8,128)(2,1)} %get-tuple-element.292.refs_1_), channel_id=1, source_target_pairs={{0,8},{8,0},{1,9},{9,1},{2,10},{10,2},{3,11},{11,3},{4,12},{12,4},... | collective-permute-start | bytes 1572872 | tf_op jit(solution)/shard_map/ppermute | solution.py:628
  183.7 23.3 %collective-permute-start.32 = (bf16[128,2048]{1,0:T(8,128)(2,1)}, bf16[128,2048]{1,0:T(8,128)(2,1)S(1)}, u32[]{:S(2)}, u32[]{:S(2)}) collective-permute-start(bf16[128,2048]{1,0:T(8,128)(2,1)} %get-tuple-element.291.refs_0_), channel_id=1, source_target_pairs={{0,16},{16,0},{1,17},{17,1},{2,18},{18,2},{3,19},{19,3},{4,20},{20... | collective-permute-start | bytes 1572872 | tf_op jit(solution)/shard_map/ppermute | solution.py:630
  196.2 16.5 %collective-permute-start.34 = (bf16[128,2048]{1,0:T(8,128)(2,1)S(1)}, bf16[128,2048]{1,0:T(8,128)(2,1)S(1)}, u32[]{:S(2)}, u32[]{:S(2)}) collective-permute-start(bf16[128,2048]{1,0:T(8,128)(2,1)S(1)} %collective-permute-done.30.refs_2_), channel_id=1, source_target_pairs={{0,16},{16,0},{1,17},{17,1},{2,18},{18,2},{3,19},{19,3},{4,20},{20... | collective-permute-start | bytes 1572872 | tf_op jit(solution)/shard_map/ppermute | solution.py:630
  196.8 15.9 %collective-permute-start.35 = (bf16[128,2048]{1,0:T(8,128)(2,1)S(1)}, bf16[128,2048]{1,0:T(8,128)(2,1)S(1)}, u32[]{:S(2)}, u32[]{:S(2)}) collective-permute-start(bf16[128,2048]{1,0:T(8,128)(2,1)S(1)} %collective-permute-done.33.refs_5_), channel_id=1, source_target_pairs={{0,8},{8,0},{1,9},{9,1},{2,10},{10,2},{3,11},{11,3},{4,12},{12,4},... | collective-permute-start | bytes 1572872 | tf_op jit(solution)/shard_map/ppermute | solution.py:628
  279.6 25.4 %collective-permute-start.37 = (bf16[352,512]{1,0:T(8,128)(2,1)S(1)}, bf16[352,512]{1,0:T(8,128)(2,1)S(1)}, u32[]{:S(2)}, u32[]{:S(2)}) collective-permute-start(bf16[352,512]{1,0:T(8,128)(2,1)S(1)} %get-tuple-element.302), channel_id=1, source_target_pairs={{0,2},{1,3},{2,0},{3,1},{4,6},{5,7},{6,4},{7,5},{8,10},{9,11},{10,... | collective-permute-start | bytes 1081352 | tf_op jit(solution)/shard_map/ppermute | solution.py:634
  304.9 27.9 %collective-permute-start.40 = (bf16[1024,2816]{1,0:T(8,128)(2,1)}, bf16[1024,2816]{1,0:T(8,128)(2,1)}, u32[]{:S(2)}, u32[]{:S(2)}) collective-permute-start(bf16[1024,2816]{1,0:T(8,128)(2,1)} %weight_grad.4), channel_id=1, source_target_pairs={{0,4},{4,0},{1,5},{5,1},{2,6},{6,2},{3,7},{7,3},{8,12},{12,8},{9,1... | collective-permute-start | bytes 17301512 | tf_op jit(solution)/shard_map/ppermute | solution.py:703
  305.0 27.1 %collective-permute-start.38 = (bf16[352,512]{1,0:T(8,128)(2,1)}, bf16[352,512]{1,0:T(8,128)(2,1)S(1)}, u32[]{:S(2)}, u32[]{:S(2)}) collective-permute-start(bf16[352,512]{1,0:T(8,128)(2,1)} %get-tuple-element.305), channel_id=1, source_target_pairs={{0,2},{1,3},{2,0},{3,1},{4,6},{5,7},{6,4},{7,5},{8,10},{9,11},{10,... | collective-permute-start | bytes 1081352 | tf_op jit(solution)/shard_map/ppermute | solution.py:634
  306.9 38.8 %collective-permute-start.41 = (bf16[352,512]{1,0:T(8,128)(2,1)}, bf16[352,512]{1,0:T(8,128)(2,1)S(1)}, u32[]{:S(2)}, u32[]{:S(2)}) collective-permute-start(bf16[352,512]{1,0:T(8,128)(2,1)} %get-tuple-element.308), channel_id=1, source_target_pairs={{0,2},{1,3},{2,0},{3,1},{4,6},{5,7},{6,4},{7,5},{8,10},{9,11},{10,... | collective-permute-start | bytes 1081352 | tf_op jit(solution)/shard_map/ppermute | solution.py:634
  346.4 228.1 %reduce-scatter.6.cloned.1.call-start = ((), (), s32[]{:S(2)}) async-start(), calls=%async_computation.8 | async-start | bytes 1638400 | tf_op jit(solution)/shard_map/reduce_scatter | solution.py:713
  347.7 14.8 %collective-permute-start.42 = (bf16[128,2048]{1,0:T(8,128)(2,1)S(1)}, bf16[128,2048]{1,0:T(8,128)(2,1)S(1)}, u32[]{:S(2)}, u32[]{:S(2)}) collective-permute-start(bf16[128,2048]{1,0:T(8,128)(2,1)S(1)} %get-tuple-element.446), channel_id=1, source_target_pairs={{0,16},{16,0},{1,17},{17,1},{2,18},{18,2},{3,19},{19,3},{4,20},{20... | collective-permute-start | bytes 1572872 | tf_op jit(solution)/shard_map/ppermute | solution.py:630
  352.6 26.7 %collective-permute-start.39 = (bf16[128,2048]{1,0:T(8,128)(2,1)S(1)}, bf16[128,2048]{1,0:T(8,128)(2,1)S(1)}, u32[]{:S(2)}, u32[]{:S(2)}) collective-permute-start(bf16[128,2048]{1,0:T(8,128)(2,1)S(1)} %get-tuple-element.448), channel_id=1, source_target_pairs={{0,16},{16,0},{1,17},{17,1},{2,18},{18,2},{3,19},{19,3},{4,20},{20... | collective-permute-start | bytes 1572872 | tf_op jit(solution)/shard_map/ppermute | solution.py:630
  353.0 26.3 %collective-permute-start.44 = (bf16[128,2048]{1,0:T(8,128)(2,1)S(1)}, bf16[128,2048]{1,0:T(8,128)(2,1)S(1)}, u32[]{:S(2)}, u32[]{:S(2)}) collective-permute-start(bf16[128,2048]{1,0:T(8,128)(2,1)S(1)} %get-tuple-element.447), channel_id=1, source_target_pairs={{0,8},{8,0},{1,9},{9,1},{2,10},{10,2},{3,11},{11,3},{4,12},{12,4},... | collective-permute-start | bytes 1572872 | tf_op jit(solution)/shard_map/ppermute | solution.py:628
  365.9 19.7 %collective-permute-start.43 = (bf16[128,2048]{1,0:T(8,128)(2,1)S(1)}, bf16[128,2048]{1,0:T(8,128)(2,1)}, u32[]{:S(2)}, u32[]{:S(2)}) collective-permute-start(bf16[128,2048]{1,0:T(8,128)(2,1)S(1)} %get-tuple-element.444), channel_id=1, source_target_pairs={{0,8},{8,0},{1,9},{9,1},{2,10},{10,2},{3,11},{11,3},{4,12},{12,4},... | collective-permute-start | bytes 1572872 | tf_op jit(solution)/shard_map/ppermute | solution.py:628
  367.5 18.2 %collective-permute-start.46 = (bf16[128,2048]{1,0:T(8,128)(2,1)S(1)}, bf16[128,2048]{1,0:T(8,128)(2,1)}, u32[]{:S(2)}, u32[]{:S(2)}) collective-permute-start(bf16[128,2048]{1,0:T(8,128)(2,1)S(1)} %get-tuple-element.443), channel_id=1, source_target_pairs={{0,16},{16,0},{1,17},{17,1},{2,18},{18,2},{3,19},{19,3},{4,20},{20... | collective-permute-start | bytes 1572872 | tf_op jit(solution)/shard_map/ppermute | solution.py:630
  391.7 16.3 %collective-permute-start.47 = (bf16[128,2048]{1,0:T(8,128)(2,1)}, bf16[128,2048]{1,0:T(8,128)(2,1)S(1)}, u32[]{:S(2)}, u32[]{:S(2)}) collective-permute-start(bf16[128,2048]{1,0:T(8,128)(2,1)} %get-tuple-element.366.refs_7_.refs_4_), channel_id=1, source_target_pairs={{0,8},{8,0},{1,9},{9,1},{2,10},{10,2},{3,11},{11,3},{4,12},{12,4},... | collective-permute-start | bytes 1572872 | tf_op jit(solution)/shard_map/ppermute | solution.py:628
  393.1 26.4 %collective-permute-start.49 = (bf16[128,2048]{1,0:T(8,128)(2,1)}, bf16[128,2048]{1,0:T(8,128)(2,1)}, u32[]{:S(2)}, u32[]{:S(2)}) collective-permute-start(bf16[128,2048]{1,0:T(8,128)(2,1)} %get-tuple-element.366.refs_7_.refs_4_), channel_id=1, source_target_pairs={{0,16},{16,0},{1,17},{17,1},{2,18},{18,2},{3,19},{19,3},{4,20},{20... | collective-permute-start | bytes 1572872 | tf_op jit(solution)/shard_map/ppermute | solution.py:630
  393.7 25.8 %collective-permute-start.48 = (bf16[128,2048]{1,0:T(8,128)(2,1)}, bf16[128,2048]{1,0:T(8,128)(2,1)}, u32[]{:S(2)}, u32[]{:S(2)}) collective-permute-start(bf16[128,2048]{1,0:T(8,128)(2,1)} %get-tuple-element.367.refs_8_.refs_5_), channel_id=1, source_target_pairs={{0,16},{16,0},{1,17},{17,1},{2,18},{18,2},{3,19},{19,3},{4,20},{20... | collective-permute-start | bytes 1572872 | tf_op jit(solution)/shard_map/ppermute | solution.py:630
  395.1 24.4 %collective-permute-start.50 = (bf16[128,2048]{1,0:T(8,128)(2,1)}, bf16[128,2048]{1,0:T(8,128)(2,1)}, u32[]{:S(2)}, u32[]{:S(2)}) collective-permute-start(bf16[128,2048]{1,0:T(8,128)(2,1)} %get-tuple-element.367.refs_8_.refs_5_), channel_id=1, source_target_pairs={{0,8},{8,0},{1,9},{9,1},{2,10},{10,2},{3,11},{11,3},{4,12},{12,4},... | collective-permute-start | bytes 1572872 | tf_op jit(solution)/shard_map/ppermute | solution.py:628
  398.0 40.4 %collective-permute-start.53 = (bf16[128,2048]{1,0:T(8,128)(2,1)}, bf16[128,2048]{1,0:T(8,128)(2,1)S(1)}, u32[]{:S(2)}, u32[]{:S(2)}) collective-permute-start(bf16[128,2048]{1,0:T(8,128)(2,1)} %get-tuple-element.442), channel_id=1, source_target_pairs={{0,16},{16,0},{1,17},{17,1},{2,18},{18,2},{3,19},{19,3},{4,20},{20... | collective-permute-start | bytes 1572872 | tf_op jit(solution)/shard_map/ppermute | solution.py:630
  408.8 29.6 %collective-permute-start.54 = (bf16[128,2048]{1,0:T(8,128)(2,1)}, bf16[128,2048]{1,0:T(8,128)(2,1)S(1)}, u32[]{:S(2)}, u32[]{:S(2)}) collective-permute-start(bf16[128,2048]{1,0:T(8,128)(2,1)} %get-tuple-element.441), channel_id=1, source_target_pairs={{0,8},{8,0},{1,9},{9,1},{2,10},{10,2},{3,11},{11,3},{4,12},{12,4},... | collective-permute-start | bytes 1572872 | tf_op jit(solution)/shard_map/ppermute | solution.py:628
  419.5 20.0 %collective-permute-start.51 = (bf16[128,2048]{1,0:T(8,128)(2,1)}, bf16[128,2048]{1,0:T(8,128)(2,1)}, u32[]{:S(2)}, u32[]{:S(2)}) collective-permute-start(bf16[128,2048]{1,0:T(8,128)(2,1)} %copy-done.49), channel_id=1, source_target_pairs={{0,16},{16,0},{1,17},{17,1},{2,18},{18,2},{3,19},{19,3},{4,20},{20... | collective-permute-start | bytes 1572872 | tf_op jit(solution)/shard_map/ppermute | solution.py:630
  420.1 19.4 %collective-permute-start.52 = (bf16[128,2048]{1,0:T(8,128)(2,1)}, bf16[128,2048]{1,0:T(8,128)(2,1)}, u32[]{:S(2)}, u32[]{:S(2)}) collective-permute-start(bf16[128,2048]{1,0:T(8,128)(2,1)} %collective-permute-done.48.refs_20_.refs_9_), channel_id=1, source_target_pairs={{0,8},{8,0},{1,9},{9,1},{2,10},{10,2},{3,11},{11,3},{4,12},{12,4},... | collective-permute-start | bytes 1572872 | tf_op jit(solution)/shard_map/ppermute | solution.py:628
  441.3 15.7 %collective-permute-start.57 = (bf16[3,256,128]{2,1,0:T(8,128)(2,1)}, bf16[3,256,128]{2,1,0:T(8,128)(2,1)}, u32[]{:S(2)}, u32[]{:S(2)}) collective-permute-start(bf16[3,256,128]{2,1,0:T(8,128)(2,1)} %pad_maximum_fusion.2), channel_id=1, source_target_pairs={{0,3},{1,2},{2,1},{3,0},{4,7},{5,6},{6,5},{7,4},{8,11},{9,10},{10,... | collective-permute-start | bytes 589832 | tf_op jit(solution)/shard_map/ppermute | solution.py:634
  442.0 21.6 %collective-permute-start.56 = (bf16[3,256,128]{2,1,0:T(8,128)(2,1)}, bf16[3,256,128]{2,1,0:T(8,128)(2,1)}, u32[]{:S(2)}, u32[]{:S(2)}) collective-permute-start(bf16[3,256,128]{2,1,0:T(8,128)(2,1)} %pad_maximum_fusion.1), channel_id=1, source_target_pairs={{0,2},{1,3},{2,0},{3,1},{4,6},{5,7},{6,4},{7,5},{8,10},{9,11},{10,... | collective-permute-start | bytes 589832 | tf_op jit(solution)/shard_map/ppermute | solution.py:634
  442.7 20.9 %collective-permute-start.55 = (bf16[3,256,128]{2,1,0:T(8,128)(2,1)}, bf16[3,256,128]{2,1,0:T(8,128)(2,1)}, u32[]{:S(2)}, u32[]{:S(2)}) collective-permute-start(bf16[3,256,128]{2,1,0:T(8,128)(2,1)} %pad_maximum_fusion), channel_id=1, source_target_pairs={{0,1},{1,0},{2,3},{3,2},{4,5},{5,4},{6,7},{7,6},{8,9},{9,8},{10,11... | collective-permute-start | bytes 589832 | tf_op jit(solution)/shard_map/ppermute | solution.py:634
  465.8 19.1 %collective-permute-start.61 = (bf16[128,2048]{1,0:T(8,128)(2,1)}, bf16[128,2048]{1,0:T(8,128)(2,1)S(1)}, u32[]{:S(2)}, u32[]{:S(2)}) collective-permute-start(bf16[128,2048]{1,0:T(8,128)(2,1)} %get-tuple-element.440), channel_id=1, source_target_pairs={{0,16},{16,0},{1,17},{17,1},{2,18},{18,2},{3,19},{19,3},{4,20},{20... | collective-permute-start | bytes 1572872 | tf_op jit(solution)/shard_map/ppermute | solution.py:630
  467.3 17.7 %collective-permute-start.62 = (bf16[128,2048]{1,0:T(8,128)(2,1)}, bf16[128,2048]{1,0:T(8,128)(2,1)S(1)}, u32[]{:S(2)}, u32[]{:S(2)}) collective-permute-start(bf16[128,2048]{1,0:T(8,128)(2,1)} %get-tuple-element.439), channel_id=1, source_target_pairs={{0,8},{8,0},{1,9},{9,1},{2,10},{10,2},{3,11},{11,3},{4,12},{12,4},... | collective-permute-start | bytes 1572872 | tf_op jit(solution)/shard_map/ppermute | solution.py:628
  483.8 17.2 %collective-permute-start.64 = (bf16[128,2048]{1,0:T(8,128)(2,1)}, bf16[128,2048]{1,0:T(8,128)(2,1)}, u32[]{:S(2)}, u32[]{:S(2)}) collective-permute-start(bf16[128,2048]{1,0:T(8,128)(2,1)} %get-tuple-element.438), channel_id=1, source_target_pairs={{0,8},{8,0},{1,9},{9,1},{2,10},{10,2},{3,11},{11,3},{4,12},{12,4},... | collective-permute-start | bytes 1572872 | tf_op jit(solution)/shard_map/ppermute | solution.py:628
  484.4 16.6 %collective-permute-start.65 = (bf16[128,2048]{1,0:T(8,128)(2,1)}, bf16[128,2048]{1,0:T(8,128)(2,1)}, u32[]{:S(2)}, u32[]{:S(2)}) collective-permute-start(bf16[128,2048]{1,0:T(8,128)(2,1)} %get-tuple-element.437), channel_id=1, source_target_pairs={{0,16},{16,0},{1,17},{17,1},{2,18},{18,2},{3,19},{19,3},{4,20},{20... | collective-permute-start | bytes 1572872 | tf_op jit(solution)/shard_map/ppermute | solution.py:630
  484.9 16.0 %collective-permute-start.63 = (bf16[352,512]{1,0:T(8,128)(2,1)}, bf16[352,512]{1,0:T(8,128)(2,1)}, u32[]{:S(2)}, u32[]{:S(2)}) collective-permute-start(bf16[352,512]{1,0:T(8,128)(2,1)} %get-tuple-element.385), channel_id=1, source_target_pairs={{0,2},{1,3},{2,0},{3,1},{4,6},{5,7},{6,4},{7,5},{8,10},{9,11},{10,... | collective-permute-start | bytes 1081352 | tf_op jit(solution)/shard_map/ppermute | solution.py:634
  508.5 15.0 %collective-permute-start.67 = (bf16[128,2048]{1,0:T(8,128)(2,1)}, bf16[128,2048]{1,0:T(8,128)(2,1)}, u32[]{:S(2)}, u32[]{:S(2)}) collective-permute-start(bf16[128,2048]{1,0:T(8,128)(2,1)} %get-tuple-element.391), channel_id=1, source_target_pairs={{0,16},{16,0},{1,17},{17,1},{2,18},{18,2},{3,19},{19,3},{4,20},{20... | collective-permute-start | bytes 1572872 | tf_op jit(solution)/shard_map/ppermute | solution.py:630
  509.6 15.1 %collective-permute-start.68 = (bf16[128,2048]{1,0:T(8,128)(2,1)}, bf16[128,2048]{1,0:T(8,128)(2,1)}, u32[]{:S(2)}, u32[]{:S(2)}) collective-permute-start(bf16[128,2048]{1,0:T(8,128)(2,1)} %get-tuple-element.392), channel_id=1, source_target_pairs={{0,8},{8,0},{1,9},{9,1},{2,10},{10,2},{3,11},{11,3},{4,12},{12,4},... | collective-permute-start | bytes 1572872 | tf_op jit(solution)/shard_map/ppermute | solution.py:628
  510.8 25.3 %collective-permute-start.66 = (bf16[128,2048]{1,0:T(8,128)(2,1)}, bf16[128,2048]{1,0:T(8,128)(2,1)S(1)}, u32[]{:S(2)}, u32[]{:S(2)}) collective-permute-start(bf16[128,2048]{1,0:T(8,128)(2,1)} %get-tuple-element.436), channel_id=1, source_target_pairs={{0,16},{16,0},{1,17},{17,1},{2,18},{18,2},{3,19},{19,3},{4,20},{20... | collective-permute-start | bytes 1572872 | tf_op jit(solution)/shard_map/ppermute | solution.py:630
  511.6 24.5 %collective-permute-start.71 = (bf16[128,2048]{1,0:T(8,128)(2,1)}, bf16[128,2048]{1,0:T(8,128)(2,1)}, u32[]{:S(2)}, u32[]{:S(2)}) collective-permute-start(bf16[128,2048]{1,0:T(8,128)(2,1)} %get-tuple-element.433), channel_id=1, source_target_pairs={{0,8},{8,0},{1,9},{9,1},{2,10},{10,2},{3,11},{11,3},{4,12},{12,4},... | collective-permute-start | bytes 1572872 | tf_op jit(solution)/shard_map/ppermute | solution.py:628
  524.7 76.3 %reduce-scatter.8.cloned.1.call-start = ((), (), s32[]{:S(2)}) async-start(), calls=%async_computation.9 | async-start | bytes 1310720 | tf_op jit(solution)/shard_map/reduce_scatter | solution.py:713
  527.9 18.5 %collective-permute-start.70 = (bf16[128,2048]{1,0:T(8,128)(2,1)}, bf16[128,2048]{1,0:T(8,128)(2,1)}, u32[]{:S(2)}, u32[]{:S(2)}) collective-permute-start(bf16[128,2048]{1,0:T(8,128)(2,1)} %get-tuple-element.432), channel_id=1, source_target_pairs={{0,8},{8,0},{1,9},{9,1},{2,10},{10,2},{3,11},{11,3},{4,12},{12,4},... | collective-permute-start | bytes 1572872 | tf_op jit(solution)/shard_map/ppermute | solution.py:628
  529.1 17.3 %collective-permute-start.72 = (bf16[128,2048]{1,0:T(8,128)(2,1)}, bf16[128,2048]{1,0:T(8,128)(2,1)}, u32[]{:S(2)}, u32[]{:S(2)}) collective-permute-start(bf16[128,2048]{1,0:T(8,128)(2,1)} %get-tuple-element.431), channel_id=1, source_target_pairs={{0,16},{16,0},{1,17},{17,1},{2,18},{18,2},{3,19},{19,3},{4,20},{20... | collective-permute-start | bytes 1572872 | tf_op jit(solution)/shard_map/ppermute | solution.py:630
  532.2 27.3 %collective-permute-start.76 = (bf16[256,2048]{1,0:T(8,128)(2,1)}, bf16[256,2048]{1,0:T(8,128)(2,1)}, u32[]{:S(2)}, u32[]{:S(2)}) collective-permute-start(bf16[256,2048]{1,0:T(8,128)(2,1)} %constant_dynamic-slice_fusion.4), channel_id=1, source_target_pairs={{0,4},{4,0},{1,5},{5,1},{2,6},{6,2},{3,7},{7,3},{8,12},{12,8},{9,1... | collective-permute-start | bytes 3145736 | tf_op jit(solution)/shard_map/ppermute | solution.py:686
  557.0 15.7 %collective-permute-start.78 = (bf16[1,64,2816]{2,1,0:T(8,128)(2,1)S(1)}, bf16[1,64,2816]{2,1,0:T(8,128)(2,1)}, u32[]{:S(2)}, u32[]{:S(2)}) collective-permute-start(bf16[1,64,2816]{2,1,0:T(8,128)(2,1)S(1)} %get-tuple-element.450), channel_id=1, source_target_pairs={{0,16},{16,0},{1,17},{17,1},{2,18},{18,2},{3,19},{19,3},{4,20},{20... | collective-permute-start | bytes 1081352 | tf_op jit(solution)/shard_map/ppermute | solution.py:630
  563.2 34.1 %collective-permute-start.80 = (bf16[176,2048]{1,0:T(8,128)(2,1)}, bf16[176,2048]{1,0:T(8,128)(2,1)}, u32[]{:S(2)}, u32[]{:S(2)}) collective-permute-start(bf16[176,2048]{1,0:T(8,128)(2,1)} %fusion.8), channel_id=1, source_target_pairs={{0,1},{1,0},{2,3},{3,2},{4,5},{5,4},{6,7},{7,6},{8,9},{9,8},{10,11... | collective-permute-start | bytes 2162696 | tf_op jit(solution)/shard_map/ppermute | solution.py:634
  (75 other events, 851.9 us)
Sparse Core Ops, SparseCore 0:
  9.6 31.7 all-gather.4
  43.1 33.3 all-gather.6
  109.8 109.5 all-gather.10
  220.8 58.7 all-gather.8
  345.8 103.1 reduce-scatter.3
  524.8 29.9 reduce-scatter.5
  562.4 35.5 reduce-scatter.7

commit v5 on v4

--- a/solution.py
+++ b/solution.py
@@ -247,23 +247,24 @@
     return [results[4 * i : 4 * i + 4] for i in range(count)]
 
 
-def out_gradient(mixed, grads):
-    n, rows = mixed[0].shape
-    width = grads[0].shape[1]
-
-    def kernel(*refs):
-        total = 0.0
+def out_gradient(mixed, grads, parts, index, come=None):
+    n, width = mixed[0].shape[0] // parts, grads[0].shape[1]
+
+    def kernel(index_ref, *refs):
+        at = pl.ds(pl.multiple_of(index_ref[0] * n, n), n)
+        total = 0.0 if come is None else refs[3 * TP][...].astype(f32)
         for k in range(TP):
             db = jnp.concatenate([refs[TP + 2 * k][...], refs[TP + 2 * k + 1][...]], axis=0)
-            total = total + nn(refs[k][...], db)
+            total = total + nn(refs[k][at, :], db)
         refs[-1][...] = total.astype(bf16)
 
     return small_call(
         kernel,
         "out_gradient",
-        [*mixed, *grads],
+        [index[None], *mixed, *grads] + ([] if come is None else [come]),
         [like((n, width), bf16)],
-        flops=2 * TP * rows * n * width,
+        flops=2 * TP * mixed[0].shape[1] * n * width,
+        scalars=1,
     )[0]
 
 
@@ -542,31 +543,38 @@
     )[0]
 
 
-def merge_qkv(raw, w_query, w_key, w_value, gain):
+def merge_qkv(t, pieces, w_query, w_key, w_value, gain):
     own, n = w_query.shape[0], GROUP * HD
 
-    def kernel(in_ref, q_ref, k_ref, v_ref, gain_ref, dq_ref, dk_ref, dv_ref, dgain_ref):
-        keys, values = [], []
+    def kernel(t_ref, *refs):
+        in_refs, (q_ref, k_ref, v_ref, gain_ref, dq_ref, dk_ref, dv_ref, dgain_ref) = (
+            refs[:TP],
+            refs[TP:],
+        )
+        slot = lax.broadcasted_iota(jnp.int32, (own, TP * HD), 1) // HD
         dgain = jnp.zeros((own, 1), f32)
-        for g in range(TP):
-            here = slice(g * n, (g + 1) * n)
-            part = in_ref[g, :, :n].astype(f32)
+        keys, values = 0.0, 0.0
+        for k, ref in enumerate(in_refs):
+            group = t_ref[0] ^ k
+            here = pl.ds(pl.multiple_of(group * n, n), n)
+            part = ref[:, :n].astype(f32)
             dgain += jnp.sum(part * q_ref[:, here].astype(f32), axis=1, keepdims=True)
             dq_ref[:, here] = part * gain_ref[...]
-            part = in_ref[g, :, n:].astype(f32)
-            keys.append(part[:, :HD])
-            values.append(part[:, HD:])
-        for parts, ref, out_ref in ((keys, k_ref, dk_ref), (values, v_ref, dv_ref)):
-            part = jnp.concatenate(parts, axis=1)
+            part = ref[:, n:].astype(f32)
+            mine = slot == group
+            keys += jnp.where(mine, jnp.concatenate([part[:, :HD]] * TP, axis=1), 0.0)
+            values += jnp.where(mine, jnp.concatenate([part[:, HD:]] * TP, axis=1), 0.0)
+        for part, ref, out_ref in ((keys, k_ref, dk_ref), (values, v_ref, dv_ref)):
             dgain += jnp.sum(part * ref[...].astype(f32), axis=1, keepdims=True)
             out_ref[...] = part * gain_ref[...]
-        dgain_ref[...] = dgain
+        dgain_ref[...] = dgain.T
 
     return small_call(
         kernel,
         "merge_qkv",
-        [raw, w_query, w_key, w_value, gain],
-        [like(w.shape, f32) for w in (w_query, w_key, w_value)] + [like((own, 1), f32)],
+        [t[None], *pieces, w_query, w_key, w_value, gain],
+        [like(w.shape, f32) for w in (w_query, w_key, w_value)] + [like((1, own), f32)],
+        scalars=1,
     )
 
 
@@ -589,32 +597,31 @@
     )[0]
 
 
-def merge_gate_up(raw, w_gate, w_up, gain):
+def merge_gate_up(t, pieces, w_gate, w_up, gain):
     own, total = w_gate.shape
     ff = total // TP
 
-    def kernel(in_ref, gate_ref, up_ref, gain_ref, dgate_ref, dup_ref, dgain_ref):
+    def kernel(t_ref, *refs):
+        in_refs, (gate_ref, up_ref, gain_ref, dgate_ref, dup_ref, dgain_ref) = refs[:TP], refs[TP:]
         dgain = jnp.zeros((own, LANES), f32)
-        for g in range(TP):
+        for k, in_ref in enumerate(in_refs):
+            base = (t_ref[0] ^ k) * ff
             for j in range(ff // LANES):
-                here = slice(g * ff + j * LANES, g * ff + (j + 1) * LANES)
+                here = pl.ds(pl.multiple_of(base + j * LANES, LANES), LANES)
                 for ref, out_ref, at in zip(
                     (gate_ref, up_ref), (dgate_ref, dup_ref), interleaved(j)
                 ):
-                    part = in_ref[g, :, at].astype(f32)
+                    part = in_ref[:, at].astype(f32)
                     dgain += part * ref[:, here].astype(f32)
                     out_ref[:, here] = part * gain_ref[...]
-        dgain_ref[...] = jnp.sum(dgain, axis=1, keepdims=True)
+        dgain_ref[...] = jnp.sum(dgain, axis=1, keepdims=True).T
 
     return small_call(
         kernel,
         "merge_gate_up",
-        [raw, w_gate, w_up, gain],
-        [
-            jax.ShapeDtypeStruct((own, total), f32),
-            jax.ShapeDtypeStruct((own, total), f32),
-            jax.ShapeDtypeStruct((own, 1), f32),
-        ],
+        [t[None], *pieces, w_gate, w_up, gain],
+        [like((own, total), f32), like((own, total), f32), like((1, own), f32)],
+        scalars=1,
     )
 
 
@@ -670,21 +677,12 @@
     def spread(blocks, t, *first):
         return exchange(blocks, t, *first).reshape(-1, blocks.shape[2])
 
-    def collect(summed_rows, t, *first):
-        return exchange(summed_rows.reshape(TP, -1, summed_rows.shape[1]), t, *first)
+    def collect(summed_rows, t):
+        blocks = summed_rows.reshape(TP, -1, summed_rows.shape[1])
+        return [swap(lax.dynamic_index_in_dim(blocks, t ^ k, 0, False), k) for k in range(TP)]
 
     def whole(v):
         return lax.all_gather(v, ("rep", "ctx"), axis=0, tiled=True)
-
-    def split_reps(full):
-        if reps != 2:
-            return lax.psum_scatter(full, "rep", scatter_dimension=0, tiled=True)
-        r = lax.axis_index("rep")
-        half = full.shape[0] // 2
-        sent = lax.dynamic_slice_in_dim(full, (1 - r) * half, half, 0)
-        mine = lax.dynamic_slice_in_dim(full, r * half, half, 0)
-        sent = lax.ppermute(sent, "rep", pair)
-        return (mine.astype(f32) + sent.astype(f32)).astype(bf16)
 
     def over_reps_first(left, right):
         if reps != 2:
@@ -740,15 +738,16 @@
         gain_attn = norm_attn.astype(f32)[:, None]
         gain_mlp = norm_mlp.astype(f32)[:, None]
 
-        out = whole(w_out)
         qkv_blocks = split_qkv(w_query, w_key, w_value, gain_attn)
         a, b = hold_tokens(after(tokens, qkv_blocks), held)
         qkv_mine, a, b = phase(spread(after(qkv_blocks, a), t), a, b)
+        qkv = whole(qkv_mine)
+        out = whole(after(w_out, qkv_mine))
         ax, by = swap(a, 1), swap(b, 2)
+        ax, by, a, b = phase(ax, by, a, b)
+        gate_up_blocks = split_gate_up(after(w_gate, ax), w_up, gain_mlp)
+        orders = [swap(after(span_order, qkv_mine), k) for k in range(TP)]
         ay, bx, axy, bxy = swap(a, 2), swap(b, 1), swap(ax, 2), swap(by, 1)
-        qkv = whole(after(qkv_mine, out, ax, by))
-        gate_up_blocks = split_gate_up(after(w_gate, qkv_mine), w_up, gain_mlp)
-        orders = [swap(after(span_order, qkv_mine), k) for k in range(TP)]
         ay, bx, axy, bxy, gate_up_blocks = phase(ay, bx, axy, bxy, gate_up_blocks)
         x_pieces = in_order((a, ax, ay, axy), (b, bx, by, bxy))
 
@@ -817,10 +816,10 @@
         sent, down_come[-1] = phase(sent, send_down(down))
         parts = by_member(nt(after(grad_act, sent), gate_up).astype(bf16))
         parts, down_come[-1] = phase(parts, send_down(grad_act))
+        far = scatter_far(parts)
         part_gate_up = over_reps_last(n2_all, after(grad_act, parts), sent)
-        part_gate_up, down_come[-1] = phase(part_gate_up, send_down(sent))
+        far, part_gate_up, down_come[-1] = phase(far, part_gate_up, send_down(sent))
         sum_gate_up = owned(part_gate_up)
-        far = scatter_far(after(parts, part_gate_up))
         near = scatter_near(parts, far)
         forward = nn(after(act, far), down).astype(bf16)
         near, forward = phase(near, forward)
@@ -856,13 +855,23 @@
             swap_ctx(jnp.stack([back_of[k][3][(j - 1) * count : j * count] for k in range(3)]), j)
             for j in range(1, ctxs)
         ]
+        db_pieces = in_order((a, ax, ay, axy), (b, bx, by, bxy))
+        r = lax.axis_index("rep")
+        if reps == 2:
+            part_out = out_gradient(mixed, db_pieces, 2, 1 - r)
+            part_out, axy, bxy = phase(part_out, axy, bxy)
+            part_out = lax.ppermute(part_out, "rep", pair)
         attend_back_to((3,), (axy, bxy))
         keys_near, back_of[3] = phase(keys_near, back_of[3])
         keys_last = [
             swap_ctx(back_of[3][3][None, (j - 1) * count : j * count], j) for j in range(1, ctxs)
         ]
-        db_pieces = in_order((a, ax, ay, axy), (b, bx, by, bxy))
-        part_out = out_gradient(mixed, after(db_pieces, back_of[3]))
+        db_pieces = after(db_pieces, back_of[3])
+        if reps == 2:
+            part_out = out_gradient(mixed, db_pieces, 2, r, part_out)
+        else:
+            part_out = out_gradient(mixed, db_pieces, 1, jnp.zeros((), jnp.int32))
+            part_out = lax.psum_scatter(part_out, "rep", scatter_dimension=0, tiled=True)
         forward_near = scatter_near(after(forward, keys_near), far)
         keys_last, part_out, forward_near[0], forward_near[2] = phase(
             keys_last, part_out, forward_near[0], forward_near[2]
@@ -885,25 +894,25 @@
         far_back = swap(across[0], 2), swap(across[1], 1)
         sent = over_reps_first(x_all, after(scaled_proj, across))
         part_qkv = over_reps_last(x_all, after(scaled_proj, sent), sent)
-        far_back, part_qkv = phase(far_back, part_qkv)
+        sum_out = owned(after(part_out, across))
+        far_back, part_qkv, sum_out = phase(far_back, part_qkv, sum_out)
         sum_qkv = owned(part_qkv)
         near = scatter_near(parts, far_back)
         layer_out = finish_layer(after(middle, far_back), [(forward, 0), *forward_near])
-        sum_out = owned(split_reps(after(part_out, far_back)))
-        near, layer_out = phase(near, layer_out)
+        raw_gate_up = collect(after(sum_gate_up, far_back), t)
+        part_down = half_of(after(part_down, far_back), ctxs // 2, False).astype(f32)
+        part_down = part_down + jnp.concatenate(down_come, axis=1).astype(f32)
+        near, layer_out, part_down = phase(near, layer_out, part_down)
         (input_grad,) = finish_norm_back(
             grad_middle, tokens, inverse[0], [(parts, 0), *near], natural, True
         )
-        raw_gate_up = collect(after(sum_gate_up, near), t)
         grad_gate, grad_up, grad_norm_mlp = merge_gate_up(
-            after(raw_gate_up, input_grad), w_gate, w_up, gain_mlp
-        )
-        sum_qkv = after(sum_qkv, near)
+            t, after(raw_gate_up, near), w_gate, w_up, gain_mlp
+        )
+        sum_qkv = after(sum_qkv, input_grad)
         grad_query, grad_key, grad_value, grad_norm_attn = merge_qkv(
-            collect(sum_qkv, t), w_query, w_key, w_value, gain_attn
-        )
-        part_down = half_of(after(part_down, input_grad), ctxs // 2, False).astype(f32)
-        part_down = part_down + jnp.concatenate(down_come, axis=1).astype(f32)
+            t, collect(sum_qkv, t), w_query, w_key, w_value, gain_attn
+        )
         down_come = swap_ctx(
             half_of(part_down.astype(bf16), ctxs // 4, True), ctxs // 4
         )
@@ -912,12 +921,12 @@
         return (
             layer_out,
             input_grad,
-            grad_norm_attn[:, 0],
+            grad_norm_attn[0],
             grad_query,
             grad_key,
             grad_value,
             after(sum_out, grad_query).astype(f32),
-            grad_norm_mlp[:, 0],
+            grad_norm_mlp[0],
             grad_gate,
             grad_up,
             sum_down,

time: 618 us -> 599 us (0.969)
  waiting for transfers between devices: 182 us -> 165 us
  starting transfers between devices: 86.8 us -> 95.3 us
  other arithmetic: 25.1 us -> 17.2 us
    ppermute x29, waiting for transfers between devices: 61.3 us -> 35.6 us  [swap(): return lax.ppermute(v, 'tx', pair)]
    all_gather x4, waiting for transfers between devices: 31.3 us -> 16.5 us  [whole(): return lax.all_gather(v, ('rep', 'ctx'), axis=0, tiled=True)]
    ppermute x29, waiting for transfers between devices: 56.2 us -> 66.5 us  [swap(): return lax.ppermute(v, 'ty', pair)]
    unnamed x103 -> x141, local copies, waits for them, and re-layouts: 6.26 us -> 14 us
    reduce_scatter x3, waiting for transfers between devices: 0.02 us -> 6.85 us  [owned(): return lax.psum_scatter(part, 'ctx', scatter_dimension=0, tiled=True)]
    ppermute x14, starting transfers between devices: 17.3 us -> 23.9 us  [swap_ctx(): return lax.ppermute(v, 'ctx', [(i, i ^ j) for i in range(ctxs)]) if j else v]
    dynamic_update_slice x13 -> x7, local copies, waits for them, and re-layouts: 7.41 us -> 1.23 us  [exchange(): out = lax.dynamic_update_slice_in_dim(out, come, t ^ k, 0)]
    pallas_call x21 -> x22, Pallas kernels: 136 us -> 141 us  [small_call(): pl.pallas_call(kernel, grid=(1,), in_specs=specs, out_specs=[whole_block(...]
  transfers between devices with their start and end apart: 88 -> 88, of which waited for: 38 -> 32; matrix products, arithmetic and copies ran while one was open for 18% -> 15% of each run, Pallas kernels for 32% -> 34%
where the time goes in v5:
time: 599 us; the launch traced here: 592 us
  Pallas kernels  208 us (35%)
  waiting for transfers between devices  165 us (28%)
  starting transfers between devices  95.3 us (16%)
  matrix products  48.9 us (8%)
  local copies, waits for them, and re-layouts  42.7 us (7%)
  other arithmetic  17.2 us (3%)
  between operations  15.5 us (3%)
    pallas_call x22, Pallas kernels, small_call(): pl.pallas_call(kernel, grid=(1,), in_specs=specs, out_specs=[whole_block(...  141 us
    ppermute x29, waiting for transfers between devices, swap(): return lax.ppermute(v, 'ty', pair)  66.5 us
    ppermute x29, waiting for transfers between devices, swap(): return lax.ppermute(v, 'tx', pair)  35.6 us
    ppermute x29, starting transfers between devices, swap(): return lax.ppermute(v, 'tx', pair)  34.9 us
    pallas_call x4, Pallas kernels, weight_grad(): pl.pallas_call(kernel, grid_spec=pltpu.PrefetchScalarGridSpec(num_scalar_...  33.9 us
    ppermute x14, waiting for transfers between devices, swap_ctx(): return lax.ppermute(v, 'ctx', [(i, i ^ j) for i in range(ctxs)]) if j else v  29.2 us
    ppermute x29, starting transfers between devices, swap(): return lax.ppermute(v, 'ty', pair)  28.6 us
    dot_general x2, matrix products, nt(): lax.dot_general(left, right, (((1,), (1,)), ((), ())), preferred_element_...  24.4 us
  transfers between devices with their start and end apart: 88, of which 32 were waited for; matrix products, arithmetic and copies ran while one was open for 15% of the time, Pallas kernels for 34%

profile of v5, /device:TPU:0, one launch (start us, length us, event | category | flops | bytes accessed | tf_op | source)
XLA Modules:
  0.0 591.9 jit_solution(14118964271042064166)
XLA Ops:
  10.5 2.5 hold_tokens.1
  14.0 3.0 collective-permute-start
  19.8 3.9 collective-permute-done.1
  31.0 7.6 %collective-permute-done.5 = s32[1,8]{0,1:T(8,128)S(1)} collective-permute-done((s32[1,8]{0,1:T(8,128)S(1)}, s32[1,8]{0,1:T(8,128)S(1)}, u32[]{:S(2)}, u32[]{:S(2)}) %collective-permute-start.5) | collective-permute-done | bytes 64 | tf_op jit(solution)/shard_map/ppermute | solution.py:638
  44.0 3.3 split_gate_up.1
  47.3 7.5 %collective-permute-done.8.refs_4_ = bf16[128,2048]{1,0:T(8,128)(2,1)S(1)} collective-permute-done((bf16[128,2048]{1,0:T(8,128)(2,1)}, bf16[128,2048]{1,0:T(8,128)(2,1)S(1)}, u32[]{:S(2)}, u32[]{:S(2)}) %collective-permute-start.8) | collective-permute-done | bytes 524320 | tf_op jit(solution)/shard_map/ppermute | solution.py:637
  55.9 8.1 %collective-permute-done.11.refs_7_ = bf16[128,2048]{1,0:T(8,128)(2,1)S(1)} collective-permute-done((bf16[128,2048]{1,0:T(8,128)(2,1)S(1)}, bf16[128,2048]{1,0:T(8,128)(2,1)S(1)}, u32[]{:S(2)}, u32[]{:S(2)}) %collective-permute-start.11) | collective-permute-done | bytes 524320 | tf_op jit(solution)/shard_map/ppermute | solution.py:635
  64.7 2.3 constant_dynamic-slice_fusion
  71.8 7.5 %project.1 = (bf16[4,256,128]{2,1,0:T(8,128)(2,1)}, bf16[512,256]{1,0:T(8,128)(2,1)}, bf16[512,256]{1,0:T(8,128)(2,1)}, bf16[512,256]{1,0:T(8,128)(2,1)}, bf16[5...) custom-call(bf16[128,2048]{1,0:T(8,128)(2,1)} %get-tuple-element.261.refs_, ...), custom_call_target="tpu_custom_call" | custom-call | flops 2684354560 | bytes 8392704 | tf_op jit(solution)/shard_map/project/pallas_call | solution.py:66
  79.4 3.7 collective-permute-start.14
  86.5 4.4 join_rows.3.left_ref
  92.3 3.4 collective-permute-done.14.refs_4_.refs_9_.refs_3_.refs_15_
  95.7 14.5 %collective-permute-done.13.refs_3_.refs_8_.refs_2_.refs_14_ = bf16[4,256,128]{2,1,0:T(8,128)(2,1)} collective-permute-done((bf16[4,256,128]{2,1,0:T(8,128)(2,1)}, bf16[4,256,128]{2,1,0:T(8,128)(2,1)}, u32[]{:S(2)}, u32[]{:S(2)}) %collective-permute-start.13) | collective-permute-done | bytes 262176 | tf_op jit(solution)/shard_map/ppermute | solution.py:641
  116.6 9.1 %attend.3 = (bf16[512,256]{1,0:T(8,128)(2,1)}, f32[8,256]{1,0:T(8,128)}, bf16[256,2048]{1,0:T(8,128)(2,1)}) custom-call(s32[4,8]{1,0:T(4,128)} %copy.30.order_ref, bf16[512,2048]{1,0:T(8,128)(2,1)} %all-gather.5.cloned.1.call-done.wo_ref, bf16[512,256]{1,0:T(8,128)(2,1)} %get-tuple-element.252.refs_0_.refs_4_, ...), custom_call_target="tpu_custom_call" | custom-call | flops 2684354560 | bytes 4726912 | tf_op jit(solution)/shard_map/attend/pallas_call | solution.py:66
  125.7 2.3 fusion.13
  130.9 15.5 %attend.4 = (bf16[512,256]{1,0:T(8,128)(2,1)}, f32[8,256]{1,0:T(8,128)}, bf16[256,2048]{1,0:T(8,128)(2,1)}, bf16[512,256]{1,0:T(8,128)(2,1)}, f32[8,256]{1,0:T(8,128)}, /*index=5*/bf16[256,2048]{1,0:T(8,128)(2,1)}) custom-call(s32[4,8]{1,0:T(4,128)} %copy.30.order_ref, bf16[512,2048]{1,0:T(8,128)(2,1)} %all-gather.5.cloned.1.call-done.wo_ref, ...), custom_call_target="tpu_custom_call" | custom-call | flops 5368709120 | bytes 7356544 | tf_op jit(solution)/shard_map/attend/pallas_call | solution.py:66
  159.1 4.4 join_rows.4.g_ref
  163.5 9.2 %attend.5 = (bf16[512,256]{1,0:T(8,128)(2,1)}, f32[8,256]{1,0:T(8,128)}, f32[256,2048]{1,0:T(8,128)}) custom-call(s32[4,8]{1,0:T(4,128)} %copy.30.order_ref, bf16[512,2048]{1,0:T(8,128)(2,1)} %all-gather.5.cloned.1.call-done.wo_ref, bf16[512,256]{1,0:T(8,128)(2,1)} %get-tuple-element.288.refs_0_.refs_4_, ...), custom_call_target="tpu_custom_call" | custom-call | flops 2684354560 | bytes 5775488 | tf_op jit(solution)/shard_map/attend/pallas_call | solution.py:66
  172.6 6.2 %collective-permute-done.29.refs_4_ = bf16[128,2048]{1,0:T(8,128)(2,1)S(1)} collective-permute-done((bf16[128,2048]{1,0:T(8,128)(2,1)S(1)}, bf16[128,2048]{1,0:T(8,128)(2,1)S(1)}, u32[]{:S(2)}, u32[]{:S(2)}) %collective-permute-start.29) | collective-permute-done | bytes 524320 | tf_op jit(solution)/shard_map/ppermute | solution.py:637
  180.9 5.0 finish_middle.1
  189.9 11.0 %collective-permute-done.30.refs_2_ = bf16[128,2048]{1,0:T(8,128)(2,1)S(1)} collective-permute-done((bf16[128,2048]{1,0:T(8,128)(2,1)}, bf16[128,2048]{1,0:T(8,128)(2,1)S(1)}, u32[]{:S(2)}, u32[]{:S(2)}) %collective-permute-start.30) | collective-permute-done | bytes 524320 | tf_op jit(solution)/shard_map/ppermute | solution.py:635
  203.3 9.8 %collective-permute-done.32.refs_4_ = bf16[128,2048]{1,0:T(8,128)(2,1)S(1)} collective-permute-done((bf16[128,2048]{1,0:T(8,128)(2,1)}, bf16[128,2048]{1,0:T(8,128)(2,1)S(1)}, u32[]{:S(2)}, u32[]{:S(2)}) %collective-permute-start.32) | collective-permute-done | bytes 524320 | tf_op jit(solution)/shard_map/ppermute | solution.py:637
  213.1 7.3 %collective-permute-done.34.refs_6_ = bf16[128,2048]{1,0:T(8,128)(2,1)S(1)} collective-permute-done((bf16[128,2048]{1,0:T(8,128)(2,1)S(1)}, bf16[128,2048]{1,0:T(8,128)(2,1)S(1)}, u32[]{:S(2)}, u32[]{:S(2)}) %collective-permute-start.34) | collective-permute-done | bytes 524320 | tf_op jit(solution)/shard_map/ppermute | solution.py:637
  221.4 19.7 %activate.1 = (bf16[1024,1408]{1,0:T(8,128)(2,1)}, bf16[1024,2816]{1,0:T(8,128)(2,1)}) custom-call(bf16[128,2048]{1,0:T(8,128)(2,1)} %get-tuple-element.308.refs_0_, bf16[128,2048]{1,0:T(8,128)(2,1)} %get-tuple-element.309.refs_1_, bf16[128,2048]{1,0:T(8,128)(2,1)} %copy-done.26, bf16[128,2048]{1,0:T(8,128)(2,1)} %copy-done.29, ...), custom_call_target="tpu_custom_call" | custom-call | flops 11811160064 | bytes 24379392 | tf_op jit(solution)/shard_map/activate/pallas_call | solution.py:440
  241.1 6.1 %convolution_convert_fusion.3 = bf16[704,2048]{1,0:T(8,128)(2,1)S(1)} fusion(bf16[1024,2048]{1,0:T(8,128)(2,1)} %join_rows.4.g_ref, bf16[1024,1408]{1,0:T(8,128)(2,1)} %get-tuple-element.328, s32[]{:T(128)S(6)} %select_n.100), kind=kOutput, calls=%fused_computation.4 | convolution fusion | flops 2954231808 | bytes 8650756 | tf_op jit(solution)/shard_map/dot_general | solution.py:43
  247.3 4.4 join_rows.5.left_ref
  252.7 7.2 %add_convert_fusion = bf16[704,2048]{1,0:T(8,128)(2,1)S(1)} fusion(bf16[704,2048]{1,0:T(8,128)(2,1)} %collective-permute-done.36, bf16[1024,2048]{1,0:T(8,128)(2,1)} %join_rows.4.g_ref, bf16[1024,1408]{1,0:T(8,128)(2,1)} %get-tuple-element.328, s32[]{:T(128)S(6)} %select_n.99), kind=kOutput, calls=%fused_computation | convolution fusion | flops 2957115392 | bytes 11534340 | tf_op jit(solution)/shard_map/dot_general | solution.py:43
  261.9 16.4 %all-gather.9.cloned.1.call-done.down_ref = bf16[1408,2048]{1,0:T(8,128)(2,1)} async-done(((bf16[176,2048]{1,0:T(8,128)(2,1)}), bf16[1408,2048]{1,0:T(8,128)(2,1)}) %all-gather.9.cloned.1.call-update) | async-done | bytes 5767184 | tf_op jit(solution)/shard_map/all_gather | solution.py:685
  279.5 12.8 %activate_back.1.right_ref = bf16[1024,2816]{1,0:T(8,128)(2,1)} custom-call(bf16[1024,2048]{1,0:T(8,128)(2,1)} %join_rows.4.g_ref, bf16[1408,2048]{1,0:T(8,128)(2,1)} %all-gather.9.cloned.1.call-done.down_ref, bf16[1024,2816]{1,0:T(8,128)(2,1)} %get-tuple-element.316.slope_ref), custom_call_target="tpu_custom_call" | custom-call | flops 5905580032 | bytes 21495808 | tf_op jit(solution)/shard_map/activate_back/pallas_call | solution.py:472
  292.2 11.5 %weight_grad.4 = bf16[1024,2816]{1,0:T(8,128)(2,1)} custom-call(s32[1]{0:T(128)} %bitcast.7.index_ref, bf16[1024,2048]{1,0:T(8,128)(2,1)} %join_rows.5.left_ref, bf16[1024,2816]{1,0:T(8,128)(2,1)} %activate_back.1.right_ref), custom_call_target="tpu_custom_call" | custom-call | flops 5905580032 | bytes 19398656 | tf_op jit(solution)/shard_map/weight_grad/pallas_call | solution.py:505
  305.8 16.9 %convolution_convert_fusion = bf16[1024,2048]{1,0:T(8,128)(2,1)S(1)} fusion(bf16[1024,2816]{1,0:T(8,128)(2,1)} %activate_back.1.right_ref, bf16[2048,2816]{1,0:T(8,128)(2,1)} %all-gather.11.cloned.1.call-done.refs_8_), kind=kOutput, calls=%fused_computation.1 | convolution fusion | flops 11813257216 | bytes 21495808 | tf_op jit(solution)/shard_map/dot_general | solution.py:39
  328.7 2.5 copy-done.68
  331.3 12.8 %weight_grad.5 = bf16[1024,2816]{1,0:T(8,128)(2,1)} custom-call(s32[1]{0:T(128)} %bitcast.15.index_ref, bf16[1024,2048]{1,0:T(8,128)(2,1)} %join_rows.5.left_ref, bf16[1024,2816]{1,0:T(8,128)(2,1)} %activate_back.1.right_ref, bf16[1024,2816]{1,0:T(8,128)(2,1)} %copy-done.68), custom_call_target="tpu_custom_call" | custom-call | flops 5905580032 | bytes 19398656 | tf_op jit(solution)/shard_map/weight_grad/pallas_call | solution.py:505
  351.4 11.2 %convolution_convert_fusion.2 = bf16[1024,2048]{1,0:T(8,128)(2,1)} fusion(bf16[1024,1408]{1,0:T(8,128)(2,1)S(1)} %copy-done.17, bf16[1408,2048]{1,0:T(8,128)(2,1)} %all-gather.9.cloned.1.call-done.down_ref), kind=kOutput, calls=%fused_computation.3 | convolution fusion | flops 5907677184 | bytes 12845056 | tf_op jit(solution)/shard_map/dot_general | solution.py:35
  362.6 8.0 %collective-permute-done.46.refs_4_ = bf16[128,2048]{1,0:T(8,128)(2,1)} collective-permute-done((bf16[128,2048]{1,0:T(8,128)(2,1)S(1)}, bf16[128,2048]{1,0:T(8,128)(2,1)}, u32[]{:S(2)}, u32[]{:S(2)}) %collective-permute-start.46) | collective-permute-done | bytes 524320 | tf_op jit(solution)/shard_map/ppermute | solution.py:637
  370.6 6.1 %finish_norm_back.2 = (f32[256,2048]{1,0:T(8,128)}, bf16[128,2048]{1,0:T(8,128)(2,1)}, bf16[128,2048]{1,0:T(8,128)(2,1)}) custom-call(bf16[256,2048]{1,0:T(8,128)(2,1)} %g_ref.1, f32[256,2048]{1,0:T(8,128)} %get-tuple-element.422.x_ref.mid_ref, f32[256,1]{1,0:T(8,128)} %get-tuple-element.300.inv_ref, bf16[4,256,2048]{2,1,0:T(8,128)(2,1)} %bitcast.130, ...), custom_call_target="tpu_custom_call" | custom-call | flops 12583936 | bytes 12583936 | tf_op jit(solution)/shard_map/finish_norm_back/pallas_call | solution.py:66
  380.8 2.3 fusion.11
  384.5 9.6 %attend_back.3 = (bf16[256,512]{1,0:T(8,128)(2,1)}, bf16[256,512]{1,0:T(8,128)(2,1)}, f32[256,128]{1,0:T(8,128)}, bf16[768,128]{1,0:T(8,128)(2,1)}) custom-call(s32[4,8]{1,0:T(4,128)} %copy.30.order_ref, bf16[512,2048]{1,0:T(8,128)(2,1)} %all-gather.5.cloned.1.call-done.wo_ref, bf16[4,256,128]{2,1,0:T(8,128)(2,1)} %get-tuple-element.269.refs_1_.refs_6_.refs_0_.refs_12_, ...), custom_call_target="tpu_custom_call" | custom-call | flops 5905580032 | bytes 5842048 | tf_op jit(solution)/shard_map/attend_back/pallas_call | solution.py:66
  394.8 8.8 %collective-permute-done.50.refs_8_.refs_7_ = bf16[128,2048]{1,0:T(8,128)(2,1)S(1)} collective-permute-done((bf16[128,2048]{1,0:T(8,128)(2,1)}, bf16[128,2048]{1,0:T(8,128)(2,1)S(1)}, u32[]{:S(2)}, u32[]{:S(2)}) %collective-permute-start.50) | collective-permute-done | bytes 524320 | tf_op jit(solution)/shard_map/ppermute | solution.py:635
  406.6 17.1 %attend_back.4 = (bf16[256,512]{1,0:T(8,128)(2,1)}, bf16[256,512]{1,0:T(8,128)(2,1)}, f32[256,128]{1,0:T(8,128)}, bf16[768,128]{1,0:T(8,128)(2,1)}, bf16[256,512...) custom-call(s32[4,8]{1,0:T(4,128)} %copy.30.order_ref, ...), custom_call_target="tpu_custom_call" | custom-call | flops 11811160064 | bytes 9586816 | tf_op jit(solution)/shard_map/attend_back/pallas_call | solution.py:66
  427.0 2.9 collective-permute-start.57
  429.9 4.8 out_gradient.2
  434.7 9.9 %attend_back.5 = (bf16[256,512]{1,0:T(8,128)(2,1)}, bf16[256,512]{1,0:T(8,128)(2,1)}, f32[256,128]{1,0:T(8,128)}, bf16[768,128]{1,0:T(8,128)(2,1)}) custom-call(s32[4,8]{1,0:T(4,128)} %copy.30.order_ref, bf16[512,2048]{1,0:T(8,128)(2,1)} %all-gather.5.cloned.1.call-done.wo_ref, bf16[4,256,128]{2,1,0:T(8,128)(2,1)} %get-tuple-element.269.refs_1_.refs_6_.refs_0_.refs_12_, ...), custom_call_target="tpu_custom_call" | custom-call | flops 5905580032 | bytes 5842048 | tf_op jit(solution)/shard_map/attend_back/pallas_call | solution.py:66
  444.7 10.1 %collective-permute-done.56.refs_5_ = bf16[3,256,128]{2,1,0:T(8,128)(2,1)S(1)} collective-permute-done((bf16[3,256,128]{2,1,0:T(8,128)(2,1)S(1)}, bf16[3,256,128]{2,1,0:T(8,128)(2,1)S(1)}, u32[]{:S(2)}, u32[]{:S(2)}) %collective-permute-start.56) | collective-permute-done | bytes 196640 | tf_op jit(solution)/shard_map/ppermute | solution.py:641
  455.9 9.6 %collective-permute-start.59 = (bf16[1,256,128]{2,1,0:T(8,128)(2,1)S(1)}, bf16[1,256,128]{2,1,0:T(8,128)(2,1)S(1)}, u32[]{:S(2)}, u32[]{:S(2)}) collective-permute-start(bf16[1,256,128]{2,1,0:T(8,128)(2,1)S(1)} %get-tuple-element.500), channel_id=1, source_target_pairs={{0,2},{1,3},{2,0},{3,1},{4,6},{5,7},{6,4},{7,5},{8,10},{9,11},{10,... | collective-permute-start | bytes 196616 | tf_op jit(solution)/shard_map/ppermute | solution.py:641
  465.6 2.3 slice_bitcast_fusion.4
  470.8 2.7 fusion.4
  474.5 5.1 out_gradient.3
  483.2 4.7 finish_keys.1
  487.9 7.5 %convolution_convert_fusion.1 = bf16[1024,2048]{1,0:T(8,128)(2,1)} fusion(bf16[1024,640]{1,0:T(8,128)(2,1)} %get-tuple-element.404, bf16[2048,640]{1,0:T(8,128)(2,1)} %all-gather.7.cloned.1.call-done.refs_8_), kind=kOutput, calls=%fused_computation.2 | convolution fusion | flops 2686451712 | bytes 8126464 | tf_op jit(solution)/shard_map/dot_general | solution.py:39
  496.9 3.1 slice_bitcast_fusion
  500.0 4.8 weight_grad.6
  509.2 4.7 weight_grad.7
  513.9 5.5 collective-permute-done.68
  519.7 6.8 %reduce-scatter.6.cloned.1.call-done = bf16[64,2048]{1,0:T(8,128)(2,1)} async-done(((bf16[256,2048]{1,0:T(8,128)(2,1)}), bf16[64,2048]{1,0:T(8,128)(2,1)}) %reduce-scatter.6.cloned.1.call-update) | async-done | bytes 262160 | tf_op jit(solution)/shard_map/reduce_scatter | solution.py:711
  529.6 2.6 fusion.2
  533.2 4.1 finish_layer.1
  537.4 2.2 convert_add_fusion
  543.3 9.6 %collective-permute-done.73.refs_4_ = bf16[128,2048]{1,0:T(8,128)(2,1)} collective-permute-done((bf16[128,2048]{1,0:T(8,128)(2,1)}, bf16[128,2048]{1,0:T(8,128)(2,1)}, u32[]{:S(2)}, u32[]{:S(2)}) %collective-permute-start.73) | collective-permute-done | bytes 524320 | tf_op jit(solution)/shard_map/ppermute | solution.py:637
  558.7 5.8 finish_norm_back.3
  569.1 4.8 collective-permute-done.78.refs_2_
  574.5 4.5 merge_gate_up.1
  579.0 2.4 merge_qkv.1
  582.2 2.4 bitcast_add_fusion
  (347 shorter events, 128.7 us)
Async XLA Ops:
  7.2 64.6 %all-gather.7.cloned.1.call-start = ((), (), s32[]{:S(2)}) async-start(), calls=%async_computation.4 | async-start | bytes 2949120 | tf_op jit(solution)/shard_map/all_gather | solution.py:685
  24.5 92.0 %all-gather.5.cloned.1.call-start = ((), (), s32[]{:S(2)}) async-start(), calls=%async_computation.3 | async-start | bytes 2359296 | tf_op jit(solution)/shard_map/all_gather | solution.py:685
  31.0 189.4 %all-gather.11.cloned.1.call-start = ((), (), s32[]{:S(2)}) async-start(), calls=%async_computation.6 | async-start | bytes 12976128 | tf_op jit(solution)/shard_map/all_gather | solution.py:685
  39.7 15.1 %collective-permute-start.8 = (bf16[128,2048]{1,0:T(8,128)(2,1)}, bf16[128,2048]{1,0:T(8,128)(2,1)S(1)}, u32[]{:S(2)}, u32[]{:S(2)}) collective-permute-start(bf16[128,2048]{1,0:T(8,128)(2,1)} %get-tuple-element.261.refs_0_), channel_id=1, source_target_pairs={{0,16},{16,0},{1,17},{17,1},{2,18},{18,2},{3,19},{19,3},{4,20},{20... | collective-permute-start | bytes 1572872 | tf_op jit(solution)/shard_map/ppermute | solution.py:637
  41.5 22.4 %collective-permute-start.11 = (bf16[128,2048]{1,0:T(8,128)(2,1)S(1)}, bf16[128,2048]{1,0:T(8,128)(2,1)S(1)}, u32[]{:S(2)}, u32[]{:S(2)}) collective-permute-start(bf16[128,2048]{1,0:T(8,128)(2,1)S(1)} %collective-permute-done.7.refs_5_), channel_id=1, source_target_pairs={{0,8},{8,0},{1,9},{9,1},{2,10},{10,2},{3,11},{11,3},{4,12},{12,4},... | collective-permute-start | bytes 1572872 | tf_op jit(solution)/shard_map/ppermute | solution.py:635
  42.8 21.9 %collective-permute-start.10 = (bf16[128,2048]{1,0:T(8,128)(2,1)S(1)}, bf16[128,2048]{1,0:T(8,128)(2,1)}, u32[]{:S(2)}, u32[]{:S(2)}) collective-permute-start(bf16[128,2048]{1,0:T(8,128)(2,1)S(1)} %collective-permute-done.6.refs_2_), channel_id=1, source_target_pairs={{0,16},{16,0},{1,17},{17,1},{2,18},{18,2},{3,19},{19,3},{4,20},{20... | collective-permute-start | bytes 1572872 | tf_op jit(solution)/shard_map/ppermute | solution.py:637
  67.0 16.0 %collective-permute-start.17 = (bf16[1,64,2816]{2,1,0:T(8,128)(2,1)}, bf16[1,64,2816]{2,1,0:T(8,128)(2,1)S(1)}, u32[]{:S(2)}, u32[]{:S(2)}) collective-permute-start(bf16[1,64,2816]{2,1,0:T(8,128)(2,1)} %get-tuple-element.483), channel_id=1, source_target_pairs={{0,24},{8,16},{16,8},{24,0},{1,25},{9,17},{17,9},{25,1},{2,26},{10... | collective-permute-start | bytes 1081352 | tf_op jit(solution)/shard_map/ppermute | solution.py:638
  68.5 15.4 %collective-permute-start.16 = (bf16[1,64,2816]{2,1,0:T(8,128)(2,1)}, bf16[1,64,2816]{2,1,0:T(8,128)(2,1)S(1)}, u32[]{:S(2)}, u32[]{:S(2)}) collective-permute-start(bf16[1,64,2816]{2,1,0:T(8,128)(2,1)} %get-tuple-element.484), channel_id=1, source_target_pairs={{0,16},{16,0},{1,17},{17,1},{2,18},{18,2},{3,19},{19,3},{4,20},{20... | collective-permute-start | bytes 1081352 | tf_op jit(solution)/shard_map/ppermute | solution.py:637
  79.4 16.3 %collective-permute-start.14 = (bf16[4,256,128]{2,1,0:T(8,128)(2,1)}, bf16[4,256,128]{2,1,0:T(8,128)(2,1)}, u32[]{:S(2)}, u32[]{:S(2)}) collective-permute-start(bf16[4,256,128]{2,1,0:T(8,128)(2,1)} %get-tuple-element.269.refs_1_.refs_6_.refs_0_.refs_12_), channel_id=1, source_target_pairs={{0,3},{1,2},{2,1},{3,0},{4,7},{5,6},{6,5},{7,4},{8,11},{9,10},{10,... | collective-permute-start | bytes 786440 | tf_op jit(solution)/shard_map/ppermute | solution.py:641
  83.1 27.1 %collective-permute-start.13 = (bf16[4,256,128]{2,1,0:T(8,128)(2,1)}, bf16[4,256,128]{2,1,0:T(8,128)(2,1)}, u32[]{:S(2)}, u32[]{:S(2)}) collective-permute-start(bf16[4,256,128]{2,1,0:T(8,128)(2,1)} %get-tuple-element.269.refs_1_.refs_6_.refs_0_.refs_12_), channel_id=1, source_target_pairs={{0,2},{1,3},{2,0},{3,1},{4,6},{5,7},{6,4},{7,5},{8,10},{9,11},{10,... | collective-permute-start | bytes 786440 | tf_op jit(solution)/shard_map/ppermute | solution.py:641
  83.1 27.1 %collective-permute-start.12 = (bf16[4,256,128]{2,1,0:T(8,128)(2,1)}, bf16[4,256,128]{2,1,0:T(8,128)(2,1)}, u32[]{:S(2)}, u32[]{:S(2)}) collective-permute-start(bf16[4,256,128]{2,1,0:T(8,128)(2,1)} %get-tuple-element.269.refs_1_.refs_6_.refs_0_.refs_12_), channel_id=1, source_target_pairs={{0,1},{1,0},{2,3},{3,2},{4,5},{5,4},{6,7},{7,6},{8,9},{9,8},{10,11... | collective-permute-start | bytes 786440 | tf_op jit(solution)/shard_map/ppermute | solution.py:641
  84.6 25.6 %collective-permute-start.19 = (bf16[128,2048]{1,0:T(8,128)(2,1)S(1)}, bf16[128,2048]{1,0:T(8,128)(2,1)S(1)}, u32[]{:S(2)}, u32[]{:S(2)}) collective-permute-start(bf16[128,2048]{1,0:T(8,128)(2,1)S(1)} %get-tuple-element.489.refs_1_), channel_id=1, source_target_pairs={{0,16},{16,0},{1,17},{17,1},{2,18},{18,2},{3,19},{19,3},{4,20},{20... | collective-permute-start | bytes 1572872 | tf_op jit(solution)/shard_map/ppermute | solution.py:637
  85.4 24.8 %collective-permute-start.18 = (bf16[128,2048]{1,0:T(8,128)(2,1)S(1)}, bf16[128,2048]{1,0:T(8,128)(2,1)S(1)}, u32[]{:S(2)}, u32[]{:S(2)}) collective-permute-start(bf16[128,2048]{1,0:T(8,128)(2,1)S(1)} %get-tuple-element.490.refs_0_), channel_id=1, source_target_pairs={{0,8},{8,0},{1,9},{9,1},{2,10},{10,2},{3,11},{11,3},{4,12},{12,4},... | collective-permute-start | bytes 1572872 | tf_op jit(solution)/shard_map/ppermute | solution.py:635
  111.1 167.3 %all-gather.9.cloned.1.call-start = ((), (), s32[]{:S(2)}) async-start(), calls=%async_computation.5 | async-start | bytes 6488064 | tf_op jit(solution)/shard_map/all_gather | solution.py:685
  111.6 385.3 %reduce-scatter.4.cloned.1.call-start = ((), (), s32[]{:S(2)}) async-start(), calls=%async_computation.7 | async-start | bytes 7208960 | tf_op jit(solution)/shard_map/reduce_scatter | solution.py:711
  112.5 16.9 %collective-permute-start.23 = (bf16[128,2048]{1,0:T(8,128)(2,1)S(1)}, bf16[128,2048]{1,0:T(8,128)(2,1)S(1)}, u32[]{:S(2)}, u32[]{:S(2)}) collective-permute-start(bf16[128,2048]{1,0:T(8,128)(2,1)S(1)} %get-tuple-element.489.refs_1_), channel_id=1, source_target_pairs={{0,8},{8,0},{1,9},{9,1},{2,10},{10,2},{3,11},{11,3},{4,12},{12,4},... | collective-permute-start | bytes 1572872 | tf_op jit(solution)/shard_map/ppermute | solution.py:635
  114.0 16.9 %collective-permute-start.22 = (bf16[128,2048]{1,0:T(8,128)(2,1)S(1)}, bf16[128,2048]{1,0:T(8,128)(2,1)S(1)}, u32[]{:S(2)}, u32[]{:S(2)}) collective-permute-start(bf16[128,2048]{1,0:T(8,128)(2,1)S(1)} %get-tuple-element.490.refs_0_), channel_id=1, source_target_pairs={{0,16},{16,0},{1,17},{17,1},{2,18},{18,2},{3,19},{19,3},{4,20},{20... | collective-permute-start | bytes 1572872 | tf_op jit(solution)/shard_map/ppermute | solution.py:637
  115.5 31.0 %collective-permute-start.24 = (bf16[128,2048]{1,0:T(8,128)(2,1)}, bf16[128,2048]{1,0:T(8,128)(2,1)}, u32[]{:S(2)}, u32[]{:S(2)}) collective-permute-start(bf16[128,2048]{1,0:T(8,128)(2,1)} %copy-done.25), channel_id=1, source_target_pairs={{0,16},{16,0},{1,17},{17,1},{2,18},{18,2},{3,19},{19,3},{4,20},{20... | collective-permute-start | bytes 1572872 | tf_op jit(solution)/shard_map/ppermute | solution.py:637
  116.0 30.4 %collective-permute-start.25 = (bf16[128,2048]{1,0:T(8,128)(2,1)S(1)}, bf16[128,2048]{1,0:T(8,128)(2,1)}, u32[]{:S(2)}, u32[]{:S(2)}) collective-permute-start(bf16[128,2048]{1,0:T(8,128)(2,1)S(1)} %collective-permute-done.19.refs_5_), channel_id=1, source_target_pairs={{0,8},{8,0},{1,9},{9,1},{2,10},{10,2},{3,11},{11,3},{4,12},{12,4},... | collective-permute-start | bytes 1572872 | tf_op jit(solution)/shard_map/ppermute | solution.py:635
  127.9 20.4 %collective-permute-start.21 = (bf16[128,2048]{1,0:T(8,128)(2,1)}, bf16[128,2048]{1,0:T(8,128)(2,1)S(1)}, u32[]{:S(2)}, u32[]{:S(2)}) collective-permute-start(bf16[128,2048]{1,0:T(8,128)(2,1)} %get-tuple-element.487), channel_id=1, source_target_pairs={{0,8},{8,0},{1,9},{9,1},{2,10},{10,2},{3,11},{11,3},{4,12},{12,4},... | collective-permute-start | bytes 1572872 | tf_op jit(solution)/shard_map/ppermute | solution.py:635
  129.4 20.2 %collective-permute-start.20 = (bf16[128,2048]{1,0:T(8,128)(2,1)}, bf16[128,2048]{1,0:T(8,128)(2,1)S(1)}, u32[]{:S(2)}, u32[]{:S(2)}) collective-permute-start(bf16[128,2048]{1,0:T(8,128)(2,1)} %get-tuple-element.488), channel_id=1, source_target_pairs={{0,16},{16,0},{1,17},{17,1},{2,18},{18,2},{3,19},{19,3},{4,20},{20... | collective-permute-start | bytes 1572872 | tf_op jit(solution)/shard_map/ppermute | solution.py:637
  155.0 17.7 %collective-permute-start.26 = (bf16[128,2048]{1,0:T(8,128)(2,1)}, bf16[128,2048]{1,0:T(8,128)(2,1)S(1)}, u32[]{:S(2)}, u32[]{:S(2)}) collective-permute-start(bf16[128,2048]{1,0:T(8,128)(2,1)} %slice.187), channel_id=1, source_target_pairs={{0,16},{16,0},{1,17},{17,1},{2,18},{18,2},{3,19},{19,3},{4,20},{20... | collective-permute-start | bytes 1572872 | tf_op jit(solution)/shard_map/ppermute | solution.py:637
  156.5 22.3 %collective-permute-start.29 = (bf16[128,2048]{1,0:T(8,128)(2,1)S(1)}, bf16[128,2048]{1,0:T(8,128)(2,1)S(1)}, u32[]{:S(2)}, u32[]{:S(2)}) collective-permute-start(bf16[128,2048]{1,0:T(8,128)(2,1)S(1)} %add_convert_fusion.1), channel_id=1, source_target_pairs={{0,16},{16,0},{1,17},{17,1},{2,18},{18,2},{3,19},{19,3},{4,20},{20... | collective-permute-start | bytes 1572872 | tf_op jit(solution)/shard_map/ppermute | solution.py:637
  157.1 21.8 %collective-permute-start.28 = (bf16[128,2048]{1,0:T(8,128)(2,1)S(1)}, bf16[128,2048]{1,0:T(8,128)(2,1)S(1)}, u32[]{:S(2)}, u32[]{:S(2)}) collective-permute-start(bf16[128,2048]{1,0:T(8,128)(2,1)S(1)} %slice.189), channel_id=1, source_target_pairs={{0,8},{8,0},{1,9},{9,1},{2,10},{10,2},{3,11},{11,3},{4,12},{12,4},... | collective-permute-start | bytes 1572872 | tf_op jit(solution)/shard_map/ppermute | solution.py:635
  157.5 22.5 %collective-permute-start.27 = (bf16[128,2048]{1,0:T(8,128)(2,1)S(1)}, bf16[128,2048]{1,0:T(8,128)(2,1)S(1)}, u32[]{:S(2)}, u32[]{:S(2)}) collective-permute-start(bf16[128,2048]{1,0:T(8,128)(2,1)S(1)} %add_convert_fusion.2), channel_id=1, source_target_pairs={{0,8},{8,0},{1,9},{9,1},{2,10},{10,2},{3,11},{11,3},{4,12},{12,4},... | collective-permute-start | bytes 1572872 | tf_op jit(solution)/shard_map/ppermute | solution.py:635
  186.7 15.7 %collective-permute-start.33 = (bf16[128,2048]{1,0:T(8,128)(2,1)}, bf16[128,2048]{1,0:T(8,128)(2,1)S(1)}, u32[]{:S(2)}, u32[]{:S(2)}) collective-permute-start(bf16[128,2048]{1,0:T(8,128)(2,1)} %get-tuple-element.309.refs_1_), channel_id=1, source_target_pairs={{0,16},{16,0},{1,17},{17,1},{2,18},{18,2},{3,19},{19,3},{4,20},{20... | collective-permute-start | bytes 1572872 | tf_op jit(solution)/shard_map/ppermute | solution.py:637
  188.2 24.8 %collective-permute-start.32 = (bf16[128,2048]{1,0:T(8,128)(2,1)}, bf16[128,2048]{1,0:T(8,128)(2,1)S(1)}, u32[]{:S(2)}, u32[]{:S(2)}) collective-permute-start(bf16[128,2048]{1,0:T(8,128)(2,1)} %get-tuple-element.308.refs_0_), channel_id=1, source_target_pairs={{0,16},{16,0},{1,17},{17,1},{2,18},{18,2},{3,19},{19,3},{4,20},{20... | collective-permute-start | bytes 1572872 | tf_op jit(solution)/shard_map/ppermute | solution.py:637
  188.8 24.3 %collective-permute-start.31 = (bf16[128,2048]{1,0:T(8,128)(2,1)}, bf16[128,2048]{1,0:T(8,128)(2,1)S(1)}, u32[]{:S(2)}, u32[]{:S(2)}) collective-permute-start(bf16[128,2048]{1,0:T(8,128)(2,1)} %get-tuple-element.309.refs_1_), channel_id=1, source_target_pairs={{0,8},{8,0},{1,9},{9,1},{2,10},{10,2},{3,11},{11,3},{4,12},{12,4},... | collective-permute-start | bytes 1572872 | tf_op jit(solution)/shard_map/ppermute | solution.py:635
  201.0 19.4 %collective-permute-start.34 = (bf16[128,2048]{1,0:T(8,128)(2,1)S(1)}, bf16[128,2048]{1,0:T(8,128)(2,1)S(1)}, u32[]{:S(2)}, u32[]{:S(2)}) collective-permute-start(bf16[128,2048]{1,0:T(8,128)(2,1)S(1)} %collective-permute-done.30.refs_2_), channel_id=1, source_target_pairs={{0,16},{16,0},{1,17},{17,1},{2,18},{18,2},{3,19},{19,3},{4,20},{20... | collective-permute-start | bytes 1572872 | tf_op jit(solution)/shard_map/ppermute | solution.py:637
  202.4 18.0 %collective-permute-start.35 = (bf16[128,2048]{1,0:T(8,128)(2,1)S(1)}, bf16[128,2048]{1,0:T(8,128)(2,1)S(1)}, u32[]{:S(2)}, u32[]{:S(2)}) collective-permute-start(bf16[128,2048]{1,0:T(8,128)(2,1)S(1)} %collective-permute-done.33.refs_5_), channel_id=1, source_target_pairs={{0,8},{8,0},{1,9},{9,1},{2,10},{10,2},{3,11},{11,3},{4,12},{12,4},... | collective-permute-start | bytes 1572872 | tf_op jit(solution)/shard_map/ppermute | solution.py:635
  278.4 25.4 %collective-permute-start.37 = (bf16[352,512]{1,0:T(8,128)(2,1)}, bf16[352,512]{1,0:T(8,128)(2,1)S(1)}, u32[]{:S(2)}, u32[]{:S(2)}) collective-permute-start(bf16[352,512]{1,0:T(8,128)(2,1)} %get-tuple-element.319), channel_id=1, source_target_pairs={{0,2},{1,3},{2,0},{3,1},{4,6},{5,7},{6,4},{7,5},{8,10},{9,11},{10,... | collective-permute-start | bytes 1081352 | tf_op jit(solution)/shard_map/ppermute | solution.py:641
  303.8 25.0 %collective-permute-start.42 = (bf16[1024,2816]{1,0:T(8,128)(2,1)}, bf16[1024,2816]{1,0:T(8,128)(2,1)S(1)}, u32[]{:S(2)}, u32[]{:S(2)}) collective-permute-start(bf16[1024,2816]{1,0:T(8,128)(2,1)} %weight_grad.4), channel_id=1, source_target_pairs={{0,4},{4,0},{1,5},{5,1},{2,6},{6,2},{3,7},{7,3},{8,12},{12,8},{9,1... | collective-permute-start | bytes 17301512 | tf_op jit(solution)/shard_map/ppermute | solution.py:701
  303.9 19.1 %collective-permute-start.38 = (bf16[352,512]{1,0:T(8,128)(2,1)S(1)}, bf16[352,512]{1,0:T(8,128)(2,1)S(1)}, u32[]{:S(2)}, u32[]{:S(2)}) collective-permute-start(bf16[352,512]{1,0:T(8,128)(2,1)S(1)} %copy-done.58), channel_id=1, source_target_pairs={{0,2},{1,3},{2,0},{3,1},{4,6},{5,7},{6,4},{7,5},{8,10},{9,11},{10,... | collective-permute-start | bytes 1081352 | tf_op jit(solution)/shard_map/ppermute | solution.py:641
  323.0 21.1 %collective-permute-start.43 = (bf16[352,512]{1,0:T(8,128)(2,1)S(1)}, bf16[352,512]{1,0:T(8,128)(2,1)S(1)}, u32[]{:S(2)}, u32[]{:S(2)}) collective-permute-start(bf16[352,512]{1,0:T(8,128)(2,1)S(1)} %get-tuple-element.325), channel_id=1, source_target_pairs={{0,2},{1,3},{2,0},{3,1},{4,6},{5,7},{6,4},{7,5},{8,10},{9,11},{10,... | collective-permute-start | bytes 1081352 | tf_op jit(solution)/shard_map/ppermute | solution.py:641
  325.8 18.3 %collective-permute-start.41 = (bf16[128,2048]{1,0:T(8,128)(2,1)S(1)}, bf16[128,2048]{1,0:T(8,128)(2,1)S(1)}, u32[]{:S(2)}, u32[]{:S(2)}) collective-permute-start(bf16[128,2048]{1,0:T(8,128)(2,1)S(1)} %get-tuple-element.472), channel_id=1, source_target_pairs={{0,8},{8,0},{1,9},{9,1},{2,10},{10,2},{3,11},{11,3},{4,12},{12,4},... | collective-permute-start | bytes 1572872 | tf_op jit(solution)/shard_map/ppermute | solution.py:635
  327.3 16.9 %collective-permute-start.40 = (bf16[128,2048]{1,0:T(8,128)(2,1)S(1)}, bf16[128,2048]{1,0:T(8,128)(2,1)S(1)}, u32[]{:S(2)}, u32[]{:S(2)}) collective-permute-start(bf16[128,2048]{1,0:T(8,128)(2,1)S(1)} %get-tuple-element.473), channel_id=1, source_target_pairs={{0,16},{16,0},{1,17},{17,1},{2,18},{18,2},{3,19},{19,3},{4,20},{20... | collective-permute-start | bytes 1572872 | tf_op jit(solution)/shard_map/ppermute | solution.py:637
  345.2 181.3 %reduce-scatter.6.cloned.1.call-start = ((), (), s32[]{:S(2)}) async-start(), calls=%async_computation.8 | async-start | bytes 1310720 | tf_op jit(solution)/shard_map/reduce_scatter | solution.py:711
  345.3 17.3 %collective-permute-start.45 = (bf16[128,2048]{1,0:T(8,128)(2,1)}, bf16[128,2048]{1,0:T(8,128)(2,1)S(1)}, u32[]{:S(2)}, u32[]{:S(2)}) collective-permute-start(bf16[128,2048]{1,0:T(8,128)(2,1)} %get-tuple-element.471), channel_id=1, source_target_pairs={{0,8},{8,0},{1,9},{9,1},{2,10},{10,2},{3,11},{11,3},{4,12},{12,4},... | collective-permute-start | bytes 1572872 | tf_op jit(solution)/shard_map/ppermute | solution.py:635
  345.9 16.7 %collective-permute-start.39 = (bf16[128,2048]{1,0:T(8,128)(2,1)}, bf16[128,2048]{1,0:T(8,128)(2,1)S(1)}, u32[]{:S(2)}, u32[]{:S(2)}) collective-permute-start(bf16[128,2048]{1,0:T(8,128)(2,1)} %get-tuple-element.474), channel_id=1, source_target_pairs={{0,16},{16,0},{1,17},{17,1},{2,18},{18,2},{3,19},{19,3},{4,20},{20... | collective-permute-start | bytes 1572872 | tf_op jit(solution)/shard_map/ppermute | solution.py:637
  348.4 22.2 %collective-permute-start.46 = (bf16[128,2048]{1,0:T(8,128)(2,1)S(1)}, bf16[128,2048]{1,0:T(8,128)(2,1)}, u32[]{:S(2)}, u32[]{:S(2)}) collective-permute-start(bf16[128,2048]{1,0:T(8,128)(2,1)S(1)} %get-tuple-element.469), channel_id=1, source_target_pairs={{0,16},{16,0},{1,17},{17,1},{2,18},{18,2},{3,19},{19,3},{4,20},{20... | collective-permute-start | bytes 1572872 | tf_op jit(solution)/shard_map/ppermute | solution.py:637
  349.9 20.7 %collective-permute-start.44 = (bf16[128,2048]{1,0:T(8,128)(2,1)S(1)}, bf16[128,2048]{1,0:T(8,128)(2,1)}, u32[]{:S(2)}, u32[]{:S(2)}) collective-permute-start(bf16[128,2048]{1,0:T(8,128)(2,1)S(1)} %get-tuple-element.470), channel_id=1, source_target_pairs={{0,8},{8,0},{1,9},{9,1},{2,10},{10,2},{3,11},{11,3},{4,12},{12,4},... | collective-permute-start | bytes 1572872 | tf_op jit(solution)/shard_map/ppermute | solution.py:635
  376.7 17.4 %collective-permute-start.49 = (bf16[128,2048]{1,0:T(8,128)(2,1)}, bf16[128,2048]{1,0:T(8,128)(2,1)S(1)}, u32[]{:S(2)}, u32[]{:S(2)}) collective-permute-start(bf16[128,2048]{1,0:T(8,128)(2,1)} %get-tuple-element.385.refs_7_.refs_4_), channel_id=1, source_target_pairs={{0,16},{16,0},{1,17},{17,1},{2,18},{18,2},{3,19},{19,3},{4,20},{20... | collective-permute-start | bytes 1572872 | tf_op jit(solution)/shard_map/ppermute | solution.py:637
  377.3 17.5 %collective-permute-start.47 = (bf16[128,2048]{1,0:T(8,128)(2,1)}, bf16[128,2048]{1,0:T(8,128)(2,1)S(1)}, u32[]{:S(2)}, u32[]{:S(2)}) collective-permute-start(bf16[128,2048]{1,0:T(8,128)(2,1)} %get-tuple-element.385.refs_7_.refs_4_), channel_id=1, source_target_pairs={{0,8},{8,0},{1,9},{9,1},{2,10},{10,2},{3,11},{11,3},{4,12},{12,4},... | collective-permute-start | bytes 1572872 | tf_op jit(solution)/shard_map/ppermute | solution.py:635
  378.8 24.8 %collective-permute-start.50 = (bf16[128,2048]{1,0:T(8,128)(2,1)}, bf16[128,2048]{1,0:T(8,128)(2,1)S(1)}, u32[]{:S(2)}, u32[]{:S(2)}) collective-permute-start(bf16[128,2048]{1,0:T(8,128)(2,1)} %get-tuple-element.386.refs_8_.refs_5_), channel_id=1, source_target_pairs={{0,8},{8,0},{1,9},{9,1},{2,10},{10,2},{3,11},{11,3},{4,12},{12,4},... | collective-permute-start | bytes 1572872 | tf_op jit(solution)/shard_map/ppermute | solution.py:635
  379.3 24.3 %collective-permute-start.48 = (bf16[128,2048]{1,0:T(8,128)(2,1)}, bf16[128,2048]{1,0:T(8,128)(2,1)S(1)}, u32[]{:S(2)}, u32[]{:S(2)}) collective-permute-start(bf16[128,2048]{1,0:T(8,128)(2,1)} %get-tuple-element.386.refs_8_.refs_5_), channel_id=1, source_target_pairs={{0,16},{16,0},{1,17},{17,1},{2,18},{18,2},{3,19},{19,3},{4,20},{20... | collective-permute-start | bytes 1572872 | tf_op jit(solution)/shard_map/ppermute | solution.py:637
  383.1 40.7 %collective-permute-start.54 = (bf16[128,2048]{1,0:T(8,128)(2,1)}, bf16[128,2048]{1,0:T(8,128)(2,1)S(1)}, u32[]{:S(2)}, u32[]{:S(2)}) collective-permute-start(bf16[128,2048]{1,0:T(8,128)(2,1)} %get-tuple-element.467), channel_id=1, source_target_pairs={{0,8},{8,0},{1,9},{9,1},{2,10},{10,2},{3,11},{11,3},{4,12},{12,4},... | collective-permute-start | bytes 1572872 | tf_op jit(solution)/shard_map/ppermute | solution.py:635
  394.2 29.5 %collective-permute-start.53 = (bf16[128,2048]{1,0:T(8,128)(2,1)}, bf16[128,2048]{1,0:T(8,128)(2,1)}, u32[]{:S(2)}, u32[]{:S(2)}) collective-permute-start(bf16[128,2048]{1,0:T(8,128)(2,1)} %get-tuple-element.468), channel_id=1, source_target_pairs={{0,16},{16,0},{1,17},{17,1},{2,18},{18,2},{3,19},{19,3},{4,20},{20... | collective-permute-start | bytes 1572872 | tf_op jit(solution)/shard_map/ppermute | solution.py:637
  403.6 20.1 %collective-permute-start.51 = (bf16[128,2048]{1,0:T(8,128)(2,1)S(1)}, bf16[128,2048]{1,0:T(8,128)(2,1)S(1)}, u32[]{:S(2)}, u32[]{:S(2)}) collective-permute-start(bf16[128,2048]{1,0:T(8,128)(2,1)S(1)} %collective-permute-done.47.refs_7_.refs_6_), channel_id=1, source_target_pairs={{0,16},{16,0},{1,17},{17,1},{2,18},{18,2},{3,19},{19,3},{4,20},{20... | collective-permute-start | bytes 1572872 | tf_op jit(solution)/shard_map/ppermute | solution.py:637
  405.1 18.6 %collective-permute-start.52 = (bf16[128,2048]{1,0:T(8,128)(2,1)S(1)}, bf16[128,2048]{1,0:T(8,128)(2,1)S(1)}, u32[]{:S(2)}, u32[]{:S(2)}) collective-permute-start(bf16[128,2048]{1,0:T(8,128)(2,1)S(1)} %collective-permute-done.48.refs_20_.refs_9_), channel_id=1, source_target_pairs={{0,8},{8,0},{1,9},{9,1},{2,10},{10,2},{3,11},{11,3},{4,12},{12,4},... | collective-permute-start | bytes 1572872 | tf_op jit(solution)/shard_map/ppermute | solution.py:635
  425.2 19.5 %collective-permute-start.55 = (bf16[3,256,128]{2,1,0:T(8,128)(2,1)S(1)}, bf16[3,256,128]{2,1,0:T(8,128)(2,1)S(1)}, u32[]{:S(2)}, u32[]{:S(2)}) collective-permute-start(bf16[3,256,128]{2,1,0:T(8,128)(2,1)S(1)} %pad_maximum_fusion), channel_id=1, source_target_pairs={{0,1},{1,0},{2,3},{3,2},{4,5},{5,4},{6,7},{7,6},{8,9},{9,8},{10,11... | collective-permute-start | bytes 589832 | tf_op jit(solution)/shard_map/ppermute | solution.py:641
  425.3 29.5 %collective-permute-start.56 = (bf16[3,256,128]{2,1,0:T(8,128)(2,1)S(1)}, bf16[3,256,128]{2,1,0:T(8,128)(2,1)S(1)}, u32[]{:S(2)}, u32[]{:S(2)}) collective-permute-start(bf16[3,256,128]{2,1,0:T(8,128)(2,1)S(1)} %pad_maximum_fusion.1), channel_id=1, source_target_pairs={{0,2},{1,3},{2,0},{3,1},{4,6},{5,7},{6,4},{7,5},{8,10},{9,11},{10,... | collective-permute-start | bytes 589832 | tf_op jit(solution)/shard_map/ppermute | solution.py:641
  427.0 27.8 %collective-permute-start.57 = (bf16[3,256,128]{2,1,0:T(8,128)(2,1)S(1)}, bf16[3,256,128]{2,1,0:T(8,128)(2,1)S(1)}, u32[]{:S(2)}, u32[]{:S(2)}) collective-permute-start(bf16[3,256,128]{2,1,0:T(8,128)(2,1)S(1)} %pad_maximum_fusion.2), channel_id=1, source_target_pairs={{0,3},{1,2},{2,1},{3,0},{4,7},{5,6},{6,5},{7,4},{8,11},{9,10},{10,... | collective-permute-start | bytes 589832 | tf_op jit(solution)/shard_map/ppermute | solution.py:641
  434.7 38.8 %collective-permute-start.61 = (bf16[256,2048]{1,0:T(8,128)(2,1)}, bf16[256,2048]{1,0:T(8,128)(2,1)S(1)}, u32[]{:S(2)}, u32[]{:S(2)}) collective-permute-start(bf16[256,2048]{1,0:T(8,128)(2,1)} %out_gradient.2), channel_id=1, source_target_pairs={{0,4},{4,0},{1,5},{5,1},{2,6},{6,2},{3,7},{7,3},{8,12},{12,8},{9,1... | collective-permute-start | bytes 3145736 | tf_op jit(solution)/shard_map/ppermute | solution.py:863
  455.9 23.7 %collective-permute-start.60 = (bf16[1,256,128]{2,1,0:T(8,128)(2,1)S(1)}, bf16[1,256,128]{2,1,0:T(8,128)(2,1)S(1)}, u32[]{:S(2)}, u32[]{:S(2)}) collective-permute-start(bf16[1,256,128]{2,1,0:T(8,128)(2,1)S(1)} %get-tuple-element.499), channel_id=1, source_target_pairs={{0,3},{1,2},{2,1},{3,0},{4,7},{5,6},{6,5},{7,4},{8,11},{9,10},{10,... | collective-permute-start | bytes 196616 | tf_op jit(solution)/shard_map/ppermute | solution.py:641
  455.9 24.9 %collective-permute-start.59 = (bf16[1,256,128]{2,1,0:T(8,128)(2,1)S(1)}, bf16[1,256,128]{2,1,0:T(8,128)(2,1)S(1)}, u32[]{:S(2)}, u32[]{:S(2)}) collective-permute-start(bf16[1,256,128]{2,1,0:T(8,128)(2,1)S(1)} %get-tuple-element.500), channel_id=1, source_target_pairs={{0,2},{1,3},{2,0},{3,1},{4,6},{5,7},{6,4},{7,5},{8,10},{9,11},{10,... | collective-permute-start | bytes 196616 | tf_op jit(solution)/shard_map/ppermute | solution.py:641
  467.8 15.3 %collective-permute-start.63 = (bf16[128,2048]{1,0:T(8,128)(2,1)}, bf16[128,2048]{1,0:T(8,128)(2,1)S(1)}, u32[]{:S(2)}, u32[]{:S(2)}) collective-permute-start(bf16[128,2048]{1,0:T(8,128)(2,1)} %get-tuple-element.465), channel_id=1, source_target_pairs={{0,8},{8,0},{1,9},{9,1},{2,10},{10,2},{3,11},{11,3},{4,12},{12,4},... | collective-permute-start | bytes 1572872 | tf_op jit(solution)/shard_map/ppermute | solution.py:635
  479.6 16.5 %collective-permute-start.64 = (bf16[352,512]{1,0:T(8,128)(2,1)}, bf16[352,512]{1,0:T(8,128)(2,1)S(1)}, u32[]{:S(2)}, u32[]{:S(2)}) collective-permute-start(bf16[352,512]{1,0:T(8,128)(2,1)} %get-tuple-element.405), channel_id=1, source_target_pairs={{0,2},{1,3},{2,0},{3,1},{4,6},{5,7},{6,4},{7,5},{8,10},{9,11},{10,... | collective-permute-start | bytes 1081352 | tf_op jit(solution)/shard_map/ppermute | solution.py:641
  500.0 64.4 %reduce-scatter.8.cloned.1.call-start = ((), (), s32[]{:S(2)}) async-start(), calls=%async_computation.9 | async-start | bytes 1638400 | tf_op jit(solution)/shard_map/reduce_scatter | solution.py:711
  528.1 15.2 %collective-permute-start.67 = (bf16[128,2048]{1,0:T(8,128)(2,1)}, bf16[128,2048]{1,0:T(8,128)(2,1)}, u32[]{:S(2)}, u32[]{:S(2)}) collective-permute-start(bf16[128,2048]{1,0:T(8,128)(2,1)} %get-tuple-element.462), channel_id=1, source_target_pairs={{0,16},{16,0},{1,17},{17,1},{2,18},{18,2},{3,19},{19,3},{4,20},{20... | collective-permute-start | bytes 1572872 | tf_op jit(solution)/shard_map/ppermute | solution.py:637
  532.1 20.7 %collective-permute-start.73 = (bf16[128,2048]{1,0:T(8,128)(2,1)}, bf16[128,2048]{1,0:T(8,128)(2,1)}, u32[]{:S(2)}, u32[]{:S(2)}) collective-permute-start(bf16[128,2048]{1,0:T(8,128)(2,1)} %get-tuple-element.457), channel_id=1, source_target_pairs={{0,16},{16,0},{1,17},{17,1},{2,18},{18,2},{3,19},{19,3},{4,20},{20... | collective-permute-start | bytes 1572872 | tf_op jit(solution)/shard_map/ppermute | solution.py:637
  532.7 20.2 %collective-permute-start.71 = (bf16[128,2048]{1,0:T(8,128)(2,1)}, bf16[128,2048]{1,0:T(8,128)(2,1)}, u32[]{:S(2)}, u32[]{:S(2)}) collective-permute-start(bf16[128,2048]{1,0:T(8,128)(2,1)} %get-tuple-element.458), channel_id=1, source_target_pairs={{0,8},{8,0},{1,9},{9,1},{2,10},{10,2},{3,11},{11,3},{4,12},{12,4},... | collective-permute-start | bytes 1572872 | tf_op jit(solution)/shard_map/ppermute | solution.py:635
  554.0 28.2 %collective-permute-start.80 = (bf16[176,2048]{1,0:T(8,128)(2,1)}, bf16[176,2048]{1,0:T(8,128)(2,1)}, u32[]{:S(2)}, u32[]{:S(2)}) collective-permute-start(bf16[176,2048]{1,0:T(8,128)(2,1)} %dynamic-slice_bitcast_fusion.1), channel_id=1, source_target_pairs={{0,1},{1,0},{2,3},{3,2},{4,5},{5,4},{6,7},{7,6},{8,9},{9,8},{10,11... | collective-permute-start | bytes 2162696 | tf_op jit(solution)/shard_map/ppermute | solution.py:641
  556.6 17.3 %collective-permute-start.78 = (bf16[64,2816]{1,0:T(8,128)(2,1)}, bf16[64,2816]{1,0:T(8,128)(2,1)}, u32[]{:S(2)}, u32[]{:S(2)}) collective-permute-start(bf16[64,2816]{1,0:T(8,128)(2,1)} %get-tuple-element.476), channel_id=1, source_target_pairs={{0,16},{16,0},{1,17},{17,1},{2,18},{18,2},{3,19},{19,3},{4,20},{20... | collective-permute-start | bytes 1081352 | tf_op jit(solution)/shard_map/ppermute | solution.py:637
  557.2 17.3 %collective-permute-start.77 = (bf16[64,2816]{1,0:T(8,128)(2,1)}, bf16[64,2816]{1,0:T(8,128)(2,1)}, u32[]{:S(2)}, u32[]{:S(2)}) collective-permute-start(bf16[64,2816]{1,0:T(8,128)(2,1)} %get-tuple-element.477), channel_id=1, source_target_pairs={{0,8},{8,0},{1,9},{9,1},{2,10},{10,2},{3,11},{11,3},{4,12},{12,4},... | collective-permute-start | bytes 1081352 | tf_op jit(solution)/shard_map/ppermute | solution.py:635
  (94 other events, 929.8 us)
Sparse Core Ops, SparseCore 0:
  24.7 34.1 all-gather.6
  60.4 43.4 all-gather.4
  111.2 106.9 all-gather.10
  219.6 58.7 all-gather.8
  345.3 112.8 reduce-scatter.3
  500.1 26.3 reduce-scatter.5
  529.5 31.1 reduce-scatter.7

commit v6 on v5

--- a/solution.py
+++ b/solution.py
@@ -862,7 +862,8 @@
             part_out, axy, bxy = phase(part_out, axy, bxy)
             part_out = lax.ppermute(part_out, "rep", pair)
         attend_back_to((3,), (axy, bxy))
-        keys_near, back_of[3] = phase(keys_near, back_of[3])
+        forward_near = scatter_near(forward, far)
+        keys_near, back_of[3], forward_near = phase(keys_near, back_of[3], forward_near)
         keys_last = [
             swap_ctx(back_of[3][3][None, (j - 1) * count : j * count], j) for j in range(1, ctxs)
         ]
@@ -872,10 +873,8 @@
         else:
             part_out = out_gradient(mixed, db_pieces, 1, jnp.zeros((), jnp.int32))
             part_out = lax.psum_scatter(part_out, "rep", scatter_dimension=0, tiled=True)
-        forward_near = scatter_near(after(forward, keys_near), far)
-        keys_last, part_out, forward_near[0], forward_near[2] = phase(
-            keys_last, part_out, forward_near[0], forward_near[2]
-        )
+        raw_gate_up = collect(after(sum_gate_up, keys_near), t)
+        keys_last, part_out, raw_gate_up = phase(keys_last, part_out, raw_gate_up)
         grad_proj, scaled_proj = finish_keys(
             [v[2] for v in back_of],
             keys_near,
@@ -887,9 +886,7 @@
             sine,
         )
         parts = by_member(nt(grad_proj, qkv).astype(bf16))
-        parts, down_come[-1], forward_near, sum_gate_up = phase(
-            parts, send_down(keys_near), forward_near, sum_gate_up
-        )
+        parts, down_come[-1] = phase(parts, send_down(keys_near))
         across = phase(*halves(parts[3]))
         far_back = swap(across[0], 2), swap(across[1], 1)
         sent = over_reps_first(x_all, after(scaled_proj, across))
@@ -899,15 +896,16 @@
         sum_qkv = owned(part_qkv)
         near = scatter_near(parts, far_back)
         layer_out = finish_layer(after(middle, far_back), [(forward, 0), *forward_near])
-        raw_gate_up = collect(after(sum_gate_up, far_back), t)
         part_down = half_of(after(part_down, far_back), ctxs // 2, False).astype(f32)
         part_down = part_down + jnp.concatenate(down_come, axis=1).astype(f32)
-        near, layer_out, part_down = phase(near, layer_out, part_down)
+        grad_gate, grad_up, grad_norm_mlp = merge_gate_up(
+            t, after(raw_gate_up, far_back), w_gate, w_up, gain_mlp
+        )
+        near, layer_out, part_down, grad_norm_mlp = phase(
+            near, layer_out, part_down, grad_norm_mlp
+        )
         (input_grad,) = finish_norm_back(
             grad_middle, tokens, inverse[0], [(parts, 0), *near], natural, True
-        )
-        grad_gate, grad_up, grad_norm_mlp = merge_gate_up(
-            t, after(raw_gate_up, near), w_gate, w_up, gain_mlp
         )
         sum_qkv = after(sum_qkv, input_grad)
         grad_query, grad_key, grad_value, grad_norm_attn = merge_qkv(

time: 599 us -> 591 us (0.987)
    ppermute x29, waiting for transfers between devices: 35.6 us -> 43.2 us  [swap(): return lax.ppermute(v, 'tx', pair)]
    slice x8 -> x7, local copies, waits for them, and re-layouts: 14.1 us -> 10.6 us  [halves(): return (v[:half], v[half:])]
    unnamed x141 -> x149, local copies, waits for them, and re-layouts: 14 us -> 11.9 us
  transfers between devices with their start and end apart: 88 -> 88, of which waited for: 32 -> 33; matrix products, arithmetic and copies ran while one was open for 15% -> 15% of each run, Pallas kernels for 34% -> 35%
where the time goes in v6:
time: 591 us; the launch traced here: 584 us
  Pallas kernels  207 us (35%)
  waiting for transfers between devices  165 us (28%)
  starting transfers between devices  91.9 us (16%)
  matrix products  47 us (8%)
  local copies, waits for them, and re-layouts  38.2 us (6%)
  other arithmetic  18.7 us (3%)
  between operations  15.5 us (3%)
    pallas_call x22, Pallas kernels, small_call(): pl.pallas_call(kernel, grid=(1,), in_specs=specs, out_specs=[whole_block(...  141 us
    ppermute x29, waiting for transfers between devices, swap(): return lax.ppermute(v, 'ty', pair)  61.1 us
    ppermute x29, waiting for transfers between devices, swap(): return lax.ppermute(v, 'tx', pair)  43.2 us
    ppermute x29, starting transfers between devices, swap(): return lax.ppermute(v, 'tx', pair)  34.3 us
    pallas_call x4, Pallas kernels, weight_grad(): pl.pallas_call(kernel, grid_spec=pltpu.PrefetchScalarGridSpec(num_scalar_...  34 us
    ppermute x29, starting transfers between devices, swap(): return lax.ppermute(v, 'ty', pair)  29.6 us
    ppermute x14, waiting for transfers between devices, swap_ctx(): return lax.ppermute(v, 'ctx', [(i, i ^ j) for i in range(ctxs)]) if j else v  27.4 us
    dot_general x2, matrix products, nt(): lax.dot_general(left, right, (((1,), (1,)), ((), ())), preferred_element_...  22.5 us
  transfers between devices with their start and end apart: 88, of which 33 were waited for; matrix products, arithmetic and copies ran while one was open for 15% of the time, Pallas kernels for 35%

profile of v6, /device:TPU:0, one launch (start us, length us, event | category | flops | bytes accessed | tf_op | source)
XLA Modules:
  0.0 583.7 jit_solution(15493645313148360543)
XLA Ops:
  10.5 2.5 hold_tokens.1
  14.0 3.0 collective-permute-start
  19.8 3.9 collective-permute-done.1
  31.0 7.6 %collective-permute-done.5 = s32[1,8]{0,1:T(8,128)S(1)} collective-permute-done((s32[1,8]{0,1:T(8,128)S(1)}, s32[1,8]{0,1:T(8,128)S(1)}, u32[]{:S(2)}, u32[]{:S(2)}) %collective-permute-start.5) | collective-permute-done | bytes 64 | tf_op jit(solution)/shard_map/ppermute | solution.py:638
  44.0 3.3 split_gate_up.1
  47.3 7.5 %collective-permute-done.8.refs_4_ = bf16[128,2048]{1,0:T(8,128)(2,1)S(1)} collective-permute-done((bf16[128,2048]{1,0:T(8,128)(2,1)}, bf16[128,2048]{1,0:T(8,128)(2,1)S(1)}, u32[]{:S(2)}, u32[]{:S(2)}) %collective-permute-start.8) | collective-permute-done | bytes 524320 | tf_op jit(solution)/shard_map/ppermute | solution.py:637
  55.8 8.1 %collective-permute-done.11.refs_7_ = bf16[128,2048]{1,0:T(8,128)(2,1)S(1)} collective-permute-done((bf16[128,2048]{1,0:T(8,128)(2,1)S(1)}, bf16[128,2048]{1,0:T(8,128)(2,1)S(1)}, u32[]{:S(2)}, u32[]{:S(2)}) %collective-permute-start.11) | collective-permute-done | bytes 524320 | tf_op jit(solution)/shard_map/ppermute | solution.py:635
  64.7 2.3 constant_dynamic-slice_fusion
  71.8 7.5 %project.1 = (bf16[4,256,128]{2,1,0:T(8,128)(2,1)}, bf16[512,256]{1,0:T(8,128)(2,1)}, bf16[512,256]{1,0:T(8,128)(2,1)}, bf16[512,256]{1,0:T(8,128)(2,1)}, bf16[5...) custom-call(bf16[128,2048]{1,0:T(8,128)(2,1)} %get-tuple-element.262.refs_, ...), custom_call_target="tpu_custom_call" | custom-call | flops 2684354560 | bytes 8392704 | tf_op jit(solution)/shard_map/project/pallas_call | solution.py:66
  79.3 3.7 collective-permute-start.14
  86.5 4.4 join_rows.3.left_ref
  92.3 3.4 collective-permute-done.14.refs_4_.refs_9_.refs_3_.refs_15_
  95.7 14.5 %collective-permute-done.13.refs_3_.refs_8_.refs_2_.refs_14_ = bf16[4,256,128]{2,1,0:T(8,128)(2,1)} collective-permute-done((bf16[4,256,128]{2,1,0:T(8,128)(2,1)}, bf16[4,256,128]{2,1,0:T(8,128)(2,1)}, u32[]{:S(2)}, u32[]{:S(2)}) %collective-permute-start.13) | collective-permute-done | bytes 262176 | tf_op jit(solution)/shard_map/ppermute | solution.py:641
  116.6 9.1 %attend.3 = (bf16[512,256]{1,0:T(8,128)(2,1)}, f32[8,256]{1,0:T(8,128)}, bf16[256,2048]{1,0:T(8,128)(2,1)}) custom-call(s32[4,8]{1,0:T(4,128)} %copy.30.order_ref, bf16[512,2048]{1,0:T(8,128)(2,1)} %all-gather.5.cloned.1.call-done.wo_ref, bf16[512,256]{1,0:T(8,128)(2,1)} %get-tuple-element.253.refs_0_.refs_4_, ...), custom_call_target="tpu_custom_call" | custom-call | flops 2684354560 | bytes 4726912 | tf_op jit(solution)/shard_map/attend/pallas_call | solution.py:66
  125.7 2.3 fusion.11
  130.9 15.5 %attend.4 = (bf16[512,256]{1,0:T(8,128)(2,1)}, f32[8,256]{1,0:T(8,128)}, bf16[256,2048]{1,0:T(8,128)(2,1)}, bf16[512,256]{1,0:T(8,128)(2,1)}, f32[8,256]{1,0:T(8,128)}, /*index=5*/bf16[256,2048]{1,0:T(8,128)(2,1)}) custom-call(s32[4,8]{1,0:T(4,128)} %copy.30.order_ref, bf16[512,2048]{1,0:T(8,128)(2,1)} %all-gather.5.cloned.1.call-done.wo_ref, ...), custom_call_target="tpu_custom_call" | custom-call | flops 5368709120 | bytes 7356544 | tf_op jit(solution)/shard_map/attend/pallas_call | solution.py:66
  159.1 4.4 join_rows.4.g_ref
  163.5 9.2 %attend.5 = (bf16[512,256]{1,0:T(8,128)(2,1)}, f32[8,256]{1,0:T(8,128)}, f32[256,2048]{1,0:T(8,128)}) custom-call(s32[4,8]{1,0:T(4,128)} %copy.30.order_ref, bf16[512,2048]{1,0:T(8,128)(2,1)} %all-gather.5.cloned.1.call-done.wo_ref, bf16[512,256]{1,0:T(8,128)(2,1)} %get-tuple-element.289.refs_0_.refs_4_, ...), custom_call_target="tpu_custom_call" | custom-call | flops 2684354560 | bytes 5775488 | tf_op jit(solution)/shard_map/attend/pallas_call | solution.py:66
  172.7 6.2 %collective-permute-done.29.refs_4_ = bf16[128,2048]{1,0:T(8,128)(2,1)S(1)} collective-permute-done((bf16[128,2048]{1,0:T(8,128)(2,1)S(1)}, bf16[128,2048]{1,0:T(8,128)(2,1)S(1)}, u32[]{:S(2)}, u32[]{:S(2)}) %collective-permute-start.29) | collective-permute-done | bytes 524320 | tf_op jit(solution)/shard_map/ppermute | solution.py:637
  180.9 5.0 finish_middle.1
  189.9 11.0 %collective-permute-done.30.refs_2_ = bf16[128,2048]{1,0:T(8,128)(2,1)S(1)} collective-permute-done((bf16[128,2048]{1,0:T(8,128)(2,1)}, bf16[128,2048]{1,0:T(8,128)(2,1)S(1)}, u32[]{:S(2)}, u32[]{:S(2)}) %collective-permute-start.30) | collective-permute-done | bytes 524320 | tf_op jit(solution)/shard_map/ppermute | solution.py:635
  203.3 9.8 %collective-permute-done.32.refs_4_ = bf16[128,2048]{1,0:T(8,128)(2,1)S(1)} collective-permute-done((bf16[128,2048]{1,0:T(8,128)(2,1)}, bf16[128,2048]{1,0:T(8,128)(2,1)S(1)}, u32[]{:S(2)}, u32[]{:S(2)}) %collective-permute-start.32) | collective-permute-done | bytes 524320 | tf_op jit(solution)/shard_map/ppermute | solution.py:637
  213.1 7.3 %collective-permute-done.34.refs_6_ = bf16[128,2048]{1,0:T(8,128)(2,1)S(1)} collective-permute-done((bf16[128,2048]{1,0:T(8,128)(2,1)S(1)}, bf16[128,2048]{1,0:T(8,128)(2,1)S(1)}, u32[]{:S(2)}, u32[]{:S(2)}) %collective-permute-start.34) | collective-permute-done | bytes 524320 | tf_op jit(solution)/shard_map/ppermute | solution.py:637
  221.4 19.7 %activate.1 = (bf16[1024,1408]{1,0:T(8,128)(2,1)}, bf16[1024,2816]{1,0:T(8,128)(2,1)}) custom-call(bf16[128,2048]{1,0:T(8,128)(2,1)} %get-tuple-element.309.refs_0_, bf16[128,2048]{1,0:T(8,128)(2,1)} %get-tuple-element.310.refs_1_, bf16[128,2048]{1,0:T(8,128)(2,1)} %copy-done.26, bf16[128,2048]{1,0:T(8,128)(2,1)} %copy-done.29, ...), custom_call_target="tpu_custom_call" | custom-call | flops 11811160064 | bytes 24379392 | tf_op jit(solution)/shard_map/activate/pallas_call | solution.py:440
  241.1 6.1 %convolution_convert_fusion.3 = bf16[704,2048]{1,0:T(8,128)(2,1)S(1)} fusion(bf16[1024,2048]{1,0:T(8,128)(2,1)} %join_rows.4.g_ref, bf16[1024,1408]{1,0:T(8,128)(2,1)} %get-tuple-element.329, s32[]{:T(128)S(6)} %select_n.100), kind=kOutput, calls=%fused_computation.4 | convolution fusion | flops 2954231808 | bytes 8650756 | tf_op jit(solution)/shard_map/dot_general | solution.py:43
  247.3 4.4 join_rows.5.left_ref
  252.7 7.2 %add_convert_fusion = bf16[704,2048]{1,0:T(8,128)(2,1)S(1)} fusion(bf16[704,2048]{1,0:T(8,128)(2,1)} %collective-permute-done.36, bf16[1024,2048]{1,0:T(8,128)(2,1)} %join_rows.4.g_ref, bf16[1024,1408]{1,0:T(8,128)(2,1)} %get-tuple-element.329, s32[]{:T(128)S(6)} %select_n.99), kind=kOutput, calls=%fused_computation | convolution fusion | flops 2957115392 | bytes 11534340 | tf_op jit(solution)/shard_map/dot_general | solution.py:43
  261.9 16.5 %all-gather.9.cloned.1.call-done.down_ref = bf16[1408,2048]{1,0:T(8,128)(2,1)} async-done(((bf16[176,2048]{1,0:T(8,128)(2,1)}), bf16[1408,2048]{1,0:T(8,128)(2,1)}) %all-gather.9.cloned.1.call-update) | async-done | bytes 5767184 | tf_op jit(solution)/shard_map/all_gather | solution.py:685
  279.4 12.8 %activate_back.1.right_ref = bf16[1024,2816]{1,0:T(8,128)(2,1)} custom-call(bf16[1024,2048]{1,0:T(8,128)(2,1)} %join_rows.4.g_ref, bf16[1408,2048]{1,0:T(8,128)(2,1)} %all-gather.9.cloned.1.call-done.down_ref, bf16[1024,2816]{1,0:T(8,128)(2,1)} %get-tuple-element.317.slope_ref), custom_call_target="tpu_custom_call" | custom-call | flops 5905580032 | bytes 21495808 | tf_op jit(solution)/shard_map/activate_back/pallas_call | solution.py:472
  292.2 11.6 %weight_grad.4 = bf16[1024,2816]{1,0:T(8,128)(2,1)} custom-call(s32[1]{0:T(128)} %bitcast.7.index_ref, bf16[1024,2048]{1,0:T(8,128)(2,1)} %join_rows.5.left_ref, bf16[1024,2816]{1,0:T(8,128)(2,1)} %activate_back.1.right_ref), custom_call_target="tpu_custom_call" | custom-call | flops 5905580032 | bytes 19398656 | tf_op jit(solution)/shard_map/weight_grad/pallas_call | solution.py:505
  305.8 16.9 %convolution_convert_fusion = bf16[1024,2048]{1,0:T(8,128)(2,1)S(1)} fusion(bf16[1024,2816]{1,0:T(8,128)(2,1)} %activate_back.1.right_ref, bf16[2048,2816]{1,0:T(8,128)(2,1)} %all-gather.11.cloned.1.call-done.refs_8_), kind=kOutput, calls=%fused_computation.1 | convolution fusion | flops 11813257216 | bytes 21495808 | tf_op jit(solution)/shard_map/dot_general | solution.py:39
  328.8 2.5 copy-done.72
  331.3 12.8 %weight_grad.5 = bf16[1024,2816]{1,0:T(8,128)(2,1)} custom-call(s32[1]{0:T(128)} %bitcast.15.index_ref, bf16[1024,2048]{1,0:T(8,128)(2,1)} %join_rows.5.left_ref, bf16[1024,2816]{1,0:T(8,128)(2,1)} %activate_back.1.right_ref, bf16[1024,2816]{1,0:T(8,128)(2,1)} %copy-done.72), custom_call_target="tpu_custom_call" | custom-call | flops 5905580032 | bytes 19398656 | tf_op jit(solution)/shard_map/weight_grad/pallas_call | solution.py:505
  351.4 11.2 %convolution_convert_fusion.2 = bf16[1024,2048]{1,0:T(8,128)(2,1)} fusion(bf16[1024,1408]{1,0:T(8,128)(2,1)S(1)} %copy-done.17, bf16[1408,2048]{1,0:T(8,128)(2,1)} %all-gather.9.cloned.1.call-done.down_ref), kind=kOutput, calls=%fused_computation.3 | convolution fusion | flops 5907677184 | bytes 12845056 | tf_op jit(solution)/shard_map/dot_general | solution.py:35
  362.6 8.0 %collective-permute-done.46.refs_4_ = bf16[128,2048]{1,0:T(8,128)(2,1)} collective-permute-done((bf16[128,2048]{1,0:T(8,128)(2,1)S(1)}, bf16[128,2048]{1,0:T(8,128)(2,1)}, u32[]{:S(2)}, u32[]{:S(2)}) %collective-permute-start.46) | collective-permute-done | bytes 524320 | tf_op jit(solution)/shard_map/ppermute | solution.py:637
  370.6 6.0 %finish_norm_back.2 = (f32[256,2048]{1,0:T(8,128)}, bf16[128,2048]{1,0:T(8,128)(2,1)}, bf16[128,2048]{1,0:T(8,128)(2,1)}) custom-call(bf16[256,2048]{1,0:T(8,128)(2,1)} %g_ref.1, f32[256,2048]{1,0:T(8,128)} %get-tuple-element.421.x_ref.mid_ref, f32[256,1]{1,0:T(8,128)} %get-tuple-element.301.inv_ref, bf16[4,256,2048]{2,1,0:T(8,128)(2,1)} %bitcast.120, ...), custom_call_target="tpu_custom_call" | custom-call | flops 12583936 | bytes 12583936 | tf_op jit(solution)/shard_map/finish_norm_back/pallas_call | solution.py:66
  380.7 2.9 fusion.9
  385.0 9.6 %attend_back.3 = (bf16[256,512]{1,0:T(8,128)(2,1)}, bf16[256,512]{1,0:T(8,128)(2,1)}, f32[256,128]{1,0:T(8,128)}, bf16[768,128]{1,0:T(8,128)(2,1)}) custom-call(s32[4,8]{1,0:T(4,128)} %copy.30.order_ref, bf16[512,2048]{1,0:T(8,128)(2,1)} %all-gather.5.cloned.1.call-done.wo_ref, bf16[4,256,128]{2,1,0:T(8,128)(2,1)} %get-tuple-element.270.refs_1_.refs_6_.refs_0_.refs_12_, ...), custom_call_target="tpu_custom_call" | custom-call | flops 5905580032 | bytes 5842048 | tf_op jit(solution)/shard_map/attend_back/pallas_call | solution.py:66
  395.9 7.6 %collective-permute-done.50.refs_8_.refs_7_ = bf16[128,2048]{1,0:T(8,128)(2,1)S(1)} collective-permute-done((bf16[128,2048]{1,0:T(8,128)(2,1)}, bf16[128,2048]{1,0:T(8,128)(2,1)S(1)}, u32[]{:S(2)}, u32[]{:S(2)}) %collective-permute-start.50) | collective-permute-done | bytes 524320 | tf_op jit(solution)/shard_map/ppermute | solution.py:635
  406.5 17.1 %attend_back.4 = (bf16[256,512]{1,0:T(8,128)(2,1)}, bf16[256,512]{1,0:T(8,128)(2,1)}, f32[256,128]{1,0:T(8,128)}, bf16[768,128]{1,0:T(8,128)(2,1)}, bf16[256,512...) custom-call(s32[4,8]{1,0:T(4,128)} %copy.30.order_ref, ...), custom_call_target="tpu_custom_call" | custom-call | flops 11811160064 | bytes 9586816 | tf_op jit(solution)/shard_map/attend_back/pallas_call | solution.py:66
  423.6 2.4 collective-permute-done.54
  427.6 6.7 %collective-permute-done.52.refs_11_.refs_8_ = bf16[128,2048]{1,0:T(8,128)(2,1)S(1)} collective-permute-done((bf16[128,2048]{1,0:T(8,128)(2,1)S(1)}, bf16[128,2048]{1,0:T(8,128)(2,1)S(1)}, u32[]{:S(2)}, u32[]{:S(2)}) %collective-permute-start.52) | collective-permute-done | bytes 524320 | tf_op jit(solution)/shard_map/ppermute | solution.py:635
  438.6 2.7 collective-permute-start.57
  441.4 2.9 add_convert_fusion.1
  444.2 4.7 out_gradient.2
  452.0 9.9 %attend_back.5 = (bf16[256,512]{1,0:T(8,128)(2,1)}, bf16[256,512]{1,0:T(8,128)(2,1)}, f32[256,128]{1,0:T(8,128)}, bf16[768,128]{1,0:T(8,128)(2,1)}) custom-call(s32[4,8]{1,0:T(4,128)} %copy.30.order_ref, bf16[512,2048]{1,0:T(8,128)(2,1)} %all-gather.5.cloned.1.call-done.wo_ref, bf16[4,256,128]{2,1,0:T(8,128)(2,1)} %get-tuple-element.270.refs_1_.refs_6_.refs_0_.refs_12_, ...), custom_call_target="tpu_custom_call" | custom-call | flops 5905580032 | bytes 5842048 | tf_op jit(solution)/shard_map/attend_back/pallas_call | solution.py:66
  462.0 2.9 dynamic-slice_bitcast_fusion.2
  470.7 4.5 collective-permute-done.64.refs_9_
  477.3 5.0 out_gradient.3
  484.8 4.3 finish_keys.1
  489.1 5.6 convolution_convert_fusion.1
  494.8 4.8 collective-permute-done.69
  500.9 4.8 weight_grad.6
  510.0 4.8 weight_grad.7
  514.8 5.2 collective-permute-done.71
  521.5 5.7 reduce-scatter.6.cloned.1.call-done
  530.2 2.6 fusion.2
  534.0 4.6 merge_gate_up.1
  538.5 3.9 finish_layer.1
  544.7 8.8 %collective-permute-done.76.refs_4_ = bf16[128,2048]{1,0:T(8,128)(2,1)} collective-permute-done((bf16[128,2048]{1,0:T(8,128)(2,1)}, bf16[128,2048]{1,0:T(8,128)(2,1)}, u32[]{:S(2)}, u32[]{:S(2)}) %collective-permute-start.76) | collective-permute-done | bytes 524320 | tf_op jit(solution)/shard_map/ppermute | solution.py:637
  554.7 5.8 finish_norm_back.3
  562.2 3.0 collective-permute-start.79
  570.8 2.3 merge_qkv.1
  574.0 2.4 bitcast_add_fusion
  (354 shorter events, 133.3 us)
Async XLA Ops:
  7.2 64.6 %all-gather.7.cloned.1.call-start = ((), (), s32[]{:S(2)}) async-start(), calls=%async_computation.4 | async-start | bytes 2949120 | tf_op jit(solution)/shard_map/all_gather | solution.py:685
  24.5 92.0 %all-gather.5.cloned.1.call-start = ((), (), s32[]{:S(2)}) async-start(), calls=%async_computation.3 | async-start | bytes 2359296 | tf_op jit(solution)/shard_map/all_gather | solution.py:685
  31.0 189.4 %all-gather.11.cloned.1.call-start = ((), (), s32[]{:S(2)}) async-start(), calls=%async_computation.6 | async-start | bytes 12976128 | tf_op jit(solution)/shard_map/all_gather | solution.py:685
  41.5 22.4 %collective-permute-start.11 = (bf16[128,2048]{1,0:T(8,128)(2,1)S(1)}, bf16[128,2048]{1,0:T(8,128)(2,1)S(1)}, u32[]{:S(2)}, u32[]{:S(2)}) collective-permute-start(bf16[128,2048]{1,0:T(8,128)(2,1)S(1)} %collective-permute-done.7.refs_5_), channel_id=1, source_target_pairs={{0,8},{8,0},{1,9},{9,1},{2,10},{10,2},{3,11},{11,3},{4,12},{12,4},... | collective-permute-start | bytes 1572872 | tf_op jit(solution)/shard_map/ppermute | solution.py:635
  42.8 21.9 %collective-permute-start.10 = (bf16[128,2048]{1,0:T(8,128)(2,1)S(1)}, bf16[128,2048]{1,0:T(8,128)(2,1)}, u32[]{:S(2)}, u32[]{:S(2)}) collective-permute-start(bf16[128,2048]{1,0:T(8,128)(2,1)S(1)} %collective-permute-done.6.refs_2_), channel_id=1, source_target_pairs={{0,16},{16,0},{1,17},{17,1},{2,18},{18,2},{3,19},{19,3},{4,20},{20... | collective-permute-start | bytes 1572872 | tf_op jit(solution)/shard_map/ppermute | solution.py:637
  67.0 16.0 %collective-permute-start.17 = (bf16[1,64,2816]{2,1,0:T(8,128)(2,1)}, bf16[1,64,2816]{2,1,0:T(8,128)(2,1)S(1)}, u32[]{:S(2)}, u32[]{:S(2)}) collective-permute-start(bf16[1,64,2816]{2,1,0:T(8,128)(2,1)} %get-tuple-element.485), channel_id=1, source_target_pairs={{0,24},{8,16},{16,8},{24,0},{1,25},{9,17},{17,9},{25,1},{2,26},{10... | collective-permute-start | bytes 1081352 | tf_op jit(solution)/shard_map/ppermute | solution.py:638
  68.4 15.4 %collective-permute-start.16 = (bf16[1,64,2816]{2,1,0:T(8,128)(2,1)}, bf16[1,64,2816]{2,1,0:T(8,128)(2,1)S(1)}, u32[]{:S(2)}, u32[]{:S(2)}) collective-permute-start(bf16[1,64,2816]{2,1,0:T(8,128)(2,1)} %get-tuple-element.486), channel_id=1, source_target_pairs={{0,16},{16,0},{1,17},{17,1},{2,18},{18,2},{3,19},{19,3},{4,20},{20... | collective-permute-start | bytes 1081352 | tf_op jit(solution)/shard_map/ppermute | solution.py:637
  79.3 16.3 %collective-permute-start.14 = (bf16[4,256,128]{2,1,0:T(8,128)(2,1)}, bf16[4,256,128]{2,1,0:T(8,128)(2,1)}, u32[]{:S(2)}, u32[]{:S(2)}) collective-permute-start(bf16[4,256,128]{2,1,0:T(8,128)(2,1)} %get-tuple-element.270.refs_1_.refs_6_.refs_0_.refs_12_), channel_id=1, source_target_pairs={{0,3},{1,2},{2,1},{3,0},{4,7},{5,6},{6,5},{7,4},{8,11},{9,10},{10,... | collective-permute-start | bytes 786440 | tf_op jit(solution)/shard_map/ppermute | solution.py:641
  83.0 27.1 %collective-permute-start.13 = (bf16[4,256,128]{2,1,0:T(8,128)(2,1)}, bf16[4,256,128]{2,1,0:T(8,128)(2,1)}, u32[]{:S(2)}, u32[]{:S(2)}) collective-permute-start(bf16[4,256,128]{2,1,0:T(8,128)(2,1)} %get-tuple-element.270.refs_1_.refs_6_.refs_0_.refs_12_), channel_id=1, source_target_pairs={{0,2},{1,3},{2,0},{3,1},{4,6},{5,7},{6,4},{7,5},{8,10},{9,11},{10,... | collective-permute-start | bytes 786440 | tf_op jit(solution)/shard_map/ppermute | solution.py:641
  83.1 27.1 %collective-permute-start.12 = (bf16[4,256,128]{2,1,0:T(8,128)(2,1)}, bf16[4,256,128]{2,1,0:T(8,128)(2,1)}, u32[]{:S(2)}, u32[]{:S(2)}) collective-permute-start(bf16[4,256,128]{2,1,0:T(8,128)(2,1)} %get-tuple-element.270.refs_1_.refs_6_.refs_0_.refs_12_), channel_id=1, source_target_pairs={{0,1},{1,0},{2,3},{3,2},{4,5},{5,4},{6,7},{7,6},{8,9},{9,8},{10,11... | collective-permute-start | bytes 786440 | tf_op jit(solution)/shard_map/ppermute | solution.py:641
  84.6 25.6 %collective-permute-start.19 = (bf16[128,2048]{1,0:T(8,128)(2,1)S(1)}, bf16[128,2048]{1,0:T(8,128)(2,1)S(1)}, u32[]{:S(2)}, u32[]{:S(2)}) collective-permute-start(bf16[128,2048]{1,0:T(8,128)(2,1)S(1)} %get-tuple-element.491.refs_1_), channel_id=1, source_target_pairs={{0,16},{16,0},{1,17},{17,1},{2,18},{18,2},{3,19},{19,3},{4,20},{20... | collective-permute-start | bytes 1572872 | tf_op jit(solution)/shard_map/ppermute | solution.py:637
  85.3 24.8 %collective-permute-start.18 = (bf16[128,2048]{1,0:T(8,128)(2,1)S(1)}, bf16[128,2048]{1,0:T(8,128)(2,1)S(1)}, u32[]{:S(2)}, u32[]{:S(2)}) collective-permute-start(bf16[128,2048]{1,0:T(8,128)(2,1)S(1)} %get-tuple-element.492.refs_0_), channel_id=1, source_target_pairs={{0,8},{8,0},{1,9},{9,1},{2,10},{10,2},{3,11},{11,3},{4,12},{12,4},... | collective-permute-start | bytes 1572872 | tf_op jit(solution)/shard_map/ppermute | solution.py:635
  111.1 167.3 %all-gather.9.cloned.1.call-start = ((), (), s32[]{:S(2)}) async-start(), calls=%async_computation.5 | async-start | bytes 6488064 | tf_op jit(solution)/shard_map/all_gather | solution.py:685
  111.6 350.4 %reduce-scatter.4.cloned.1.call-start = ((), (), s32[]{:S(2)}) async-start(), calls=%async_computation.7 | async-start | bytes 7208960 | tf_op jit(solution)/shard_map/reduce_scatter | solution.py:711
  112.5 16.9 %collective-permute-start.23 = (bf16[128,2048]{1,0:T(8,128)(2,1)S(1)}, bf16[128,2048]{1,0:T(8,128)(2,1)S(1)}, u32[]{:S(2)}, u32[]{:S(2)}) collective-permute-start(bf16[128,2048]{1,0:T(8,128)(2,1)S(1)} %get-tuple-element.491.refs_1_), channel_id=1, source_target_pairs={{0,8},{8,0},{1,9},{9,1},{2,10},{10,2},{3,11},{11,3},{4,12},{12,4},... | collective-permute-start | bytes 1572872 | tf_op jit(solution)/shard_map/ppermute | solution.py:635
  114.0 16.9 %collective-permute-start.22 = (bf16[128,2048]{1,0:T(8,128)(2,1)S(1)}, bf16[128,2048]{1,0:T(8,128)(2,1)S(1)}, u32[]{:S(2)}, u32[]{:S(2)}) collective-permute-start(bf16[128,2048]{1,0:T(8,128)(2,1)S(1)} %get-tuple-element.492.refs_0_), channel_id=1, source_target_pairs={{0,16},{16,0},{1,17},{17,1},{2,18},{18,2},{3,19},{19,3},{4,20},{20... | collective-permute-start | bytes 1572872 | tf_op jit(solution)/shard_map/ppermute | solution.py:637
  115.5 31.0 %collective-permute-start.24 = (bf16[128,2048]{1,0:T(8,128)(2,1)}, bf16[128,2048]{1,0:T(8,128)(2,1)}, u32[]{:S(2)}, u32[]{:S(2)}) collective-permute-start(bf16[128,2048]{1,0:T(8,128)(2,1)} %copy-done.25), channel_id=1, source_target_pairs={{0,16},{16,0},{1,17},{17,1},{2,18},{18,2},{3,19},{19,3},{4,20},{20... | collective-permute-start | bytes 1572872 | tf_op jit(solution)/shard_map/ppermute | solution.py:637
  116.0 30.4 %collective-permute-start.25 = (bf16[128,2048]{1,0:T(8,128)(2,1)S(1)}, bf16[128,2048]{1,0:T(8,128)(2,1)}, u32[]{:S(2)}, u32[]{:S(2)}) collective-permute-start(bf16[128,2048]{1,0:T(8,128)(2,1)S(1)} %collective-permute-done.19.refs_5_), channel_id=1, source_target_pairs={{0,8},{8,0},{1,9},{9,1},{2,10},{10,2},{3,11},{11,3},{4,12},{12,4},... | collective-permute-start | bytes 1572872 | tf_op jit(solution)/shard_map/ppermute | solution.py:635
  127.9 20.4 %collective-permute-start.21 = (bf16[128,2048]{1,0:T(8,128)(2,1)}, bf16[128,2048]{1,0:T(8,128)(2,1)S(1)}, u32[]{:S(2)}, u32[]{:S(2)}) collective-permute-start(bf16[128,2048]{1,0:T(8,128)(2,1)} %get-tuple-element.489), channel_id=1, source_target_pairs={{0,8},{8,0},{1,9},{9,1},{2,10},{10,2},{3,11},{11,3},{4,12},{12,4},... | collective-permute-start | bytes 1572872 | tf_op jit(solution)/shard_map/ppermute | solution.py:635
  129.4 20.2 %collective-permute-start.20 = (bf16[128,2048]{1,0:T(8,128)(2,1)}, bf16[128,2048]{1,0:T(8,128)(2,1)S(1)}, u32[]{:S(2)}, u32[]{:S(2)}) collective-permute-start(bf16[128,2048]{1,0:T(8,128)(2,1)} %get-tuple-element.490), channel_id=1, source_target_pairs={{0,16},{16,0},{1,17},{17,1},{2,18},{18,2},{3,19},{19,3},{4,20},{20... | collective-permute-start | bytes 1572872 | tf_op jit(solution)/shard_map/ppermute | solution.py:637
  155.0 17.7 %collective-permute-start.26 = (bf16[128,2048]{1,0:T(8,128)(2,1)}, bf16[128,2048]{1,0:T(8,128)(2,1)S(1)}, u32[]{:S(2)}, u32[]{:S(2)}) collective-permute-start(bf16[128,2048]{1,0:T(8,128)(2,1)} %slice.183), channel_id=1, source_target_pairs={{0,16},{16,0},{1,17},{17,1},{2,18},{18,2},{3,19},{19,3},{4,20},{20... | collective-permute-start | bytes 1572872 | tf_op jit(solution)/shard_map/ppermute | solution.py:637
  156.5 22.3 %collective-permute-start.29 = (bf16[128,2048]{1,0:T(8,128)(2,1)S(1)}, bf16[128,2048]{1,0:T(8,128)(2,1)S(1)}, u32[]{:S(2)}, u32[]{:S(2)}) collective-permute-start(bf16[128,2048]{1,0:T(8,128)(2,1)S(1)} %add_convert_fusion.3), channel_id=1, source_target_pairs={{0,16},{16,0},{1,17},{17,1},{2,18},{18,2},{3,19},{19,3},{4,20},{20... | collective-permute-start | bytes 1572872 | tf_op jit(solution)/shard_map/ppermute | solution.py:637
  157.1 21.8 %collective-permute-start.28 = (bf16[128,2048]{1,0:T(8,128)(2,1)S(1)}, bf16[128,2048]{1,0:T(8,128)(2,1)S(1)}, u32[]{:S(2)}, u32[]{:S(2)}) collective-permute-start(bf16[128,2048]{1,0:T(8,128)(2,1)S(1)} %slice.185), channel_id=1, source_target_pairs={{0,8},{8,0},{1,9},{9,1},{2,10},{10,2},{3,11},{11,3},{4,12},{12,4},... | collective-permute-start | bytes 1572872 | tf_op jit(solution)/shard_map/ppermute | solution.py:635
  157.5 22.5 %collective-permute-start.27 = (bf16[128,2048]{1,0:T(8,128)(2,1)S(1)}, bf16[128,2048]{1,0:T(8,128)(2,1)S(1)}, u32[]{:S(2)}, u32[]{:S(2)}) collective-permute-start(bf16[128,2048]{1,0:T(8,128)(2,1)S(1)} %add_convert_fusion.4), channel_id=1, source_target_pairs={{0,8},{8,0},{1,9},{9,1},{2,10},{10,2},{3,11},{11,3},{4,12},{12,4},... | collective-permute-start | bytes 1572872 | tf_op jit(solution)/shard_map/ppermute | solution.py:635
  186.7 15.7 %collective-permute-start.33 = (bf16[128,2048]{1,0:T(8,128)(2,1)}, bf16[128,2048]{1,0:T(8,128)(2,1)S(1)}, u32[]{:S(2)}, u32[]{:S(2)}) collective-permute-start(bf16[128,2048]{1,0:T(8,128)(2,1)} %get-tuple-element.310.refs_1_), channel_id=1, source_target_pairs={{0,16},{16,0},{1,17},{17,1},{2,18},{18,2},{3,19},{19,3},{4,20},{20... | collective-permute-start | bytes 1572872 | tf_op jit(solution)/shard_map/ppermute | solution.py:637
  188.2 24.8 %collective-permute-start.32 = (bf16[128,2048]{1,0:T(8,128)(2,1)}, bf16[128,2048]{1,0:T(8,128)(2,1)S(1)}, u32[]{:S(2)}, u32[]{:S(2)}) collective-permute-start(bf16[128,2048]{1,0:T(8,128)(2,1)} %get-tuple-element.309.refs_0_), channel_id=1, source_target_pairs={{0,16},{16,0},{1,17},{17,1},{2,18},{18,2},{3,19},{19,3},{4,20},{20... | collective-permute-start | bytes 1572872 | tf_op jit(solution)/shard_map/ppermute | solution.py:637
  188.8 24.3 %collective-permute-start.31 = (bf16[128,2048]{1,0:T(8,128)(2,1)}, bf16[128,2048]{1,0:T(8,128)(2,1)S(1)}, u32[]{:S(2)}, u32[]{:S(2)}) collective-permute-start(bf16[128,2048]{1,0:T(8,128)(2,1)} %get-tuple-element.310.refs_1_), channel_id=1, source_target_pairs={{0,8},{8,0},{1,9},{9,1},{2,10},{10,2},{3,11},{11,3},{4,12},{12,4},... | collective-permute-start | bytes 1572872 | tf_op jit(solution)/shard_map/ppermute | solution.py:635
  201.0 19.4 %collective-permute-start.34 = (bf16[128,2048]{1,0:T(8,128)(2,1)S(1)}, bf16[128,2048]{1,0:T(8,128)(2,1)S(1)}, u32[]{:S(2)}, u32[]{:S(2)}) collective-permute-start(bf16[128,2048]{1,0:T(8,128)(2,1)S(1)} %collective-permute-done.30.refs_2_), channel_id=1, source_target_pairs={{0,16},{16,0},{1,17},{17,1},{2,18},{18,2},{3,19},{19,3},{4,20},{20... | collective-permute-start | bytes 1572872 | tf_op jit(solution)/shard_map/ppermute | solution.py:637
  202.4 18.0 %collective-permute-start.35 = (bf16[128,2048]{1,0:T(8,128)(2,1)S(1)}, bf16[128,2048]{1,0:T(8,128)(2,1)S(1)}, u32[]{:S(2)}, u32[]{:S(2)}) collective-permute-start(bf16[128,2048]{1,0:T(8,128)(2,1)S(1)} %collective-permute-done.33.refs_5_), channel_id=1, source_target_pairs={{0,8},{8,0},{1,9},{9,1},{2,10},{10,2},{3,11},{11,3},{4,12},{12,4},... | collective-permute-start | bytes 1572872 | tf_op jit(solution)/shard_map/ppermute | solution.py:635
  278.3 25.4 %collective-permute-start.37 = (bf16[352,512]{1,0:T(8,128)(2,1)}, bf16[352,512]{1,0:T(8,128)(2,1)S(1)}, u32[]{:S(2)}, u32[]{:S(2)}) collective-permute-start(bf16[352,512]{1,0:T(8,128)(2,1)} %get-tuple-element.320), channel_id=1, source_target_pairs={{0,2},{1,3},{2,0},{3,1},{4,6},{5,7},{6,4},{7,5},{8,10},{9,11},{10,... | collective-permute-start | bytes 1081352 | tf_op jit(solution)/shard_map/ppermute | solution.py:641
  303.8 25.0 %collective-permute-start.42 = (bf16[1024,2816]{1,0:T(8,128)(2,1)}, bf16[1024,2816]{1,0:T(8,128)(2,1)S(1)}, u32[]{:S(2)}, u32[]{:S(2)}) collective-permute-start(bf16[1024,2816]{1,0:T(8,128)(2,1)} %weight_grad.4), channel_id=1, source_target_pairs={{0,4},{4,0},{1,5},{5,1},{2,6},{6,2},{3,7},{7,3},{8,12},{12,8},{9,1... | collective-permute-start | bytes 17301512 | tf_op jit(solution)/shard_map/ppermute | solution.py:701
  303.9 19.1 %collective-permute-start.38 = (bf16[352,512]{1,0:T(8,128)(2,1)S(1)}, bf16[352,512]{1,0:T(8,128)(2,1)S(1)}, u32[]{:S(2)}, u32[]{:S(2)}) collective-permute-start(bf16[352,512]{1,0:T(8,128)(2,1)S(1)} %copy-done.59), channel_id=1, source_target_pairs={{0,2},{1,3},{2,0},{3,1},{4,6},{5,7},{6,4},{7,5},{8,10},{9,11},{10,... | collective-permute-start | bytes 1081352 | tf_op jit(solution)/shard_map/ppermute | solution.py:641
  323.0 21.1 %collective-permute-start.43 = (bf16[352,512]{1,0:T(8,128)(2,1)S(1)}, bf16[352,512]{1,0:T(8,128)(2,1)S(1)}, u32[]{:S(2)}, u32[]{:S(2)}) collective-permute-start(bf16[352,512]{1,0:T(8,128)(2,1)S(1)} %get-tuple-element.326), channel_id=1, source_target_pairs={{0,2},{1,3},{2,0},{3,1},{4,6},{5,7},{6,4},{7,5},{8,10},{9,11},{10,... | collective-permute-start | bytes 1081352 | tf_op jit(solution)/shard_map/ppermute | solution.py:641
  325.8 18.3 %collective-permute-start.41 = (bf16[128,2048]{1,0:T(8,128)(2,1)S(1)}, bf16[128,2048]{1,0:T(8,128)(2,1)S(1)}, u32[]{:S(2)}, u32[]{:S(2)}) collective-permute-start(bf16[128,2048]{1,0:T(8,128)(2,1)S(1)} %get-tuple-element.474), channel_id=1, source_target_pairs={{0,8},{8,0},{1,9},{9,1},{2,10},{10,2},{3,11},{11,3},{4,12},{12,4},... | collective-permute-start | bytes 1572872 | tf_op jit(solution)/shard_map/ppermute | solution.py:635
  327.3 16.8 %collective-permute-start.40 = (bf16[128,2048]{1,0:T(8,128)(2,1)S(1)}, bf16[128,2048]{1,0:T(8,128)(2,1)S(1)}, u32[]{:S(2)}, u32[]{:S(2)}) collective-permute-start(bf16[128,2048]{1,0:T(8,128)(2,1)S(1)} %get-tuple-element.475), channel_id=1, source_target_pairs={{0,16},{16,0},{1,17},{17,1},{2,18},{18,2},{3,19},{19,3},{4,20},{20... | collective-permute-start | bytes 1572872 | tf_op jit(solution)/shard_map/ppermute | solution.py:637
  345.2 182.0 %reduce-scatter.6.cloned.1.call-start = ((), (), s32[]{:S(2)}) async-start(), calls=%async_computation.8 | async-start | bytes 1310720 | tf_op jit(solution)/shard_map/reduce_scatter | solution.py:711
  345.3 17.3 %collective-permute-start.45 = (bf16[128,2048]{1,0:T(8,128)(2,1)}, bf16[128,2048]{1,0:T(8,128)(2,1)S(1)}, u32[]{:S(2)}, u32[]{:S(2)}) collective-permute-start(bf16[128,2048]{1,0:T(8,128)(2,1)} %get-tuple-element.473), channel_id=1, source_target_pairs={{0,8},{8,0},{1,9},{9,1},{2,10},{10,2},{3,11},{11,3},{4,12},{12,4},... | collective-permute-start | bytes 1572872 | tf_op jit(solution)/shard_map/ppermute | solution.py:635
  345.9 16.7 %collective-permute-start.39 = (bf16[128,2048]{1,0:T(8,128)(2,1)}, bf16[128,2048]{1,0:T(8,128)(2,1)S(1)}, u32[]{:S(2)}, u32[]{:S(2)}) collective-permute-start(bf16[128,2048]{1,0:T(8,128)(2,1)} %get-tuple-element.476), channel_id=1, source_target_pairs={{0,16},{16,0},{1,17},{17,1},{2,18},{18,2},{3,19},{19,3},{4,20},{20... | collective-permute-start | bytes 1572872 | tf_op jit(solution)/shard_map/ppermute | solution.py:637
  348.4 22.2 %collective-permute-start.46 = (bf16[128,2048]{1,0:T(8,128)(2,1)S(1)}, bf16[128,2048]{1,0:T(8,128)(2,1)}, u32[]{:S(2)}, u32[]{:S(2)}) collective-permute-start(bf16[128,2048]{1,0:T(8,128)(2,1)S(1)} %get-tuple-element.471), channel_id=1, source_target_pairs={{0,16},{16,0},{1,17},{17,1},{2,18},{18,2},{3,19},{19,3},{4,20},{20... | collective-permute-start | bytes 1572872 | tf_op jit(solution)/shard_map/ppermute | solution.py:637
  349.9 20.7 %collective-permute-start.44 = (bf16[128,2048]{1,0:T(8,128)(2,1)S(1)}, bf16[128,2048]{1,0:T(8,128)(2,1)}, u32[]{:S(2)}, u32[]{:S(2)}) collective-permute-start(bf16[128,2048]{1,0:T(8,128)(2,1)S(1)} %get-tuple-element.472), channel_id=1, source_target_pairs={{0,8},{8,0},{1,9},{9,1},{2,10},{10,2},{3,11},{11,3},{4,12},{12,4},... | collective-permute-start | bytes 1572872 | tf_op jit(solution)/shard_map/ppermute | solution.py:635
  376.6 18.0 %collective-permute-start.49 = (bf16[128,2048]{1,0:T(8,128)(2,1)}, bf16[128,2048]{1,0:T(8,128)(2,1)S(1)}, u32[]{:S(2)}, u32[]{:S(2)}) collective-permute-start(bf16[128,2048]{1,0:T(8,128)(2,1)} %get-tuple-element.388.refs_7_.refs_4_), channel_id=1, source_target_pairs={{0,16},{16,0},{1,17},{17,1},{2,18},{18,2},{3,19},{19,3},{4,20},{20... | collective-permute-start | bytes 1572872 | tf_op jit(solution)/shard_map/ppermute | solution.py:637
  377.2 18.1 %collective-permute-start.47 = (bf16[128,2048]{1,0:T(8,128)(2,1)}, bf16[128,2048]{1,0:T(8,128)(2,1)S(1)}, u32[]{:S(2)}, u32[]{:S(2)}) collective-permute-start(bf16[128,2048]{1,0:T(8,128)(2,1)} %get-tuple-element.388.refs_7_.refs_4_), channel_id=1, source_target_pairs={{0,8},{8,0},{1,9},{9,1},{2,10},{10,2},{3,11},{11,3},{4,12},{12,4},... | collective-permute-start | bytes 1572872 | tf_op jit(solution)/shard_map/ppermute | solution.py:635
  378.7 24.8 %collective-permute-start.50 = (bf16[128,2048]{1,0:T(8,128)(2,1)}, bf16[128,2048]{1,0:T(8,128)(2,1)S(1)}, u32[]{:S(2)}, u32[]{:S(2)}) collective-permute-start(bf16[128,2048]{1,0:T(8,128)(2,1)} %get-tuple-element.389.refs_8_.refs_5_), channel_id=1, source_target_pairs={{0,8},{8,0},{1,9},{9,1},{2,10},{10,2},{3,11},{11,3},{4,12},{12,4},... | collective-permute-start | bytes 1572872 | tf_op jit(solution)/shard_map/ppermute | solution.py:635
  379.2 24.3 %collective-permute-start.48 = (bf16[128,2048]{1,0:T(8,128)(2,1)}, bf16[128,2048]{1,0:T(8,128)(2,1)S(1)}, u32[]{:S(2)}, u32[]{:S(2)}) collective-permute-start(bf16[128,2048]{1,0:T(8,128)(2,1)} %get-tuple-element.389.refs_8_.refs_5_), channel_id=1, source_target_pairs={{0,16},{16,0},{1,17},{17,1},{2,18},{18,2},{3,19},{19,3},{4,20},{20... | collective-permute-start | bytes 1572872 | tf_op jit(solution)/shard_map/ppermute | solution.py:637
  383.6 65.4 %collective-permute-start.60 = (bf16[128,2048]{1,0:T(8,128)(2,1)}, bf16[128,2048]{1,0:T(8,128)(2,1)S(1)}, u32[]{:S(2)}, u32[]{:S(2)}) collective-permute-start(bf16[128,2048]{1,0:T(8,128)(2,1)} %get-tuple-element.467), channel_id=1, source_target_pairs={{0,8},{8,0},{1,9},{9,1},{2,10},{10,2},{3,11},{11,3},{4,12},{12,4},... | collective-permute-start | bytes 1572872 | tf_op jit(solution)/shard_map/ppermute | solution.py:635
  394.7 31.4 %collective-permute-start.54 = (bf16[128,2048]{1,0:T(8,128)(2,1)}, bf16[128,2048]{1,0:T(8,128)(2,1)}, u32[]{:S(2)}, u32[]{:S(2)}) collective-permute-start(bf16[128,2048]{1,0:T(8,128)(2,1)} %get-tuple-element.469), channel_id=1, source_target_pairs={{0,8},{8,0},{1,9},{9,1},{2,10},{10,2},{3,11},{11,3},{4,12},{12,4},... | collective-permute-start | bytes 1572872 | tf_op jit(solution)/shard_map/ppermute | solution.py:635
  395.3 32.2 %collective-permute-start.53 = (bf16[128,2048]{1,0:T(8,128)(2,1)}, bf16[128,2048]{1,0:T(8,128)(2,1)}, u32[]{:S(2)}, u32[]{:S(2)}) collective-permute-start(bf16[128,2048]{1,0:T(8,128)(2,1)} %get-tuple-element.470), channel_id=1, source_target_pairs={{0,16},{16,0},{1,17},{17,1},{2,18},{18,2},{3,19},{19,3},{4,20},{20... | collective-permute-start | bytes 1572872 | tf_op jit(solution)/shard_map/ppermute | solution.py:637
  403.5 24.1 %collective-permute-start.51 = (bf16[128,2048]{1,0:T(8,128)(2,1)S(1)}, bf16[128,2048]{1,0:T(8,128)(2,1)S(1)}, u32[]{:S(2)}, u32[]{:S(2)}) collective-permute-start(bf16[128,2048]{1,0:T(8,128)(2,1)S(1)} %collective-permute-done.47.refs_7_.refs_6_), channel_id=1, source_target_pairs={{0,16},{16,0},{1,17},{17,1},{2,18},{18,2},{3,19},{19,3},{4,20},{20... | collective-permute-start | bytes 1572872 | tf_op jit(solution)/shard_map/ppermute | solution.py:637
  405.0 29.2 %collective-permute-start.52 = (bf16[128,2048]{1,0:T(8,128)(2,1)S(1)}, bf16[128,2048]{1,0:T(8,128)(2,1)S(1)}, u32[]{:S(2)}, u32[]{:S(2)}) collective-permute-start(bf16[128,2048]{1,0:T(8,128)(2,1)S(1)} %collective-permute-done.48.refs_20_.refs_9_), channel_id=1, source_target_pairs={{0,8},{8,0},{1,9},{9,1},{2,10},{10,2},{3,11},{11,3},{4,12},{12,4},... | collective-permute-start | bytes 1572872 | tf_op jit(solution)/shard_map/ppermute | solution.py:635
  426.1 24.4 %collective-permute-start.58 = (bf16[128,2048]{1,0:T(8,128)(2,1)}, bf16[128,2048]{1,0:T(8,128)(2,1)S(1)}, u32[]{:S(2)}, u32[]{:S(2)}) collective-permute-start(bf16[128,2048]{1,0:T(8,128)(2,1)} %get-tuple-element.468), channel_id=1, source_target_pairs={{0,16},{16,0},{1,17},{17,1},{2,18},{18,2},{3,19},{19,3},{4,20},{20... | collective-permute-start | bytes 1572872 | tf_op jit(solution)/shard_map/ppermute | solution.py:637
  435.5 16.4 %collective-permute-start.55 = (bf16[3,256,128]{2,1,0:T(8,128)(2,1)S(1)}, bf16[3,256,128]{2,1,0:T(8,128)(2,1)S(1)}, u32[]{:S(2)}, u32[]{:S(2)}) collective-permute-start(bf16[3,256,128]{2,1,0:T(8,128)(2,1)S(1)} %pad_maximum_fusion), channel_id=1, source_target_pairs={{0,1},{1,0},{2,3},{3,2},{4,5},{5,4},{6,7},{7,6},{8,9},{9,8},{10,11... | collective-permute-start | bytes 589832 | tf_op jit(solution)/shard_map/ppermute | solution.py:641
  436.3 25.6 %collective-permute-start.56 = (bf16[3,256,128]{2,1,0:T(8,128)(2,1)}, bf16[3,256,128]{2,1,0:T(8,128)(2,1)S(1)}, u32[]{:S(2)}, u32[]{:S(2)}) collective-permute-start(bf16[3,256,128]{2,1,0:T(8,128)(2,1)} %pad_maximum_fusion.1), channel_id=1, source_target_pairs={{0,2},{1,3},{2,0},{3,1},{4,6},{5,7},{6,4},{7,5},{8,10},{9,11},{10,... | collective-permute-start | bytes 589832 | tf_op jit(solution)/shard_map/ppermute | solution.py:641
  438.6 23.3 %collective-permute-start.57 = (bf16[3,256,128]{2,1,0:T(8,128)(2,1)}, bf16[3,256,128]{2,1,0:T(8,128)(2,1)}, u32[]{:S(2)}, u32[]{:S(2)}) collective-permute-start(bf16[3,256,128]{2,1,0:T(8,128)(2,1)} %pad_maximum_fusion.2), channel_id=1, source_target_pairs={{0,3},{1,2},{2,1},{3,0},{4,7},{5,6},{6,5},{7,4},{8,11},{9,10},{10,... | collective-permute-start | bytes 589832 | tf_op jit(solution)/shard_map/ppermute | solution.py:641
  452.0 23.2 %collective-permute-start.65 = (bf16[256,2048]{1,0:T(8,128)(2,1)}, bf16[256,2048]{1,0:T(8,128)(2,1)S(1)}, u32[]{:S(2)}, u32[]{:S(2)}) collective-permute-start(bf16[256,2048]{1,0:T(8,128)(2,1)} %out_gradient.2), channel_id=1, source_target_pairs={{0,4},{4,0},{1,5},{5,1},{2,6},{6,2},{3,7},{7,3},{8,12},{12,8},{9,1... | collective-permute-start | bytes 3145736 | tf_op jit(solution)/shard_map/ppermute | solution.py:863
  464.9 19.2 %collective-permute-start.68 = (bf16[64,2816]{1,0:T(8,128)(2,1)}, bf16[64,2816]{1,0:T(8,128)(2,1)S(1)}, u32[]{:S(2)}, u32[]{:S(2)}) collective-permute-start(bf16[64,2816]{1,0:T(8,128)(2,1)} %get-tuple-element.481), channel_id=1, source_target_pairs={{0,24},{8,16},{16,8},{24,0},{1,25},{9,17},{17,9},{25,1},{2,26},{10... | collective-permute-start | bytes 1081352 | tf_op jit(solution)/shard_map/ppermute | solution.py:638
  466.6 17.9 %collective-permute-start.67 = (bf16[64,2816]{1,0:T(8,128)(2,1)}, bf16[64,2816]{1,0:T(8,128)(2,1)S(1)}, u32[]{:S(2)}, u32[]{:S(2)}) collective-permute-start(bf16[64,2816]{1,0:T(8,128)(2,1)} %get-tuple-element.482), channel_id=1, source_target_pairs={{0,16},{16,0},{1,17},{17,1},{2,18},{18,2},{3,19},{19,3},{4,20},{20... | collective-permute-start | bytes 1081352 | tf_op jit(solution)/shard_map/ppermute | solution.py:637
  467.1 17.4 %collective-permute-start.66 = (bf16[64,2816]{1,0:T(8,128)(2,1)}, bf16[64,2816]{1,0:T(8,128)(2,1)S(1)}, u32[]{:S(2)}, u32[]{:S(2)}) collective-permute-start(bf16[64,2816]{1,0:T(8,128)(2,1)} %get-tuple-element.483), channel_id=1, source_target_pairs={{0,8},{8,0},{1,9},{9,1},{2,10},{10,2},{3,11},{11,3},{4,12},{12,4},... | collective-permute-start | bytes 1081352 | tf_op jit(solution)/shard_map/ppermute | solution.py:635
  482.4 17.2 %collective-permute-start.69 = (bf16[352,512]{1,0:T(8,128)(2,1)}, bf16[352,512]{1,0:T(8,128)(2,1)S(1)}, u32[]{:S(2)}, u32[]{:S(2)}) collective-permute-start(bf16[352,512]{1,0:T(8,128)(2,1)} %get-tuple-element.409), channel_id=1, source_target_pairs={{0,2},{1,3},{2,0},{3,1},{4,6},{5,7},{6,4},{7,5},{8,10},{9,11},{10,... | collective-permute-start | bytes 1081352 | tf_op jit(solution)/shard_map/ppermute | solution.py:641
  500.8 59.7 %reduce-scatter.8.cloned.1.call-start = ((), (), s32[]{:S(2)}) async-start(), calls=%async_computation.9 | async-start | bytes 1638400 | tf_op jit(solution)/shard_map/reduce_scatter | solution.py:711
  527.2 17.4 %collective-permute-start.75 = (bf16[128,2048]{1,0:T(8,128)(2,1)}, bf16[128,2048]{1,0:T(8,128)(2,1)S(1)}, u32[]{:S(2)}, u32[]{:S(2)}) collective-permute-start(bf16[128,2048]{1,0:T(8,128)(2,1)} %get-tuple-element.461), channel_id=1, source_target_pairs={{0,8},{8,0},{1,9},{9,1},{2,10},{10,2},{3,11},{11,3},{4,12},{12,4},... | collective-permute-start | bytes 1572872 | tf_op jit(solution)/shard_map/ppermute | solution.py:635
  528.8 15.9 %collective-permute-start.70 = (bf16[128,2048]{1,0:T(8,128)(2,1)}, bf16[128,2048]{1,0:T(8,128)(2,1)}, u32[]{:S(2)}, u32[]{:S(2)}) collective-permute-start(bf16[128,2048]{1,0:T(8,128)(2,1)} %get-tuple-element.464), channel_id=1, source_target_pairs={{0,16},{16,0},{1,17},{17,1},{2,18},{18,2},{3,19},{19,3},{4,20},{20... | collective-permute-start | bytes 1572872 | tf_op jit(solution)/shard_map/ppermute | solution.py:637
  532.8 20.7 %collective-permute-start.76 = (bf16[128,2048]{1,0:T(8,128)(2,1)}, bf16[128,2048]{1,0:T(8,128)(2,1)}, u32[]{:S(2)}, u32[]{:S(2)}) collective-permute-start(bf16[128,2048]{1,0:T(8,128)(2,1)} %get-tuple-element.459), channel_id=1, source_target_pairs={{0,16},{16,0},{1,17},{17,1},{2,18},{18,2},{3,19},{19,3},{4,20},{20... | collective-permute-start | bytes 1572872 | tf_op jit(solution)/shard_map/ppermute | solution.py:637
  533.4 20.1 %collective-permute-start.74 = (bf16[128,2048]{1,0:T(8,128)(2,1)}, bf16[128,2048]{1,0:T(8,128)(2,1)}, u32[]{:S(2)}, u32[]{:S(2)}) collective-permute-start(bf16[128,2048]{1,0:T(8,128)(2,1)} %get-tuple-element.460), channel_id=1, source_target_pairs={{0,8},{8,0},{1,9},{9,1},{2,10},{10,2},{3,11},{11,3},{4,12},{12,4},... | collective-permute-start | bytes 1572872 | tf_op jit(solution)/shard_map/ppermute | solution.py:635
  554.7 19.3 %collective-permute-start.80 = (bf16[176,2048]{1,0:T(8,128)(2,1)}, bf16[176,2048]{1,0:T(8,128)(2,1)}, u32[]{:S(2)}, u32[]{:S(2)}) collective-permute-start(bf16[176,2048]{1,0:T(8,128)(2,1)} %dynamic-slice_bitcast_fusion.1), channel_id=1, source_target_pairs={{0,1},{1,0},{2,3},{3,2},{4,5},{5,4},{6,7},{7,6},{8,9},{9,8},{10,11... | collective-permute-start | bytes 2162696 | tf_op jit(solution)/shard_map/ppermute | solution.py:641
  (98 other events, 901.2 us)
Sparse Core Ops, SparseCore 0:
  24.7 34.1 all-gather.6
  60.4 43.4 all-gather.4
  111.2 106.9 all-gather.10
  219.6 58.7 all-gather.8
  345.3 105.9 reduce-scatter.3
  500.9 26.2 reduce-scatter.5
  529.6 30.5 reduce-scatter.7

commit v7 on v6

--- a/solution.py
+++ b/solution.py
@@ -874,7 +874,10 @@
             part_out = out_gradient(mixed, db_pieces, 1, jnp.zeros((), jnp.int32))
             part_out = lax.psum_scatter(part_out, "rep", scatter_dimension=0, tiled=True)
         raw_gate_up = collect(after(sum_gate_up, keys_near), t)
-        keys_last, part_out, raw_gate_up = phase(keys_last, part_out, raw_gate_up)
+        come = send_down(keys_near)
+        keys_last, part_out, raw_gate_up, down_come[-1] = phase(
+            keys_last, part_out, raw_gate_up, come
+        )
         grad_proj, scaled_proj = finish_keys(
             [v[2] for v in back_of],
             keys_near,
@@ -886,12 +889,11 @@
             sine,
         )
         parts = by_member(nt(grad_proj, qkv).astype(bf16))
-        parts, down_come[-1] = phase(parts, send_down(keys_near))
         across = phase(*halves(parts[3]))
         far_back = swap(across[0], 2), swap(across[1], 1)
         sent = over_reps_first(x_all, after(scaled_proj, across))
         part_qkv = over_reps_last(x_all, after(scaled_proj, sent), sent)
-        sum_out = owned(after(part_out, across))
+        sum_out = owned(after(part_out, keys_last))
         far_back, part_qkv, sum_out = phase(far_back, part_qkv, sum_out)
         sum_qkv = owned(part_qkv)
         near = scatter_near(parts, far_back)

time: 591 us -> 586 us (level)
  waiting for transfers between devices: 165 us -> 159 us
    unnamed x149 -> x145, local copies, waits for them, and re-layouts: 11.9 us -> 14.7 us
  transfers between devices with their start and end apart: 88 -> 88, of which waited for: 33 -> 32; matrix products, arithmetic and copies ran while one was open for 15% -> 15% of each run, Pallas kernels for 35% -> 35%
where the time goes in v7:
time: 586 us; the launch traced here: 578 us
  Pallas kernels  207 us (35%)
  waiting for transfers between devices  159 us (27%)
  starting transfers between devices  90.1 us (15%)
  matrix products  47.2 us (8%)
  local copies, waits for them, and re-layouts  41 us (7%)
  other arithmetic  18.7 us (3%)
  between operations  15.5 us (3%)
    pallas_call x22, Pallas kernels, small_call(): pl.pallas_call(kernel, grid=(1,), in_specs=specs, out_specs=[whole_block(...  141 us
    ppermute x29, waiting for transfers between devices, swap(): return lax.ppermute(v, 'ty', pair)  59.6 us
    ppermute x29, waiting for transfers between devices, swap(): return lax.ppermute(v, 'tx', pair)  42.9 us
    ppermute x29, starting transfers between devices, swap(): return lax.ppermute(v, 'tx', pair)  35.1 us
    pallas_call x4, Pallas kernels, weight_grad(): pl.pallas_call(kernel, grid_spec=pltpu.PrefetchScalarGridSpec(num_scalar_...  34.1 us
    ppermute x29, starting transfers between devices, swap(): return lax.ppermute(v, 'ty', pair)  28.4 us
    ppermute x14, waiting for transfers between devices, swap_ctx(): return lax.ppermute(v, 'ctx', [(i, i ^ j) for i in range(ctxs)]) if j else v  27.1 us
    dot_general x2, matrix products, nt(): lax.dot_general(left, right, (((1,), (1,)), ((), ())), preferred_element_...  22.7 us
  transfers between devices with their start and end apart: 88, of which 32 were waited for; matrix products, arithmetic and copies ran while one was open for 15% of the time, Pallas kernels for 35%

profile of v7, /device:TPU:0, one launch (start us, length us, event | category | flops | bytes accessed | tf_op | source)
XLA Modules:
  0.0 578.3 jit_solution(5065932047271946765)
XLA Ops:
  10.5 2.5 hold_tokens.1
  14.0 3.0 collective-permute-start
  19.8 3.9 collective-permute-done.1
  31.0 7.6 %collective-permute-done.5 = s32[1,8]{0,1:T(8,128)S(1)} collective-permute-done((s32[1,8]{0,1:T(8,128)S(1)}, s32[1,8]{0,1:T(8,128)S(1)}, u32[]{:S(2)}, u32[]{:S(2)}) %collective-permute-start.5) | collective-permute-done | bytes 64 | tf_op jit(solution)/shard_map/ppermute | solution.py:638
  44.0 3.3 split_gate_up.1
  47.3 7.5 %collective-permute-done.8.refs_4_ = bf16[128,2048]{1,0:T(8,128)(2,1)S(1)} collective-permute-done((bf16[128,2048]{1,0:T(8,128)(2,1)}, bf16[128,2048]{1,0:T(8,128)(2,1)S(1)}, u32[]{:S(2)}, u32[]{:S(2)}) %collective-permute-start.8) | collective-permute-done | bytes 524320 | tf_op jit(solution)/shard_map/ppermute | solution.py:637
  55.8 8.1 %collective-permute-done.11.refs_7_ = bf16[128,2048]{1,0:T(8,128)(2,1)S(1)} collective-permute-done((bf16[128,2048]{1,0:T(8,128)(2,1)S(1)}, bf16[128,2048]{1,0:T(8,128)(2,1)S(1)}, u32[]{:S(2)}, u32[]{:S(2)}) %collective-permute-start.11) | collective-permute-done | bytes 524320 | tf_op jit(solution)/shard_map/ppermute | solution.py:635
  64.7 2.3 constant_dynamic-slice_fusion
  71.8 7.5 %project.1 = (bf16[4,256,128]{2,1,0:T(8,128)(2,1)}, bf16[512,256]{1,0:T(8,128)(2,1)}, bf16[512,256]{1,0:T(8,128)(2,1)}, bf16[512,256]{1,0:T(8,128)(2,1)}, bf16[5...) custom-call(bf16[128,2048]{1,0:T(8,128)(2,1)} %get-tuple-element.261.refs_, ...), custom_call_target="tpu_custom_call" | custom-call | flops 2684354560 | bytes 8392704 | tf_op jit(solution)/shard_map/project/pallas_call | solution.py:66
  79.3 3.7 collective-permute-start.14
  86.5 4.4 join_rows.3.left_ref
  92.3 3.4 collective-permute-done.14.refs_4_.refs_9_.refs_3_.refs_15_
  95.7 14.5 %collective-permute-done.13.refs_3_.refs_8_.refs_2_.refs_14_ = bf16[4,256,128]{2,1,0:T(8,128)(2,1)} collective-permute-done((bf16[4,256,128]{2,1,0:T(8,128)(2,1)}, bf16[4,256,128]{2,1,0:T(8,128)(2,1)}, u32[]{:S(2)}, u32[]{:S(2)}) %collective-permute-start.13) | collective-permute-done | bytes 262176 | tf_op jit(solution)/shard_map/ppermute | solution.py:641
  116.6 9.1 %attend.3 = (bf16[512,256]{1,0:T(8,128)(2,1)}, f32[8,256]{1,0:T(8,128)}, bf16[256,2048]{1,0:T(8,128)(2,1)}) custom-call(s32[4,8]{1,0:T(4,128)} %copy.30.order_ref, bf16[512,2048]{1,0:T(8,128)(2,1)} %all-gather.5.cloned.1.call-done.wo_ref, bf16[512,256]{1,0:T(8,128)(2,1)} %get-tuple-element.252.refs_0_.refs_4_, ...), custom_call_target="tpu_custom_call" | custom-call | flops 2684354560 | bytes 4726912 | tf_op jit(solution)/shard_map/attend/pallas_call | solution.py:66
  130.9 15.5 %attend.4 = (bf16[512,256]{1,0:T(8,128)(2,1)}, f32[8,256]{1,0:T(8,128)}, bf16[256,2048]{1,0:T(8,128)(2,1)}, bf16[512,256]{1,0:T(8,128)(2,1)}, f32[8,256]{1,0:T(8,128)}, /*index=5*/bf16[256,2048]{1,0:T(8,128)(2,1)}) custom-call(s32[4,8]{1,0:T(4,128)} %copy.30.order_ref, bf16[512,2048]{1,0:T(8,128)(2,1)} %all-gather.5.cloned.1.call-done.wo_ref, ...), custom_call_target="tpu_custom_call" | custom-call | flops 5368709120 | bytes 7356544 | tf_op jit(solution)/shard_map/attend/pallas_call | solution.py:66
  159.1 4.4 join_rows.4.g_ref
  163.5 9.2 %attend.5 = (bf16[512,256]{1,0:T(8,128)(2,1)}, f32[8,256]{1,0:T(8,128)}, f32[256,2048]{1,0:T(8,128)}) custom-call(s32[4,8]{1,0:T(4,128)} %copy.30.order_ref, bf16[512,2048]{1,0:T(8,128)(2,1)} %all-gather.5.cloned.1.call-done.wo_ref, bf16[512,256]{1,0:T(8,128)(2,1)} %get-tuple-element.288.refs_0_.refs_4_, ...), custom_call_target="tpu_custom_call" | custom-call | flops 2684354560 | bytes 5775488 | tf_op jit(solution)/shard_map/attend/pallas_call | solution.py:66
  172.7 6.2 %collective-permute-done.29.refs_4_ = bf16[128,2048]{1,0:T(8,128)(2,1)S(1)} collective-permute-done((bf16[128,2048]{1,0:T(8,128)(2,1)S(1)}, bf16[128,2048]{1,0:T(8,128)(2,1)S(1)}, u32[]{:S(2)}, u32[]{:S(2)}) %collective-permute-start.29) | collective-permute-done | bytes 524320 | tf_op jit(solution)/shard_map/ppermute | solution.py:637
  180.9 5.0 finish_middle.1
  190.0 11.0 %collective-permute-done.30.refs_2_ = bf16[128,2048]{1,0:T(8,128)(2,1)S(1)} collective-permute-done((bf16[128,2048]{1,0:T(8,128)(2,1)}, bf16[128,2048]{1,0:T(8,128)(2,1)S(1)}, u32[]{:S(2)}, u32[]{:S(2)}) %collective-permute-start.30) | collective-permute-done | bytes 524320 | tf_op jit(solution)/shard_map/ppermute | solution.py:635
  203.3 9.8 %collective-permute-done.32.refs_4_ = bf16[128,2048]{1,0:T(8,128)(2,1)S(1)} collective-permute-done((bf16[128,2048]{1,0:T(8,128)(2,1)}, bf16[128,2048]{1,0:T(8,128)(2,1)S(1)}, u32[]{:S(2)}, u32[]{:S(2)}) %collective-permute-start.32) | collective-permute-done | bytes 524320 | tf_op jit(solution)/shard_map/ppermute | solution.py:637
  213.1 7.3 %collective-permute-done.34.refs_6_ = bf16[128,2048]{1,0:T(8,128)(2,1)S(1)} collective-permute-done((bf16[128,2048]{1,0:T(8,128)(2,1)S(1)}, bf16[128,2048]{1,0:T(8,128)(2,1)S(1)}, u32[]{:S(2)}, u32[]{:S(2)}) %collective-permute-start.34) | collective-permute-done | bytes 524320 | tf_op jit(solution)/shard_map/ppermute | solution.py:637
  221.4 19.7 %activate.1 = (bf16[1024,1408]{1,0:T(8,128)(2,1)}, bf16[1024,2816]{1,0:T(8,128)(2,1)}) custom-call(bf16[128,2048]{1,0:T(8,128)(2,1)} %get-tuple-element.308.refs_0_, bf16[128,2048]{1,0:T(8,128)(2,1)} %get-tuple-element.309.refs_1_, bf16[128,2048]{1,0:T(8,128)(2,1)} %copy-done.26, bf16[128,2048]{1,0:T(8,128)(2,1)} %copy-done.29, ...), custom_call_target="tpu_custom_call" | custom-call | flops 11811160064 | bytes 24379392 | tf_op jit(solution)/shard_map/activate/pallas_call | solution.py:440
  241.1 6.1 %convolution_convert_fusion.3 = bf16[704,2048]{1,0:T(8,128)(2,1)S(1)} fusion(bf16[1024,2048]{1,0:T(8,128)(2,1)} %join_rows.4.g_ref, bf16[1024,1408]{1,0:T(8,128)(2,1)} %get-tuple-element.328, s32[]{:T(128)S(6)} %select_n.100), kind=kOutput, calls=%fused_computation.4 | convolution fusion | flops 2954231808 | bytes 8650756 | tf_op jit(solution)/shard_map/dot_general | solution.py:43
  247.3 4.4 join_rows.5.left_ref
  252.7 7.2 %add_convert_fusion = bf16[704,2048]{1,0:T(8,128)(2,1)S(1)} fusion(bf16[704,2048]{1,0:T(8,128)(2,1)} %collective-permute-done.36, bf16[1024,2048]{1,0:T(8,128)(2,1)} %join_rows.4.g_ref, bf16[1024,1408]{1,0:T(8,128)(2,1)} %get-tuple-element.328, s32[]{:T(128)S(6)} %select_n.99), kind=kOutput, calls=%fused_computation | convolution fusion | flops 2957115392 | bytes 11534340 | tf_op jit(solution)/shard_map/dot_general | solution.py:43
  261.9 16.4 %all-gather.9.cloned.1.call-done.down_ref = bf16[1408,2048]{1,0:T(8,128)(2,1)} async-done(((bf16[176,2048]{1,0:T(8,128)(2,1)}), bf16[1408,2048]{1,0:T(8,128)(2,1)}) %all-gather.9.cloned.1.call-update) | async-done | bytes 5767184 | tf_op jit(solution)/shard_map/all_gather | solution.py:685
  279.4 12.8 %activate_back.1.right_ref = bf16[1024,2816]{1,0:T(8,128)(2,1)} custom-call(bf16[1024,2048]{1,0:T(8,128)(2,1)} %join_rows.4.g_ref, bf16[1408,2048]{1,0:T(8,128)(2,1)} %all-gather.9.cloned.1.call-done.down_ref, bf16[1024,2816]{1,0:T(8,128)(2,1)} %get-tuple-element.316.slope_ref), custom_call_target="tpu_custom_call" | custom-call | flops 5905580032 | bytes 21495808 | tf_op jit(solution)/shard_map/activate_back/pallas_call | solution.py:472
  292.3 11.6 %weight_grad.4 = bf16[1024,2816]{1,0:T(8,128)(2,1)} custom-call(s32[1]{0:T(128)} %bitcast.7.index_ref, bf16[1024,2048]{1,0:T(8,128)(2,1)} %join_rows.5.left_ref, bf16[1024,2816]{1,0:T(8,128)(2,1)} %activate_back.1.right_ref), custom_call_target="tpu_custom_call" | custom-call | flops 5905580032 | bytes 19398656 | tf_op jit(solution)/shard_map/weight_grad/pallas_call | solution.py:505
  305.9 16.9 %convolution_convert_fusion = bf16[1024,2048]{1,0:T(8,128)(2,1)S(1)} fusion(bf16[1024,2816]{1,0:T(8,128)(2,1)} %activate_back.1.right_ref, bf16[2048,2816]{1,0:T(8,128)(2,1)} %all-gather.11.cloned.1.call-done.refs_8_), kind=kOutput, calls=%fused_computation.1 | convolution fusion | flops 11813257216 | bytes 21495808 | tf_op jit(solution)/shard_map/dot_general | solution.py:39
  328.8 2.5 copy-done.70
  331.4 12.8 %weight_grad.5 = bf16[1024,2816]{1,0:T(8,128)(2,1)} custom-call(s32[1]{0:T(128)} %bitcast.15.index_ref, bf16[1024,2048]{1,0:T(8,128)(2,1)} %join_rows.5.left_ref, bf16[1024,2816]{1,0:T(8,128)(2,1)} %activate_back.1.right_ref, bf16[1024,2816]{1,0:T(8,128)(2,1)} %copy-done.70), custom_call_target="tpu_custom_call" | custom-call | flops 5905580032 | bytes 19398656 | tf_op jit(solution)/shard_map/weight_grad/pallas_call | solution.py:505
  351.5 11.2 %convolution_convert_fusion.2 = bf16[1024,2048]{1,0:T(8,128)(2,1)} fusion(bf16[1024,1408]{1,0:T(8,128)(2,1)S(1)} %copy-done.17, bf16[1408,2048]{1,0:T(8,128)(2,1)} %all-gather.9.cloned.1.call-done.down_ref), kind=kOutput, calls=%fused_computation.3 | convolution fusion | flops 5907677184 | bytes 12845056 | tf_op jit(solution)/shard_map/dot_general | solution.py:35
  362.8 8.0 %collective-permute-done.46.refs_4_ = bf16[128,2048]{1,0:T(8,128)(2,1)} collective-permute-done((bf16[128,2048]{1,0:T(8,128)(2,1)S(1)}, bf16[128,2048]{1,0:T(8,128)(2,1)}, u32[]{:S(2)}, u32[]{:S(2)}) %collective-permute-start.46) | collective-permute-done | bytes 524320 | tf_op jit(solution)/shard_map/ppermute | solution.py:637
  370.7 6.0 %finish_norm_back.2 = (f32[256,2048]{1,0:T(8,128)}, bf16[128,2048]{1,0:T(8,128)(2,1)}, bf16[128,2048]{1,0:T(8,128)(2,1)}) custom-call(bf16[256,2048]{1,0:T(8,128)(2,1)} %g_ref.1, f32[256,2048]{1,0:T(8,128)} %get-tuple-element.419.x_ref.mid_ref, f32[256,1]{1,0:T(8,128)} %get-tuple-element.300.inv_ref, bf16[4,256,2048]{2,1,0:T(8,128)(2,1)} %bitcast.106, ...), custom_call_target="tpu_custom_call" | custom-call | flops 12583936 | bytes 12583936 | tf_op jit(solution)/shard_map/finish_norm_back/pallas_call | solution.py:66
  380.8 2.9 fusion.8
  385.1 9.6 %attend_back.3 = (bf16[256,512]{1,0:T(8,128)(2,1)}, bf16[256,512]{1,0:T(8,128)(2,1)}, f32[256,128]{1,0:T(8,128)}, bf16[768,128]{1,0:T(8,128)(2,1)}) custom-call(s32[4,8]{1,0:T(4,128)} %copy.30.order_ref, bf16[512,2048]{1,0:T(8,128)(2,1)} %all-gather.5.cloned.1.call-done.wo_ref, bf16[4,256,128]{2,1,0:T(8,128)(2,1)} %get-tuple-element.269.refs_1_.refs_6_.refs_0_.refs_12_, ...), custom_call_target="tpu_custom_call" | custom-call | flops 5905580032 | bytes 5842048 | tf_op jit(solution)/shard_map/attend_back/pallas_call | solution.py:66
  396.0 7.6 %collective-permute-done.50.refs_8_.refs_7_ = bf16[128,2048]{1,0:T(8,128)(2,1)S(1)} collective-permute-done((bf16[128,2048]{1,0:T(8,128)(2,1)}, bf16[128,2048]{1,0:T(8,128)(2,1)S(1)}, u32[]{:S(2)}, u32[]{:S(2)}) %collective-permute-start.50) | collective-permute-done | bytes 524320 | tf_op jit(solution)/shard_map/ppermute | solution.py:635
  406.6 17.1 %attend_back.4 = (bf16[256,512]{1,0:T(8,128)(2,1)}, bf16[256,512]{1,0:T(8,128)(2,1)}, f32[256,128]{1,0:T(8,128)}, bf16[768,128]{1,0:T(8,128)(2,1)}, bf16[256,512...) custom-call(s32[4,8]{1,0:T(4,128)} %copy.30.order_ref, ...), custom_call_target="tpu_custom_call" | custom-call | flops 11811160064 | bytes 9586816 | tf_op jit(solution)/shard_map/attend_back/pallas_call | solution.py:66
  423.7 2.4 collective-permute-done.54
  427.6 6.7 %collective-permute-done.52.refs_11_.refs_8_ = bf16[128,2048]{1,0:T(8,128)(2,1)S(1)} collective-permute-done((bf16[128,2048]{1,0:T(8,128)(2,1)S(1)}, bf16[128,2048]{1,0:T(8,128)(2,1)S(1)}, u32[]{:S(2)}, u32[]{:S(2)}) %collective-permute-start.52) | collective-permute-done | bytes 524320 | tf_op jit(solution)/shard_map/ppermute | solution.py:635
  438.7 2.7 collective-permute-start.57
  441.4 2.9 add_convert_fusion.3
  444.3 4.7 out_gradient.2
  452.0 9.9 %attend_back.5 = (bf16[256,512]{1,0:T(8,128)(2,1)}, bf16[256,512]{1,0:T(8,128)(2,1)}, f32[256,128]{1,0:T(8,128)}, bf16[768,128]{1,0:T(8,128)(2,1)}) custom-call(s32[4,8]{1,0:T(4,128)} %copy.30.order_ref, bf16[512,2048]{1,0:T(8,128)(2,1)} %all-gather.5.cloned.1.call-done.wo_ref, bf16[4,256,128]{2,1,0:T(8,128)(2,1)} %get-tuple-element.269.refs_1_.refs_6_.refs_0_.refs_12_, ...), custom_call_target="tpu_custom_call" | custom-call | flops 5905580032 | bytes 5842048 | tf_op jit(solution)/shard_map/attend_back/pallas_call | solution.py:66
  465.0 2.9 collective-permute-start.69
  467.9 2.4 dynamic-slice_bitcast_fusion.2
  470.3 2.6 collective-permute-start.68
  473.5 6.6 %collective-permute-done.63.refs_8_ = bf16[1,256,128]{2,1,0:T(8,128)(2,1)S(1)} collective-permute-done((bf16[1,256,128]{2,1,0:T(8,128)(2,1)S(1)}, bf16[1,256,128]{2,1,0:T(8,128)(2,1)S(1)}, u32[]{:S(2)}, u32[]{:S(2)}) %collective-permute-start.63) | collective-permute-done | bytes 65568 | tf_op jit(solution)/shard_map/ppermute | solution.py:641
  481.9 5.0 out_gradient.3
  486.9 2.3 collective-permute-done.62.refs_7_
  490.7 4.4 finish_keys.1
  495.1 5.8 convolution_convert_fusion.1
  504.1 4.8 weight_grad.6
  513.2 4.8 weight_grad.7
  518.1 5.2 collective-permute-done.71
  525.7 2.6 add_convert_fusion.1
  530.3 4.5 merge_gate_up.1
  534.8 3.9 finish_layer.1
  541.0 8.6 %collective-permute-done.76.refs_4_ = bf16[128,2048]{1,0:T(8,128)(2,1)} collective-permute-done((bf16[128,2048]{1,0:T(8,128)(2,1)}, bf16[128,2048]{1,0:T(8,128)(2,1)}, u32[]{:S(2)}, u32[]{:S(2)}) %collective-permute-start.76) | collective-permute-done | bytes 524320 | tf_op jit(solution)/shard_map/ppermute | solution.py:637
  550.8 5.8 %finish_norm_back.3 = f32[256,2048]{1,0:T(8,128)} custom-call(f32[256,2048]{1,0:T(8,128)} %get-tuple-element.439.g_ref, bf16[256,2048]{1,0:T(8,128)(2,1)} %x_ref.4, f32[256,1]{1,0:T(8,128)} %get-tuple-element.337.refs_9_.refs_18_.inv_ref, bf16[4,256,2048]{2,1,0:T(8,128)(2,1)} %bitcast.108, bf16[128,2048]{1,0:T(8,128)(2,1)} %collective-permute-done.70.refs_1_, ...), custom_call_target="tpu_custom_call" | custom-call | flops 11535360 | bytes 11535360 | tf_op jit(solution)/shard_map/finish_norm_back/pallas_call | solution.py:66
  561.8 2.3 collective-permute-done.79.refs_3_
  565.5 2.3 merge_qkv.1
  568.7 2.4 bitcast_add_fusion
  (350 shorter events, 132.0 us)
Async XLA Ops:
  7.2 64.6 %all-gather.7.cloned.1.call-start = ((), (), s32[]{:S(2)}) async-start(), calls=%async_computation.4 | async-start | bytes 2949120 | tf_op jit(solution)/shard_map/all_gather | solution.py:685
  24.5 92.1 %all-gather.5.cloned.1.call-start = ((), (), s32[]{:S(2)}) async-start(), calls=%async_computation.3 | async-start | bytes 2359296 | tf_op jit(solution)/shard_map/all_gather | solution.py:685
  31.0 189.5 %all-gather.11.cloned.1.call-start = ((), (), s32[]{:S(2)}) async-start(), calls=%async_computation.6 | async-start | bytes 12976128 | tf_op jit(solution)/shard_map/all_gather | solution.py:685
  41.5 22.4 %collective-permute-start.11 = (bf16[128,2048]{1,0:T(8,128)(2,1)S(1)}, bf16[128,2048]{1,0:T(8,128)(2,1)S(1)}, u32[]{:S(2)}, u32[]{:S(2)}) collective-permute-start(bf16[128,2048]{1,0:T(8,128)(2,1)S(1)} %collective-permute-done.7.refs_5_), channel_id=1, source_target_pairs={{0,8},{8,0},{1,9},{9,1},{2,10},{10,2},{3,11},{11,3},{4,12},{12,4},... | collective-permute-start | bytes 1572872 | tf_op jit(solution)/shard_map/ppermute | solution.py:635
  42.8 21.9 %collective-permute-start.10 = (bf16[128,2048]{1,0:T(8,128)(2,1)S(1)}, bf16[128,2048]{1,0:T(8,128)(2,1)}, u32[]{:S(2)}, u32[]{:S(2)}) collective-permute-start(bf16[128,2048]{1,0:T(8,128)(2,1)S(1)} %collective-permute-done.6.refs_2_), channel_id=1, source_target_pairs={{0,16},{16,0},{1,17},{17,1},{2,18},{18,2},{3,19},{19,3},{4,20},{20... | collective-permute-start | bytes 1572872 | tf_op jit(solution)/shard_map/ppermute | solution.py:637
  67.0 16.0 %collective-permute-start.17 = (bf16[1,64,2816]{2,1,0:T(8,128)(2,1)}, bf16[1,64,2816]{2,1,0:T(8,128)(2,1)S(1)}, u32[]{:S(2)}, u32[]{:S(2)}) collective-permute-start(bf16[1,64,2816]{2,1,0:T(8,128)(2,1)} %get-tuple-element.483), channel_id=1, source_target_pairs={{0,24},{8,16},{16,8},{24,0},{1,25},{9,17},{17,9},{25,1},{2,26},{10... | collective-permute-start | bytes 1081352 | tf_op jit(solution)/shard_map/ppermute | solution.py:638
  68.4 15.4 %collective-permute-start.16 = (bf16[1,64,2816]{2,1,0:T(8,128)(2,1)}, bf16[1,64,2816]{2,1,0:T(8,128)(2,1)S(1)}, u32[]{:S(2)}, u32[]{:S(2)}) collective-permute-start(bf16[1,64,2816]{2,1,0:T(8,128)(2,1)} %get-tuple-element.484), channel_id=1, source_target_pairs={{0,16},{16,0},{1,17},{17,1},{2,18},{18,2},{3,19},{19,3},{4,20},{20... | collective-permute-start | bytes 1081352 | tf_op jit(solution)/shard_map/ppermute | solution.py:637
  79.3 16.3 %collective-permute-start.14 = (bf16[4,256,128]{2,1,0:T(8,128)(2,1)}, bf16[4,256,128]{2,1,0:T(8,128)(2,1)}, u32[]{:S(2)}, u32[]{:S(2)}) collective-permute-start(bf16[4,256,128]{2,1,0:T(8,128)(2,1)} %get-tuple-element.269.refs_1_.refs_6_.refs_0_.refs_12_), channel_id=1, source_target_pairs={{0,3},{1,2},{2,1},{3,0},{4,7},{5,6},{6,5},{7,4},{8,11},{9,10},{10,... | collective-permute-start | bytes 786440 | tf_op jit(solution)/shard_map/ppermute | solution.py:641
  83.0 27.1 %collective-permute-start.13 = (bf16[4,256,128]{2,1,0:T(8,128)(2,1)}, bf16[4,256,128]{2,1,0:T(8,128)(2,1)}, u32[]{:S(2)}, u32[]{:S(2)}) collective-permute-start(bf16[4,256,128]{2,1,0:T(8,128)(2,1)} %get-tuple-element.269.refs_1_.refs_6_.refs_0_.refs_12_), channel_id=1, source_target_pairs={{0,2},{1,3},{2,0},{3,1},{4,6},{5,7},{6,4},{7,5},{8,10},{9,11},{10,... | collective-permute-start | bytes 786440 | tf_op jit(solution)/shard_map/ppermute | solution.py:641
  83.0 27.1 %collective-permute-start.12 = (bf16[4,256,128]{2,1,0:T(8,128)(2,1)}, bf16[4,256,128]{2,1,0:T(8,128)(2,1)}, u32[]{:S(2)}, u32[]{:S(2)}) collective-permute-start(bf16[4,256,128]{2,1,0:T(8,128)(2,1)} %get-tuple-element.269.refs_1_.refs_6_.refs_0_.refs_12_), channel_id=1, source_target_pairs={{0,1},{1,0},{2,3},{3,2},{4,5},{5,4},{6,7},{7,6},{8,9},{9,8},{10,11... | collective-permute-start | bytes 786440 | tf_op jit(solution)/shard_map/ppermute | solution.py:641
  84.5 25.6 %collective-permute-start.19 = (bf16[128,2048]{1,0:T(8,128)(2,1)S(1)}, bf16[128,2048]{1,0:T(8,128)(2,1)S(1)}, u32[]{:S(2)}, u32[]{:S(2)}) collective-permute-start(bf16[128,2048]{1,0:T(8,128)(2,1)S(1)} %get-tuple-element.489.refs_1_), channel_id=1, source_target_pairs={{0,16},{16,0},{1,17},{17,1},{2,18},{18,2},{3,19},{19,3},{4,20},{20... | collective-permute-start | bytes 1572872 | tf_op jit(solution)/shard_map/ppermute | solution.py:637
  85.3 24.8 %collective-permute-start.18 = (bf16[128,2048]{1,0:T(8,128)(2,1)S(1)}, bf16[128,2048]{1,0:T(8,128)(2,1)S(1)}, u32[]{:S(2)}, u32[]{:S(2)}) collective-permute-start(bf16[128,2048]{1,0:T(8,128)(2,1)S(1)} %get-tuple-element.490.refs_0_), channel_id=1, source_target_pairs={{0,8},{8,0},{1,9},{9,1},{2,10},{10,2},{3,11},{11,3},{4,12},{12,4},... | collective-permute-start | bytes 1572872 | tf_op jit(solution)/shard_map/ppermute | solution.py:635
  111.0 167.3 %all-gather.9.cloned.1.call-start = ((), (), s32[]{:S(2)}) async-start(), calls=%async_computation.5 | async-start | bytes 6488064 | tf_op jit(solution)/shard_map/all_gather | solution.py:685
  111.6 356.3 %reduce-scatter.4.cloned.1.call-start = ((), (), s32[]{:S(2)}) async-start(), calls=%async_computation.7 | async-start | bytes 7208960 | tf_op jit(solution)/shard_map/reduce_scatter | solution.py:711
  112.6 16.9 %collective-permute-start.23 = (bf16[128,2048]{1,0:T(8,128)(2,1)S(1)}, bf16[128,2048]{1,0:T(8,128)(2,1)S(1)}, u32[]{:S(2)}, u32[]{:S(2)}) collective-permute-start(bf16[128,2048]{1,0:T(8,128)(2,1)S(1)} %get-tuple-element.489.refs_1_), channel_id=1, source_target_pairs={{0,8},{8,0},{1,9},{9,1},{2,10},{10,2},{3,11},{11,3},{4,12},{12,4},... | collective-permute-start | bytes 1572872 | tf_op jit(solution)/shard_map/ppermute | solution.py:635
  114.0 16.9 %collective-permute-start.22 = (bf16[128,2048]{1,0:T(8,128)(2,1)S(1)}, bf16[128,2048]{1,0:T(8,128)(2,1)S(1)}, u32[]{:S(2)}, u32[]{:S(2)}) collective-permute-start(bf16[128,2048]{1,0:T(8,128)(2,1)S(1)} %get-tuple-element.490.refs_0_), channel_id=1, source_target_pairs={{0,16},{16,0},{1,17},{17,1},{2,18},{18,2},{3,19},{19,3},{4,20},{20... | collective-permute-start | bytes 1572872 | tf_op jit(solution)/shard_map/ppermute | solution.py:637
  115.5 31.0 %collective-permute-start.24 = (bf16[128,2048]{1,0:T(8,128)(2,1)}, bf16[128,2048]{1,0:T(8,128)(2,1)}, u32[]{:S(2)}, u32[]{:S(2)}) collective-permute-start(bf16[128,2048]{1,0:T(8,128)(2,1)} %copy-done.25), channel_id=1, source_target_pairs={{0,16},{16,0},{1,17},{17,1},{2,18},{18,2},{3,19},{19,3},{4,20},{20... | collective-permute-start | bytes 1572872 | tf_op jit(solution)/shard_map/ppermute | solution.py:637
  116.0 30.4 %collective-permute-start.25 = (bf16[128,2048]{1,0:T(8,128)(2,1)S(1)}, bf16[128,2048]{1,0:T(8,128)(2,1)}, u32[]{:S(2)}, u32[]{:S(2)}) collective-permute-start(bf16[128,2048]{1,0:T(8,128)(2,1)S(1)} %collective-permute-done.19.refs_5_), channel_id=1, source_target_pairs={{0,8},{8,0},{1,9},{9,1},{2,10},{10,2},{3,11},{11,3},{4,12},{12,4},... | collective-permute-start | bytes 1572872 | tf_op jit(solution)/shard_map/ppermute | solution.py:635
  128.0 20.4 %collective-permute-start.21 = (bf16[128,2048]{1,0:T(8,128)(2,1)}, bf16[128,2048]{1,0:T(8,128)(2,1)S(1)}, u32[]{:S(2)}, u32[]{:S(2)}) collective-permute-start(bf16[128,2048]{1,0:T(8,128)(2,1)} %get-tuple-element.487), channel_id=1, source_target_pairs={{0,8},{8,0},{1,9},{9,1},{2,10},{10,2},{3,11},{11,3},{4,12},{12,4},... | collective-permute-start | bytes 1572872 | tf_op jit(solution)/shard_map/ppermute | solution.py:635
  129.4 20.2 %collective-permute-start.20 = (bf16[128,2048]{1,0:T(8,128)(2,1)}, bf16[128,2048]{1,0:T(8,128)(2,1)S(1)}, u32[]{:S(2)}, u32[]{:S(2)}) collective-permute-start(bf16[128,2048]{1,0:T(8,128)(2,1)} %get-tuple-element.488), channel_id=1, source_target_pairs={{0,16},{16,0},{1,17},{17,1},{2,18},{18,2},{3,19},{19,3},{4,20},{20... | collective-permute-start | bytes 1572872 | tf_op jit(solution)/shard_map/ppermute | solution.py:637
  155.0 17.7 %collective-permute-start.26 = (bf16[128,2048]{1,0:T(8,128)(2,1)}, bf16[128,2048]{1,0:T(8,128)(2,1)S(1)}, u32[]{:S(2)}, u32[]{:S(2)}) collective-permute-start(bf16[128,2048]{1,0:T(8,128)(2,1)} %slice.175), channel_id=1, source_target_pairs={{0,16},{16,0},{1,17},{17,1},{2,18},{18,2},{3,19},{19,3},{4,20},{20... | collective-permute-start | bytes 1572872 | tf_op jit(solution)/shard_map/ppermute | solution.py:637
  156.5 22.3 %collective-permute-start.29 = (bf16[128,2048]{1,0:T(8,128)(2,1)S(1)}, bf16[128,2048]{1,0:T(8,128)(2,1)S(1)}, u32[]{:S(2)}, u32[]{:S(2)}) collective-permute-start(bf16[128,2048]{1,0:T(8,128)(2,1)S(1)} %add_convert_fusion.5), channel_id=1, source_target_pairs={{0,16},{16,0},{1,17},{17,1},{2,18},{18,2},{3,19},{19,3},{4,20},{20... | collective-permute-start | bytes 1572872 | tf_op jit(solution)/shard_map/ppermute | solution.py:637
  157.1 21.8 %collective-permute-start.28 = (bf16[128,2048]{1,0:T(8,128)(2,1)S(1)}, bf16[128,2048]{1,0:T(8,128)(2,1)S(1)}, u32[]{:S(2)}, u32[]{:S(2)}) collective-permute-start(bf16[128,2048]{1,0:T(8,128)(2,1)S(1)} %slice.177), channel_id=1, source_target_pairs={{0,8},{8,0},{1,9},{9,1},{2,10},{10,2},{3,11},{11,3},{4,12},{12,4},... | collective-permute-start | bytes 1572872 | tf_op jit(solution)/shard_map/ppermute | solution.py:635
  157.6 22.5 %collective-permute-start.27 = (bf16[128,2048]{1,0:T(8,128)(2,1)S(1)}, bf16[128,2048]{1,0:T(8,128)(2,1)S(1)}, u32[]{:S(2)}, u32[]{:S(2)}) collective-permute-start(bf16[128,2048]{1,0:T(8,128)(2,1)S(1)} %add_convert_fusion.6), channel_id=1, source_target_pairs={{0,8},{8,0},{1,9},{9,1},{2,10},{10,2},{3,11},{11,3},{4,12},{12,4},... | collective-permute-start | bytes 1572872 | tf_op jit(solution)/shard_map/ppermute | solution.py:635
  186.8 15.7 %collective-permute-start.33 = (bf16[128,2048]{1,0:T(8,128)(2,1)}, bf16[128,2048]{1,0:T(8,128)(2,1)S(1)}, u32[]{:S(2)}, u32[]{:S(2)}) collective-permute-start(bf16[128,2048]{1,0:T(8,128)(2,1)} %get-tuple-element.309.refs_1_), channel_id=1, source_target_pairs={{0,16},{16,0},{1,17},{17,1},{2,18},{18,2},{3,19},{19,3},{4,20},{20... | collective-permute-start | bytes 1572872 | tf_op jit(solution)/shard_map/ppermute | solution.py:637
  188.2 24.8 %collective-permute-start.32 = (bf16[128,2048]{1,0:T(8,128)(2,1)}, bf16[128,2048]{1,0:T(8,128)(2,1)S(1)}, u32[]{:S(2)}, u32[]{:S(2)}) collective-permute-start(bf16[128,2048]{1,0:T(8,128)(2,1)} %get-tuple-element.308.refs_0_), channel_id=1, source_target_pairs={{0,16},{16,0},{1,17},{17,1},{2,18},{18,2},{3,19},{19,3},{4,20},{20... | collective-permute-start | bytes 1572872 | tf_op jit(solution)/shard_map/ppermute | solution.py:637
  188.8 24.3 %collective-permute-start.31 = (bf16[128,2048]{1,0:T(8,128)(2,1)}, bf16[128,2048]{1,0:T(8,128)(2,1)S(1)}, u32[]{:S(2)}, u32[]{:S(2)}) collective-permute-start(bf16[128,2048]{1,0:T(8,128)(2,1)} %get-tuple-element.309.refs_1_), channel_id=1, source_target_pairs={{0,8},{8,0},{1,9},{9,1},{2,10},{10,2},{3,11},{11,3},{4,12},{12,4},... | collective-permute-start | bytes 1572872 | tf_op jit(solution)/shard_map/ppermute | solution.py:635
  201.0 19.4 %collective-permute-start.34 = (bf16[128,2048]{1,0:T(8,128)(2,1)S(1)}, bf16[128,2048]{1,0:T(8,128)(2,1)S(1)}, u32[]{:S(2)}, u32[]{:S(2)}) collective-permute-start(bf16[128,2048]{1,0:T(8,128)(2,1)S(1)} %collective-permute-done.30.refs_2_), channel_id=1, source_target_pairs={{0,16},{16,0},{1,17},{17,1},{2,18},{18,2},{3,19},{19,3},{4,20},{20... | collective-permute-start | bytes 1572872 | tf_op jit(solution)/shard_map/ppermute | solution.py:637
  202.5 18.0 %collective-permute-start.35 = (bf16[128,2048]{1,0:T(8,128)(2,1)S(1)}, bf16[128,2048]{1,0:T(8,128)(2,1)S(1)}, u32[]{:S(2)}, u32[]{:S(2)}) collective-permute-start(bf16[128,2048]{1,0:T(8,128)(2,1)S(1)} %collective-permute-done.33.refs_5_), channel_id=1, source_target_pairs={{0,8},{8,0},{1,9},{9,1},{2,10},{10,2},{3,11},{11,3},{4,12},{12,4},... | collective-permute-start | bytes 1572872 | tf_op jit(solution)/shard_map/ppermute | solution.py:635
  278.3 25.5 %collective-permute-start.37 = (bf16[352,512]{1,0:T(8,128)(2,1)}, bf16[352,512]{1,0:T(8,128)(2,1)S(1)}, u32[]{:S(2)}, u32[]{:S(2)}) collective-permute-start(bf16[352,512]{1,0:T(8,128)(2,1)} %get-tuple-element.319), channel_id=1, source_target_pairs={{0,2},{1,3},{2,0},{3,1},{4,6},{5,7},{6,4},{7,5},{8,10},{9,11},{10,... | collective-permute-start | bytes 1081352 | tf_op jit(solution)/shard_map/ppermute | solution.py:641
  303.9 25.0 %collective-permute-start.42 = (bf16[1024,2816]{1,0:T(8,128)(2,1)}, bf16[1024,2816]{1,0:T(8,128)(2,1)S(1)}, u32[]{:S(2)}, u32[]{:S(2)}) collective-permute-start(bf16[1024,2816]{1,0:T(8,128)(2,1)} %weight_grad.4), channel_id=1, source_target_pairs={{0,4},{4,0},{1,5},{5,1},{2,6},{6,2},{3,7},{7,3},{8,12},{12,8},{9,1... | collective-permute-start | bytes 17301512 | tf_op jit(solution)/shard_map/ppermute | solution.py:701
  304.0 19.1 %collective-permute-start.38 = (bf16[352,512]{1,0:T(8,128)(2,1)S(1)}, bf16[352,512]{1,0:T(8,128)(2,1)S(1)}, u32[]{:S(2)}, u32[]{:S(2)}) collective-permute-start(bf16[352,512]{1,0:T(8,128)(2,1)S(1)} %copy-done.58), channel_id=1, source_target_pairs={{0,2},{1,3},{2,0},{3,1},{4,6},{5,7},{6,4},{7,5},{8,10},{9,11},{10,... | collective-permute-start | bytes 1081352 | tf_op jit(solution)/shard_map/ppermute | solution.py:641
  323.1 21.2 %collective-permute-start.43 = (bf16[352,512]{1,0:T(8,128)(2,1)S(1)}, bf16[352,512]{1,0:T(8,128)(2,1)S(1)}, u32[]{:S(2)}, u32[]{:S(2)}) collective-permute-start(bf16[352,512]{1,0:T(8,128)(2,1)S(1)} %get-tuple-element.325), channel_id=1, source_target_pairs={{0,2},{1,3},{2,0},{3,1},{4,6},{5,7},{6,4},{7,5},{8,10},{9,11},{10,... | collective-permute-start | bytes 1081352 | tf_op jit(solution)/shard_map/ppermute | solution.py:641
  325.9 18.3 %collective-permute-start.41 = (bf16[128,2048]{1,0:T(8,128)(2,1)S(1)}, bf16[128,2048]{1,0:T(8,128)(2,1)S(1)}, u32[]{:S(2)}, u32[]{:S(2)}) collective-permute-start(bf16[128,2048]{1,0:T(8,128)(2,1)S(1)} %get-tuple-element.472), channel_id=1, source_target_pairs={{0,8},{8,0},{1,9},{9,1},{2,10},{10,2},{3,11},{11,3},{4,12},{12,4},... | collective-permute-start | bytes 1572872 | tf_op jit(solution)/shard_map/ppermute | solution.py:635
  327.4 16.9 %collective-permute-start.40 = (bf16[128,2048]{1,0:T(8,128)(2,1)S(1)}, bf16[128,2048]{1,0:T(8,128)(2,1)S(1)}, u32[]{:S(2)}, u32[]{:S(2)}) collective-permute-start(bf16[128,2048]{1,0:T(8,128)(2,1)S(1)} %get-tuple-element.473), channel_id=1, source_target_pairs={{0,16},{16,0},{1,17},{17,1},{2,18},{18,2},{3,19},{19,3},{4,20},{20... | collective-permute-start | bytes 1572872 | tf_op jit(solution)/shard_map/ppermute | solution.py:637
  345.3 178.2 %reduce-scatter.6.cloned.1.call-start = ((), (), s32[]{:S(2)}) async-start(), calls=%async_computation.8 | async-start | bytes 1310720 | tf_op jit(solution)/shard_map/reduce_scatter | solution.py:711
  345.4 17.3 %collective-permute-start.45 = (bf16[128,2048]{1,0:T(8,128)(2,1)}, bf16[128,2048]{1,0:T(8,128)(2,1)S(1)}, u32[]{:S(2)}, u32[]{:S(2)}) collective-permute-start(bf16[128,2048]{1,0:T(8,128)(2,1)} %get-tuple-element.471), channel_id=1, source_target_pairs={{0,8},{8,0},{1,9},{9,1},{2,10},{10,2},{3,11},{11,3},{4,12},{12,4},... | collective-permute-start | bytes 1572872 | tf_op jit(solution)/shard_map/ppermute | solution.py:635
  346.0 16.7 %collective-permute-start.39 = (bf16[128,2048]{1,0:T(8,128)(2,1)}, bf16[128,2048]{1,0:T(8,128)(2,1)S(1)}, u32[]{:S(2)}, u32[]{:S(2)}) collective-permute-start(bf16[128,2048]{1,0:T(8,128)(2,1)} %get-tuple-element.474), channel_id=1, source_target_pairs={{0,16},{16,0},{1,17},{17,1},{2,18},{18,2},{3,19},{19,3},{4,20},{20... | collective-permute-start | bytes 1572872 | tf_op jit(solution)/shard_map/ppermute | solution.py:637
  348.5 22.2 %collective-permute-start.46 = (bf16[128,2048]{1,0:T(8,128)(2,1)S(1)}, bf16[128,2048]{1,0:T(8,128)(2,1)}, u32[]{:S(2)}, u32[]{:S(2)}) collective-permute-start(bf16[128,2048]{1,0:T(8,128)(2,1)S(1)} %get-tuple-element.469), channel_id=1, source_target_pairs={{0,16},{16,0},{1,17},{17,1},{2,18},{18,2},{3,19},{19,3},{4,20},{20... | collective-permute-start | bytes 1572872 | tf_op jit(solution)/shard_map/ppermute | solution.py:637
  350.0 20.7 %collective-permute-start.44 = (bf16[128,2048]{1,0:T(8,128)(2,1)S(1)}, bf16[128,2048]{1,0:T(8,128)(2,1)}, u32[]{:S(2)}, u32[]{:S(2)}) collective-permute-start(bf16[128,2048]{1,0:T(8,128)(2,1)S(1)} %get-tuple-element.470), channel_id=1, source_target_pairs={{0,8},{8,0},{1,9},{9,1},{2,10},{10,2},{3,11},{11,3},{4,12},{12,4},... | collective-permute-start | bytes 1572872 | tf_op jit(solution)/shard_map/ppermute | solution.py:635
  376.7 18.0 %collective-permute-start.49 = (bf16[128,2048]{1,0:T(8,128)(2,1)}, bf16[128,2048]{1,0:T(8,128)(2,1)S(1)}, u32[]{:S(2)}, u32[]{:S(2)}) collective-permute-start(bf16[128,2048]{1,0:T(8,128)(2,1)} %get-tuple-element.387.refs_7_.refs_4_), channel_id=1, source_target_pairs={{0,16},{16,0},{1,17},{17,1},{2,18},{18,2},{3,19},{19,3},{4,20},{20... | collective-permute-start | bytes 1572872 | tf_op jit(solution)/shard_map/ppermute | solution.py:637
  377.3 18.1 %collective-permute-start.47 = (bf16[128,2048]{1,0:T(8,128)(2,1)}, bf16[128,2048]{1,0:T(8,128)(2,1)S(1)}, u32[]{:S(2)}, u32[]{:S(2)}) collective-permute-start(bf16[128,2048]{1,0:T(8,128)(2,1)} %get-tuple-element.387.refs_7_.refs_4_), channel_id=1, source_target_pairs={{0,8},{8,0},{1,9},{9,1},{2,10},{10,2},{3,11},{11,3},{4,12},{12,4},... | collective-permute-start | bytes 1572872 | tf_op jit(solution)/shard_map/ppermute | solution.py:635
  378.7 24.8 %collective-permute-start.50 = (bf16[128,2048]{1,0:T(8,128)(2,1)}, bf16[128,2048]{1,0:T(8,128)(2,1)S(1)}, u32[]{:S(2)}, u32[]{:S(2)}) collective-permute-start(bf16[128,2048]{1,0:T(8,128)(2,1)} %get-tuple-element.388.refs_8_.refs_5_), channel_id=1, source_target_pairs={{0,8},{8,0},{1,9},{9,1},{2,10},{10,2},{3,11},{11,3},{4,12},{12,4},... | collective-permute-start | bytes 1572872 | tf_op jit(solution)/shard_map/ppermute | solution.py:635
  379.3 24.3 %collective-permute-start.48 = (bf16[128,2048]{1,0:T(8,128)(2,1)}, bf16[128,2048]{1,0:T(8,128)(2,1)S(1)}, u32[]{:S(2)}, u32[]{:S(2)}) collective-permute-start(bf16[128,2048]{1,0:T(8,128)(2,1)} %get-tuple-element.388.refs_8_.refs_5_), channel_id=1, source_target_pairs={{0,16},{16,0},{1,17},{17,1},{2,18},{18,2},{3,19},{19,3},{4,20},{20... | collective-permute-start | bytes 1572872 | tf_op jit(solution)/shard_map/ppermute | solution.py:637
  383.6 65.4 %collective-permute-start.60 = (bf16[128,2048]{1,0:T(8,128)(2,1)}, bf16[128,2048]{1,0:T(8,128)(2,1)S(1)}, u32[]{:S(2)}, u32[]{:S(2)}) collective-permute-start(bf16[128,2048]{1,0:T(8,128)(2,1)} %get-tuple-element.465), channel_id=1, source_target_pairs={{0,8},{8,0},{1,9},{9,1},{2,10},{10,2},{3,11},{11,3},{4,12},{12,4},... | collective-permute-start | bytes 1572872 | tf_op jit(solution)/shard_map/ppermute | solution.py:635
  394.8 31.4 %collective-permute-start.54 = (bf16[128,2048]{1,0:T(8,128)(2,1)}, bf16[128,2048]{1,0:T(8,128)(2,1)}, u32[]{:S(2)}, u32[]{:S(2)}) collective-permute-start(bf16[128,2048]{1,0:T(8,128)(2,1)} %get-tuple-element.467), channel_id=1, source_target_pairs={{0,8},{8,0},{1,9},{9,1},{2,10},{10,2},{3,11},{11,3},{4,12},{12,4},... | collective-permute-start | bytes 1572872 | tf_op jit(solution)/shard_map/ppermute | solution.py:635
  395.4 32.2 %collective-permute-start.53 = (bf16[128,2048]{1,0:T(8,128)(2,1)}, bf16[128,2048]{1,0:T(8,128)(2,1)}, u32[]{:S(2)}, u32[]{:S(2)}) collective-permute-start(bf16[128,2048]{1,0:T(8,128)(2,1)} %get-tuple-element.468), channel_id=1, source_target_pairs={{0,16},{16,0},{1,17},{17,1},{2,18},{18,2},{3,19},{19,3},{4,20},{20... | collective-permute-start | bytes 1572872 | tf_op jit(solution)/shard_map/ppermute | solution.py:637
  403.6 24.0 %collective-permute-start.51 = (bf16[128,2048]{1,0:T(8,128)(2,1)S(1)}, bf16[128,2048]{1,0:T(8,128)(2,1)S(1)}, u32[]{:S(2)}, u32[]{:S(2)}) collective-permute-start(bf16[128,2048]{1,0:T(8,128)(2,1)S(1)} %collective-permute-done.47.refs_7_.refs_6_), channel_id=1, source_target_pairs={{0,16},{16,0},{1,17},{17,1},{2,18},{18,2},{3,19},{19,3},{4,20},{20... | collective-permute-start | bytes 1572872 | tf_op jit(solution)/shard_map/ppermute | solution.py:637
  405.1 29.2 %collective-permute-start.52 = (bf16[128,2048]{1,0:T(8,128)(2,1)S(1)}, bf16[128,2048]{1,0:T(8,128)(2,1)S(1)}, u32[]{:S(2)}, u32[]{:S(2)}) collective-permute-start(bf16[128,2048]{1,0:T(8,128)(2,1)S(1)} %collective-permute-done.48.refs_20_.refs_9_), channel_id=1, source_target_pairs={{0,8},{8,0},{1,9},{9,1},{2,10},{10,2},{3,11},{11,3},{4,12},{12,4},... | collective-permute-start | bytes 1572872 | tf_op jit(solution)/shard_map/ppermute | solution.py:635
  426.2 24.4 %collective-permute-start.58 = (bf16[128,2048]{1,0:T(8,128)(2,1)}, bf16[128,2048]{1,0:T(8,128)(2,1)S(1)}, u32[]{:S(2)}, u32[]{:S(2)}) collective-permute-start(bf16[128,2048]{1,0:T(8,128)(2,1)} %get-tuple-element.466), channel_id=1, source_target_pairs={{0,16},{16,0},{1,17},{17,1},{2,18},{18,2},{3,19},{19,3},{4,20},{20... | collective-permute-start | bytes 1572872 | tf_op jit(solution)/shard_map/ppermute | solution.py:637
  435.6 16.4 %collective-permute-start.55 = (bf16[3,256,128]{2,1,0:T(8,128)(2,1)S(1)}, bf16[3,256,128]{2,1,0:T(8,128)(2,1)S(1)}, u32[]{:S(2)}, u32[]{:S(2)}) collective-permute-start(bf16[3,256,128]{2,1,0:T(8,128)(2,1)S(1)} %pad_maximum_fusion), channel_id=1, source_target_pairs={{0,1},{1,0},{2,3},{3,2},{4,5},{5,4},{6,7},{7,6},{8,9},{9,8},{10,11... | collective-permute-start | bytes 589832 | tf_op jit(solution)/shard_map/ppermute | solution.py:641
  436.4 25.6 %collective-permute-start.56 = (bf16[3,256,128]{2,1,0:T(8,128)(2,1)}, bf16[3,256,128]{2,1,0:T(8,128)(2,1)S(1)}, u32[]{:S(2)}, u32[]{:S(2)}) collective-permute-start(bf16[3,256,128]{2,1,0:T(8,128)(2,1)} %pad_maximum_fusion.1), channel_id=1, source_target_pairs={{0,2},{1,3},{2,0},{3,1},{4,6},{5,7},{6,4},{7,5},{8,10},{9,11},{10,... | collective-permute-start | bytes 589832 | tf_op jit(solution)/shard_map/ppermute | solution.py:641
  438.7 23.3 %collective-permute-start.57 = (bf16[3,256,128]{2,1,0:T(8,128)(2,1)}, bf16[3,256,128]{2,1,0:T(8,128)(2,1)}, u32[]{:S(2)}, u32[]{:S(2)}) collective-permute-start(bf16[3,256,128]{2,1,0:T(8,128)(2,1)} %pad_maximum_fusion.2), channel_id=1, source_target_pairs={{0,3},{1,2},{2,1},{3,0},{4,7},{5,6},{6,5},{7,4},{8,11},{9,10},{10,... | collective-permute-start | bytes 589832 | tf_op jit(solution)/shard_map/ppermute | solution.py:641
  452.0 28.9 %collective-permute-start.65 = (bf16[256,2048]{1,0:T(8,128)(2,1)}, bf16[256,2048]{1,0:T(8,128)(2,1)S(1)}, u32[]{:S(2)}, u32[]{:S(2)}) collective-permute-start(bf16[256,2048]{1,0:T(8,128)(2,1)} %out_gradient.2), channel_id=1, source_target_pairs={{0,4},{4,0},{1,5},{5,1},{2,6},{6,2},{3,7},{7,3},{8,12},{12,8},{9,1... | collective-permute-start | bytes 3145736 | tf_op jit(solution)/shard_map/ppermute | solution.py:863
  465.0 15.2 %collective-permute-start.63 = (bf16[1,256,128]{2,1,0:T(8,128)(2,1)S(1)}, bf16[1,256,128]{2,1,0:T(8,128)(2,1)S(1)}, u32[]{:S(2)}, u32[]{:S(2)}) collective-permute-start(bf16[1,256,128]{2,1,0:T(8,128)(2,1)S(1)} %get-tuple-element.500), channel_id=1, source_target_pairs={{0,2},{1,3},{2,0},{3,1},{4,6},{5,7},{6,4},{7,5},{8,10},{9,11},{10,... | collective-permute-start | bytes 196616 | tf_op jit(solution)/shard_map/ppermute | solution.py:641
  465.0 24.2 %collective-permute-start.69 = (bf16[352,512]{1,0:T(8,128)(2,1)}, bf16[352,512]{1,0:T(8,128)(2,1)}, u32[]{:S(2)}, u32[]{:S(2)}) collective-permute-start(bf16[352,512]{1,0:T(8,128)(2,1)} %get-tuple-element.398), channel_id=1, source_target_pairs={{0,2},{1,3},{2,0},{3,1},{4,6},{5,7},{6,4},{7,5},{8,10},{9,11},{10,... | collective-permute-start | bytes 1081352 | tf_op jit(solution)/shard_map/ppermute | solution.py:641
  470.3 18.9 %collective-permute-start.68 = (bf16[64,2816]{1,0:T(8,128)(2,1)}, bf16[64,2816]{1,0:T(8,128)(2,1)S(1)}, u32[]{:S(2)}, u32[]{:S(2)}) collective-permute-start(bf16[64,2816]{1,0:T(8,128)(2,1)} %get-tuple-element.479), channel_id=1, source_target_pairs={{0,24},{8,16},{16,8},{24,0},{1,25},{9,17},{17,9},{25,1},{2,26},{10... | collective-permute-start | bytes 1081352 | tf_op jit(solution)/shard_map/ppermute | solution.py:638
  472.9 16.3 %collective-permute-start.67 = (bf16[64,2816]{1,0:T(8,128)(2,1)}, bf16[64,2816]{1,0:T(8,128)(2,1)S(1)}, u32[]{:S(2)}, u32[]{:S(2)}) collective-permute-start(bf16[64,2816]{1,0:T(8,128)(2,1)} %get-tuple-element.480), channel_id=1, source_target_pairs={{0,16},{16,0},{1,17},{17,1},{2,18},{18,2},{3,19},{19,3},{4,20},{20... | collective-permute-start | bytes 1081352 | tf_op jit(solution)/shard_map/ppermute | solution.py:637
  490.7 65.9 %reduce-scatter.8.cloned.1.call-start = ((), (), s32[]{:S(2)}) async-start(), calls=%async_computation.9 | async-start | bytes 1638400 | tf_op jit(solution)/shard_map/reduce_scatter | solution.py:711
  523.6 17.4 %collective-permute-start.75 = (bf16[128,2048]{1,0:T(8,128)(2,1)}, bf16[128,2048]{1,0:T(8,128)(2,1)S(1)}, u32[]{:S(2)}, u32[]{:S(2)}) collective-permute-start(bf16[128,2048]{1,0:T(8,128)(2,1)} %get-tuple-element.459), channel_id=1, source_target_pairs={{0,8},{8,0},{1,9},{9,1},{2,10},{10,2},{3,11},{11,3},{4,12},{12,4},... | collective-permute-start | bytes 1572872 | tf_op jit(solution)/shard_map/ppermute | solution.py:635
  525.1 15.9 %collective-permute-start.70 = (bf16[128,2048]{1,0:T(8,128)(2,1)}, bf16[128,2048]{1,0:T(8,128)(2,1)}, u32[]{:S(2)}, u32[]{:S(2)}) collective-permute-start(bf16[128,2048]{1,0:T(8,128)(2,1)} %get-tuple-element.462), channel_id=1, source_target_pairs={{0,16},{16,0},{1,17},{17,1},{2,18},{18,2},{3,19},{19,3},{4,20},{20... | collective-permute-start | bytes 1572872 | tf_op jit(solution)/shard_map/ppermute | solution.py:637
  528.3 21.4 %collective-permute-start.76 = (bf16[128,2048]{1,0:T(8,128)(2,1)}, bf16[128,2048]{1,0:T(8,128)(2,1)}, u32[]{:S(2)}, u32[]{:S(2)}) collective-permute-start(bf16[128,2048]{1,0:T(8,128)(2,1)} %get-tuple-element.457), channel_id=1, source_target_pairs={{0,16},{16,0},{1,17},{17,1},{2,18},{18,2},{3,19},{19,3},{4,20},{20... | collective-permute-start | bytes 1572872 | tf_op jit(solution)/shard_map/ppermute | solution.py:637
  529.7 19.9 %collective-permute-start.74 = (bf16[128,2048]{1,0:T(8,128)(2,1)}, bf16[128,2048]{1,0:T(8,128)(2,1)}, u32[]{:S(2)}, u32[]{:S(2)}) collective-permute-start(bf16[128,2048]{1,0:T(8,128)(2,1)} %get-tuple-element.458), channel_id=1, source_target_pairs={{0,8},{8,0},{1,9},{9,1},{2,10},{10,2},{3,11},{11,3},{4,12},{12,4},... | collective-permute-start | bytes 1572872 | tf_op jit(solution)/shard_map/ppermute | solution.py:635
  550.8 17.9 %collective-permute-start.80 = (bf16[176,2048]{1,0:T(8,128)(2,1)}, bf16[176,2048]{1,0:T(8,128)(2,1)}, u32[]{:S(2)}, u32[]{:S(2)}) collective-permute-start(bf16[176,2048]{1,0:T(8,128)(2,1)} %dynamic-slice_bitcast_fusion.1), channel_id=1, source_target_pairs={{0,1},{1,0},{2,3},{3,2},{4,5},{5,4},{6,7},{7,6},{8,9},{9,8},{10,11... | collective-permute-start | bytes 2162696 | tf_op jit(solution)/shard_map/ppermute | solution.py:641
  (96 other events, 925.2 us)
Sparse Core Ops, SparseCore 0:
  24.7 34.1 all-gather.6
  60.4 43.4 all-gather.4
  111.2 106.9 all-gather.10
  219.6 58.7 all-gather.8
  345.4 106.0 reduce-scatter.3
  490.8 26.5 reduce-scatter.5
  523.7 30.6 reduce-scatter.7

commit v8 on v7

--- a/solution.py
+++ b/solution.py
@@ -815,10 +815,12 @@
         sent = over_reps_first(n2_all, grad_act)
         sent, down_come[-1] = phase(sent, send_down(down))
         parts = by_member(nt(after(grad_act, sent), gate_up).astype(bf16))
-        parts, down_come[-1] = phase(parts, send_down(grad_act))
+        come = send_down(grad_act)
         far = scatter_far(parts)
         part_gate_up = over_reps_last(n2_all, after(grad_act, parts), sent)
-        far, part_gate_up, down_come[-1] = phase(far, part_gate_up, send_down(sent))
+        far, part_gate_up, down_come[1], down_come[2] = phase(
+            far, part_gate_up, come, send_down(parts)
+        )
         sum_gate_up = owned(part_gate_up)
         near = scatter_near(parts, far)
         forward = nn(after(act, far), down).astype(bf16)

time: 586 us -> 584 us (level)
    unnamed x145 -> x141, local copies, waits for them, and re-layouts: 14.7 us -> 11.9 us
  transfers between devices with their start and end apart: 88 -> 88, of which waited for: 32 -> 34; matrix products, arithmetic and copies ran while one was open for 15% -> 15% of each run, Pallas kernels for 35% -> 35%
where the time goes in v8:
time: 584 us; the launch traced here: 577 us
  Pallas kernels  207 us (35%)
  waiting for transfers between devices  161 us (28%)
  starting transfers between devices  89.1 us (15%)
  matrix products  47.2 us (8%)
  local copies, waits for them, and re-layouts  38.2 us (7%)
  other arithmetic  18.7 us (3%)
  between operations  15.5 us (3%)
    pallas_call x22, Pallas kernels, small_call(): pl.pallas_call(kernel, grid=(1,), in_specs=specs, out_specs=[whole_block(...  140 us
    ppermute x29, waiting for transfers between devices, swap(): return lax.ppermute(v, 'ty', pair)  60.7 us
    ppermute x29, waiting for transfers between devices, swap(): return lax.ppermute(v, 'tx', pair)  45.8 us
    pallas_call x4, Pallas kernels, weight_grad(): pl.pallas_call(kernel, grid_spec=pltpu.PrefetchScalarGridSpec(num_scalar_...  33.9 us
    ppermute x29, starting transfers between devices, swap(): return lax.ppermute(v, 'tx', pair)  33.8 us
    ppermute x29, starting transfers between devices, swap(): return lax.ppermute(v, 'ty', pair)  28.2 us
    ppermute x14, waiting for transfers between devices, swap_ctx(): return lax.ppermute(v, 'ctx', [(i, i ^ j) for i in range(ctxs)]) if j else v  26 us
    dot_general x2, matrix products, nt(): lax.dot_general(left, right, (((1,), (1,)), ((), ())), preferred_element_...  22.6 us
  transfers between devices with their start and end apart: 88, of which 34 were waited for; matrix products, arithmetic and copies ran while one was open for 15% of the time, Pallas kernels for 35%

profile of v8, /device:TPU:0, one launch (start us, length us, event | category | flops | bytes accessed | tf_op | source)
XLA Modules:
  0.0 577.0 jit_solution(6006770843002622353)
XLA Ops:
  10.5 2.5 hold_tokens.1
  14.0 3.0 collective-permute-start
  19.8 3.9 collective-permute-done.1
  31.0 7.6 %collective-permute-done.5 = s32[1,8]{0,1:T(8,128)S(1)} collective-permute-done((s32[1,8]{0,1:T(8,128)S(1)}, s32[1,8]{0,1:T(8,128)S(1)}, u32[]{:S(2)}, u32[]{:S(2)}) %collective-permute-start.5) | collective-permute-done | bytes 64 | tf_op jit(solution)/shard_map/ppermute | solution.py:638
  44.0 3.3 split_gate_up.1
  47.3 7.5 %collective-permute-done.8.refs_4_ = bf16[128,2048]{1,0:T(8,128)(2,1)S(1)} collective-permute-done((bf16[128,2048]{1,0:T(8,128)(2,1)}, bf16[128,2048]{1,0:T(8,128)(2,1)S(1)}, u32[]{:S(2)}, u32[]{:S(2)}) %collective-permute-start.8) | collective-permute-done | bytes 524320 | tf_op jit(solution)/shard_map/ppermute | solution.py:637
  55.9 8.1 %collective-permute-done.11.refs_7_ = bf16[128,2048]{1,0:T(8,128)(2,1)S(1)} collective-permute-done((bf16[128,2048]{1,0:T(8,128)(2,1)S(1)}, bf16[128,2048]{1,0:T(8,128)(2,1)S(1)}, u32[]{:S(2)}, u32[]{:S(2)}) %collective-permute-start.11) | collective-permute-done | bytes 524320 | tf_op jit(solution)/shard_map/ppermute | solution.py:635
  64.7 2.3 constant_dynamic-slice_fusion
  71.8 7.6 %project.1 = (bf16[4,256,128]{2,1,0:T(8,128)(2,1)}, bf16[512,256]{1,0:T(8,128)(2,1)}, bf16[512,256]{1,0:T(8,128)(2,1)}, bf16[512,256]{1,0:T(8,128)(2,1)}, bf16[5...) custom-call(bf16[128,2048]{1,0:T(8,128)(2,1)} %get-tuple-element.260.refs_, ...), custom_call_target="tpu_custom_call" | custom-call | flops 2684354560 | bytes 8392704 | tf_op jit(solution)/shard_map/project/pallas_call | solution.py:66
  79.4 3.7 collective-permute-start.14
  86.5 4.4 join_rows.3.left_ref
  92.2 3.4 collective-permute-done.14.refs_4_.refs_9_.refs_3_.refs_15_
  95.7 14.5 %collective-permute-done.13.refs_3_.refs_8_.refs_2_.refs_14_ = bf16[4,256,128]{2,1,0:T(8,128)(2,1)} collective-permute-done((bf16[4,256,128]{2,1,0:T(8,128)(2,1)}, bf16[4,256,128]{2,1,0:T(8,128)(2,1)}, u32[]{:S(2)}, u32[]{:S(2)}) %collective-permute-start.13) | collective-permute-done | bytes 262176 | tf_op jit(solution)/shard_map/ppermute | solution.py:641
  116.6 9.1 %attend.3 = (bf16[512,256]{1,0:T(8,128)(2,1)}, f32[8,256]{1,0:T(8,128)}, bf16[256,2048]{1,0:T(8,128)(2,1)}) custom-call(s32[4,8]{1,0:T(4,128)} %copy.30.order_ref, bf16[512,2048]{1,0:T(8,128)(2,1)} %all-gather.5.cloned.1.call-done.wo_ref, bf16[512,256]{1,0:T(8,128)(2,1)} %get-tuple-element.251.refs_0_.refs_4_, ...), custom_call_target="tpu_custom_call" | custom-call | flops 2684354560 | bytes 4726912 | tf_op jit(solution)/shard_map/attend/pallas_call | solution.py:66
  125.7 2.3 fusion.9
  130.9 15.5 %attend.4 = (bf16[512,256]{1,0:T(8,128)(2,1)}, f32[8,256]{1,0:T(8,128)}, bf16[256,2048]{1,0:T(8,128)(2,1)}, bf16[512,256]{1,0:T(8,128)(2,1)}, f32[8,256]{1,0:T(8,128)}, /*index=5*/bf16[256,2048]{1,0:T(8,128)(2,1)}) custom-call(s32[4,8]{1,0:T(4,128)} %copy.30.order_ref, bf16[512,2048]{1,0:T(8,128)(2,1)} %all-gather.5.cloned.1.call-done.wo_ref, ...), custom_call_target="tpu_custom_call" | custom-call | flops 5368709120 | bytes 7356544 | tf_op jit(solution)/shard_map/attend/pallas_call | solution.py:66
  159.1 4.4 join_rows.4.g_ref
  163.5 9.2 %attend.5 = (bf16[512,256]{1,0:T(8,128)(2,1)}, f32[8,256]{1,0:T(8,128)}, f32[256,2048]{1,0:T(8,128)}) custom-call(s32[4,8]{1,0:T(4,128)} %copy.30.order_ref, bf16[512,2048]{1,0:T(8,128)(2,1)} %all-gather.5.cloned.1.call-done.wo_ref, bf16[512,256]{1,0:T(8,128)(2,1)} %get-tuple-element.287.refs_0_.refs_4_, ...), custom_call_target="tpu_custom_call" | custom-call | flops 2684354560 | bytes 5775488 | tf_op jit(solution)/shard_map/attend/pallas_call | solution.py:66
  172.7 6.2 %collective-permute-done.29.refs_4_ = bf16[128,2048]{1,0:T(8,128)(2,1)S(1)} collective-permute-done((bf16[128,2048]{1,0:T(8,128)(2,1)S(1)}, bf16[128,2048]{1,0:T(8,128)(2,1)S(1)}, u32[]{:S(2)}, u32[]{:S(2)}) %collective-permute-start.29) | collective-permute-done | bytes 524320 | tf_op jit(solution)/shard_map/ppermute | solution.py:637
  180.9 5.0 finish_middle.1
  190.0 11.0 %collective-permute-done.30.refs_2_ = bf16[128,2048]{1,0:T(8,128)(2,1)S(1)} collective-permute-done((bf16[128,2048]{1,0:T(8,128)(2,1)}, bf16[128,2048]{1,0:T(8,128)(2,1)S(1)}, u32[]{:S(2)}, u32[]{:S(2)}) %collective-permute-start.30) | collective-permute-done | bytes 524320 | tf_op jit(solution)/shard_map/ppermute | solution.py:635
  203.3 9.8 %collective-permute-done.32.refs_4_ = bf16[128,2048]{1,0:T(8,128)(2,1)S(1)} collective-permute-done((bf16[128,2048]{1,0:T(8,128)(2,1)}, bf16[128,2048]{1,0:T(8,128)(2,1)S(1)}, u32[]{:S(2)}, u32[]{:S(2)}) %collective-permute-start.32) | collective-permute-done | bytes 524320 | tf_op jit(solution)/shard_map/ppermute | solution.py:637
  213.1 7.3 %collective-permute-done.34.refs_6_ = bf16[128,2048]{1,0:T(8,128)(2,1)S(1)} collective-permute-done((bf16[128,2048]{1,0:T(8,128)(2,1)S(1)}, bf16[128,2048]{1,0:T(8,128)(2,1)S(1)}, u32[]{:S(2)}, u32[]{:S(2)}) %collective-permute-start.34) | collective-permute-done | bytes 524320 | tf_op jit(solution)/shard_map/ppermute | solution.py:637
  221.4 19.7 %activate.1 = (bf16[1024,1408]{1,0:T(8,128)(2,1)}, bf16[1024,2816]{1,0:T(8,128)(2,1)}) custom-call(bf16[128,2048]{1,0:T(8,128)(2,1)} %get-tuple-element.307.refs_0_, bf16[128,2048]{1,0:T(8,128)(2,1)} %get-tuple-element.308.refs_1_, bf16[128,2048]{1,0:T(8,128)(2,1)} %copy-done.26, bf16[128,2048]{1,0:T(8,128)(2,1)} %copy-done.29, ...), custom_call_target="tpu_custom_call" | custom-call | flops 11811160064 | bytes 24379392 | tf_op jit(solution)/shard_map/activate/pallas_call | solution.py:440
  241.1 6.1 %convolution_convert_fusion.3 = bf16[704,2048]{1,0:T(8,128)(2,1)S(1)} fusion(bf16[1024,2048]{1,0:T(8,128)(2,1)} %join_rows.4.g_ref, bf16[1024,1408]{1,0:T(8,128)(2,1)} %get-tuple-element.326, s32[]{:T(128)S(6)} %select_n.100), kind=kOutput, calls=%fused_computation.4 | convolution fusion | flops 2954231808 | bytes 8650756 | tf_op jit(solution)/shard_map/dot_general | solution.py:43
  247.4 4.4 join_rows.5.left_ref
  252.7 7.2 %add_convert_fusion = bf16[704,2048]{1,0:T(8,128)(2,1)S(1)} fusion(bf16[704,2048]{1,0:T(8,128)(2,1)} %collective-permute-done.36, bf16[1024,2048]{1,0:T(8,128)(2,1)} %join_rows.4.g_ref, bf16[1024,1408]{1,0:T(8,128)(2,1)} %get-tuple-element.326, s32[]{:T(128)S(6)} %select_n.99), kind=kOutput, calls=%fused_computation | convolution fusion | flops 2957115392 | bytes 11534340 | tf_op jit(solution)/shard_map/dot_general | solution.py:43
  261.8 16.5 %all-gather.9.cloned.1.call-done.down_ref = bf16[1408,2048]{1,0:T(8,128)(2,1)} async-done(((bf16[176,2048]{1,0:T(8,128)(2,1)}), bf16[1408,2048]{1,0:T(8,128)(2,1)}) %all-gather.9.cloned.1.call-update) | async-done | bytes 5767184 | tf_op jit(solution)/shard_map/all_gather | solution.py:685
  279.4 12.8 %activate_back.1.right_ref = bf16[1024,2816]{1,0:T(8,128)(2,1)} custom-call(bf16[1024,2048]{1,0:T(8,128)(2,1)} %join_rows.4.g_ref, bf16[1408,2048]{1,0:T(8,128)(2,1)} %all-gather.9.cloned.1.call-done.down_ref, bf16[1024,2816]{1,0:T(8,128)(2,1)} %get-tuple-element.315.slope_ref), custom_call_target="tpu_custom_call" | custom-call | flops 5905580032 | bytes 21495808 | tf_op jit(solution)/shard_map/activate_back/pallas_call | solution.py:472
  292.3 11.5 %weight_grad.4 = bf16[1024,2816]{1,0:T(8,128)(2,1)} custom-call(s32[1]{0:T(128)} %bitcast.7.index_ref, bf16[1024,2048]{1,0:T(8,128)(2,1)} %join_rows.5.left_ref, bf16[1024,2816]{1,0:T(8,128)(2,1)} %activate_back.1.right_ref), custom_call_target="tpu_custom_call" | custom-call | flops 5905580032 | bytes 19398656 | tf_op jit(solution)/shard_map/weight_grad/pallas_call | solution.py:505
  305.7 16.8 %convolution_convert_fusion = bf16[1024,2048]{1,0:T(8,128)(2,1)S(1)} fusion(bf16[1024,2816]{1,0:T(8,128)(2,1)} %activate_back.1.right_ref, bf16[2048,2816]{1,0:T(8,128)(2,1)} %all-gather.11.cloned.1.call-done.refs_8_), kind=kOutput, calls=%fused_computation.1 | convolution fusion | flops 11813257216 | bytes 21495808 | tf_op jit(solution)/shard_map/dot_general | solution.py:39
  328.6 12.8 %weight_grad.5 = bf16[1024,2816]{1,0:T(8,128)(2,1)} custom-call(s32[1]{0:T(128)} %bitcast.11.index_ref, bf16[1024,2048]{1,0:T(8,128)(2,1)} %join_rows.5.left_ref, bf16[1024,2816]{1,0:T(8,128)(2,1)} %activate_back.1.right_ref, bf16[1024,2816]{1,0:T(8,128)(2,1)} %collective-permute-done.41.refs_0_), custom_call_target="tpu_custom_call" | custom-call | flops 5905580032 | bytes 19398656 | tf_op jit(solution)/shard_map/weight_grad/pallas_call | solution.py:505
  348.8 11.2 %convolution_convert_fusion.2 = bf16[1024,2048]{1,0:T(8,128)(2,1)} fusion(bf16[1024,1408]{1,0:T(8,128)(2,1)S(1)} %copy-done.17, bf16[1408,2048]{1,0:T(8,128)(2,1)} %all-gather.9.cloned.1.call-done.down_ref), kind=kOutput, calls=%fused_computation.3 | convolution fusion | flops 5907677184 | bytes 12845056 | tf_op jit(solution)/shard_map/dot_general | solution.py:35
  360.1 8.4 %collective-permute-done.46.refs_4_ = bf16[128,2048]{1,0:T(8,128)(2,1)} collective-permute-done((bf16[128,2048]{1,0:T(8,128)(2,1)S(1)}, bf16[128,2048]{1,0:T(8,128)(2,1)}, u32[]{:S(2)}, u32[]{:S(2)}) %collective-permute-start.46) | collective-permute-done | bytes 524320 | tf_op jit(solution)/shard_map/ppermute | solution.py:637
  368.6 6.0 %finish_norm_back.2 = (f32[256,2048]{1,0:T(8,128)}, bf16[128,2048]{1,0:T(8,128)(2,1)}, bf16[128,2048]{1,0:T(8,128)(2,1)}) custom-call(bf16[256,2048]{1,0:T(8,128)(2,1)} %g_ref.1, f32[256,2048]{1,0:T(8,128)} %get-tuple-element.417.x_ref.mid_ref, f32[256,1]{1,0:T(8,128)} %get-tuple-element.299.inv_ref, bf16[4,256,2048]{2,1,0:T(8,128)(2,1)} %bitcast.90, ...), custom_call_target="tpu_custom_call" | custom-call | flops 12583936 | bytes 12583936 | tf_op jit(solution)/shard_map/finish_norm_back/pallas_call | solution.py:66
  378.6 2.9 fusion.6
  382.5 9.6 %attend_back.3 = (bf16[256,512]{1,0:T(8,128)(2,1)}, bf16[256,512]{1,0:T(8,128)(2,1)}, f32[256,128]{1,0:T(8,128)}, bf16[768,128]{1,0:T(8,128)(2,1)}) custom-call(s32[4,8]{1,0:T(4,128)} %copy.30.order_ref, bf16[512,2048]{1,0:T(8,128)(2,1)} %all-gather.5.cloned.1.call-done.wo_ref, bf16[4,256,128]{2,1,0:T(8,128)(2,1)} %get-tuple-element.268.refs_1_.refs_6_.refs_0_.refs_12_, ...), custom_call_target="tpu_custom_call" | custom-call | flops 5905580032 | bytes 5842048 | tf_op jit(solution)/shard_map/attend_back/pallas_call | solution.py:66
  394.7 7.6 %collective-permute-done.50.refs_8_.refs_7_ = bf16[128,2048]{1,0:T(8,128)(2,1)S(1)} collective-permute-done((bf16[128,2048]{1,0:T(8,128)(2,1)}, bf16[128,2048]{1,0:T(8,128)(2,1)S(1)}, u32[]{:S(2)}, u32[]{:S(2)}) %collective-permute-start.50) | collective-permute-done | bytes 524320 | tf_op jit(solution)/shard_map/ppermute | solution.py:635
  404.0 17.1 %attend_back.4 = (bf16[256,512]{1,0:T(8,128)(2,1)}, bf16[256,512]{1,0:T(8,128)(2,1)}, f32[256,128]{1,0:T(8,128)}, bf16[768,128]{1,0:T(8,128)(2,1)}, bf16[256,512...) custom-call(s32[4,8]{1,0:T(4,128)} %copy.30.order_ref, ...), custom_call_target="tpu_custom_call" | custom-call | flops 11811160064 | bytes 9586816 | tf_op jit(solution)/shard_map/attend_back/pallas_call | solution.py:66
  421.1 3.9 collective-permute-done.54
  425.5 8.2 %collective-permute-done.52.refs_11_.refs_8_ = bf16[128,2048]{1,0:T(8,128)(2,1)S(1)} collective-permute-done((bf16[128,2048]{1,0:T(8,128)(2,1)S(1)}, bf16[128,2048]{1,0:T(8,128)(2,1)S(1)}, u32[]{:S(2)}, u32[]{:S(2)}) %collective-permute-start.52) | collective-permute-done | bytes 524320 | tf_op jit(solution)/shard_map/ppermute | solution.py:635
  437.6 3.1 collective-permute-start.57
  440.7 2.9 add_convert_fusion.3
  443.6 4.7 out_gradient.2
  450.2 9.9 %attend_back.5 = (bf16[256,512]{1,0:T(8,128)(2,1)}, bf16[256,512]{1,0:T(8,128)(2,1)}, f32[256,128]{1,0:T(8,128)}, bf16[768,128]{1,0:T(8,128)(2,1)}) custom-call(s32[4,8]{1,0:T(4,128)} %copy.30.order_ref, bf16[512,2048]{1,0:T(8,128)(2,1)} %all-gather.5.cloned.1.call-done.wo_ref, bf16[4,256,128]{2,1,0:T(8,128)(2,1)} %get-tuple-element.268.refs_1_.refs_6_.refs_0_.refs_12_, ...), custom_call_target="tpu_custom_call" | custom-call | flops 5905580032 | bytes 5842048 | tf_op jit(solution)/shard_map/attend_back/pallas_call | solution.py:66
  461.3 2.8 collective-permute-start.64
  464.1 2.9 collective-permute-start.69
  467.0 2.4 dynamic-slice_bitcast_fusion.2
  472.5 5.8 collective-permute-done.63.refs_8_
  480.6 5.0 out_gradient.3
  488.9 4.4 finish_keys.1
  493.2 5.8 %convolution_convert_fusion.1 = bf16[1024,2048]{1,0:T(8,128)(2,1)S(1)} fusion(bf16[1024,640]{1,0:T(8,128)(2,1)} %get-tuple-element.406, bf16[2048,640]{1,0:T(8,128)(2,1)} %all-gather.7.cloned.1.call-done.refs_8_), kind=kOutput, calls=%fused_computation.2 | convolution fusion | flops 2686451712 | bytes 8126464 | tf_op jit(solution)/shard_map/dot_general | solution.py:39
  502.3 4.8 weight_grad.6
  511.4 4.8 weight_grad.7
  516.2 5.2 collective-permute-done.71
  524.6 2.6 add_convert_fusion.1
  529.1 4.5 merge_gate_up.1
  533.7 4.0 finish_layer.1
  537.6 2.2 convert_add_fusion
  539.9 8.3 %collective-permute-done.76.refs_4_ = bf16[128,2048]{1,0:T(8,128)(2,1)} collective-permute-done((bf16[128,2048]{1,0:T(8,128)(2,1)}, bf16[128,2048]{1,0:T(8,128)(2,1)}, u32[]{:S(2)}, u32[]{:S(2)}) %collective-permute-start.76) | collective-permute-done | bytes 524320 | tf_op jit(solution)/shard_map/ppermute | solution.py:637
  549.3 5.8 %finish_norm_back.3 = f32[256,2048]{1,0:T(8,128)} custom-call(f32[256,2048]{1,0:T(8,128)} %get-tuple-element.437.g_ref, bf16[256,2048]{1,0:T(8,128)(2,1)} %x_ref.4, f32[256,1]{1,0:T(8,128)} %get-tuple-element.335.refs_9_.refs_18_.inv_ref, bf16[4,256,2048]{2,1,0:T(8,128)(2,1)} %bitcast.92, bf16[128,2048]{1,0:T(8,128)(2,1)} %collective-permute-done.70.refs_1_, ...), custom_call_target="tpu_custom_call" | custom-call | flops 11535360 | bytes 11535360 | tf_op jit(solution)/shard_map/finish_norm_back/pallas_call | solution.py:66
  560.3 2.2 collective-permute-done.79.refs_3_
  564.2 2.3 merge_qkv.1
  567.4 2.4 bitcast_add_fusion
  (346 shorter events, 128.4 us)
Async XLA Ops:
  7.2 64.6 %all-gather.7.cloned.1.call-start = ((), (), s32[]{:S(2)}) async-start(), calls=%async_computation.4 | async-start | bytes 2949120 | tf_op jit(solution)/shard_map/all_gather | solution.py:685
  24.5 92.1 %all-gather.5.cloned.1.call-start = ((), (), s32[]{:S(2)}) async-start(), calls=%async_computation.3 | async-start | bytes 2359296 | tf_op jit(solution)/shard_map/all_gather | solution.py:685
  31.0 189.5 %all-gather.11.cloned.1.call-start = ((), (), s32[]{:S(2)}) async-start(), calls=%async_computation.6 | async-start | bytes 12976128 | tf_op jit(solution)/shard_map/all_gather | solution.py:685
  39.7 15.1 %collective-permute-start.8 = (bf16[128,2048]{1,0:T(8,128)(2,1)}, bf16[128,2048]{1,0:T(8,128)(2,1)S(1)}, u32[]{:S(2)}, u32[]{:S(2)}) collective-permute-start(bf16[128,2048]{1,0:T(8,128)(2,1)} %get-tuple-element.260.refs_0_), channel_id=1, source_target_pairs={{0,16},{16,0},{1,17},{17,1},{2,18},{18,2},{3,19},{19,3},{4,20},{20... | collective-permute-start | bytes 1572872 | tf_op jit(solution)/shard_map/ppermute | solution.py:637
  40.8 15.1 %collective-permute-start.9 = (bf16[128,2048]{1,0:T(8,128)(2,1)}, bf16[128,2048]{1,0:T(8,128)(2,1)S(1)}, u32[]{:S(2)}, u32[]{:S(2)}) collective-permute-start(bf16[128,2048]{1,0:T(8,128)(2,1)} %get-tuple-element.261.refs_1_), channel_id=1, source_target_pairs={{0,8},{8,0},{1,9},{9,1},{2,10},{10,2},{3,11},{11,3},{4,12},{12,4},... | collective-permute-start | bytes 1572872 | tf_op jit(solution)/shard_map/ppermute | solution.py:635
  41.5 22.4 %collective-permute-start.11 = (bf16[128,2048]{1,0:T(8,128)(2,1)S(1)}, bf16[128,2048]{1,0:T(8,128)(2,1)S(1)}, u32[]{:S(2)}, u32[]{:S(2)}) collective-permute-start(bf16[128,2048]{1,0:T(8,128)(2,1)S(1)} %collective-permute-done.7.refs_5_), channel_id=1, source_target_pairs={{0,8},{8,0},{1,9},{9,1},{2,10},{10,2},{3,11},{11,3},{4,12},{12,4},... | collective-permute-start | bytes 1572872 | tf_op jit(solution)/shard_map/ppermute | solution.py:635
  42.8 21.9 %collective-permute-start.10 = (bf16[128,2048]{1,0:T(8,128)(2,1)S(1)}, bf16[128,2048]{1,0:T(8,128)(2,1)}, u32[]{:S(2)}, u32[]{:S(2)}) collective-permute-start(bf16[128,2048]{1,0:T(8,128)(2,1)S(1)} %collective-permute-done.6.refs_2_), channel_id=1, source_target_pairs={{0,16},{16,0},{1,17},{17,1},{2,18},{18,2},{3,19},{19,3},{4,20},{20... | collective-permute-start | bytes 1572872 | tf_op jit(solution)/shard_map/ppermute | solution.py:637
  67.0 16.0 %collective-permute-start.17 = (bf16[1,64,2816]{2,1,0:T(8,128)(2,1)}, bf16[1,64,2816]{2,1,0:T(8,128)(2,1)S(1)}, u32[]{:S(2)}, u32[]{:S(2)}) collective-permute-start(bf16[1,64,2816]{2,1,0:T(8,128)(2,1)} %get-tuple-element.481), channel_id=1, source_target_pairs={{0,24},{8,16},{16,8},{24,0},{1,25},{9,17},{17,9},{25,1},{2,26},{10... | collective-permute-start | bytes 1081352 | tf_op jit(solution)/shard_map/ppermute | solution.py:638
  68.4 15.4 %collective-permute-start.16 = (bf16[1,64,2816]{2,1,0:T(8,128)(2,1)}, bf16[1,64,2816]{2,1,0:T(8,128)(2,1)S(1)}, u32[]{:S(2)}, u32[]{:S(2)}) collective-permute-start(bf16[1,64,2816]{2,1,0:T(8,128)(2,1)} %get-tuple-element.482), channel_id=1, source_target_pairs={{0,16},{16,0},{1,17},{17,1},{2,18},{18,2},{3,19},{19,3},{4,20},{20... | collective-permute-start | bytes 1081352 | tf_op jit(solution)/shard_map/ppermute | solution.py:637
  79.4 16.3 %collective-permute-start.14 = (bf16[4,256,128]{2,1,0:T(8,128)(2,1)}, bf16[4,256,128]{2,1,0:T(8,128)(2,1)}, u32[]{:S(2)}, u32[]{:S(2)}) collective-permute-start(bf16[4,256,128]{2,1,0:T(8,128)(2,1)} %get-tuple-element.268.refs_1_.refs_6_.refs_0_.refs_12_), channel_id=1, source_target_pairs={{0,3},{1,2},{2,1},{3,0},{4,7},{5,6},{6,5},{7,4},{8,11},{9,10},{10,... | collective-permute-start | bytes 786440 | tf_op jit(solution)/shard_map/ppermute | solution.py:641
  83.0 27.1 %collective-permute-start.13 = (bf16[4,256,128]{2,1,0:T(8,128)(2,1)}, bf16[4,256,128]{2,1,0:T(8,128)(2,1)}, u32[]{:S(2)}, u32[]{:S(2)}) collective-permute-start(bf16[4,256,128]{2,1,0:T(8,128)(2,1)} %get-tuple-element.268.refs_1_.refs_6_.refs_0_.refs_12_), channel_id=1, source_target_pairs={{0,2},{1,3},{2,0},{3,1},{4,6},{5,7},{6,4},{7,5},{8,10},{9,11},{10,... | collective-permute-start | bytes 786440 | tf_op jit(solution)/shard_map/ppermute | solution.py:641
  83.1 27.1 %collective-permute-start.12 = (bf16[4,256,128]{2,1,0:T(8,128)(2,1)}, bf16[4,256,128]{2,1,0:T(8,128)(2,1)}, u32[]{:S(2)}, u32[]{:S(2)}) collective-permute-start(bf16[4,256,128]{2,1,0:T(8,128)(2,1)} %get-tuple-element.268.refs_1_.refs_6_.refs_0_.refs_12_), channel_id=1, source_target_pairs={{0,1},{1,0},{2,3},{3,2},{4,5},{5,4},{6,7},{7,6},{8,9},{9,8},{10,11... | collective-permute-start | bytes 786440 | tf_op jit(solution)/shard_map/ppermute | solution.py:641
  84.6 25.6 %collective-permute-start.19 = (bf16[128,2048]{1,0:T(8,128)(2,1)S(1)}, bf16[128,2048]{1,0:T(8,128)(2,1)S(1)}, u32[]{:S(2)}, u32[]{:S(2)}) collective-permute-start(bf16[128,2048]{1,0:T(8,128)(2,1)S(1)} %get-tuple-element.487.refs_1_), channel_id=1, source_target_pairs={{0,16},{16,0},{1,17},{17,1},{2,18},{18,2},{3,19},{19,3},{4,20},{20... | collective-permute-start | bytes 1572872 | tf_op jit(solution)/shard_map/ppermute | solution.py:637
  85.4 24.8 %collective-permute-start.18 = (bf16[128,2048]{1,0:T(8,128)(2,1)S(1)}, bf16[128,2048]{1,0:T(8,128)(2,1)S(1)}, u32[]{:S(2)}, u32[]{:S(2)}) collective-permute-start(bf16[128,2048]{1,0:T(8,128)(2,1)S(1)} %get-tuple-element.488.refs_0_), channel_id=1, source_target_pairs={{0,8},{8,0},{1,9},{9,1},{2,10},{10,2},{3,11},{11,3},{4,12},{12,4},... | collective-permute-start | bytes 1572872 | tf_op jit(solution)/shard_map/ppermute | solution.py:635
  111.1 167.3 %all-gather.9.cloned.1.call-start = ((), (), s32[]{:S(2)}) async-start(), calls=%async_computation.5 | async-start | bytes 6488064 | tf_op jit(solution)/shard_map/all_gather | solution.py:685
  111.6 355.4 %reduce-scatter.4.cloned.1.call-start = ((), (), s32[]{:S(2)}) async-start(), calls=%async_computation.7 | async-start | bytes 7208960 | tf_op jit(solution)/shard_map/reduce_scatter | solution.py:711
  112.5 16.9 %collective-permute-start.23 = (bf16[128,2048]{1,0:T(8,128)(2,1)S(1)}, bf16[128,2048]{1,0:T(8,128)(2,1)S(1)}, u32[]{:S(2)}, u32[]{:S(2)}) collective-permute-start(bf16[128,2048]{1,0:T(8,128)(2,1)S(1)} %get-tuple-element.487.refs_1_), channel_id=1, source_target_pairs={{0,8},{8,0},{1,9},{9,1},{2,10},{10,2},{3,11},{11,3},{4,12},{12,4},... | collective-permute-start | bytes 1572872 | tf_op jit(solution)/shard_map/ppermute | solution.py:635
  114.0 16.9 %collective-permute-start.22 = (bf16[128,2048]{1,0:T(8,128)(2,1)S(1)}, bf16[128,2048]{1,0:T(8,128)(2,1)S(1)}, u32[]{:S(2)}, u32[]{:S(2)}) collective-permute-start(bf16[128,2048]{1,0:T(8,128)(2,1)S(1)} %get-tuple-element.488.refs_0_), channel_id=1, source_target_pairs={{0,16},{16,0},{1,17},{17,1},{2,18},{18,2},{3,19},{19,3},{4,20},{20... | collective-permute-start | bytes 1572872 | tf_op jit(solution)/shard_map/ppermute | solution.py:637
  115.5 31.0 %collective-permute-start.24 = (bf16[128,2048]{1,0:T(8,128)(2,1)}, bf16[128,2048]{1,0:T(8,128)(2,1)}, u32[]{:S(2)}, u32[]{:S(2)}) collective-permute-start(bf16[128,2048]{1,0:T(8,128)(2,1)} %copy-done.25), channel_id=1, source_target_pairs={{0,16},{16,0},{1,17},{17,1},{2,18},{18,2},{3,19},{19,3},{4,20},{20... | collective-permute-start | bytes 1572872 | tf_op jit(solution)/shard_map/ppermute | solution.py:637
  116.0 30.4 %collective-permute-start.25 = (bf16[128,2048]{1,0:T(8,128)(2,1)S(1)}, bf16[128,2048]{1,0:T(8,128)(2,1)}, u32[]{:S(2)}, u32[]{:S(2)}) collective-permute-start(bf16[128,2048]{1,0:T(8,128)(2,1)S(1)} %collective-permute-done.19.refs_5_), channel_id=1, source_target_pairs={{0,8},{8,0},{1,9},{9,1},{2,10},{10,2},{3,11},{11,3},{4,12},{12,4},... | collective-permute-start | bytes 1572872 | tf_op jit(solution)/shard_map/ppermute | solution.py:635
  128.0 20.4 %collective-permute-start.21 = (bf16[128,2048]{1,0:T(8,128)(2,1)}, bf16[128,2048]{1,0:T(8,128)(2,1)S(1)}, u32[]{:S(2)}, u32[]{:S(2)}) collective-permute-start(bf16[128,2048]{1,0:T(8,128)(2,1)} %get-tuple-element.485), channel_id=1, source_target_pairs={{0,8},{8,0},{1,9},{9,1},{2,10},{10,2},{3,11},{11,3},{4,12},{12,4},... | collective-permute-start | bytes 1572872 | tf_op jit(solution)/shard_map/ppermute | solution.py:635
  129.4 20.2 %collective-permute-start.20 = (bf16[128,2048]{1,0:T(8,128)(2,1)}, bf16[128,2048]{1,0:T(8,128)(2,1)S(1)}, u32[]{:S(2)}, u32[]{:S(2)}) collective-permute-start(bf16[128,2048]{1,0:T(8,128)(2,1)} %get-tuple-element.486), channel_id=1, source_target_pairs={{0,16},{16,0},{1,17},{17,1},{2,18},{18,2},{3,19},{19,3},{4,20},{20... | collective-permute-start | bytes 1572872 | tf_op jit(solution)/shard_map/ppermute | solution.py:637
  155.0 17.7 %collective-permute-start.26 = (bf16[128,2048]{1,0:T(8,128)(2,1)}, bf16[128,2048]{1,0:T(8,128)(2,1)S(1)}, u32[]{:S(2)}, u32[]{:S(2)}) collective-permute-start(bf16[128,2048]{1,0:T(8,128)(2,1)} %slice.167), channel_id=1, source_target_pairs={{0,16},{16,0},{1,17},{17,1},{2,18},{18,2},{3,19},{19,3},{4,20},{20... | collective-permute-start | bytes 1572872 | tf_op jit(solution)/shard_map/ppermute | solution.py:637
  156.5 22.3 %collective-permute-start.29 = (bf16[128,2048]{1,0:T(8,128)(2,1)S(1)}, bf16[128,2048]{1,0:T(8,128)(2,1)S(1)}, u32[]{:S(2)}, u32[]{:S(2)}) collective-permute-start(bf16[128,2048]{1,0:T(8,128)(2,1)S(1)} %add_convert_fusion.7), channel_id=1, source_target_pairs={{0,16},{16,0},{1,17},{17,1},{2,18},{18,2},{3,19},{19,3},{4,20},{20... | collective-permute-start | bytes 1572872 | tf_op jit(solution)/shard_map/ppermute | solution.py:637
  157.1 21.8 %collective-permute-start.28 = (bf16[128,2048]{1,0:T(8,128)(2,1)S(1)}, bf16[128,2048]{1,0:T(8,128)(2,1)S(1)}, u32[]{:S(2)}, u32[]{:S(2)}) collective-permute-start(bf16[128,2048]{1,0:T(8,128)(2,1)S(1)} %slice.169), channel_id=1, source_target_pairs={{0,8},{8,0},{1,9},{9,1},{2,10},{10,2},{3,11},{11,3},{4,12},{12,4},... | collective-permute-start | bytes 1572872 | tf_op jit(solution)/shard_map/ppermute | solution.py:635
  157.6 22.5 %collective-permute-start.27 = (bf16[128,2048]{1,0:T(8,128)(2,1)S(1)}, bf16[128,2048]{1,0:T(8,128)(2,1)S(1)}, u32[]{:S(2)}, u32[]{:S(2)}) collective-permute-start(bf16[128,2048]{1,0:T(8,128)(2,1)S(1)} %add_convert_fusion.8), channel_id=1, source_target_pairs={{0,8},{8,0},{1,9},{9,1},{2,10},{10,2},{3,11},{11,3},{4,12},{12,4},... | collective-permute-start | bytes 1572872 | tf_op jit(solution)/shard_map/ppermute | solution.py:635
  186.8 15.7 %collective-permute-start.33 = (bf16[128,2048]{1,0:T(8,128)(2,1)}, bf16[128,2048]{1,0:T(8,128)(2,1)S(1)}, u32[]{:S(2)}, u32[]{:S(2)}) collective-permute-start(bf16[128,2048]{1,0:T(8,128)(2,1)} %get-tuple-element.308.refs_1_), channel_id=1, source_target_pairs={{0,16},{16,0},{1,17},{17,1},{2,18},{18,2},{3,19},{19,3},{4,20},{20... | collective-permute-start | bytes 1572872 | tf_op jit(solution)/shard_map/ppermute | solution.py:637
  188.2 24.9 %collective-permute-start.32 = (bf16[128,2048]{1,0:T(8,128)(2,1)}, bf16[128,2048]{1,0:T(8,128)(2,1)S(1)}, u32[]{:S(2)}, u32[]{:S(2)}) collective-permute-start(bf16[128,2048]{1,0:T(8,128)(2,1)} %get-tuple-element.307.refs_0_), channel_id=1, source_target_pairs={{0,16},{16,0},{1,17},{17,1},{2,18},{18,2},{3,19},{19,3},{4,20},{20... | collective-permute-start | bytes 1572872 | tf_op jit(solution)/shard_map/ppermute | solution.py:637
  188.8 24.3 %collective-permute-start.31 = (bf16[128,2048]{1,0:T(8,128)(2,1)}, bf16[128,2048]{1,0:T(8,128)(2,1)S(1)}, u32[]{:S(2)}, u32[]{:S(2)}) collective-permute-start(bf16[128,2048]{1,0:T(8,128)(2,1)} %get-tuple-element.308.refs_1_), channel_id=1, source_target_pairs={{0,8},{8,0},{1,9},{9,1},{2,10},{10,2},{3,11},{11,3},{4,12},{12,4},... | collective-permute-start | bytes 1572872 | tf_op jit(solution)/shard_map/ppermute | solution.py:635
  201.0 19.4 %collective-permute-start.34 = (bf16[128,2048]{1,0:T(8,128)(2,1)S(1)}, bf16[128,2048]{1,0:T(8,128)(2,1)S(1)}, u32[]{:S(2)}, u32[]{:S(2)}) collective-permute-start(bf16[128,2048]{1,0:T(8,128)(2,1)S(1)} %collective-permute-done.30.refs_2_), channel_id=1, source_target_pairs={{0,16},{16,0},{1,17},{17,1},{2,18},{18,2},{3,19},{19,3},{4,20},{20... | collective-permute-start | bytes 1572872 | tf_op jit(solution)/shard_map/ppermute | solution.py:637
  202.5 18.0 %collective-permute-start.35 = (bf16[128,2048]{1,0:T(8,128)(2,1)S(1)}, bf16[128,2048]{1,0:T(8,128)(2,1)S(1)}, u32[]{:S(2)}, u32[]{:S(2)}) collective-permute-start(bf16[128,2048]{1,0:T(8,128)(2,1)S(1)} %collective-permute-done.33.refs_5_), channel_id=1, source_target_pairs={{0,8},{8,0},{1,9},{9,1},{2,10},{10,2},{3,11},{11,3},{4,12},{12,4},... | collective-permute-start | bytes 1572872 | tf_op jit(solution)/shard_map/ppermute | solution.py:635
  278.3 25.4 %collective-permute-start.37 = (bf16[352,512]{1,0:T(8,128)(2,1)}, bf16[352,512]{1,0:T(8,128)(2,1)S(1)}, u32[]{:S(2)}, u32[]{:S(2)}) collective-permute-start(bf16[352,512]{1,0:T(8,128)(2,1)} %get-tuple-element.318), channel_id=1, source_target_pairs={{0,2},{1,3},{2,0},{3,1},{4,6},{5,7},{6,4},{7,5},{8,10},{9,11},{10,... | collective-permute-start | bytes 1081352 | tf_op jit(solution)/shard_map/ppermute | solution.py:641
  303.7 24.8 %collective-permute-start.41 = (bf16[1024,2816]{1,0:T(8,128)(2,1)}, bf16[1024,2816]{1,0:T(8,128)(2,1)}, u32[]{:S(2)}, u32[]{:S(2)}) collective-permute-start(bf16[1024,2816]{1,0:T(8,128)(2,1)} %weight_grad.4), channel_id=1, source_target_pairs={{0,4},{4,0},{1,5},{5,1},{2,6},{6,2},{3,7},{7,3},{8,12},{12,8},{9,1... | collective-permute-start | bytes 17301512 | tf_op jit(solution)/shard_map/ppermute | solution.py:701
  303.8 37.6 %collective-permute-start.42 = (bf16[352,512]{1,0:T(8,128)(2,1)}, bf16[352,512]{1,0:T(8,128)(2,1)S(1)}, u32[]{:S(2)}, u32[]{:S(2)}) collective-permute-start(bf16[352,512]{1,0:T(8,128)(2,1)} %get-tuple-element.322), channel_id=1, source_target_pairs={{0,2},{1,3},{2,0},{3,1},{4,6},{5,7},{6,4},{7,5},{8,10},{9,11},{10,... | collective-permute-start | bytes 1081352 | tf_op jit(solution)/shard_map/ppermute | solution.py:641
  322.6 18.9 %collective-permute-start.43 = (bf16[352,512]{1,0:T(8,128)(2,1)S(1)}, bf16[352,512]{1,0:T(8,128)(2,1)S(1)}, u32[]{:S(2)}, u32[]{:S(2)}) collective-permute-start(bf16[352,512]{1,0:T(8,128)(2,1)S(1)} %get-tuple-element.323), channel_id=1, source_target_pairs={{0,2},{1,3},{2,0},{3,1},{4,6},{5,7},{6,4},{7,5},{8,10},{9,11},{10,... | collective-permute-start | bytes 1081352 | tf_op jit(solution)/shard_map/ppermute | solution.py:641
  325.6 15.8 %collective-permute-start.40 = (bf16[128,2048]{1,0:T(8,128)(2,1)S(1)}, bf16[128,2048]{1,0:T(8,128)(2,1)S(1)}, u32[]{:S(2)}, u32[]{:S(2)}) collective-permute-start(bf16[128,2048]{1,0:T(8,128)(2,1)S(1)} %get-tuple-element.470), channel_id=1, source_target_pairs={{0,8},{8,0},{1,9},{9,1},{2,10},{10,2},{3,11},{11,3},{4,12},{12,4},... | collective-permute-start | bytes 1572872 | tf_op jit(solution)/shard_map/ppermute | solution.py:635
  342.7 179.7 %reduce-scatter.6.cloned.1.call-start = ((), (), s32[]{:S(2)}) async-start(), calls=%async_computation.8 | async-start | bytes 1310720 | tf_op jit(solution)/shard_map/reduce_scatter | solution.py:711
  342.7 17.4 %collective-permute-start.45 = (bf16[128,2048]{1,0:T(8,128)(2,1)}, bf16[128,2048]{1,0:T(8,128)(2,1)S(1)}, u32[]{:S(2)}, u32[]{:S(2)}) collective-permute-start(bf16[128,2048]{1,0:T(8,128)(2,1)} %get-tuple-element.469), channel_id=1, source_target_pairs={{0,8},{8,0},{1,9},{9,1},{2,10},{10,2},{3,11},{11,3},{4,12},{12,4},... | collective-permute-start | bytes 1572872 | tf_op jit(solution)/shard_map/ppermute | solution.py:635
  343.4 16.7 %collective-permute-start.38 = (bf16[128,2048]{1,0:T(8,128)(2,1)}, bf16[128,2048]{1,0:T(8,128)(2,1)S(1)}, u32[]{:S(2)}, u32[]{:S(2)}) collective-permute-start(bf16[128,2048]{1,0:T(8,128)(2,1)} %get-tuple-element.472), channel_id=1, source_target_pairs={{0,16},{16,0},{1,17},{17,1},{2,18},{18,2},{3,19},{19,3},{4,20},{20... | collective-permute-start | bytes 1572872 | tf_op jit(solution)/shard_map/ppermute | solution.py:637
  346.8 21.7 %collective-permute-start.46 = (bf16[128,2048]{1,0:T(8,128)(2,1)S(1)}, bf16[128,2048]{1,0:T(8,128)(2,1)}, u32[]{:S(2)}, u32[]{:S(2)}) collective-permute-start(bf16[128,2048]{1,0:T(8,128)(2,1)S(1)} %get-tuple-element.467), channel_id=1, source_target_pairs={{0,16},{16,0},{1,17},{17,1},{2,18},{18,2},{3,19},{19,3},{4,20},{20... | collective-permute-start | bytes 1572872 | tf_op jit(solution)/shard_map/ppermute | solution.py:637
  347.4 21.1 %collective-permute-start.44 = (bf16[128,2048]{1,0:T(8,128)(2,1)S(1)}, bf16[128,2048]{1,0:T(8,128)(2,1)}, u32[]{:S(2)}, u32[]{:S(2)}) collective-permute-start(bf16[128,2048]{1,0:T(8,128)(2,1)S(1)} %get-tuple-element.468), channel_id=1, source_target_pairs={{0,8},{8,0},{1,9},{9,1},{2,10},{10,2},{3,11},{11,3},{4,12},{12,4},... | collective-permute-start | bytes 1572872 | tf_op jit(solution)/shard_map/ppermute | solution.py:635
  374.6 17.6 %collective-permute-start.49 = (bf16[128,2048]{1,0:T(8,128)(2,1)}, bf16[128,2048]{1,0:T(8,128)(2,1)S(1)}, u32[]{:S(2)}, u32[]{:S(2)}) collective-permute-start(bf16[128,2048]{1,0:T(8,128)(2,1)} %get-tuple-element.385.refs_7_.refs_4_), channel_id=1, source_target_pairs={{0,16},{16,0},{1,17},{17,1},{2,18},{18,2},{3,19},{19,3},{4,20},{20... | collective-permute-start | bytes 1572872 | tf_op jit(solution)/shard_map/ppermute | solution.py:637
  376.1 17.2 %collective-permute-start.47 = (bf16[128,2048]{1,0:T(8,128)(2,1)}, bf16[128,2048]{1,0:T(8,128)(2,1)S(1)}, u32[]{:S(2)}, u32[]{:S(2)}) collective-permute-start(bf16[128,2048]{1,0:T(8,128)(2,1)} %get-tuple-element.385.refs_7_.refs_4_), channel_id=1, source_target_pairs={{0,8},{8,0},{1,9},{9,1},{2,10},{10,2},{3,11},{11,3},{4,12},{12,4},... | collective-permute-start | bytes 1572872 | tf_op jit(solution)/shard_map/ppermute | solution.py:635
  376.6 25.8 %collective-permute-start.50 = (bf16[128,2048]{1,0:T(8,128)(2,1)}, bf16[128,2048]{1,0:T(8,128)(2,1)S(1)}, u32[]{:S(2)}, u32[]{:S(2)}) collective-permute-start(bf16[128,2048]{1,0:T(8,128)(2,1)} %get-tuple-element.386.refs_8_.refs_5_), channel_id=1, source_target_pairs={{0,8},{8,0},{1,9},{9,1},{2,10},{10,2},{3,11},{11,3},{4,12},{12,4},... | collective-permute-start | bytes 1572872 | tf_op jit(solution)/shard_map/ppermute | solution.py:635
  378.1 24.3 %collective-permute-start.48 = (bf16[128,2048]{1,0:T(8,128)(2,1)}, bf16[128,2048]{1,0:T(8,128)(2,1)S(1)}, u32[]{:S(2)}, u32[]{:S(2)}) collective-permute-start(bf16[128,2048]{1,0:T(8,128)(2,1)} %get-tuple-element.386.refs_8_.refs_5_), channel_id=1, source_target_pairs={{0,16},{16,0},{1,17},{17,1},{2,18},{18,2},{3,19},{19,3},{4,20},{20... | collective-permute-start | bytes 1572872 | tf_op jit(solution)/shard_map/ppermute | solution.py:637
  381.5 66.8 %collective-permute-start.60 = (bf16[128,2048]{1,0:T(8,128)(2,1)}, bf16[128,2048]{1,0:T(8,128)(2,1)S(1)}, u32[]{:S(2)}, u32[]{:S(2)}) collective-permute-start(bf16[128,2048]{1,0:T(8,128)(2,1)} %get-tuple-element.463), channel_id=1, source_target_pairs={{0,8},{8,0},{1,9},{9,1},{2,10},{10,2},{3,11},{11,3},{4,12},{12,4},... | collective-permute-start | bytes 1572872 | tf_op jit(solution)/shard_map/ppermute | solution.py:635
  392.1 32.8 %collective-permute-start.54 = (bf16[128,2048]{1,0:T(8,128)(2,1)}, bf16[128,2048]{1,0:T(8,128)(2,1)}, u32[]{:S(2)}, u32[]{:S(2)}) collective-permute-start(bf16[128,2048]{1,0:T(8,128)(2,1)} %get-tuple-element.465), channel_id=1, source_target_pairs={{0,8},{8,0},{1,9},{9,1},{2,10},{10,2},{3,11},{11,3},{4,12},{12,4},... | collective-permute-start | bytes 1572872 | tf_op jit(solution)/shard_map/ppermute | solution.py:635
  393.2 32.2 %collective-permute-start.53 = (bf16[128,2048]{1,0:T(8,128)(2,1)}, bf16[128,2048]{1,0:T(8,128)(2,1)}, u32[]{:S(2)}, u32[]{:S(2)}) collective-permute-start(bf16[128,2048]{1,0:T(8,128)(2,1)} %get-tuple-element.466), channel_id=1, source_target_pairs={{0,16},{16,0},{1,17},{17,1},{2,18},{18,2},{3,19},{19,3},{4,20},{20... | collective-permute-start | bytes 1572872 | tf_op jit(solution)/shard_map/ppermute | solution.py:637
  402.4 23.1 %collective-permute-start.51 = (bf16[128,2048]{1,0:T(8,128)(2,1)S(1)}, bf16[128,2048]{1,0:T(8,128)(2,1)S(1)}, u32[]{:S(2)}, u32[]{:S(2)}) collective-permute-start(bf16[128,2048]{1,0:T(8,128)(2,1)S(1)} %collective-permute-done.47.refs_7_.refs_6_), channel_id=1, source_target_pairs={{0,16},{16,0},{1,17},{17,1},{2,18},{18,2},{3,19},{19,3},{4,20},{20... | collective-permute-start | bytes 1572872 | tf_op jit(solution)/shard_map/ppermute | solution.py:637
  403.0 30.7 %collective-permute-start.52 = (bf16[128,2048]{1,0:T(8,128)(2,1)S(1)}, bf16[128,2048]{1,0:T(8,128)(2,1)S(1)}, u32[]{:S(2)}, u32[]{:S(2)}) collective-permute-start(bf16[128,2048]{1,0:T(8,128)(2,1)S(1)} %collective-permute-done.48.refs_20_.refs_9_), channel_id=1, source_target_pairs={{0,8},{8,0},{1,9},{9,1},{2,10},{10,2},{3,11},{11,3},{4,12},{12,4},... | collective-permute-start | bytes 1572872 | tf_op jit(solution)/shard_map/ppermute | solution.py:635
  424.9 24.0 %collective-permute-start.58 = (bf16[128,2048]{1,0:T(8,128)(2,1)}, bf16[128,2048]{1,0:T(8,128)(2,1)S(1)}, u32[]{:S(2)}, u32[]{:S(2)}) collective-permute-start(bf16[128,2048]{1,0:T(8,128)(2,1)} %get-tuple-element.464), channel_id=1, source_target_pairs={{0,16},{16,0},{1,17},{17,1},{2,18},{18,2},{3,19},{19,3},{4,20},{20... | collective-permute-start | bytes 1572872 | tf_op jit(solution)/shard_map/ppermute | solution.py:637
  434.9 15.3 %collective-permute-start.55 = (bf16[3,256,128]{2,1,0:T(8,128)(2,1)S(1)}, bf16[3,256,128]{2,1,0:T(8,128)(2,1)S(1)}, u32[]{:S(2)}, u32[]{:S(2)}) collective-permute-start(bf16[3,256,128]{2,1,0:T(8,128)(2,1)S(1)} %pad_maximum_fusion), channel_id=1, source_target_pairs={{0,1},{1,0},{2,3},{3,2},{4,5},{5,4},{6,7},{7,6},{8,9},{9,8},{10,11... | collective-permute-start | bytes 589832 | tf_op jit(solution)/shard_map/ppermute | solution.py:641
  435.7 24.5 %collective-permute-start.56 = (bf16[3,256,128]{2,1,0:T(8,128)(2,1)}, bf16[3,256,128]{2,1,0:T(8,128)(2,1)S(1)}, u32[]{:S(2)}, u32[]{:S(2)}) collective-permute-start(bf16[3,256,128]{2,1,0:T(8,128)(2,1)} %pad_maximum_fusion.1), channel_id=1, source_target_pairs={{0,2},{1,3},{2,0},{3,1},{4,6},{5,7},{6,4},{7,5},{8,10},{9,11},{10,... | collective-permute-start | bytes 589832 | tf_op jit(solution)/shard_map/ppermute | solution.py:641
  437.6 22.5 %collective-permute-start.57 = (bf16[3,256,128]{2,1,0:T(8,128)(2,1)}, bf16[3,256,128]{2,1,0:T(8,128)(2,1)}, u32[]{:S(2)}, u32[]{:S(2)}) collective-permute-start(bf16[3,256,128]{2,1,0:T(8,128)(2,1)} %pad_maximum_fusion.2), channel_id=1, source_target_pairs={{0,3},{1,2},{2,1},{3,0},{4,7},{5,6},{6,5},{7,4},{8,11},{9,10},{10,... | collective-permute-start | bytes 589832 | tf_op jit(solution)/shard_map/ppermute | solution.py:641
  450.2 29.5 %collective-permute-start.65 = (bf16[256,2048]{1,0:T(8,128)(2,1)}, bf16[256,2048]{1,0:T(8,128)(2,1)S(1)}, u32[]{:S(2)}, u32[]{:S(2)}) collective-permute-start(bf16[256,2048]{1,0:T(8,128)(2,1)} %out_gradient.2), channel_id=1, source_target_pairs={{0,4},{4,0},{1,5},{5,1},{2,6},{6,2},{3,7},{7,3},{8,12},{12,8},{9,1... | collective-permute-start | bytes 3145736 | tf_op jit(solution)/shard_map/ppermute | solution.py:865
  464.1 23.2 %collective-permute-start.69 = (bf16[352,512]{1,0:T(8,128)(2,1)}, bf16[352,512]{1,0:T(8,128)(2,1)}, u32[]{:S(2)}, u32[]{:S(2)}) collective-permute-start(bf16[352,512]{1,0:T(8,128)(2,1)} %get-tuple-element.396), channel_id=1, source_target_pairs={{0,2},{1,3},{2,0},{3,1},{4,6},{5,7},{6,4},{7,5},{8,10},{9,11},{10,... | collective-permute-start | bytes 1081352 | tf_op jit(solution)/shard_map/ppermute | solution.py:641
  469.5 17.9 %collective-permute-start.68 = (bf16[64,2816]{1,0:T(8,128)(2,1)}, bf16[64,2816]{1,0:T(8,128)(2,1)S(1)}, u32[]{:S(2)}, u32[]{:S(2)}) collective-permute-start(bf16[64,2816]{1,0:T(8,128)(2,1)} %get-tuple-element.477), channel_id=1, source_target_pairs={{0,24},{8,16},{16,8},{24,0},{1,25},{9,17},{17,9},{25,1},{2,26},{10... | collective-permute-start | bytes 1081352 | tf_op jit(solution)/shard_map/ppermute | solution.py:638
  471.6 16.8 %collective-permute-start.67 = (bf16[64,2816]{1,0:T(8,128)(2,1)}, bf16[64,2816]{1,0:T(8,128)(2,1)S(1)}, u32[]{:S(2)}, u32[]{:S(2)}) collective-permute-start(bf16[64,2816]{1,0:T(8,128)(2,1)} %get-tuple-element.478), channel_id=1, source_target_pairs={{0,16},{16,0},{1,17},{17,1},{2,18},{18,2},{3,19},{19,3},{4,20},{20... | collective-permute-start | bytes 1081352 | tf_op jit(solution)/shard_map/ppermute | solution.py:637
  488.8 66.3 %reduce-scatter.8.cloned.1.call-start = ((), (), s32[]{:S(2)}) async-start(), calls=%async_computation.9 | async-start | bytes 1638400 | tf_op jit(solution)/shard_map/reduce_scatter | solution.py:711
  522.4 17.4 %collective-permute-start.75 = (bf16[128,2048]{1,0:T(8,128)(2,1)}, bf16[128,2048]{1,0:T(8,128)(2,1)S(1)}, u32[]{:S(2)}, u32[]{:S(2)}) collective-permute-start(bf16[128,2048]{1,0:T(8,128)(2,1)} %get-tuple-element.457), channel_id=1, source_target_pairs={{0,8},{8,0},{1,9},{9,1},{2,10},{10,2},{3,11},{11,3},{4,12},{12,4},... | collective-permute-start | bytes 1572872 | tf_op jit(solution)/shard_map/ppermute | solution.py:635
  523.6 16.2 %collective-permute-start.70 = (bf16[128,2048]{1,0:T(8,128)(2,1)}, bf16[128,2048]{1,0:T(8,128)(2,1)}, u32[]{:S(2)}, u32[]{:S(2)}) collective-permute-start(bf16[128,2048]{1,0:T(8,128)(2,1)} %get-tuple-element.460), channel_id=1, source_target_pairs={{0,16},{16,0},{1,17},{17,1},{2,18},{18,2},{3,19},{19,3},{4,20},{20... | collective-permute-start | bytes 1572872 | tf_op jit(solution)/shard_map/ppermute | solution.py:637
  527.2 21.0 %collective-permute-start.76 = (bf16[128,2048]{1,0:T(8,128)(2,1)}, bf16[128,2048]{1,0:T(8,128)(2,1)}, u32[]{:S(2)}, u32[]{:S(2)}) collective-permute-start(bf16[128,2048]{1,0:T(8,128)(2,1)} %get-tuple-element.455), channel_id=1, source_target_pairs={{0,16},{16,0},{1,17},{17,1},{2,18},{18,2},{3,19},{19,3},{4,20},{20... | collective-permute-start | bytes 1572872 | tf_op jit(solution)/shard_map/ppermute | solution.py:637
  528.3 19.9 %collective-permute-start.74 = (bf16[128,2048]{1,0:T(8,128)(2,1)}, bf16[128,2048]{1,0:T(8,128)(2,1)}, u32[]{:S(2)}, u32[]{:S(2)}) collective-permute-start(bf16[128,2048]{1,0:T(8,128)(2,1)} %get-tuple-element.456), channel_id=1, source_target_pairs={{0,8},{8,0},{1,9},{9,1},{2,10},{10,2},{3,11},{11,3},{4,12},{12,4},... | collective-permute-start | bytes 1572872 | tf_op jit(solution)/shard_map/ppermute | solution.py:635
  549.3 18.1 %collective-permute-start.80 = (bf16[176,2048]{1,0:T(8,128)(2,1)}, bf16[176,2048]{1,0:T(8,128)(2,1)}, u32[]{:S(2)}, u32[]{:S(2)}) collective-permute-start(bf16[176,2048]{1,0:T(8,128)(2,1)} %dynamic-slice_bitcast_fusion.1), channel_id=1, source_target_pairs={{0,1},{1,0},{2,3},{3,2},{4,5},{5,4},{6,7},{7,6},{8,9},{9,8},{10,11... | collective-permute-start | bytes 2162696 | tf_op jit(solution)/shard_map/ppermute | solution.py:641
  (94 other events, 900.3 us)
Sparse Core Ops, SparseCore 0:
  24.7 34.1 all-gather.6
  60.4 43.4 all-gather.4
  111.2 106.9 all-gather.10
  219.6 58.7 all-gather.8
  342.8 105.6 reduce-scatter.3
  488.9 26.7 reduce-scatter.5
  522.5 30.3 reduce-scatter.7

commit v9 on v8

--- a/solution.py
+++ b/solution.py
@@ -13,7 +13,7 @@
 LANES = 128
 ROWS = 64
 ROOM = 60 << 20
-ATTEND_ROOM = 60 << 20
+ATTEND_ROOM = 32 << 20
 DOWN_STEPS = 4
 
 epsilon = 1e-05

time: 584 us -> 585 us (level)
  Pallas kernels: 207 us -> 193 us
  local copies, waits for them, and re-layouts: 38.2 us -> 45.7 us
  waiting for transfers between devices: 161 us -> 168 us
    pallas_call x22, Pallas kernels: 140 us -> 126 us  [small_call(): pl.pallas_call(kernel, grid=(1,), in_specs=specs, out_specs=[whole_block(...]
    unnamed x141 -> x231, local copies, waits for them, and re-layouts: 11.9 us -> 24.4 us
  transfers between devices with their start and end apart: 88 -> 88, of which waited for: 34 -> 36; matrix products, arithmetic and copies ran while one was open for 15% -> 14% of each run, Pallas kernels for 35% -> 33%
where the time goes in v9:
time: 585 us; the launch traced here: 578 us
  Pallas kernels  193 us (33%)
  waiting for transfers between devices  168 us (29%)
  starting transfers between devices  89.5 us (15%)
  matrix products  48.1 us (8%)
  local copies, waits for them, and re-layouts  45.7 us (8%)
  other arithmetic  18.7 us (3%)
  between operations  15.9 us (3%)
    pallas_call x22, Pallas kernels, small_call(): pl.pallas_call(kernel, grid=(1,), in_specs=specs, out_specs=[whole_block(...  126 us
    ppermute x29, waiting for transfers between devices, swap(): return lax.ppermute(v, 'ty', pair)  59.6 us
    ppermute x29, waiting for transfers between devices, swap(): return lax.ppermute(v, 'tx', pair)  50.6 us
    pallas_call x4, Pallas kernels, weight_grad(): pl.pallas_call(kernel, grid_spec=pltpu.PrefetchScalarGridSpec(num_scalar_...  34 us
    ppermute x29, starting transfers between devices, swap(): return lax.ppermute(v, 'tx', pair)  33.9 us
    ppermute x29, starting transfers between devices, swap(): return lax.ppermute(v, 'ty', pair)  28 us
    ppermute x14, waiting for transfers between devices, swap_ctx(): return lax.ppermute(v, 'ctx', [(i, i ^ j) for i in range(ctxs)]) if j else v  26.3 us
    unnamed x231, local copies, waits for them, and re-layouts  24.4 us
  transfers between devices with their start and end apart: 88, of which 36 were waited for; matrix products, arithmetic and copies ran while one was open for 14% of the time, Pallas kernels for 33%

profile of v9, /device:TPU:0, one launch (start us, length us, event | category | flops | bytes accessed | tf_op | source)
XLA Modules:
  0.0 578.2 jit_solution(900440473032771135)
XLA Ops:
  10.5 2.5 hold_tokens.1
  14.0 3.0 collective-permute-start
  19.8 3.9 collective-permute-done.1
  31.0 7.6 %collective-permute-done.5 = s32[1,8]{0,1:T(8,128)S(1)} collective-permute-done((s32[1,8]{0,1:T(8,128)S(1)}, s32[1,8]{0,1:T(8,128)S(1)}, u32[]{:S(2)}, u32[]{:S(2)}) %collective-permute-start.5) | collective-permute-done | bytes 64 | tf_op jit(solution)/shard_map/ppermute | solution.py:638
  44.0 3.3 split_gate_up.1
  47.3 7.5 %collective-permute-done.8.refs_4_ = bf16[128,2048]{1,0:T(8,128)(2,1)S(1)} collective-permute-done((bf16[128,2048]{1,0:T(8,128)(2,1)}, bf16[128,2048]{1,0:T(8,128)(2,1)S(1)}, u32[]{:S(2)}, u32[]{:S(2)}) %collective-permute-start.8) | collective-permute-done | bytes 524320 | tf_op jit(solution)/shard_map/ppermute | solution.py:637
  55.8 8.1 %collective-permute-done.11.refs_7_ = bf16[128,2048]{1,0:T(8,128)(2,1)S(1)} collective-permute-done((bf16[128,2048]{1,0:T(8,128)(2,1)S(1)}, bf16[128,2048]{1,0:T(8,128)(2,1)S(1)}, u32[]{:S(2)}, u32[]{:S(2)}) %collective-permute-start.11) | collective-permute-done | bytes 524320 | tf_op jit(solution)/shard_map/ppermute | solution.py:635
  63.9 2.5 constant_dynamic-slice_fusion
  71.2 7.5 %project.1 = (bf16[4,256,128]{2,1,0:T(8,128)(2,1)}, bf16[512,256]{1,0:T(8,128)(2,1)}, bf16[512,256]{1,0:T(8,128)(2,1)}, bf16[512,256]{1,0:T(8,128)(2,1)}, bf16[5...) custom-call(bf16[128,2048]{1,0:T(8,128)(2,1)} %get-tuple-element.260.refs_, ...), custom_call_target="tpu_custom_call" | custom-call | flops 2684354560 | bytes 8392704 | tf_op jit(solution)/shard_map/project/pallas_call | solution.py:66
  78.7 3.7 collective-permute-start.14
  86.2 4.5 join_rows.3.left_ref
  93.0 2.4 collective-permute-done.14.refs_4_.refs_9_.refs_3_.refs_15_
  95.4 14.6 %collective-permute-done.13.refs_3_.refs_8_.refs_2_.refs_14_ = bf16[4,256,128]{2,1,0:T(8,128)(2,1)S(1)} collective-permute-done((bf16[4,256,128]{2,1,0:T(8,128)(2,1)}, bf16[4,256,128]{2,1,0:T(8,128)(2,1)S(1)}, u32[]{:S(2)}, u32[]{:S(2)}) %collective-permute-start.13) | collective-permute-done | bytes 262176 | tf_op jit(solution)/shard_map/ppermute | solution.py:641
  116.9 6.7 %attend.3 = (bf16[512,256]{1,0:T(8,128)(2,1)S(1)}, f32[8,256]{1,0:T(8,128)S(1)}, bf16[256,2048]{1,0:T(8,128)(2,1)S(1)}) custom-call(s32[4,8]{1,0:T(4,128)S(1)} %copy.30.order_ref, bf16[512,2048]{1,0:T(8,128)(2,1)S(1)} %copy-done.38, bf16[512,256]{1,0:T(8,128)(2,1)S(1)} %copy-done.55, bf16[4,256,128]{2,1,0:T(8,128)(2,1)S(1)} %copy-done.42, ...), custom_call_target="tpu_custom_call" | custom-call | flops 2684354560 | bytes 4726912 | tf_op jit(solution)/shard_map/attend/pallas_call | solution.py:66
  127.7 13.0 %attend.4 = (bf16[512,256]{1,0:T(8,128)(2,1)S(1)}, f32[8,256]{1,0:T(8,128)S(1)}, bf16[256,2048]{1,0:T(8,128)(2,1)S(1)}, bf16[512,256]{1,0:T(8,128)(2,1)S(1)}, f3...) custom-call(s32[4,8]{1,0:T(4,128)S(1)} %copy.30.order_ref, bf16[512,2048]{1,0:T(8,128)(2,1)S(1)} %copy-done.39, ...), custom_call_target="tpu_custom_call" | custom-call | flops 5368709120 | bytes 7356544 | tf_op jit(solution)/shard_map/attend/pallas_call | solution.py:66
  140.8 6.3 %collective-permute-done.21 = bf16[128,2048]{1,0:T(8,128)(2,1)S(1)} collective-permute-done((bf16[128,2048]{1,0:T(8,128)(2,1)S(1)}, bf16[128,2048]{1,0:T(8,128)(2,1)S(1)}, u32[]{:S(2)}, u32[]{:S(2)}) %collective-permute-start.21) | collective-permute-done | bytes 524320 | tf_op jit(solution)/shard_map/ppermute | solution.py:635
  155.8 4.5 join_rows.4.g_ref
  160.4 6.7 %attend.5 = (bf16[512,256]{1,0:T(8,128)(2,1)S(1)}, f32[8,256]{1,0:T(8,128)S(1)}, f32[256,2048]{1,0:T(8,128)S(1)}) custom-call(s32[4,8]{1,0:T(4,128)S(1)} %copy.30.order_ref, bf16[512,2048]{1,0:T(8,128)(2,1)S(1)} %copy-done.39, bf16[512,256]{1,0:T(8,128)(2,1)S(1)} %copy-done.61, bf16[4,256,128]{2,1,0:T(8,128)(2,1)S(1)} %copy-done.42, ...), custom_call_target="tpu_custom_call" | custom-call | flops 2684354560 | bytes 5775488 | tf_op jit(solution)/shard_map/attend/pallas_call | solution.py:66
  169.7 6.0 %collective-permute-done.29.refs_4_ = bf16[128,2048]{1,0:T(8,128)(2,1)} collective-permute-done((bf16[128,2048]{1,0:T(8,128)(2,1)}, bf16[128,2048]{1,0:T(8,128)(2,1)}, u32[]{:S(2)}, u32[]{:S(2)}) %collective-permute-start.29) | collective-permute-done | bytes 524320 | tf_op jit(solution)/shard_map/ppermute | solution.py:637
  177.1 5.1 finish_middle.1
  186.2 11.0 %collective-permute-done.30.refs_2_ = bf16[128,2048]{1,0:T(8,128)(2,1)S(1)} collective-permute-done((bf16[128,2048]{1,0:T(8,128)(2,1)}, bf16[128,2048]{1,0:T(8,128)(2,1)S(1)}, u32[]{:S(2)}, u32[]{:S(2)}) %collective-permute-start.30) | collective-permute-done | bytes 524320 | tf_op jit(solution)/shard_map/ppermute | solution.py:635
  199.3 9.8 %collective-permute-done.32.refs_4_ = bf16[128,2048]{1,0:T(8,128)(2,1)S(1)} collective-permute-done((bf16[128,2048]{1,0:T(8,128)(2,1)}, bf16[128,2048]{1,0:T(8,128)(2,1)S(1)}, u32[]{:S(2)}, u32[]{:S(2)}) %collective-permute-start.32) | collective-permute-done | bytes 524320 | tf_op jit(solution)/shard_map/ppermute | solution.py:637
  209.1 6.8 %collective-permute-done.34.refs_6_ = bf16[128,2048]{1,0:T(8,128)(2,1)S(1)} collective-permute-done((bf16[128,2048]{1,0:T(8,128)(2,1)S(1)}, bf16[128,2048]{1,0:T(8,128)(2,1)S(1)}, u32[]{:S(2)}, u32[]{:S(2)}) %collective-permute-start.34) | collective-permute-done | bytes 524320 | tf_op jit(solution)/shard_map/ppermute | solution.py:637
  217.2 19.7 %activate.1 = (bf16[1024,1408]{1,0:T(8,128)(2,1)}, bf16[1024,2816]{1,0:T(8,128)(2,1)}) custom-call(bf16[128,2048]{1,0:T(8,128)(2,1)} %get-tuple-element.307.refs_0_, bf16[128,2048]{1,0:T(8,128)(2,1)} %get-tuple-element.308.refs_1_, bf16[128,2048]{1,0:T(8,128)(2,1)} %copy-done.82, bf16[128,2048]{1,0:T(8,128)(2,1)} %copy-done.85, ...), custom_call_target="tpu_custom_call" | custom-call | flops 11811160064 | bytes 24379392 | tf_op jit(solution)/shard_map/activate/pallas_call | solution.py:440
  236.9 7.8 %convolution_convert_fusion.3 = bf16[704,2048]{1,0:T(8,128)(2,1)} fusion(bf16[1024,2048]{1,0:T(8,128)(2,1)} %join_rows.4.g_ref, bf16[1024,1408]{1,0:T(8,128)(2,1)} %get-tuple-element.326, s32[]{:T(128)S(6)} %select_n.100), kind=kOutput, calls=%fused_computation.4 | convolution fusion | flops 2954231808 | bytes 8650756 | tf_op jit(solution)/shard_map/dot_general | solution.py:43
  245.0 4.5 join_rows.5.left_ref
  250.4 6.2 %add_convert_fusion = bf16[704,2048]{1,0:T(8,128)(2,1)S(1)} fusion(bf16[704,2048]{1,0:T(8,128)(2,1)S(1)} %collective-permute-done.36, bf16[1024,2048]{1,0:T(8,128)(2,1)} %join_rows.4.g_ref, bf16[1024,1408]{1,0:T(8,128)(2,1)} %get-tuple-element.326, s32[]{:T(128)S(6)} %select_n.99), kind=kOutput, calls=%fused_computation | convolution fusion | flops 2957115392 | bytes 11534340 | tf_op jit(solution)/shard_map/dot_general | solution.py:43
  259.3 18.1 %all-gather.9.cloned.1.call-done.down_ref = bf16[1408,2048]{1,0:T(8,128)(2,1)} async-done(((bf16[176,2048]{1,0:T(8,128)(2,1)}), bf16[1408,2048]{1,0:T(8,128)(2,1)}) %all-gather.9.cloned.1.call-update) | async-done | bytes 5767184 | tf_op jit(solution)/shard_map/all_gather | solution.py:685
  278.5 12.8 %activate_back.1.right_ref = bf16[1024,2816]{1,0:T(8,128)(2,1)} custom-call(bf16[1024,2048]{1,0:T(8,128)(2,1)} %join_rows.4.g_ref, bf16[1408,2048]{1,0:T(8,128)(2,1)} %all-gather.9.cloned.1.call-done.down_ref, bf16[1024,2816]{1,0:T(8,128)(2,1)} %get-tuple-element.315.slope_ref), custom_call_target="tpu_custom_call" | custom-call | flops 5905580032 | bytes 21495808 | tf_op jit(solution)/shard_map/activate_back/pallas_call | solution.py:472
  291.3 11.5 %weight_grad.4 = bf16[1024,2816]{1,0:T(8,128)(2,1)} custom-call(s32[1]{0:T(128)} %bitcast.7.index_ref, bf16[1024,2048]{1,0:T(8,128)(2,1)} %join_rows.5.left_ref, bf16[1024,2816]{1,0:T(8,128)(2,1)} %activate_back.1.right_ref), custom_call_target="tpu_custom_call" | custom-call | flops 5905580032 | bytes 19398656 | tf_op jit(solution)/shard_map/weight_grad/pallas_call | solution.py:505
  304.8 16.8 %convolution_convert_fusion = bf16[1024,2048]{1,0:T(8,128)(2,1)S(1)} fusion(bf16[1024,2816]{1,0:T(8,128)(2,1)} %activate_back.1.right_ref, bf16[2048,2816]{1,0:T(8,128)(2,1)} %all-gather.11.cloned.1.call-done.refs_8_), kind=kOutput, calls=%fused_computation.1 | convolution fusion | flops 11813257216 | bytes 21495808 | tf_op jit(solution)/shard_map/dot_general | solution.py:39
  327.7 12.8 %weight_grad.5 = bf16[1024,2816]{1,0:T(8,128)(2,1)} custom-call(s32[1]{0:T(128)} %bitcast.11.index_ref, bf16[1024,2048]{1,0:T(8,128)(2,1)} %join_rows.5.left_ref, bf16[1024,2816]{1,0:T(8,128)(2,1)} %activate_back.1.right_ref, bf16[1024,2816]{1,0:T(8,128)(2,1)} %collective-permute-done.41.refs_0_), custom_call_target="tpu_custom_call" | custom-call | flops 5905580032 | bytes 19398656 | tf_op jit(solution)/shard_map/weight_grad/pallas_call | solution.py:505
  347.9 11.4 %convolution_convert_fusion.2 = bf16[1024,2048]{1,0:T(8,128)(2,1)} fusion(bf16[1024,1408]{1,0:T(8,128)(2,1)S(1)} %copy-done.76, bf16[1408,2048]{1,0:T(8,128)(2,1)} %all-gather.9.cloned.1.call-done.down_ref), kind=kOutput, calls=%fused_computation.3 | convolution fusion | flops 5907677184 | bytes 12845056 | tf_op jit(solution)/shard_map/dot_general | solution.py:35
  359.4 8.2 %collective-permute-done.46.refs_4_ = bf16[128,2048]{1,0:T(8,128)(2,1)} collective-permute-done((bf16[128,2048]{1,0:T(8,128)(2,1)S(1)}, bf16[128,2048]{1,0:T(8,128)(2,1)}, u32[]{:S(2)}, u32[]{:S(2)}) %collective-permute-start.46) | collective-permute-done | bytes 524320 | tf_op jit(solution)/shard_map/ppermute | solution.py:637
  367.6 6.0 %finish_norm_back.2 = (f32[256,2048]{1,0:T(8,128)}, bf16[128,2048]{1,0:T(8,128)(2,1)}, bf16[128,2048]{1,0:T(8,128)(2,1)}) custom-call(bf16[256,2048]{1,0:T(8,128)(2,1)} %g_ref.1, f32[256,2048]{1,0:T(8,128)} %get-tuple-element.417.x_ref.mid_ref, f32[256,1]{1,0:T(8,128)} %get-tuple-element.299.inv_ref, bf16[4,256,2048]{2,1,0:T(8,128)(2,1)} %bitcast.90, ...), custom_call_target="tpu_custom_call" | custom-call | flops 12583936 | bytes 12583936 | tf_op jit(solution)/shard_map/finish_norm_back/pallas_call | solution.py:66
  377.8 2.7 fusion.6
  385.4 7.4 %attend_back.3 = (bf16[256,512]{1,0:T(8,128)(2,1)S(1)}, bf16[256,512]{1,0:T(8,128)(2,1)S(1)}, f32[256,128]{1,0:T(8,128)S(1)}, bf16[768,128]{1,0:T(8,128)(2,1)S(1)}) custom-call(s32[4,8]{1,0:T(4,128)S(1)} %copy.30.order_ref, bf16[512,2048]{1,0:T(8,128)(2,1)S(1)} %copy-done.40, bf16[4,256,128]{2,1,0:T(8,128)(2,1)S(1)} %copy-done.43, ...), custom_call_target="tpu_custom_call" | custom-call | flops 5905580032 | bytes 5842048 | tf_op jit(solution)/shard_map/attend_back/pallas_call | solution.py:66
  397.4 4.1 collective-permute-done.50.refs_8_.refs_7_
  403.2 14.1 %attend_back.4 = (bf16[256,512]{1,0:T(8,128)(2,1)S(1)}, bf16[256,512]{1,0:T(8,128)(2,1)S(1)}, f32[256,128]{1,0:T(8,128)S(1)}, bf16[768,128]{1,0:T(8,128)(2,1)S(1...) custom-call(s32[4,8]{1,0:T(4,128)S(1)} %copy.30.order_ref, ...), custom_call_target="tpu_custom_call" | custom-call | flops 11811160064 | bytes 9586816 | tf_op jit(solution)/shard_map/attend_back/pallas_call | solution.py:66
  417.5 6.5 %collective-permute-done.54 = bf16[128,2048]{1,0:T(8,128)(2,1)S(1)} collective-permute-done((bf16[128,2048]{1,0:T(8,128)(2,1)S(1)}, bf16[128,2048]{1,0:T(8,128)(2,1)S(1)}, u32[]{:S(2)}, u32[]{:S(2)}) %collective-permute-start.54) | collective-permute-done | bytes 524320 | tf_op jit(solution)/shard_map/ppermute | solution.py:635
  424.6 8.2 %collective-permute-done.52.refs_11_.refs_8_ = bf16[128,2048]{1,0:T(8,128)(2,1)S(1)} collective-permute-done((bf16[128,2048]{1,0:T(8,128)(2,1)S(1)}, bf16[128,2048]{1,0:T(8,128)(2,1)S(1)}, u32[]{:S(2)}, u32[]{:S(2)}) %collective-permute-start.52) | collective-permute-done | bytes 524320 | tf_op jit(solution)/shard_map/ppermute | solution.py:635
  436.3 3.1 collective-permute-start.57
  439.4 2.6 add_convert_fusion.3
  442.1 4.8 out_gradient.2
  452.9 7.6 %attend_back.5 = (bf16[256,512]{1,0:T(8,128)(2,1)S(1)}, bf16[256,512]{1,0:T(8,128)(2,1)S(1)}, f32[256,128]{1,0:T(8,128)S(1)}, bf16[768,128]{1,0:T(8,128)(2,1)S(1)}) custom-call(s32[4,8]{1,0:T(4,128)S(1)} %copy.30.order_ref, bf16[512,2048]{1,0:T(8,128)(2,1)S(1)} %copy-done.41, bf16[4,256,128]{2,1,0:T(8,128)(2,1)S(1)} %copy-done.44, ...), custom_call_target="tpu_custom_call" | custom-call | flops 5905580032 | bytes 5842048 | tf_op jit(solution)/shard_map/attend_back/pallas_call | solution.py:66
  462.8 3.0 collective-permute-start.64
  465.7 2.9 collective-permute-start.69
  473.8 5.9 %collective-permute-done.63.refs_8_ = bf16[1,256,128]{2,1,0:T(8,128)(2,1)S(1)} collective-permute-done((bf16[1,256,128]{2,1,0:T(8,128)(2,1)S(1)}, bf16[1,256,128]{2,1,0:T(8,128)(2,1)S(1)}, u32[]{:S(2)}, u32[]{:S(2)}) %collective-permute-start.63) | collective-permute-done | bytes 65568 | tf_op jit(solution)/shard_map/ppermute | solution.py:641
  481.3 5.0 out_gradient.3
  486.3 2.4 collective-permute-done.62.refs_7_
  490.0 4.4 finish_keys.1
  494.4 5.8 convolution_convert_fusion.1
  503.4 4.8 weight_grad.6
  512.5 4.8 weight_grad.7
  517.4 5.2 collective-permute-done.71
  525.7 2.6 add_convert_fusion.1
  530.3 4.5 merge_gate_up.1
  534.8 3.9 finish_layer.1
  538.8 2.2 convert_add_fusion
  541.0 8.5 %collective-permute-done.76.refs_4_ = bf16[128,2048]{1,0:T(8,128)(2,1)} collective-permute-done((bf16[128,2048]{1,0:T(8,128)(2,1)}, bf16[128,2048]{1,0:T(8,128)(2,1)}, u32[]{:S(2)}, u32[]{:S(2)}) %collective-permute-start.76) | collective-permute-done | bytes 524320 | tf_op jit(solution)/shard_map/ppermute | solution.py:637
  550.6 5.8 %finish_norm_back.3 = f32[256,2048]{1,0:T(8,128)} custom-call(f32[256,2048]{1,0:T(8,128)} %get-tuple-element.437.g_ref, bf16[256,2048]{1,0:T(8,128)(2,1)} %x_ref.4, f32[256,1]{1,0:T(8,128)} %get-tuple-element.335.refs_9_.refs_18_.inv_ref, bf16[4,256,2048]{2,1,0:T(8,128)(2,1)} %bitcast.92, bf16[128,2048]{1,0:T(8,128)(2,1)} %collective-permute-done.70.refs_1_, ...), custom_call_target="tpu_custom_call" | custom-call | flops 11535360 | bytes 11535360 | tf_op jit(solution)/shard_map/finish_norm_back/pallas_call | solution.py:66
  561.6 2.2 collective-permute-done.79.refs_3_
  565.3 2.3 merge_qkv.1
  568.5 2.4 bitcast_add_fusion
  (436 shorter events, 139.6 us)
Async XLA Ops:
  7.2 63.9 %all-gather.7.cloned.1.call-start = ((), (), s32[]{:S(2)}) async-start(), calls=%async_computation.4 | async-start | bytes 2949120 | tf_op jit(solution)/shard_map/all_gather | solution.py:685
  24.5 90.5 %all-gather.5.cloned.1.call-start = ((), (), s32[]{:S(2)}) async-start(), calls=%async_computation.3 | async-start | bytes 2359296 | tf_op jit(solution)/shard_map/all_gather | solution.py:685
  31.0 186.2 %all-gather.11.cloned.1.call-start = ((), (), s32[]{:S(2)}) async-start(), calls=%async_computation.6 | async-start | bytes 12976128 | tf_op jit(solution)/shard_map/all_gather | solution.py:685
  39.7 15.1 %collective-permute-start.8 = (bf16[128,2048]{1,0:T(8,128)(2,1)}, bf16[128,2048]{1,0:T(8,128)(2,1)S(1)}, u32[]{:S(2)}, u32[]{:S(2)}) collective-permute-start(bf16[128,2048]{1,0:T(8,128)(2,1)} %get-tuple-element.260.refs_0_), channel_id=1, source_target_pairs={{0,16},{16,0},{1,17},{17,1},{2,18},{18,2},{3,19},{19,3},{4,20},{20... | collective-permute-start | bytes 1572872 | tf_op jit(solution)/shard_map/ppermute | solution.py:637
  41.5 22.4 %collective-permute-start.11 = (bf16[128,2048]{1,0:T(8,128)(2,1)S(1)}, bf16[128,2048]{1,0:T(8,128)(2,1)S(1)}, u32[]{:S(2)}, u32[]{:S(2)}) collective-permute-start(bf16[128,2048]{1,0:T(8,128)(2,1)S(1)} %collective-permute-done.7.refs_5_), channel_id=1, source_target_pairs={{0,8},{8,0},{1,9},{9,1},{2,10},{10,2},{3,11},{11,3},{4,12},{12,4},... | collective-permute-start | bytes 1572872 | tf_op jit(solution)/shard_map/ppermute | solution.py:635
  42.8 21.1 %collective-permute-start.10 = (bf16[128,2048]{1,0:T(8,128)(2,1)S(1)}, bf16[128,2048]{1,0:T(8,128)(2,1)}, u32[]{:S(2)}, u32[]{:S(2)}) collective-permute-start(bf16[128,2048]{1,0:T(8,128)(2,1)S(1)} %collective-permute-done.6.refs_2_), channel_id=1, source_target_pairs={{0,16},{16,0},{1,17},{17,1},{2,18},{18,2},{3,19},{19,3},{4,20},{20... | collective-permute-start | bytes 1572872 | tf_op jit(solution)/shard_map/ppermute | solution.py:637
  66.4 16.0 %collective-permute-start.17 = (bf16[1,64,2816]{2,1,0:T(8,128)(2,1)}, bf16[1,64,2816]{2,1,0:T(8,128)(2,1)S(1)}, u32[]{:S(2)}, u32[]{:S(2)}) collective-permute-start(bf16[1,64,2816]{2,1,0:T(8,128)(2,1)} %get-tuple-element.481), channel_id=1, source_target_pairs={{0,24},{8,16},{16,8},{24,0},{1,25},{9,17},{17,9},{25,1},{2,26},{10... | collective-permute-start | bytes 1081352 | tf_op jit(solution)/shard_map/ppermute | solution.py:638
  67.8 15.3 %collective-permute-start.16 = (bf16[1,64,2816]{2,1,0:T(8,128)(2,1)}, bf16[1,64,2816]{2,1,0:T(8,128)(2,1)}, u32[]{:S(2)}, u32[]{:S(2)}) collective-permute-start(bf16[1,64,2816]{2,1,0:T(8,128)(2,1)} %get-tuple-element.482), channel_id=1, source_target_pairs={{0,16},{16,0},{1,17},{17,1},{2,18},{18,2},{3,19},{19,3},{4,20},{20... | collective-permute-start | bytes 1081352 | tf_op jit(solution)/shard_map/ppermute | solution.py:637
  78.7 16.7 %collective-permute-start.14 = (bf16[4,256,128]{2,1,0:T(8,128)(2,1)}, bf16[4,256,128]{2,1,0:T(8,128)(2,1)S(1)}, u32[]{:S(2)}, u32[]{:S(2)}) collective-permute-start(bf16[4,256,128]{2,1,0:T(8,128)(2,1)} %get-tuple-element.268.refs_1_.refs_6_.refs_0_.refs_12_), channel_id=1, source_target_pairs={{0,3},{1,2},{2,1},{3,0},{4,7},{5,6},{6,5},{7,4},{8,11},{9,10},{10,... | collective-permute-start | bytes 786440 | tf_op jit(solution)/shard_map/ppermute | solution.py:641
  82.4 27.7 %collective-permute-start.13 = (bf16[4,256,128]{2,1,0:T(8,128)(2,1)}, bf16[4,256,128]{2,1,0:T(8,128)(2,1)S(1)}, u32[]{:S(2)}, u32[]{:S(2)}) collective-permute-start(bf16[4,256,128]{2,1,0:T(8,128)(2,1)} %get-tuple-element.268.refs_1_.refs_6_.refs_0_.refs_12_), channel_id=1, source_target_pairs={{0,2},{1,3},{2,0},{3,1},{4,6},{5,7},{6,4},{7,5},{8,10},{9,11},{10,... | collective-permute-start | bytes 786440 | tf_op jit(solution)/shard_map/ppermute | solution.py:641
  82.4 27.7 %collective-permute-start.12 = (bf16[4,256,128]{2,1,0:T(8,128)(2,1)}, bf16[4,256,128]{2,1,0:T(8,128)(2,1)S(1)}, u32[]{:S(2)}, u32[]{:S(2)}) collective-permute-start(bf16[4,256,128]{2,1,0:T(8,128)(2,1)} %get-tuple-element.268.refs_1_.refs_6_.refs_0_.refs_12_), channel_id=1, source_target_pairs={{0,1},{1,0},{2,3},{3,2},{4,5},{5,4},{6,7},{7,6},{8,9},{9,8},{10,11... | collective-permute-start | bytes 786440 | tf_op jit(solution)/shard_map/ppermute | solution.py:641
  84.3 25.8 %collective-permute-start.19 = (bf16[128,2048]{1,0:T(8,128)(2,1)}, bf16[128,2048]{1,0:T(8,128)(2,1)}, u32[]{:S(2)}, u32[]{:S(2)}) collective-permute-start(bf16[128,2048]{1,0:T(8,128)(2,1)} %get-tuple-element.487.refs_1_), channel_id=1, source_target_pairs={{0,16},{16,0},{1,17},{17,1},{2,18},{18,2},{3,19},{19,3},{4,20},{20... | collective-permute-start | bytes 1572872 | tf_op jit(solution)/shard_map/ppermute | solution.py:637
  85.1 25.0 %collective-permute-start.18 = (bf16[128,2048]{1,0:T(8,128)(2,1)}, bf16[128,2048]{1,0:T(8,128)(2,1)}, u32[]{:S(2)}, u32[]{:S(2)}) collective-permute-start(bf16[128,2048]{1,0:T(8,128)(2,1)} %get-tuple-element.488.refs_0_), channel_id=1, source_target_pairs={{0,8},{8,0},{1,9},{9,1},{2,10},{10,2},{3,11},{11,3},{4,12},{12,4},... | collective-permute-start | bytes 1572872 | tf_op jit(solution)/shard_map/ppermute | solution.py:635
  110.1 167.3 %all-gather.9.cloned.1.call-start = ((), (), s32[]{:S(2)}) async-start(), calls=%async_computation.5 | async-start | bytes 6488064 | tf_op jit(solution)/shard_map/all_gather | solution.py:685
  110.7 358.0 %reduce-scatter.4.cloned.1.call-start = ((), (), s32[]{:S(2)}) async-start(), calls=%async_computation.7 | async-start | bytes 7208960 | tf_op jit(solution)/shard_map/reduce_scatter | solution.py:711
  111.0 15.2 %collective-permute-start.23 = (bf16[128,2048]{1,0:T(8,128)(2,1)}, bf16[128,2048]{1,0:T(8,128)(2,1)}, u32[]{:S(2)}, u32[]{:S(2)}) collective-permute-start(bf16[128,2048]{1,0:T(8,128)(2,1)} %get-tuple-element.487.refs_1_), channel_id=1, source_target_pairs={{0,8},{8,0},{1,9},{9,1},{2,10},{10,2},{3,11},{11,3},{4,12},{12,4},... | collective-permute-start | bytes 1572872 | tf_op jit(solution)/shard_map/ppermute | solution.py:635
  112.5 15.2 %collective-permute-start.22 = (bf16[128,2048]{1,0:T(8,128)(2,1)}, bf16[128,2048]{1,0:T(8,128)(2,1)}, u32[]{:S(2)}, u32[]{:S(2)}) collective-permute-start(bf16[128,2048]{1,0:T(8,128)(2,1)} %get-tuple-element.488.refs_0_), channel_id=1, source_target_pairs={{0,16},{16,0},{1,17},{17,1},{2,18},{18,2},{3,19},{19,3},{4,20},{20... | collective-permute-start | bytes 1572872 | tf_op jit(solution)/shard_map/ppermute | solution.py:637
  114.0 26.8 %collective-permute-start.24 = (bf16[128,2048]{1,0:T(8,128)(2,1)}, bf16[128,2048]{1,0:T(8,128)(2,1)}, u32[]{:S(2)}, u32[]{:S(2)}) collective-permute-start(bf16[128,2048]{1,0:T(8,128)(2,1)} %collective-permute-done.18.refs_2_), channel_id=1, source_target_pairs={{0,16},{16,0},{1,17},{17,1},{2,18},{18,2},{3,19},{19,3},{4,20},{20... | collective-permute-start | bytes 1572872 | tf_op jit(solution)/shard_map/ppermute | solution.py:637
  114.5 26.3 %collective-permute-start.25 = (bf16[128,2048]{1,0:T(8,128)(2,1)}, bf16[128,2048]{1,0:T(8,128)(2,1)}, u32[]{:S(2)}, u32[]{:S(2)}) collective-permute-start(bf16[128,2048]{1,0:T(8,128)(2,1)} %collective-permute-done.19.refs_5_), channel_id=1, source_target_pairs={{0,8},{8,0},{1,9},{9,1},{2,10},{10,2},{3,11},{11,3},{4,12},{12,4},... | collective-permute-start | bytes 1572872 | tf_op jit(solution)/shard_map/ppermute | solution.py:635
  123.7 23.4 %collective-permute-start.21 = (bf16[128,2048]{1,0:T(8,128)(2,1)S(1)}, bf16[128,2048]{1,0:T(8,128)(2,1)S(1)}, u32[]{:S(2)}, u32[]{:S(2)}) collective-permute-start(bf16[128,2048]{1,0:T(8,128)(2,1)S(1)} %get-tuple-element.485), channel_id=1, source_target_pairs={{0,8},{8,0},{1,9},{9,1},{2,10},{10,2},{3,11},{11,3},{4,12},{12,4},... | collective-permute-start | bytes 1572872 | tf_op jit(solution)/shard_map/ppermute | solution.py:635
  126.2 22.1 %collective-permute-start.20 = (bf16[128,2048]{1,0:T(8,128)(2,1)S(1)}, bf16[128,2048]{1,0:T(8,128)(2,1)S(1)}, u32[]{:S(2)}, u32[]{:S(2)}) collective-permute-start(bf16[128,2048]{1,0:T(8,128)(2,1)S(1)} %get-tuple-element.486), channel_id=1, source_target_pairs={{0,16},{16,0},{1,17},{17,1},{2,18},{18,2},{3,19},{19,3},{4,20},{20... | collective-permute-start | bytes 1572872 | tf_op jit(solution)/shard_map/ppermute | solution.py:637
  151.8 17.9 %collective-permute-start.26 = (bf16[128,2048]{1,0:T(8,128)(2,1)}, bf16[128,2048]{1,0:T(8,128)(2,1)}, u32[]{:S(2)}, u32[]{:S(2)}) collective-permute-start(bf16[128,2048]{1,0:T(8,128)(2,1)} %slice.167), channel_id=1, source_target_pairs={{0,16},{16,0},{1,17},{17,1},{2,18},{18,2},{3,19},{19,3},{4,20},{20... | collective-permute-start | bytes 1572872 | tf_op jit(solution)/shard_map/ppermute | solution.py:637
  153.3 22.4 %collective-permute-start.29 = (bf16[128,2048]{1,0:T(8,128)(2,1)}, bf16[128,2048]{1,0:T(8,128)(2,1)}, u32[]{:S(2)}, u32[]{:S(2)}) collective-permute-start(bf16[128,2048]{1,0:T(8,128)(2,1)} %add_convert_fusion.7), channel_id=1, source_target_pairs={{0,16},{16,0},{1,17},{17,1},{2,18},{18,2},{3,19},{19,3},{4,20},{20... | collective-permute-start | bytes 1572872 | tf_op jit(solution)/shard_map/ppermute | solution.py:637
  153.8 21.8 %collective-permute-start.28 = (bf16[128,2048]{1,0:T(8,128)(2,1)}, bf16[128,2048]{1,0:T(8,128)(2,1)}, u32[]{:S(2)}, u32[]{:S(2)}) collective-permute-start(bf16[128,2048]{1,0:T(8,128)(2,1)} %slice.169), channel_id=1, source_target_pairs={{0,8},{8,0},{1,9},{9,1},{2,10},{10,2},{3,11},{11,3},{4,12},{12,4},... | collective-permute-start | bytes 1572872 | tf_op jit(solution)/shard_map/ppermute | solution.py:635
  154.4 22.7 %collective-permute-start.27 = (bf16[128,2048]{1,0:T(8,128)(2,1)}, bf16[128,2048]{1,0:T(8,128)(2,1)}, u32[]{:S(2)}, u32[]{:S(2)}) collective-permute-start(bf16[128,2048]{1,0:T(8,128)(2,1)} %add_convert_fusion.8), channel_id=1, source_target_pairs={{0,8},{8,0},{1,9},{9,1},{2,10},{10,2},{3,11},{11,3},{4,12},{12,4},... | collective-permute-start | bytes 1572872 | tf_op jit(solution)/shard_map/ppermute | solution.py:635
  182.2 15.1 %collective-permute-start.30 = (bf16[128,2048]{1,0:T(8,128)(2,1)}, bf16[128,2048]{1,0:T(8,128)(2,1)S(1)}, u32[]{:S(2)}, u32[]{:S(2)}) collective-permute-start(bf16[128,2048]{1,0:T(8,128)(2,1)} %get-tuple-element.307.refs_0_), channel_id=1, source_target_pairs={{0,8},{8,0},{1,9},{9,1},{2,10},{10,2},{3,11},{11,3},{4,12},{12,4},... | collective-permute-start | bytes 1572872 | tf_op jit(solution)/shard_map/ppermute | solution.py:635
  182.8 15.9 %collective-permute-start.33 = (bf16[128,2048]{1,0:T(8,128)(2,1)}, bf16[128,2048]{1,0:T(8,128)(2,1)S(1)}, u32[]{:S(2)}, u32[]{:S(2)}) collective-permute-start(bf16[128,2048]{1,0:T(8,128)(2,1)} %get-tuple-element.308.refs_1_), channel_id=1, source_target_pairs={{0,16},{16,0},{1,17},{17,1},{2,18},{18,2},{3,19},{19,3},{4,20},{20... | collective-permute-start | bytes 1572872 | tf_op jit(solution)/shard_map/ppermute | solution.py:637
  184.2 24.9 %collective-permute-start.32 = (bf16[128,2048]{1,0:T(8,128)(2,1)}, bf16[128,2048]{1,0:T(8,128)(2,1)S(1)}, u32[]{:S(2)}, u32[]{:S(2)}) collective-permute-start(bf16[128,2048]{1,0:T(8,128)(2,1)} %get-tuple-element.307.refs_0_), channel_id=1, source_target_pairs={{0,16},{16,0},{1,17},{17,1},{2,18},{18,2},{3,19},{19,3},{4,20},{20... | collective-permute-start | bytes 1572872 | tf_op jit(solution)/shard_map/ppermute | solution.py:637
  184.8 24.3 %collective-permute-start.31 = (bf16[128,2048]{1,0:T(8,128)(2,1)}, bf16[128,2048]{1,0:T(8,128)(2,1)S(1)}, u32[]{:S(2)}, u32[]{:S(2)}) collective-permute-start(bf16[128,2048]{1,0:T(8,128)(2,1)} %get-tuple-element.308.refs_1_), channel_id=1, source_target_pairs={{0,8},{8,0},{1,9},{9,1},{2,10},{10,2},{3,11},{11,3},{4,12},{12,4},... | collective-permute-start | bytes 1572872 | tf_op jit(solution)/shard_map/ppermute | solution.py:635
  197.3 18.7 %collective-permute-start.34 = (bf16[128,2048]{1,0:T(8,128)(2,1)S(1)}, bf16[128,2048]{1,0:T(8,128)(2,1)S(1)}, u32[]{:S(2)}, u32[]{:S(2)}) collective-permute-start(bf16[128,2048]{1,0:T(8,128)(2,1)S(1)} %collective-permute-done.30.refs_2_), channel_id=1, source_target_pairs={{0,16},{16,0},{1,17},{17,1},{2,18},{18,2},{3,19},{19,3},{4,20},{20... | collective-permute-start | bytes 1572872 | tf_op jit(solution)/shard_map/ppermute | solution.py:637
  198.7 17.2 %collective-permute-start.35 = (bf16[128,2048]{1,0:T(8,128)(2,1)S(1)}, bf16[128,2048]{1,0:T(8,128)(2,1)S(1)}, u32[]{:S(2)}, u32[]{:S(2)}) collective-permute-start(bf16[128,2048]{1,0:T(8,128)(2,1)S(1)} %collective-permute-done.33.refs_5_), channel_id=1, source_target_pairs={{0,8},{8,0},{1,9},{9,1},{2,10},{10,2},{3,11},{11,3},{4,12},{12,4},... | collective-permute-start | bytes 1572872 | tf_op jit(solution)/shard_map/ppermute | solution.py:635
  277.4 25.4 %collective-permute-start.37 = (bf16[352,512]{1,0:T(8,128)(2,1)S(1)}, bf16[352,512]{1,0:T(8,128)(2,1)S(1)}, u32[]{:S(2)}, u32[]{:S(2)}) collective-permute-start(bf16[352,512]{1,0:T(8,128)(2,1)S(1)} %get-tuple-element.318), channel_id=1, source_target_pairs={{0,2},{1,3},{2,0},{3,1},{4,6},{5,7},{6,4},{7,5},{8,10},{9,11},{10,... | collective-permute-start | bytes 1081352 | tf_op jit(solution)/shard_map/ppermute | solution.py:641
  302.8 24.9 %collective-permute-start.41 = (bf16[1024,2816]{1,0:T(8,128)(2,1)}, bf16[1024,2816]{1,0:T(8,128)(2,1)}, u32[]{:S(2)}, u32[]{:S(2)}) collective-permute-start(bf16[1024,2816]{1,0:T(8,128)(2,1)} %weight_grad.4), channel_id=1, source_target_pairs={{0,4},{4,0},{1,5},{5,1},{2,6},{6,2},{3,7},{7,3},{8,12},{12,8},{9,1... | collective-permute-start | bytes 17301512 | tf_op jit(solution)/shard_map/ppermute | solution.py:701
  302.9 37.6 %collective-permute-start.42 = (bf16[352,512]{1,0:T(8,128)(2,1)}, bf16[352,512]{1,0:T(8,128)(2,1)S(1)}, u32[]{:S(2)}, u32[]{:S(2)}) collective-permute-start(bf16[352,512]{1,0:T(8,128)(2,1)} %get-tuple-element.322), channel_id=1, source_target_pairs={{0,2},{1,3},{2,0},{3,1},{4,6},{5,7},{6,4},{7,5},{8,10},{9,11},{10,... | collective-permute-start | bytes 1081352 | tf_op jit(solution)/shard_map/ppermute | solution.py:641
  321.6 18.9 %collective-permute-start.43 = (bf16[352,512]{1,0:T(8,128)(2,1)S(1)}, bf16[352,512]{1,0:T(8,128)(2,1)S(1)}, u32[]{:S(2)}, u32[]{:S(2)}) collective-permute-start(bf16[352,512]{1,0:T(8,128)(2,1)S(1)} %get-tuple-element.323), channel_id=1, source_target_pairs={{0,2},{1,3},{2,0},{3,1},{4,6},{5,7},{6,4},{7,5},{8,10},{9,11},{10,... | collective-permute-start | bytes 1081352 | tf_op jit(solution)/shard_map/ppermute | solution.py:641
  324.7 15.8 %collective-permute-start.40 = (bf16[128,2048]{1,0:T(8,128)(2,1)S(1)}, bf16[128,2048]{1,0:T(8,128)(2,1)S(1)}, u32[]{:S(2)}, u32[]{:S(2)}) collective-permute-start(bf16[128,2048]{1,0:T(8,128)(2,1)S(1)} %get-tuple-element.470), channel_id=1, source_target_pairs={{0,8},{8,0},{1,9},{9,1},{2,10},{10,2},{3,11},{11,3},{4,12},{12,4},... | collective-permute-start | bytes 1572872 | tf_op jit(solution)/shard_map/ppermute | solution.py:635
  341.8 181.8 %reduce-scatter.6.cloned.1.call-start = ((), (), s32[]{:S(2)}) async-start(), calls=%async_computation.8 | async-start | bytes 1310720 | tf_op jit(solution)/shard_map/reduce_scatter | solution.py:711
  341.8 17.5 %collective-permute-start.45 = (bf16[128,2048]{1,0:T(8,128)(2,1)}, bf16[128,2048]{1,0:T(8,128)(2,1)S(1)}, u32[]{:S(2)}, u32[]{:S(2)}) collective-permute-start(bf16[128,2048]{1,0:T(8,128)(2,1)} %get-tuple-element.469), channel_id=1, source_target_pairs={{0,8},{8,0},{1,9},{9,1},{2,10},{10,2},{3,11},{11,3},{4,12},{12,4},... | collective-permute-start | bytes 1572872 | tf_op jit(solution)/shard_map/ppermute | solution.py:635
  342.5 16.9 %collective-permute-start.38 = (bf16[128,2048]{1,0:T(8,128)(2,1)}, bf16[128,2048]{1,0:T(8,128)(2,1)}, u32[]{:S(2)}, u32[]{:S(2)}) collective-permute-start(bf16[128,2048]{1,0:T(8,128)(2,1)} %get-tuple-element.472), channel_id=1, source_target_pairs={{0,16},{16,0},{1,17},{17,1},{2,18},{18,2},{3,19},{19,3},{4,20},{20... | collective-permute-start | bytes 1572872 | tf_op jit(solution)/shard_map/ppermute | solution.py:637
  345.8 21.8 %collective-permute-start.46 = (bf16[128,2048]{1,0:T(8,128)(2,1)S(1)}, bf16[128,2048]{1,0:T(8,128)(2,1)}, u32[]{:S(2)}, u32[]{:S(2)}) collective-permute-start(bf16[128,2048]{1,0:T(8,128)(2,1)S(1)} %get-tuple-element.467), channel_id=1, source_target_pairs={{0,16},{16,0},{1,17},{17,1},{2,18},{18,2},{3,19},{19,3},{4,20},{20... | collective-permute-start | bytes 1572872 | tf_op jit(solution)/shard_map/ppermute | solution.py:637
  346.5 21.1 %collective-permute-start.44 = (bf16[128,2048]{1,0:T(8,128)(2,1)S(1)}, bf16[128,2048]{1,0:T(8,128)(2,1)}, u32[]{:S(2)}, u32[]{:S(2)}) collective-permute-start(bf16[128,2048]{1,0:T(8,128)(2,1)S(1)} %get-tuple-element.468), channel_id=1, source_target_pairs={{0,8},{8,0},{1,9},{9,1},{2,10},{10,2},{3,11},{11,3},{4,12},{12,4},... | collective-permute-start | bytes 1572872 | tf_op jit(solution)/shard_map/ppermute | solution.py:635
  373.7 21.2 %collective-permute-start.49 = (bf16[128,2048]{1,0:T(8,128)(2,1)}, bf16[128,2048]{1,0:T(8,128)(2,1)S(1)}, u32[]{:S(2)}, u32[]{:S(2)}) collective-permute-start(bf16[128,2048]{1,0:T(8,128)(2,1)} %get-tuple-element.385.refs_7_.refs_4_), channel_id=1, source_target_pairs={{0,16},{16,0},{1,17},{17,1},{2,18},{18,2},{3,19},{19,3},{4,20},{20... | collective-permute-start | bytes 1572872 | tf_op jit(solution)/shard_map/ppermute | solution.py:637
  375.2 20.7 %collective-permute-start.47 = (bf16[128,2048]{1,0:T(8,128)(2,1)}, bf16[128,2048]{1,0:T(8,128)(2,1)S(1)}, u32[]{:S(2)}, u32[]{:S(2)}) collective-permute-start(bf16[128,2048]{1,0:T(8,128)(2,1)} %get-tuple-element.385.refs_7_.refs_4_), channel_id=1, source_target_pairs={{0,8},{8,0},{1,9},{9,1},{2,10},{10,2},{3,11},{11,3},{4,12},{12,4},... | collective-permute-start | bytes 1572872 | tf_op jit(solution)/shard_map/ppermute | solution.py:635
  375.8 25.7 %collective-permute-start.50 = (bf16[128,2048]{1,0:T(8,128)(2,1)}, bf16[128,2048]{1,0:T(8,128)(2,1)S(1)}, u32[]{:S(2)}, u32[]{:S(2)}) collective-permute-start(bf16[128,2048]{1,0:T(8,128)(2,1)} %get-tuple-element.386.refs_8_.refs_5_), channel_id=1, source_target_pairs={{0,8},{8,0},{1,9},{9,1},{2,10},{10,2},{3,11},{11,3},{4,12},{12,4},... | collective-permute-start | bytes 1572872 | tf_op jit(solution)/shard_map/ppermute | solution.py:635
  377.2 24.3 %collective-permute-start.48 = (bf16[128,2048]{1,0:T(8,128)(2,1)}, bf16[128,2048]{1,0:T(8,128)(2,1)S(1)}, u32[]{:S(2)}, u32[]{:S(2)}) collective-permute-start(bf16[128,2048]{1,0:T(8,128)(2,1)} %get-tuple-element.386.refs_8_.refs_5_), channel_id=1, source_target_pairs={{0,16},{16,0},{1,17},{17,1},{2,18},{18,2},{3,19},{19,3},{4,20},{20... | collective-permute-start | bytes 1572872 | tf_op jit(solution)/shard_map/ppermute | solution.py:637
  380.5 66.4 %collective-permute-start.60 = (bf16[128,2048]{1,0:T(8,128)(2,1)}, bf16[128,2048]{1,0:T(8,128)(2,1)S(1)}, u32[]{:S(2)}, u32[]{:S(2)}) collective-permute-start(bf16[128,2048]{1,0:T(8,128)(2,1)} %get-tuple-element.463), channel_id=1, source_target_pairs={{0,8},{8,0},{1,9},{9,1},{2,10},{10,2},{3,11},{11,3},{4,12},{12,4},... | collective-permute-start | bytes 1572872 | tf_op jit(solution)/shard_map/ppermute | solution.py:635
  394.9 29.1 %collective-permute-start.54 = (bf16[128,2048]{1,0:T(8,128)(2,1)S(1)}, bf16[128,2048]{1,0:T(8,128)(2,1)S(1)}, u32[]{:S(2)}, u32[]{:S(2)}) collective-permute-start(bf16[128,2048]{1,0:T(8,128)(2,1)S(1)} %get-tuple-element.465), channel_id=1, source_target_pairs={{0,8},{8,0},{1,9},{9,1},{2,10},{10,2},{3,11},{11,3},{4,12},{12,4},... | collective-permute-start | bytes 1572872 | tf_op jit(solution)/shard_map/ppermute | solution.py:635
  395.9 28.6 %collective-permute-start.53 = (bf16[128,2048]{1,0:T(8,128)(2,1)S(1)}, bf16[128,2048]{1,0:T(8,128)(2,1)S(1)}, u32[]{:S(2)}, u32[]{:S(2)}) collective-permute-start(bf16[128,2048]{1,0:T(8,128)(2,1)S(1)} %get-tuple-element.466), channel_id=1, source_target_pairs={{0,16},{16,0},{1,17},{17,1},{2,18},{18,2},{3,19},{19,3},{4,20},{20... | collective-permute-start | bytes 1572872 | tf_op jit(solution)/shard_map/ppermute | solution.py:637
  401.5 23.0 %collective-permute-start.51 = (bf16[128,2048]{1,0:T(8,128)(2,1)S(1)}, bf16[128,2048]{1,0:T(8,128)(2,1)S(1)}, u32[]{:S(2)}, u32[]{:S(2)}) collective-permute-start(bf16[128,2048]{1,0:T(8,128)(2,1)S(1)} %collective-permute-done.47.refs_7_.refs_6_), channel_id=1, source_target_pairs={{0,16},{16,0},{1,17},{17,1},{2,18},{18,2},{3,19},{19,3},{4,20},{20... | collective-permute-start | bytes 1572872 | tf_op jit(solution)/shard_map/ppermute | solution.py:637
  402.1 30.6 %collective-permute-start.52 = (bf16[128,2048]{1,0:T(8,128)(2,1)S(1)}, bf16[128,2048]{1,0:T(8,128)(2,1)S(1)}, u32[]{:S(2)}, u32[]{:S(2)}) collective-permute-start(bf16[128,2048]{1,0:T(8,128)(2,1)S(1)} %collective-permute-done.48.refs_20_.refs_9_), channel_id=1, source_target_pairs={{0,8},{8,0},{1,9},{9,1},{2,10},{10,2},{3,11},{11,3},{4,12},{12,4},... | collective-permute-start | bytes 1572872 | tf_op jit(solution)/shard_map/ppermute | solution.py:635
  424.0 23.6 %collective-permute-start.58 = (bf16[128,2048]{1,0:T(8,128)(2,1)}, bf16[128,2048]{1,0:T(8,128)(2,1)}, u32[]{:S(2)}, u32[]{:S(2)}) collective-permute-start(bf16[128,2048]{1,0:T(8,128)(2,1)} %get-tuple-element.464), channel_id=1, source_target_pairs={{0,16},{16,0},{1,17},{17,1},{2,18},{18,2},{3,19},{19,3},{4,20},{20... | collective-permute-start | bytes 1572872 | tf_op jit(solution)/shard_map/ppermute | solution.py:637
  433.6 15.5 %collective-permute-start.55 = (bf16[3,256,128]{2,1,0:T(8,128)(2,1)}, bf16[3,256,128]{2,1,0:T(8,128)(2,1)S(1)}, u32[]{:S(2)}, u32[]{:S(2)}) collective-permute-start(bf16[3,256,128]{2,1,0:T(8,128)(2,1)} %pad_maximum_fusion), channel_id=1, source_target_pairs={{0,1},{1,0},{2,3},{3,2},{4,5},{5,4},{6,7},{7,6},{8,9},{9,8},{10,11... | collective-permute-start | bytes 589832 | tf_op jit(solution)/shard_map/ppermute | solution.py:641
  434.3 27.6 %collective-permute-start.56 = (bf16[3,256,128]{2,1,0:T(8,128)(2,1)}, bf16[3,256,128]{2,1,0:T(8,128)(2,1)}, u32[]{:S(2)}, u32[]{:S(2)}) collective-permute-start(bf16[3,256,128]{2,1,0:T(8,128)(2,1)} %pad_maximum_fusion.1), channel_id=1, source_target_pairs={{0,2},{1,3},{2,0},{3,1},{4,6},{5,7},{6,4},{7,5},{8,10},{9,11},{10,... | collective-permute-start | bytes 589832 | tf_op jit(solution)/shard_map/ppermute | solution.py:641
  436.3 25.6 %collective-permute-start.57 = (bf16[3,256,128]{2,1,0:T(8,128)(2,1)}, bf16[3,256,128]{2,1,0:T(8,128)(2,1)}, u32[]{:S(2)}, u32[]{:S(2)}) collective-permute-start(bf16[3,256,128]{2,1,0:T(8,128)(2,1)} %pad_maximum_fusion.2), channel_id=1, source_target_pairs={{0,3},{1,2},{2,1},{3,0},{4,7},{5,6},{6,5},{7,4},{8,11},{9,10},{10,... | collective-permute-start | bytes 589832 | tf_op jit(solution)/shard_map/ppermute | solution.py:641
  449.1 31.9 %collective-permute-start.65 = (bf16[256,2048]{1,0:T(8,128)(2,1)}, bf16[256,2048]{1,0:T(8,128)(2,1)}, u32[]{:S(2)}, u32[]{:S(2)}) collective-permute-start(bf16[256,2048]{1,0:T(8,128)(2,1)} %out_gradient.2), channel_id=1, source_target_pairs={{0,4},{4,0},{1,5},{5,1},{2,6},{6,2},{3,7},{7,3},{8,12},{12,8},{9,1... | collective-permute-start | bytes 3145736 | tf_op jit(solution)/shard_map/ppermute | solution.py:865
  465.7 23.0 %collective-permute-start.69 = (bf16[352,512]{1,0:T(8,128)(2,1)}, bf16[352,512]{1,0:T(8,128)(2,1)S(1)}, u32[]{:S(2)}, u32[]{:S(2)}) collective-permute-start(bf16[352,512]{1,0:T(8,128)(2,1)} %get-tuple-element.396), channel_id=1, source_target_pairs={{0,2},{1,3},{2,0},{3,1},{4,6},{5,7},{6,4},{7,5},{8,10},{9,11},{10,... | collective-permute-start | bytes 1081352 | tf_op jit(solution)/shard_map/ppermute | solution.py:641
  470.8 17.9 %collective-permute-start.68 = (bf16[64,2816]{1,0:T(8,128)(2,1)S(1)}, bf16[64,2816]{1,0:T(8,128)(2,1)S(1)}, u32[]{:S(2)}, u32[]{:S(2)}) collective-permute-start(bf16[64,2816]{1,0:T(8,128)(2,1)S(1)} %get-tuple-element.477), channel_id=1, source_target_pairs={{0,24},{8,16},{16,8},{24,0},{1,25},{9,17},{17,9},{25,1},{2,26},{10... | collective-permute-start | bytes 1081352 | tf_op jit(solution)/shard_map/ppermute | solution.py:638
  472.9 16.5 %collective-permute-start.67 = (bf16[64,2816]{1,0:T(8,128)(2,1)S(1)}, bf16[64,2816]{1,0:T(8,128)(2,1)S(1)}, u32[]{:S(2)}, u32[]{:S(2)}) collective-permute-start(bf16[64,2816]{1,0:T(8,128)(2,1)S(1)} %get-tuple-element.478), channel_id=1, source_target_pairs={{0,16},{16,0},{1,17},{17,1},{2,18},{18,2},{3,19},{19,3},{4,20},{20... | collective-permute-start | bytes 1081352 | tf_op jit(solution)/shard_map/ppermute | solution.py:637
  490.0 66.4 %reduce-scatter.8.cloned.1.call-start = ((), (), s32[]{:S(2)}) async-start(), calls=%async_computation.9 | async-start | bytes 1638400 | tf_op jit(solution)/shard_map/reduce_scatter | solution.py:711
  523.6 17.4 %collective-permute-start.75 = (bf16[128,2048]{1,0:T(8,128)(2,1)}, bf16[128,2048]{1,0:T(8,128)(2,1)S(1)}, u32[]{:S(2)}, u32[]{:S(2)}) collective-permute-start(bf16[128,2048]{1,0:T(8,128)(2,1)} %get-tuple-element.457), channel_id=1, source_target_pairs={{0,8},{8,0},{1,9},{9,1},{2,10},{10,2},{3,11},{11,3},{4,12},{12,4},... | collective-permute-start | bytes 1572872 | tf_op jit(solution)/shard_map/ppermute | solution.py:635
  524.9 16.0 %collective-permute-start.70 = (bf16[128,2048]{1,0:T(8,128)(2,1)}, bf16[128,2048]{1,0:T(8,128)(2,1)}, u32[]{:S(2)}, u32[]{:S(2)}) collective-permute-start(bf16[128,2048]{1,0:T(8,128)(2,1)} %get-tuple-element.460), channel_id=1, source_target_pairs={{0,16},{16,0},{1,17},{17,1},{2,18},{18,2},{3,19},{19,3},{4,20},{20... | collective-permute-start | bytes 1572872 | tf_op jit(solution)/shard_map/ppermute | solution.py:637
  528.3 21.1 %collective-permute-start.76 = (bf16[128,2048]{1,0:T(8,128)(2,1)}, bf16[128,2048]{1,0:T(8,128)(2,1)}, u32[]{:S(2)}, u32[]{:S(2)}) collective-permute-start(bf16[128,2048]{1,0:T(8,128)(2,1)} %get-tuple-element.455), channel_id=1, source_target_pairs={{0,16},{16,0},{1,17},{17,1},{2,18},{18,2},{3,19},{19,3},{4,20},{20... | collective-permute-start | bytes 1572872 | tf_op jit(solution)/shard_map/ppermute | solution.py:637
  529.5 19.9 %collective-permute-start.74 = (bf16[128,2048]{1,0:T(8,128)(2,1)}, bf16[128,2048]{1,0:T(8,128)(2,1)}, u32[]{:S(2)}, u32[]{:S(2)}) collective-permute-start(bf16[128,2048]{1,0:T(8,128)(2,1)} %get-tuple-element.456), channel_id=1, source_target_pairs={{0,8},{8,0},{1,9},{9,1},{2,10},{10,2},{3,11},{11,3},{4,12},{12,4},... | collective-permute-start | bytes 1572872 | tf_op jit(solution)/shard_map/ppermute | solution.py:635
  550.6 18.0 %collective-permute-start.80 = (bf16[176,2048]{1,0:T(8,128)(2,1)}, bf16[176,2048]{1,0:T(8,128)(2,1)}, u32[]{:S(2)}, u32[]{:S(2)}) collective-permute-start(bf16[176,2048]{1,0:T(8,128)(2,1)} %dynamic-slice_bitcast_fusion.1), channel_id=1, source_target_pairs={{0,1},{1,0},{2,3},{3,2},{4,5},{5,4},{6,7},{7,6},{8,9},{9,8},{10,11... | collective-permute-start | bytes 2162696 | tf_op jit(solution)/shard_map/ppermute | solution.py:641
  (139 other events, 1740.0 us)
Sparse Core Ops, SparseCore 0:
  24.7 34.1 all-gather.6
  60.4 43.7 all-gather.4
  110.2 106.9 all-gather.10
  218.6 58.7 all-gather.8
  341.9 105.8 reduce-scatter.3
  490.1 26.9 reduce-scatter.5
  523.7 30.3 reduce-scatter.7
